TPU v7x, 128 devices: a whole 4x4x4 slice. The times are simulated.
128 devices in a mesh: gy: 8 (over x_lo, z), gz: 16 (over y, x_hi, core).
Axes of the slice: x: 4 (x_hi: 2, x_lo: 2; x = x_hi * 2 + x_lo), y: 4, z: 4, core: 2. Of those that a mesh axis runs over, the one named last changes fastest.
Arguments:
- universe: bfloat16 [4, 64, 128, 128], P(None, 'gy', 'gz'), may hold values from -6 to 6
- kernel1: bfloat16 [27, 32, 4], replicated, may hold values from -0.625 to 0.625
- bias1: float32 [32], replicated, may hold values from -3 to 3
- kernel2: bfloat16 [27, 64, 32], replicated, may hold values from -0.21875 to 0.21875
- bias2: float32 [64], replicated, may hold values from -3 to 3
- kernel3: bfloat16 [27, 128, 64], replicated, may hold values from -0.15625 to 0.15625
- bias3: float32 [128], replicated, may hold values from -3 to 3
- cotangent: bfloat16 [128, 8, 16, 16], P('gz', 'gy'), may hold values from -10 to 10
Outputs:
- features: bfloat16 [128, 8, 16, 16], P('gz', 'gy')
- grad_kernel1: float32 [27, 32, 4], replicated
- grad_bias1: float32 [32], replicated
- grad_kernel2: float32 [27, 64, 32], replicated
- grad_bias2: float32 [64], replicated
- grad_kernel3: float32 [27, 128, 64], P(None, 'gz')
- grad_bias3: float32 [128], P('gz')
All inputs are finite; a program needn't handle non-finite values.
Results may differ from a plain program's by a relative error of at most 0.018.
The roundings to bfloat16 on the way count: a program that leaves them out, or rounds other values in their place, can miss the bound.
Values may be sent and summed in bfloat16 or wider, within the bound.
No kernel may reach another device: no remote copies, remote signals or barrier semaphores. Data moves between devices by JAX's collectives and lax.ppermute only.
A program may use at most 64 MiB of HBM per device.

v0:
```python
import jax
import jax.numpy as jnp
from jax import lax
from jax.sharding import PartitionSpec as P

SHARPNESS = 2.0
LEAK_SLOPE = 0.3


def padded_2(shard, sides, width):
    for axis, dim in sides:
        devices, length = (lax.axis_size(axis), shard.shape[dim])
        up = [(i, (i + 1) % devices) for i in range(devices - 1)]
        down = [(j, i) for i, j in up]
        last = lax.slice_in_dim(shard, length - width, length, axis=dim)
        leading = lax.slice_in_dim(shard, 0, width, axis=dim)
        before = lax.ppermute(last, axis, up)
        after = lax.ppermute(leading, axis, down)
        shard = jnp.concatenate([before, shard, after], axis=dim)
    return shard


def shifted(padded, tap, dims, flip):
    shift_x = tap // 9
    shift_y = tap // 3 % 3
    shift_z = tap % 3
    if flip:
        shift_x, shift_y, shift_z = (2 - shift_x, 2 - shift_y, 2 - shift_z)
    return padded[
        :, shift_y : shift_y + dims[0], shift_z : shift_z + dims[1], shift_x : shift_x + dims[2]
    ]


def forward_conv(padded, kernel, dims):
    result = None
    for tap in range(27):
        term = jnp.einsum(
            "oi,iyzx->oyzx",
            kernel[tap],
            shifted(padded, tap, dims, False),
            preferred_element_type=jnp.float32,
        )
        result = term if result is None else result + term
    return result


def transpose_conv(padded, kernel, dims):
    result = None
    for tap in range(27):
        term = jnp.einsum(
            "oi,oyzx->iyzx",
            kernel[tap],
            shifted(padded, tap, dims, True),
            preferred_element_type=jnp.float32,
        )
        result = term if result is None else result + term
    return result


def kernel_grad(padded, delta):
    dims = delta.shape[1:]
    return jnp.stack(
        [
            jnp.einsum(
                "oyzx,iyzx->oi",
                delta,
                shifted(padded, tap, dims, False),
                preferred_element_type=jnp.float32,
            )
            for tap in range(27)
        ]
    )


def pool_forward(pre):
    chans, rows_y, cols_z, depth = pre.shape
    active = jnp.where(pre > 0, pre, LEAK_SLOPE * pre)
    exponent = jnp.exp(SHARPNESS * active).reshape(
        chans, rows_y // 2, 2, cols_z // 2, 2, depth // 2, 2
    )
    total = exponent.sum(axis=(2, 4, 6))
    return (jnp.log(total * 0.125) / SHARPNESS).astype(jnp.bfloat16)


def pool_backward(pre, grad):
    chans, rows_y, cols_z, depth = pre.shape
    active = jnp.where(pre > 0, pre, LEAK_SLOPE * pre)
    exponent = jnp.exp(SHARPNESS * active).reshape(
        chans, rows_y // 2, 2, cols_z // 2, 2, depth // 2, 2
    )
    total = exponent.sum(axis=(2, 4, 6), keepdims=True)
    spread = grad.astype(jnp.float32)[:, :, None, :, None, :, None] * exponent / total
    spread = spread.reshape(pre.shape)
    return jnp.where(pre > 0, spread, LEAK_SLOPE * spread).astype(jnp.bfloat16)


def pad_depth(field):
    return jnp.pad(field, ((0, 0), (0, 0), (0, 0), (1, 1)))


def channel_sums(delta):
    return delta.astype(jnp.float32).sum(axis=(1, 2, 3))


def shards(universe, kernel1, bias1, kernel2, bias2, kernel3, bias3, cotangent):
    in_chans, rows_y, cols_z, depth = universe.shape
    first_chans = kernel1.shape[1]
    group = cotangent.shape[0]
    index_z = lax.axis_index("gz")
    framed = pad_depth(padded_2(universe, (("gy", 1), ("gz", 2)), 1))
    slab_rows = 8
    slab_count = rows_y // slab_rows
    dims1 = (slab_rows, cols_z, depth)

    def slab_pre():
        return (forward_conv(framed, kernel1, dims1) + bias1[:, None, None, None], framed)

    def slab_forward(index):
        return pool_forward(slab_pre()[0])

    pooled1 = lax.map(slab_forward, jnp.arange(slab_count, dtype=jnp.int32))
    hidden1 = jnp.moveaxis(pooled1, 0, 1).reshape(first_chans, rows_y // 2, cols_z // 2, depth // 2)
    framed1 = pad_depth(padded_2(hidden1, (("gy", 1), ("gz", 2)), 1))
    dims2 = (rows_y // 2, cols_z // 2, depth // 2)
    pre2 = forward_conv(framed1, kernel2, dims2) + bias2[:, None, None, None]
    hidden2 = pool_forward(pre2)
    ribbon = padded_2(hidden2, (("gy", 1),), 1)
    column = lax.all_gather(ribbon, "gz", axis=2, tiled=True)
    framed2 = jnp.pad(column, ((0, 0), (0, 0), (1, 1), (1, 1)))
    wide = (rows_y // 4, column.shape[2], depth // 4)
    own_kernel = lax.dynamic_slice_in_dim(kernel3, index_z * group, group, 1)
    own_bias = lax.dynamic_slice_in_dim(bias3, index_z * group, group, 0)
    pre3 = forward_conv(framed2, own_kernel, wide) + own_bias[:, None, None, None]
    features = pool_forward(pre3)
    delta3 = pool_backward(pre3, cotangent)
    weight3, shift3 = (
        lax.psum(kernel_grad(framed2, delta3).astype(jnp.bfloat16), "gy").astype(jnp.float32),
        lax.psum(channel_sums(delta3).astype(jnp.bfloat16), "gy").astype(jnp.float32),
    )
    ribbon_delta = padded_2(delta3, (("gy", 1),), 1)
    framed_delta = jnp.pad(ribbon_delta, ((0, 0), (0, 0), (1, 1), (1, 1)))
    partial2 = transpose_conv(framed_delta, own_kernel, wide)
    grad2 = lax.psum_scatter(partial2.astype(jnp.bfloat16), "gz", scatter_dimension=2, tiled=True)
    extra = ()
    delta2 = pool_backward(pre2, grad2)
    weight2 = kernel_grad(framed1, delta2)
    shift2 = channel_sums(delta2)
    framed_delta2 = pad_depth(padded_2(delta2, (("gy", 1), ("gz", 2)), 1))
    grad1 = transpose_conv(framed_delta2, kernel2, dims2).astype(jnp.bfloat16)

    def slab_backward(index, totals):
        pre, piece = slab_pre()
        delta = pool_backward(pre, grad1)
        return (totals[0] + kernel_grad(piece, delta), totals[1] + channel_sums(delta))

    start = (
        jnp.zeros((27, first_chans, in_chans), jnp.float32),
        jnp.zeros((first_chans,), jnp.float32),
    )
    weight1, shift1 = lax.fori_loop(0, slab_count, slab_backward, start)
    totals = lax.psum((weight1, shift1, weight2, shift2) + extra, ("gy", "gz"))
    return (features, totals[0], totals[1], totals[2], totals[3], weight3, shift3)


def solution(mesh):
    in_specs = (P(None, "gy", "gz", None), P(), P(), P(), P(), P(), P(), P("gz", "gy", None, None))
    out_specs = (P("gz", "gy", None, None), P(), P(), P(), P(), P(None, "gz", None), P("gz"))
    return jax.shard_map(shards, mesh=mesh, in_specs=in_specs, out_specs=out_specs, check_vma=False)
```

profile of v0, /device:TPU:1, one launch (start us, length us, event | category | flops | bytes accessed | tf_op | source)
XLA Modules:
  0.0 517.3 jit_solution(16522327643724479916)
XLA Ops:
  8.0 4.4 collective-permute-start
  18.6 5.5 %collective-permute-start.2 = (bf16[4,10,1,128]{3,0,2,1:T(4,128)(2,1)S(1)}, bf16[4,10,1,128]{3,0,2,1:T(4,128)(2,1)S(1)}, u32[]{:S(2)}, u32[]{:S(2)}) collective-permute-start(bf16[4,10,1,128]{3,0,2,1:T(4,128)(2,1)S(1)} %get-tuple-element.75), channel_id=1, source_target_pairs={{0,1},{1,2},{2,3},{3,4},{4,5},{5,6},{6,7},{7,8},{8,9},{9,10},{10,1... | collective-permute-start | bytes 30728 | tf_op jit(solution)/shard_map/ppermute | solution.py:17
  24.1 1.9 collective-permute-start.3
  26.7 3.9 collective-permute-done.3
  39.8 1.5 fusion.198
  41.3 2.6 copy.162
  44.0 4.9 reduce_sum.79
  49.1 4.5 collective-permute-start.4
  55.8 4.0 div.69
  59.9 2.8 copy.173
  62.7 2.2 collective-permute-start.6
  65.0 2.1 collective-permute-start.7
  69.0 2.9 collective-permute-done.7
  82.7 4.3 collective-permute-start.8
  91.7 27.9 %all_gather.3 = bf16[64,4,32,32]{0,3,2,1:T(8,128)(2,1)S(1)} all-gather(bf16[64,4,2,32]{0,3,2,1:T(8,128)(2,1)S(1)} %pad_maximum_fusion.15), channel_id=1, replica_groups=mesh['gy'=8,'gz'=16] {'gz'}, dimensions={2}, use_global_device_ids=true | all-gather | bytes 557056 | tf_op jit(solution)/shard_map/all_gather | solution.py:128
  147.8 1.9 copy.168
  162.6 4.2 collective-permute-start.10
  169.3 6.3 %collective-permute-done.11 = bf16[8,1,32,32]{3,0,2,1:T(8,128)(2,1)S(1)} collective-permute-done((bf16[8,1,32,32]{3,0,2,1:T(8,128)(2,1)S(1)}, bf16[8,1,32,32]{3,0,2,1:T(8,128)(2,1)S(1)}, u32[]{:S(2)}, u32[]{:S(2)}) %collective-permute-start.11) | collective-permute-done | bytes 16416 | tf_op jit(solution)/shard_map/ppermute | solution.py:18
  192.3 30.6 %all-reduce.7 = (bf16[27,8,64]{2,1,0:T(8,128)(2,1)S(1)}, bf16[8]{0:T(256)(128)(2,1)S(1)}) all-reduce(bf16[27,8,64]{2,1,0:T(8,128)(2,1)S(1)} %fusion.144, bf16[8]{0:T(256)(128)(2,1)S(1)} %get-tuple-element.55), channel_id=1, replica_groups=mesh['gy'=8,'gz'=16] {'gy'}, use_global_device_ids=true, to_apply=%region_11.12 | all-reduce | flops 13832 | bytes 55328 | tf_op jit(solution)/shard_map/psum | solution.py:137
  225.7 105.8 %all-reduce.13.cloned.1.call-done = bf16[64,2,32,32]{0,3,2,1:T(8,128)(2,1)} async-done(((bf16[64,2,32,32]{0,3,2,1:T(8,128)(2,1)}), bf16[64,2,32,32]{0,3,2,1:T(8,128)(2,1)}) %all-reduce.13.cloned.1.call-update) | async-done | bytes 262160
  333.4 1.6 convert_reduce_fusion.1
  357.4 3.2 collective-permute-start.12
  362.7 2.8 collective-permute-done.13
  365.6 1.9 collective-permute-start.14
  367.5 3.6 collective-permute-start.15
  371.5 3.5 collective-permute-done.15
  380.8 4.0 mul.135
  384.8 2.8 copy.172
  387.6 1.8 convert_reduce_fusion
  397.1 67.5 %all-reduce.6 = (f32[27,32,4]{1,2,0:T(4,128)}, f32[32]{0:T(128)}, f32[64]{0:T(128)}) all-reduce(f32[27,32,4]{1,2,0:T(4,128)S(1)} %fusion.116, f32[32]{0:T(128)S(1)} %get-tuple-element.59, f32[64]{0:T(128)S(1)} %get-tuple-element.57), channel_id=1, replica_groups=mesh['gy'=8,'gz'=16] {'gy','gz'}, use_global_device_ids=true, to_apply=%region_5.6 | all-reduce | flops 3552 | bytes 28416 | tf_op jit(solution)/shard_map/psum | solution.py:161
  464.5 43.7 %all-reduce.11.cloned.1.call-done = f32[27,64,32]{1,2,0:T(8,128)} async-done(((f32[27,64,32]{1,2,0:T(8,128)}), f32[27,64,32]{1,2,0:T(8,128)}) %all-reduce.11.cloned.1.call-update) | async-done | bytes 221200 | tf_op jit(solution)/shard_map/psum | solution.py:161
  508.2 1.8 copy.461
  (323 shorter events, 138.8 us)
Async XLA Ops:
  7.2 112.5 %copy-start = (bf16[27,128,64]{1,2,0:T(8,128)(2,1)S(1)}, bf16[27,128,64]{1,2,0:T(8,128)(2,1)}, u32[]{:S(2)}) copy-start(bf16[27,128,64]{1,2,0:T(8,128)(2,1)} %param.13) | copy-start | bytes 1327108
  7.2 324.3 %all-reduce.13.cloned.1.call-start = ((), (), s32[]{:S(2)}) async-start(), calls=%async_computation.1 | async-start | bytes 1048576
  8.0 10.4 %collective-permute-start = (bf16[4,1,8,128]{3,0,2,1:T(4,128)(2,1)S(1)}, bf16[4,1,8,128]{3,0,2,1:T(4,128)(2,1)S(1)}, u32[]{:S(2)}, u32[]{:S(2)}) collective-permute-start(bf16[4,1,8,128]{3,0,2,1:T(4,128)(2,1)S(1)} %copy.375), channel_id=1, source_target_pairs={{0,16},{16,32},{32,48},{48,64},{64,80},{80,96},{96,112},{1,17},{17... | collective-permute-start | bytes 24584 | tf_op jit(solution)/shard_map/ppermute | solution.py:17
  12.4 4.7 copy-start.19
  12.4 4.7 copy-start.20
  12.4 6.0 %copy-start.8 = (bf16[4,8,8,128]{3,2,1,0:T(8,128)(2,1)S(1)}, bf16[4,8,8,128]{3,2,1,0:T(8,128)(2,1)}, u32[]{:S(2)}) copy-start(bf16[4,8,8,128]{3,2,1,0:T(8,128)(2,1)} %param.8) | copy-start | bytes 196612
  12.4 13.6 %copy-start.16 = (bf16[27,32,4]{1,2,0:T(4,128)(2,1)S(1)}, bf16[27,32,4]{1,2,0:T(4,128)(2,1)}, u32[]{:S(2)}) copy-start(bf16[27,32,4]{1,2,0:T(4,128)(2,1)} %param.9) | copy-start | bytes 20740
  12.4 6.1 %collective-permute-start.1 = (bf16[4,1,8,128]{3,0,2,1:T(4,128)(2,1)S(1)}, bf16[4,1,8,128]{3,0,2,1:T(4,128)(2,1)S(1)}, u32[]{:S(2)}, u32[]{:S(2)}) collective-permute-start(bf16[4,1,8,128]{3,0,2,1:T(4,128)(2,1)S(1)} %copy.376), channel_id=1, source_target_pairs={{16,0},{32,16},{48,32},{64,48},{80,64},{96,80},{112,96},{17,1},{33... | collective-permute-start | bytes 24584 | tf_op jit(solution)/shard_map/ppermute | solution.py:18
  18.5 12.6 %copy-start.12 = (bf16[4,9,8,128]{3,0,2,1:T(4,128)(2,1)}, bf16[4,9,8,128]{3,0,2,1:T(4,128)(2,1)S(1)}, u32[]{:S(2)}) copy-start(bf16[4,9,8,128]{3,0,2,1:T(4,128)(2,1)S(1)} %get-tuple-element.77) | copy-start | bytes 221188
  18.5 8.1 %copy-start.10 = (bf16[4,9,8,128]{3,0,2,1:T(4,128)(2,1)}, bf16[4,9,8,128]{3,0,2,1:T(4,128)(2,1)S(1)}, u32[]{:S(2)}) copy-start(bf16[4,9,8,128]{3,0,2,1:T(4,128)(2,1)S(1)} %get-tuple-element.86) | copy-start | bytes 221188
  18.6 8.1 %collective-permute-start.2 = (bf16[4,10,1,128]{3,0,2,1:T(4,128)(2,1)S(1)}, bf16[4,10,1,128]{3,0,2,1:T(4,128)(2,1)S(1)}, u32[]{:S(2)}, u32[]{:S(2)}) collective-permute-start(bf16[4,10,1,128]{3,0,2,1:T(4,128)(2,1)S(1)} %get-tuple-element.75), channel_id=1, source_target_pairs={{0,1},{1,2},{2,3},{3,4},{4,5},{5,6},{6,7},{7,8},{8,9},{9,10},{10,1... | collective-permute-start | bytes 30728 | tf_op jit(solution)/shard_map/ppermute | solution.py:17
  24.1 6.5 %collective-permute-start.3 = (bf16[4,10,1,128]{3,0,2,1:T(4,128)(2,1)S(1)}, bf16[4,10,1,128]{3,0,2,1:T(4,128)(2,1)S(1)}, u32[]{:S(2)}, u32[]{:S(2)}) collective-permute-start(bf16[4,10,1,128]{3,0,2,1:T(4,128)(2,1)S(1)} %get-tuple-element.76), channel_id=1, source_target_pairs={{1,0},{2,1},{3,2},{4,3},{5,4},{6,5},{7,6},{8,7},{9,8},{10,9},{11,1... | collective-permute-start | bytes 30728 | tf_op jit(solution)/shard_map/ppermute | solution.py:18
  49.1 13.6 %collective-permute-start.4 = (bf16[32,1,4,64]{3,0,2,1:T(8,128)(2,1)S(1)}, bf16[32,1,4,64]{3,0,2,1:T(8,128)(2,1)S(1)}, u32[]{:S(2)}, u32[]{:S(2)}) collective-permute-start(bf16[32,1,4,64]{3,0,2,1:T(8,128)(2,1)S(1)} %get-tuple-element.73), channel_id=1, source_target_pairs={{0,16},{16,32},{32,48},{48,64},{64,80},{80,96},{96,112},{1,17},{17... | collective-permute-start | bytes 49160 | tf_op jit(solution)/shard_map/ppermute | solution.py:17
  53.6 9.1 %collective-permute-start.5 = (bf16[32,1,4,64]{3,0,2,1:T(8,128)(2,1)S(1)}, bf16[32,1,4,64]{3,0,2,1:T(8,128)(2,1)S(1)}, u32[]{:S(2)}, u32[]{:S(2)}) collective-permute-start(bf16[32,1,4,64]{3,0,2,1:T(8,128)(2,1)S(1)} %get-tuple-element.74), channel_id=1, source_target_pairs={{16,0},{32,16},{48,32},{64,48},{80,64},{96,80},{112,96},{17,1},{33... | collective-permute-start | bytes 49160 | tf_op jit(solution)/shard_map/ppermute | solution.py:18
  62.7 6.3 %collective-permute-start.6 = (bf16[32,6,1,64]{3,0,2,1:T(8,128)(2,1)S(1)}, bf16[32,6,1,64]{3,0,2,1:T(8,128)(2,1)S(1)}, u32[]{:S(2)}, u32[]{:S(2)}) collective-permute-start(bf16[32,6,1,64]{3,0,2,1:T(8,128)(2,1)S(1)} %get-tuple-element.69), channel_id=1, source_target_pairs={{0,1},{1,2},{2,3},{3,4},{4,5},{5,6},{6,7},{7,8},{8,9},{9,10},{10,1... | collective-permute-start | bytes 73736 | tf_op jit(solution)/shard_map/ppermute | solution.py:17
  65.0 6.9 %collective-permute-start.7 = (bf16[32,6,1,64]{3,0,2,1:T(8,128)(2,1)S(1)}, bf16[32,6,1,64]{3,0,2,1:T(8,128)(2,1)S(1)}, u32[]{:S(2)}, u32[]{:S(2)}) collective-permute-start(bf16[32,6,1,64]{3,0,2,1:T(8,128)(2,1)S(1)} %get-tuple-element.70), channel_id=1, source_target_pairs={{1,0},{2,1},{3,2},{4,3},{5,4},{6,5},{7,6},{8,7},{9,8},{10,9},{11,1... | collective-permute-start | bytes 73736 | tf_op jit(solution)/shard_map/ppermute | solution.py:18
  69.0 6.1 %copy-start.6 = (bf16[27,64,32]{1,2,0:T(8,128)(2,1)S(1)}, bf16[27,64,32]{1,2,0:T(8,128)(2,1)}, u32[]{:S(2)}) copy-start(bf16[27,64,32]{1,2,0:T(8,128)(2,1)} %param.11) | copy-start | bytes 331780
  82.7 7.7 %collective-permute-start.8 = (bf16[64,1,2,32]{0,3,2,1:T(8,128)(2,1)S(1)}, bf16[64,1,2,32]{0,3,2,1:T(8,128)(2,1)S(1)}, u32[]{:S(2)}, u32[]{:S(2)}) collective-permute-start(bf16[64,1,2,32]{0,3,2,1:T(8,128)(2,1)S(1)} %get-tuple-element.82), channel_id=1, source_target_pairs={{0,16},{16,32},{32,48},{48,64},{64,80},{80,96},{96,112},{1,17},{17... | collective-permute-start | bytes 24584 | tf_op jit(solution)/shard_map/ppermute | solution.py:17
  87.0 4.7 collective-permute-start.9
  162.6 6.0 %collective-permute-start.10 = (bf16[8,1,32,32]{3,0,2,1:T(8,128)(2,1)S(1)}, bf16[8,1,32,32]{3,0,2,1:T(8,128)(2,1)S(1)}, u32[]{:S(2)}, u32[]{:S(2)}) collective-permute-start(bf16[8,1,32,32]{3,0,2,1:T(8,128)(2,1)S(1)} %get-tuple-element.71), channel_id=1, source_target_pairs={{0,16},{16,32},{32,48},{48,64},{64,80},{80,96},{96,112},{1,17},{17... | collective-permute-start | bytes 49160 | tf_op jit(solution)/shard_map/ppermute | solution.py:17
  166.9 8.6 %collective-permute-start.11 = (bf16[8,1,32,32]{3,0,2,1:T(8,128)(2,1)S(1)}, bf16[8,1,32,32]{3,0,2,1:T(8,128)(2,1)S(1)}, u32[]{:S(2)}, u32[]{:S(2)}) collective-permute-start(bf16[8,1,32,32]{3,0,2,1:T(8,128)(2,1)S(1)} %get-tuple-element.72), channel_id=1, source_target_pairs={{16,0},{32,16},{48,32},{64,48},{80,64},{96,80},{112,96},{17,1},{33... | collective-permute-start | bytes 49160 | tf_op jit(solution)/shard_map/ppermute | solution.py:18
  190.6 1.3 copy-start.15
  191.8 316.4 %all-reduce.11.cloned.1.call-start = ((), (), s32[]{:S(2)}) async-start(), calls=%async_computation | async-start | bytes 884736 | tf_op jit(solution)/shard_map/psum | solution.py:161
  192.3 141.1 %copy-start.2 = (f32[64,4,4,64]{3,0,2,1:T(8,128)S(1)}, f32[64,4,4,64]{3,0,2,1:T(8,128)}, u32[]{:S(2)}) copy-start(f32[64,4,4,64]{3,0,2,1:T(8,128)} %get-tuple-element.91) | copy-start | bytes 786436
  337.5 5.7 %copy-start.4 = (bf16[32,6,5,64]{3,0,2,1:T(8,128)(2,1)S(1)}, bf16[32,6,5,64]{3,0,2,1:T(8,128)(2,1)}, u32[]{:S(2)}) copy-start(bf16[32,6,5,64]{3,0,2,1:T(8,128)(2,1)} %get-tuple-element.68) | copy-start | bytes 368644
  339.1 5.7 %copy-start.3 = (bf16[32,6,5,64]{3,0,2,1:T(8,128)(2,1)S(1)}, bf16[32,6,5,64]{3,0,2,1:T(8,128)(2,1)}, u32[]{:S(2)}) copy-start(bf16[32,6,5,64]{3,0,2,1:T(8,128)(2,1)} %get-tuple-element.67) | copy-start | bytes 368644
  354.8 16.4 %copy-start.7 = (bf16[27,64,32]{1,2,0:T(8,128)(2,1)S(1)}, bf16[27,64,32]{1,2,0:T(8,128)(2,1)}, u32[]{:S(2)}) copy-start(bf16[27,64,32]{1,2,0:T(8,128)(2,1)} %param.11) | copy-start | bytes 331780
  357.4 5.4 %collective-permute-start.12 = (bf16[64,1,4,64]{3,0,2,1:T(8,128)(2,1)S(1)}, bf16[64,1,4,64]{3,0,2,1:T(8,128)(2,1)S(1)}, u32[]{:S(2)}, u32[]{:S(2)}) collective-permute-start(bf16[64,1,4,64]{3,0,2,1:T(8,128)(2,1)S(1)} %get-tuple-element.65), channel_id=1, source_target_pairs={{0,16},{16,32},{32,48},{48,64},{64,80},{80,96},{96,112},{1,17},{17... | collective-permute-start | bytes 98312 | tf_op jit(solution)/shard_map/ppermute | solution.py:17
  360.5 5.0 collective-permute-start.13
  365.6 5.9 %collective-permute-start.14 = (bf16[64,6,1,64]{3,0,2,1:T(8,128)(2,1)S(1)}, bf16[64,6,1,64]{3,0,2,1:T(8,128)(2,1)S(1)}, u32[]{:S(2)}, u32[]{:S(2)}) collective-permute-start(bf16[64,6,1,64]{3,0,2,1:T(8,128)(2,1)S(1)} %get-tuple-element.63), channel_id=1, source_target_pairs={{0,1},{1,2},{2,3},{3,4},{4,5},{5,6},{6,7},{7,8},{8,9},{9,10},{10,1... | collective-permute-start | bytes 147464 | tf_op jit(solution)/shard_map/ppermute | solution.py:17
  367.5 7.4 %collective-permute-start.15 = (bf16[64,6,1,64]{3,0,2,1:T(8,128)(2,1)S(1)}, bf16[64,6,1,64]{3,0,2,1:T(8,128)(2,1)S(1)}, u32[]{:S(2)}, u32[]{:S(2)}) collective-permute-start(bf16[64,6,1,64]{3,0,2,1:T(8,128)(2,1)S(1)} %get-tuple-element.64), channel_id=1, source_target_pairs={{1,0},{2,1},{3,2},{4,3},{5,4},{6,5},{7,6},{8,7},{9,8},{10,9},{11,1... | collective-permute-start | bytes 147464 | tf_op jit(solution)/shard_map/ppermute | solution.py:18
  391.0 1.1 copy-start.13
  (7 other events, 6.2 us)
Sparse Core Ops, SparseCore 0:
  191.9 139.4 all-reduce.12
  362.8 145.3 all-reduce.10
where the time goes:
time: 527 us; the launch traced here: 517 us
  waiting for transfers between devices  170 us (32%)
  blocking collectives  126 us (24%)
  matrix products  113 us (21%)
  starting transfers between devices  44.4 us (8%)
  local copies, waits for them, and re-layouts  29.9 us (6%)
  other arithmetic  17.1 us (3%)
  between operations  16.3 us (3%)
    unnamed x3, waiting for transfers between devices  106 us
    psum x1, blocking collectives, shards(): totals = lax.psum((weight1, shift1, weight2, shift2) + extra, ('gy', 'gz'))  67.5 us
    dot_general x81, matrix products, forward_conv(): jnp.einsum('oi,iyzx->oyzx', kernel[tap], shifted(padded, tap, dims, False...  48.9 us
    psum x1, waiting for transfers between devices, shards(): totals = lax.psum((weight1, shift1, weight2, shift2) + extra, ('gy', 'gz'))  43.7 us
    dot_general x81, matrix products, kernel_grad(): jnp.einsum('oyzx,iyzx->oi', delta, shifted(padded, tap, dims, False), pre...  42.4 us
    psum x1, blocking collectives, shards(): lax.psum(kernel_grad(framed2, delta3).astype(jnp.bfloat16), 'gy')  30.6 us
    ppermute x8, starting transfers between devices, padded_2(): before = lax.ppermute(last, axis, up)  30.1 us
    all_gather x1, blocking collectives, shards(): column = lax.all_gather(ribbon, 'gz', axis=2, tiled=True)  27.9 us
  transfers between devices with their start and end apart: 18, of which 8 were waited for; matrix products, arithmetic and copies ran while one was open for 8% of the time, Pallas kernels for 0%

commit v1 on v0

v1 whole, which is shorter than its diff:
```python
import functools

import jax
import jax.numpy as jnp
import numpy as np
from jax import lax
from jax.experimental import pallas as pl
from jax.experimental.pallas import tpu as pltpu
from jax.sharding import PartitionSpec as P

F32 = jnp.float32
BF16 = jnp.bfloat16
SLOPE = 0.3
PAIRS = ((0, 1), (2, 3), (-3, -2), (4, 5), (-1, 6))
VMEM = pl.BlockSpec(memory_space=pltpu.VMEM)
SMEM = pl.BlockSpec(memory_space=pltpu.SMEM)
LIMIT = 48 * 1024 * 1024


def dot(a, b):
    return jnp.dot(a, b, preferred_element_type=F32)


def dot_tn(a, b):
    return lax.dot_general(a, b, (((0,), (0,)), ((), ())), preferred_element_type=F32)


def dot_nt(a, b):
    return lax.dot_general(a, b, (((1,), (1,)), ((), ())), preferred_element_type=F32)


def lane(shape):
    return lax.broadcasted_iota(jnp.int32, shape, len(shape) - 1)


def exps(pre):
    return jnp.exp(2.0 * jnp.maximum(pre, SLOPE * pre))


def rounded(value):
    return value.astype(BF16).astype(F32)


def roll(value, amount, axis):
    return pltpu.roll(value, amount, axis)


def down(value):
    rows = lax.broadcasted_iota(jnp.int32, value.shape, 0)
    return jnp.where(rows == 0, 0.0, roll(value, 1, 0))


def up(value):
    count = value.shape[0]
    rows = lax.broadcasted_iota(jnp.int32, value.shape, 0)
    return jnp.where(rows == count - 1, 0.0, roll(value, count - 1, 0))


def forward_kernel(
    place, top, mid, bot, pick, w1, b1, w2, b2,
    hidden2, ratio2, patches1, ratio1, fields,
    left, field, first, spread, pre2, second,
):
    base_y, base_z, size_y, size_z = place[0], place[1], place[2], place[3]

    def inside(offset_y, offset_z, scale):
        row = base_y * (4 // scale) + offset_y
        col = base_z * (4 // scale) + offset_z
        ok_y = (row >= 0) & (row < size_y * (4 // scale))
        ok_z = (col >= 0) & (col < size_z * (4 // scale))
        return jnp.where(ok_y & ok_z, 1.0, 0.0)

    def lay(source, index, target):
        rows = source[index].astype(F32)
        pieces = []
        for one, two in PAIRS:
            a, b = 8 * (one + 3), 8 * (two + 3)
            pieces.append(jnp.concatenate([rows[a : a + 16], rows[b : b + 16]], axis=1))
        left[target] = jnp.concatenate(pieces, axis=0).astype(BF16)

    def lay_top(step, carry):
        lay(top, step + 1, step)
        return carry

    def lay_mid(step, carry):
        lay(mid, step, step + 7)
        return carry

    def lay_bot(step, carry):
        lay(bot, step, step + 15)
        return carry

    lax.fori_loop(0, 7, lay_top, 0)
    lax.fori_loop(0, 8, lay_mid, 0)
    lax.fori_loop(0, 7, lay_bot, 0)

    def sift(step, carry):
        block = left[pl.ds(2 * step, 2)].reshape(160, 256)
        out = dot(block, pick[...]).astype(BF16).reshape(2, 5, 16, 512)
        for px in range(4):
            for k in range(5):
                field[pl.ds(2 * step, 2), px * 16 : px * 16 + 16, k * 128 : k * 128 + 128] = out[
                    :, k, :, px * 128 : px * 128 + 128
                ]
        return carry

    lax.fori_loop(0, 11, sift, 0)
    fields[...] = field[6:16, :, :256]
    first[:, :, 0:8] = jnp.zeros((10, 10, 8, 128), F32)
    first[:, :, 72:80] = jnp.zeros((10, 10, 8, 128), F32)

    def block1(yw, carry):
        stack = field[pl.ds(2 * yw, 4)].reshape(256, 640)
        pre = dot_tn(stack, w1[...]) + b1[...]
        e = exps(pre)
        total = e[:, :128] + e[:, 128:]
        total = total + roll(total, 64, 1)
        total = total + roll(total, 32, 1)
        mean = total * 0.125
        pooled = rounded(jnp.log(mean) * 0.5)
        for k, pair in enumerate(PAIRS):
            for h, zw in enumerate(pair):
                at = k * 128 + h * 64
                first[yw, zw + 3, 8:72] = pooled[at : at + 64] * inside(yw - 3, zw, 1)

        @pl.when((yw >= 3) & (yw < 7))
        def _():
            share = 0.125 / mean[:256]
            share = jnp.concatenate([share, share], axis=1)
            ratio1[yw - 3] = jnp.where(pre[:256] > 0, 1.0, SLOPE) * (e[:256] * share)

        return carry

    lax.fori_loop(0, 10, block1, 0)

    group1 = lane((32, 128)) // 32

    def frame(yi, carry):
        for zi in range(10):
            part = first[yi, zi, pl.ds(7, 32, stride=2), :]
            for px in range(1, 4):
                part = jnp.where(group1 == px, first[yi, zi, pl.ds(7 + px, 32, stride=2), :], part)
            spread[yi, zi] = part.astype(BF16)
        return carry

    lax.fori_loop(0, 10, frame, 0)
    patches1[...] = spread[2:8, 2:8]

    for dy in range(3):
        block = jnp.concatenate(
            [
                jnp.concatenate([spread[dy : dy + 8, 2 * zo + pz] for pz in range(4)], axis=2)[:, None]
                for zo in range(4)
            ],
            axis=1,
        ).reshape(1024, 512)
        term = dot(block, w2[dy]).reshape(8, 4, 32, 256)
        pre2[...] = term + b2[...] if dy == 0 else pre2[...] + term

    half = lane((16, 128)) < 64

    def block2(yp, carry):
        pre = pre2[pl.ds(2 * yp, 2)]
        e = exps(pre)
        both = e[0] + e[1]
        total = (both[:, :, :128] + both[:, :, 128:]).reshape(128, 128)
        total = total + roll(total, 64, 1)
        mean = total * 0.125
        pooled = rounded(jnp.log(mean) * 0.5).reshape(4, 32, 128)
        share = (0.125 / mean).reshape(4, 32, 128)
        share = jnp.concatenate([share, share], axis=2)
        scaled = jnp.where(pre > 0, 1.0, SLOPE) * (e * share[None])
        for zo in range(4):
            ok = inside(yp - 1, zo - 1, 2)
            ratio2[pl.ds(2 * yp, 2), zo] = scaled[:, zo] * ok
            second[zo] = pooled[zo] * ok
            even = second[zo, pl.ds(0, 16, stride=2), :]
            odd = second[zo, pl.ds(1, 16, stride=2), :]
            hidden2[yp, zo] = jnp.where(half, even, odd).astype(BF16)
        return carry

    lax.fori_loop(0, 4, block2, 0)


def run_forward(place, pieces, pick, w1, b1, w2, b2):
    return pl.pallas_call(
        forward_kernel,
        name="forward",
        out_shape=(
            jax.ShapeDtypeStruct((4, 4, 16, 128), BF16),
            jax.ShapeDtypeStruct((8, 4, 32, 256), F32),
            jax.ShapeDtypeStruct((6, 6, 32, 128), BF16),
            jax.ShapeDtypeStruct((4, 256, 256), F32),
            jax.ShapeDtypeStruct((10, 64, 256), BF16),
        ),
        in_specs=[SMEM] + [VMEM] * 8,
        out_specs=(VMEM,) * 5,
        scratch_shapes=[
            pltpu.VMEM((22, 80, 256), BF16),
            pltpu.VMEM((22, 64, 640), BF16),
            pltpu.VMEM((10, 10, 80, 128), F32),
            pltpu.VMEM((10, 10, 32, 128), BF16),
            pltpu.VMEM((8, 4, 32, 256), F32),
            pltpu.VMEM((4, 32, 128), F32),
        ],
        compiler_params=pltpu.CompilerParams(vmem_limit_bytes=LIMIT),
    )(place, *pieces, pick, w1, b1, w2, b2)


def backward_kernel(
    groups,
    before, middle, after, own_cot, w3, b3, w2, ratio2, patches1, ratio1, fields,
    packed,
    patches2, pre3, delta3, patch2, grad2, delta2, patch1, grad1, delta1,
):
    wide = 128 // groups
    half = lane((16, 128)) < 64

    def lay(y, source):
        for z in range(8):
            swapped = roll(source(z).astype(F32), 64, 1)
            patches2[y, z] = jnp.concatenate(
                [jnp.where(half, down(swapped), swapped), jnp.where(half, swapped, up(swapped))], axis=1
            ).astype(BF16)

    for y in range(2):
        lay(y, lambda z: before[(y * 8 + z) * 16 : (y * 8 + z + 1) * 16])
        lay(y + 6, lambda z: after[(y * 8 + z) * 16 : (y * 8 + z + 1) * 16])

    def lay_middle(y, carry):
        lay(y + 2, lambda z: middle[y, z])
        return carry

    lax.fori_loop(0, 4, lay_middle, 0)

    for tap in range(9):
        dy, dz = tap // 3, tap % 3
        block = patches2[dy : dy + 6, dz : dz + 6].reshape(576, 256)
        term = dot(block, w3[tap]).reshape(6, 6, 16, 256)
        pre3[...] = term + b3[...] if tap == 0 else pre3[...] + term

    for wy in range(3):
        for wz in range(3):
            pre = pre3[2 * wy : 2 * wy + 2, 2 * wz : 2 * wz + 2]
            e = exps(pre)
            total = e[0, 0] + e[0, 1] + e[1, 0] + e[1, 1]
            total = total[:, :128] + total[:, 128:]
            mean = total * 0.125
            if wy == 1:
                cot = own_cot[wz * 16 : wz * 16 + 16]
            else:
                cot = (before if wy == 0 else after)[256 + wz * 16 : 272 + wz * 16]
            share = cot.astype(F32) * (0.125 / mean)
            share = jnp.concatenate([share, share], axis=1)
            delta3[2 * wy : 2 * wy + 2, 2 * wz : 2 * wz + 2] = (
                jnp.where(pre > 0, 1.0, SLOPE) * (e * share)
            ).astype(BF16)
            if wy == 1 and wz == 1:
                features = rounded(jnp.log(mean) * 0.5)

    own3 = delta3[2:4, 2:4].reshape(64, 256)
    bias3 = own3.astype(F32).sum(axis=0, keepdims=True)
    bias3 = bias3[:, :128] + bias3[:, 128:]
    low, high = [], []
    for tap in range(9):
        dy, dz = tap // 3, tap % 3
        block = patches2[dy + 2 : dy + 4, dz + 2 : dz + 4].reshape(64, 256)
        full = dot_tn(own3, block)
        one = full[:128]
        low_lanes, high_lanes = roll(full[128:, :128], 64, 1), roll(full[128:, 128:], 64, 1)
        tile0 = jnp.where(lane((128, 128)) < 64, low_lanes, high_lanes)
        tile1 = high_lanes
        low.append(one[:, :128] + tile0)
        high.append(one[:, 128:] + tile1)
    first_half = lane((128, 128)) < 64
    paired = []
    for m in range(5):
        other = roll(high[2 * m + 1], 64, 1) if 2 * m + 1 < 9 else jnp.zeros((128, 128), F32)
        paired.append(jnp.where(first_half, high[2 * m], other))
    kernel3 = [piece.reshape(groups, wide, 128) for piece in low + paired]

    for tap in range(9):
        dy, dz = tap // 3, tap % 3
        block = delta3[2 - dy : 6 - dy, 2 - dz : 6 - dz].reshape(256, 256)
        term = dot_nt(block, w3[tap]).reshape(4, 4, 16, 256)
        patch2[...] = term if tap == 0 else patch2[...] + term

    for y in range(4):
        for z in range(4):
            a, b = patch2[y, z, :, :128], patch2[y, z, :, 128:]
            x = rounded(jnp.where(half, b + up(a), a + down(b)))
            swapped = roll(x, 64, 1)
            grad2[y, z, pl.ds(0, 16, stride=2), :] = jnp.where(half, swapped, x)
            grad2[y, z, pl.ds(1, 16, stride=2), :] = jnp.where(half, x, swapped)

    for y in range(6):
        value = grad2[(y + 1) // 2]
        value = jnp.concatenate([value, value], axis=2)
        delta2[y] = (value * ratio2[y + 1]).astype(BF16)

    own2 = delta2[1:5, 1:3].reshape(256, 256)
    bias2 = own2.astype(F32).sum(axis=0, keepdims=True)
    bias2 = bias2[:, :128] + bias2[:, 128:]
    bias2 = bias2 + roll(bias2, 64, 1)
    kernel2 = []
    for dy in range(3):
        block = jnp.concatenate(
            [
                jnp.concatenate([patches1[dy : dy + 4, 2 * zo + pz] for pz in range(4)], axis=2)[:, None]
                for zo in range(2)
            ],
            axis=1,
        ).reshape(256, 512)
        full = dot_tn(own2, block)
        for dz in range(3):
            lanes0 = full[:, dz * 128 : dz * 128 + 128]
            lanes1 = full[:, dz * 128 + 128 : dz * 128 + 256]
            one = lanes0[:64] + lanes1[128:192]
            two = lanes0[64:128] + lanes1[192:256]
            kernel2.append(one + roll(two, 96, 1))
    kernel2 = jnp.concatenate(kernel2, axis=0).reshape(groups, 576 // groups, 128)

    for dy in range(3):
        block = delta2[2 - dy : 6 - dy].reshape(512, 256)
        term = dot_nt(block, w2[dy]).reshape(4, 4, 32, 512)
        patch1[...] = term if dy == 0 else patch1[...] + term

    low_half = lane((32, 128)) < 64
    group = lane((32, 128)) // 32

    def widen(value, which):
        value = jnp.where(group == which, value, 0.0)
        value = value + roll(value, 32, 1)
        return value + roll(value, 64, 1)

    def gather1(y, carry):
        for z, (zo_a, pz_a, zo_b, pz_b) in enumerate(((0, 3, 1, 1), (1, 2, 2, 0), (1, 3, 2, 1), (2, 2, 3, 0))):
            value = (
                patch1[y, zo_a, :, pz_a * 128 : pz_a * 128 + 128]
                + patch1[y, zo_b, :, pz_b * 128 : pz_b * 128 + 128]
            )
            value = rounded(value + roll(jnp.where(low_half, up(value), down(value)), 64, 1))
            grad1[z, pl.ds(0, 32, stride=2), :] = widen(value, 1)
            grad1[z, pl.ds(1, 32, stride=2), :] = widen(value, 2)
        value = grad1[...].reshape(256, 128)
        value = jnp.concatenate([value, value], axis=1)
        delta1[y] = (value * ratio1[y]).astype(BF16)
        return carry

    lax.fori_loop(0, 4, gather1, 0)

    bias1 = delta1[...].astype(F32).sum(axis=0).sum(axis=0, keepdims=True)
    bias1 = bias1[:, :128] + bias1[:, 128:]
    bias1 = bias1 + roll(bias1, 64, 1)
    bias1 = bias1 + roll(bias1, 32, 1)
    full = None
    for yw in range(4):
        term = dot(fields[2 * yw : 2 * yw + 4].reshape(256, 256), delta1[yw])
        full = term if full is None else full + term
    full = full.reshape(4, 4, 16, 256)
    kernel1 = []
    for dy in range(3):
        rows = full[dy, :, :, :128] + full[dy + 1, :, :, 128:]
        for dx in range(3):
            value = rows[dx] + roll(rows[dx + 1], 96, 1)
            kernel1.append(value + roll(roll(value, 12, 0), 64, 1))
    kernel1 = jnp.concatenate(kernel1, axis=0).reshape(groups, 144 // groups, 128)

    feature_rows = jnp.concatenate([features, jnp.zeros((112, 128), F32)], axis=0).T
    feature_rows = feature_rows.reshape(groups, wide, 128)
    low_lane = lane((1, 128)) < 64
    biases = jnp.concatenate([bias3, jnp.where(low_lane, bias2, bias1)], axis=0)
    biases = jnp.broadcast_to(biases[None], (groups, 2, 128))
    rows = 14 * wide + 720 // groups + wide + 2
    fill = packed.shape[1] - rows
    pieces = kernel3 + [feature_rows, kernel2, kernel1, biases, jnp.zeros((groups, fill, 128), F32)]
    packed[...] = jnp.concatenate(pieces, axis=1).astype(BF16)


def run_backward(groups, *operands):
    rows = 14 * (128 // groups) + 720 // groups + 128 // groups + 2
    rows = -(-rows // 16) * 16
    return pl.pallas_call(
        functools.partial(backward_kernel, groups),
        name="backward",
        out_shape=jax.ShapeDtypeStruct((groups, rows, 128), BF16),
        in_specs=[VMEM] * len(operands),
        out_specs=VMEM,
        scratch_shapes=[
            pltpu.VMEM((8, 8, 16, 256), BF16),
            pltpu.VMEM((6, 6, 16, 256), F32),
            pltpu.VMEM((6, 6, 16, 256), BF16),
            pltpu.VMEM((4, 4, 16, 256), F32),
            pltpu.VMEM((4, 4, 32, 128), F32),
            pltpu.VMEM((6, 4, 32, 256), BF16),
            pltpu.VMEM((4, 4, 32, 512), F32),
            pltpu.VMEM((4, 64, 128), F32),
            pltpu.VMEM((4, 256, 256), BF16),
        ],
        compiler_params=pltpu.CompilerParams(vmem_limit_bytes=LIMIT),
    )(*operands)


def pick_matrix():
    out = np.zeros((2, 128, 4, 2, 64), np.float32)
    for px in range(4):
        for w in range(64):
            x = 2 * w - 1 + px
            if 0 <= x < 128:
                for h in range(2):
                    out[h, x, px, h, w] = 1
    return out.reshape(256, 512).astype(jnp.bfloat16)


def spread_taps(taps, axis, out_axis):
    pads = [[(0, 0)] * taps.ndim for _ in range(2)]
    pads[0][axis] = (0, 1)
    pads[1][axis] = (1, 0)
    return jnp.stack([jnp.pad(taps, pads[0]), jnp.pad(taps, pads[1])], axis=out_axis)


def weights(kernel1, kernel2, kernel3):
    k1 = kernel1.reshape(3, 3, 3, 32, 4).transpose(1, 0, 2, 4, 3)
    k1 = spread_taps(k1, 1, 4)
    k1 = spread_taps(k1, 2, 4)
    k1 = spread_taps(k1, 0, 4)
    k2 = kernel2.reshape(3, 3, 3, 64, 32).transpose(1, 2, 0, 4, 3)
    k2 = spread_taps(k2, 2, 4)
    k2 = spread_taps(k2, 1, 4)
    k3 = kernel3.reshape(3, 3, 3, 128, 64).transpose(1, 2, 0, 4, 3)
    k3 = spread_taps(k3, 2, 4)
    return k1.reshape(256, 256), k2.reshape(3, 512, 256), k3.reshape(9, 256, 256)


def both_ways(to_next, to_previous, axis):
    devices = lax.axis_size(axis)
    forth = [(i, i + 1) for i in range(devices - 1)]
    back = [(i + 1, i) for i in range(devices - 1)]
    return lax.ppermute(to_next, axis, forth), lax.ppermute(to_previous, axis, back)


def shards(universe, kernel1, bias1, kernel2, bias2, kernel3, bias3, cotangent):
    size_y, size_z = lax.axis_size("gy"), lax.axis_size("gz")
    place_y, place_z = lax.axis_index("gy"), lax.axis_index("gz")
    wide = 128 // size_z
    place = jnp.stack([place_y, place_z, jnp.int32(size_y), jnp.int32(size_z)]).astype(jnp.int32)

    tile = universe.transpose(1, 2, 0, 3).reshape(8, 32, 128)
    lower, upper = both_ways(tile, tile, "gz")
    strip = jnp.concatenate([lower[:, 4:], tile, upper[:, :28], jnp.zeros((8, 8, 128), BF16)], axis=1)
    top, bottom = both_ways(strip, strip, "gy")

    w1, w2, w3 = weights(kernel1, kernel2, kernel3)
    cot = jnp.pad(cotangent[:, 0], ((0, 0), (1, 1), (0, 0)))
    cot = jnp.stack([cot[:, d : d + size_z] for d in range(3)], axis=2)
    cot = lax.all_to_all(cot.transpose(1, 0, 2, 3), "gz", 0, 0, tiled=True)
    cot = cot.reshape(128, 3, 16).transpose(1, 2, 0).reshape(48, 128)

    hidden2, ratio2, patches1, ratio1, fields = run_forward(
        place, (top, strip, bottom), jnp.asarray(pick_matrix()), w1,
        jnp.tile(bias1, 8)[None], w2, jnp.tile(bias2, 4)[None],
    )
    lower, upper = both_ways(hidden2[:, 0:2], hidden2[:, 2:4], "gz")
    middle = jnp.concatenate([lower, hidden2, upper], axis=1)
    before, after = both_ways(
        jnp.concatenate([middle[0:2].reshape(256, 128), cot], axis=0),
        jnp.concatenate([middle[2:4].reshape(256, 128), cot], axis=0),
        "gy",
    )
    packed = run_backward(
        size_z, before, middle, after, cot, w3, jnp.tile(bias3, 2)[None], w2, ratio2, patches1, ratio1, fields
    )
    packed = lax.all_to_all(packed, "gz", 0, 0, tiled=True)
    at = 14 * wide
    features = packed[:, at : at + wide, :16].transpose(1, 0, 2)[:, None]
    partial = packed.astype(F32).sum(axis=0).astype(BF16)
    total = lax.all_gather(partial, "gy", axis=0).astype(F32).sum(axis=0)
    rows2, rows1 = 576 // size_z, 144 // size_z
    low = total[: 9 * wide].reshape(3, 3, wide, 2, 64)
    high = total[9 * wide : 14 * wide].reshape(5, wide, 2, 64).transpose(0, 2, 1, 3)
    high = high.reshape(10, wide, 64)[:9].reshape(3, 3, wide, 1, 64)
    grad3 = jnp.concatenate([low, high], axis=3).transpose(3, 0, 1, 2, 4).reshape(27, wide, 64)
    at = at + wide
    rest = lax.all_gather(total[at : at + rows2 + rows1].astype(BF16), "gz", axis=0).astype(F32)
    grad2 = rest[:, :rows2].reshape(3, 3, 64, 4, 32)[:, :, :, :3]
    grad2 = grad2.transpose(3, 0, 1, 2, 4).reshape(27, 64, 32)
    grad1 = rest[:, rows2:].reshape(3, 3, 4, 4, 128)[:, :, :3, :, :32]
    grad1 = grad1.transpose(1, 0, 2, 4, 3).reshape(27, 32, 4)
    at = at + rows2 + rows1
    shift3 = lax.dynamic_slice_in_dim(total[at], place_z * wide, wide, 0)
    return features, grad1, total[at + 1, 64:96], grad2, total[at + 1, :64], grad3, shift3


def solution(mesh):
    in_specs = (P(None, "gy", "gz", None), P(), P(), P(), P(), P(), P(), P("gz", "gy", None, None))
    out_specs = (P("gz", "gy", None, None), P(), P(), P(), P(), P(None, "gz", None), P("gz"))
    return jax.shard_map(shards, mesh=mesh, in_specs=in_specs, out_specs=out_specs, check_vma=False)
```

time: 527 us -> 165 us (0.31); the launches traced: 517 us -> 162 us
  waiting for transfers between devices: 170 us -> 18.5 us
  matrix products: 113 us -> 0 us
  blocking collectives: 126 us -> 50.9 us
  Pallas kernels: 0 us -> 18.3 us
  between operations: 16.3 us -> 1.1 us
  other arithmetic: 17.1 us -> 3.64 us
    dot_general x216 -> x0, matrix products: 113 us -> none  [the longest x81 48.9 us: forward_conv(): jnp.einsum('oi,iyzx->oyzx', kernel[tap], shifted(padded, tap, dims, False...]
    unnamed x3 -> x0, waiting for transfers between devices: 106 us -> none
    psum x2 -> x0, blocking collectives: 98 us -> none  [the longest x1 67.5 us: shards(): totals = lax.psum((weight1, shift1, weight2, shift2) + extra, ('gy', 'gz'))]
    psum x1 -> x0, waiting for transfers between devices: 43.7 us -> none  [shards(): totals = lax.psum((weight1, shift1, weight2, shift2) + extra, ('gy', 'gz'))]
    all_gather x1 -> x2, blocking collectives: 27.9 us -> 50.9 us  [the longest x1 27.2 us: shards(): lax.all_gather(total[at:at + rows2 + rows1].astype(BF16), 'gz', axis=0)]
    pallas_call x0 -> x2, Pallas kernels: none -> 18.3 us  [the longest x1 10.4 us: run_forward(): pl.pallas_call(forward_kernel, name='forward', out_shape=(jax.ShapeDtypeS...]
    ppermute x16 -> x8, starting transfers between devices: 44.3 us -> 26.9 us  [the longest x4 19 us: both_ways(): lax.ppermute(to_next, axis, forth)]
    ppermute x16 -> x8, waiting for transfers between devices: 20.6 us -> 4.79 us  [the longest x4 4.78 us: both_ways(): lax.ppermute(to_previous, axis, back)]
  transfers between devices with their start and end apart: 18 -> 10, of which waited for: 8 -> 2; matrix products, arithmetic and copies ran while one was open for 8% -> 13% of each run, Pallas kernels for 0% -> 0%
where the time goes in v1:
time: 165 us; the launch traced here: 162 us
  blocking collectives  50.9 us (31%)
  starting transfers between devices  40.6 us (25%)
  local copies, waits for them, and re-layouts  28.6 us (17%)
  waiting for transfers between devices  18.5 us (11%)
  Pallas kernels  18.3 us (11%)
  other arithmetic  3.64 us (2%)
    all_gather x1, blocking collectives, shards(): lax.all_gather(total[at:at + rows2 + rows1].astype(BF16), 'gz', axis=0)  27.2 us
    all_gather x1, blocking collectives, shards(): total = lax.all_gather(partial, 'gy', axis=0).astype(F32).sum(axis=0)  23.7 us
    ppermute x4, starting transfers between devices, both_ways(): lax.ppermute(to_next, axis, forth)  19 us
    all_to_all x1, waiting for transfers between devices, shards(): packed = lax.all_to_all(packed, 'gz', 0, 0, tiled=True)  13.7 us
    pallas_call x1, Pallas kernels, run_forward(): pl.pallas_call(forward_kernel, name='forward', out_shape=(jax.ShapeDtypeS...  10.4 us
    another operation x9, local copies, waits for them, and re-layouts, spread_taps(): jnp.stack([jnp.pad(taps, pads[0]), jnp.pad(taps, pads[1])], axis=out_axis)  8.35 us
    all_to_all x1, starting transfers between devices, shards(): cot = lax.all_to_all(cot.transpose(1, 0, 2, 3), 'gz', 0, 0, tiled=True)  7.89 us
    pallas_call x1, Pallas kernels, run_backward(): pl.pallas_call(functools.partial(backward_kernel, groups), name='backward...  7.88 us
  transfers between devices with their start and end apart: 10, of which 2 were waited for; matrix products, arithmetic and copies ran while one was open for 13% of the time, Pallas kernels for 0%

profile of v1, /device:TPU:1, one launch (start us, length us, event | category | flops | bytes accessed | tf_op | source)
XLA Modules:
  0.0 161.6 jit_solution(1408589295571857210)
XLA Ops:
  0.6 0.9 copy.76
  1.6 3.3 %collective-permute-start.1 = (bf16[8,32,128]{2,1,0:T(8,128)(2,1)S(1)}, bf16[8,32,128]{2,1,0:T(8,128)(2,1)S(1)}, u32[]{:S(2)}, u32[]{:S(2)}) collective-permute-start(bf16[8,32,128]{2,1,0:T(8,128)(2,1)S(1)} %bitcast.102), channel_id=1, source_target_pairs={{1,0},{2,1},{3,2},{4,3},{5,4},{6,5},{7,6},{8,7},{9,8},{10,9},{11,1... | collective-permute-start | bytes 196616 | tf_op jit(solution)/shard_map/ppermute | solution.py:439
  4.9 4.6 %collective-permute-start = (bf16[8,32,128]{2,1,0:T(8,128)(2,1)S(1)}, bf16[8,32,128]{2,1,0:T(8,128)(2,1)S(1)}, u32[]{:S(2)}, u32[]{:S(2)}) collective-permute-start(bf16[8,32,128]{2,1,0:T(8,128)(2,1)S(1)} %bitcast.103), channel_id=1, source_target_pairs={{0,1},{1,2},{2,3},{3,4},{4,5},{5,6},{6,7},{7,8},{8,9},{9,10},{10,1... | collective-permute-start | bytes 196616 | tf_op jit(solution)/shard_map/ppermute | solution.py:439
  9.6 0.8 copy.103
  10.4 0.7 reshape.107
  11.1 7.9 %all-to-all-start = ((bf16[16,2,192]{2,1,0:T(2,128)(2,1)}), bf16[16,2,192]{2,1,0:T(2,128)(2,1)S(1)}, u32[]{:S(2)}, u32[]{:S(2)}) async-start(bf16[16,2,192]{2,1,0:T(2,128)(2,1)} %reshape.107), calls=%async_computation | async-start | bytes 32768 | tf_op jit(solution)/shard_map/all_to_all | solution.py:456
  19.0 0.9 pad_bitcast_fusion.11
  20.5 0.8 copy-done.5
  21.3 1.3 pad_bitcast_fusion.3
  23.6 1.3 collective-permute-start.3
  24.9 4.2 %collective-permute-start.2 = (bf16[8,96,128]{2,1,0:T(8,128)(2,1)S(1)}, bf16[8,96,128]{2,1,0:T(8,128)(2,1)S(1)}, u32[]{:S(2)}, u32[]{:S(2)}) collective-permute-start(bf16[8,96,128]{2,1,0:T(8,128)(2,1)S(1)} %maximum_maximum_fusion.mid), channel_id=1, source_target_pairs={{0,16},{16,32},{32,48},{48,64},{64,80},{80,96},{96,112},{1,17},{17... | collective-permute-start | bytes 589832 | tf_op jit(solution)/shard_map/ppermute | solution.py:439
  30.7 2.8 %copy.82 = bf16[3,4,4,32,2,2,64]{6,5,4,3,2,1,0:T(2,128)(2,1)} copy(bf16[3,4,4,32,2,2,64]{6,3,1,0,2,5,4:T(8,128)(2,1)S(1)} %pad_maximum_fusion) | data formatting | bytes 1572864 | tf_op jit(solution)/shard_map/stack | solution.py:419
  33.5 3.6 %reshape.83.w2 = bf16[3,512,256]{2,1,0:T(8,128)(2,1)S(1)} reshape(bf16[3,4,4,32,2,2,64]{6,5,4,3,2,1,0:T(2,128)(2,1)} %copy.82) | data formatting | bytes 1572864 | tf_op jit(solution)/shard_map/reshape | solution.py:432
  37.3 10.4 %forward.1 = (bf16[4,4,16,128]{3,2,1,0:T(8,128)(2,1)S(1)}, f32[8,4,32,256]{3,2,1,0:T(8,128)S(1)}, bf16[6,6,32,128]{3,2,1,0:T(8,128)(2,1)S(1)}, f32[4,256,256]{2,1,0:T(8,128)S(1)}, bf16[10,64,256]{2,1,0:T(8,128)(2,1)S(1)}) custom-call(s32[4]{0:T(128)S(1)} %pad_add_fusion.place, bf16[8,96,128]{2,1,0:T(8,128)(2,1)S(1)} %collective-permute-done.2.top, ...), custom_call_target="tpu_custom_call" | custom-call | tf_op jit(solution)/shard_map/forward/pallas_call | solution.py:186
  47.7 1.0 copy-done
  48.7 0.7 copy-done.2
  49.4 5.4 %collective-permute-start.4 = (bf16[4,2,16,128]{3,2,1,0:T(8,128)(2,1)S(1)}, bf16[4,2,16,128]{3,2,1,0:T(8,128)(2,1)S(1)}, u32[]{:S(2)}, u32[]{:S(2)}) collective-permute-start(bf16[4,2,16,128]{3,2,1,0:T(8,128)(2,1)S(1)} %get-tuple-element.65), channel_id=1, source_target_pairs={{0,1},{1,2},{2,3},{3,4},{4,5},{5,6},{6,7},{7,8},{8,9},{9,10},{10,1... | collective-permute-start | bytes 98312 | tf_op jit(solution)/shard_map/ppermute | solution.py:439
  54.9 1.9 %collective-permute-start.5 = (bf16[4,2,16,128]{3,2,1,0:T(8,128)(2,1)S(1)}, bf16[4,2,16,128]{3,2,1,0:T(8,128)(2,1)S(1)}, u32[]{:S(2)}, u32[]{:S(2)}) collective-permute-start(bf16[4,2,16,128]{3,2,1,0:T(8,128)(2,1)S(1)} %get-tuple-element.64), channel_id=1, source_target_pairs={{1,0},{2,1},{3,2},{4,3},{5,4},{6,5},{7,6},{8,7},{9,8},{10,9},{11,1... | collective-permute-start | bytes 98312 | tf_op jit(solution)/shard_map/ppermute | solution.py:439
  56.9 4.8 %collective-permute-done.5 = bf16[4,2,16,128]{3,2,1,0:T(8,128)(2,1)S(1)} collective-permute-done((bf16[4,2,16,128]{3,2,1,0:T(8,128)(2,1)S(1)}, bf16[4,2,16,128]{3,2,1,0:T(8,128)(2,1)S(1)}, u32[]{:S(2)}, u32[]{:S(2)}) %collective-permute-start.5) | collective-permute-done | bytes 32800 | tf_op jit(solution)/shard_map/ppermute | solution.py:439
  62.3 1.3 collective-permute-start.7
  63.6 4.8 %collective-permute-start.6 = (bf16[304,128]{1,0:T(8,128)(2,1)}, bf16[304,128]{1,0:T(8,128)(2,1)}, u32[]{:S(2)}, u32[]{:S(2)}) collective-permute-start(bf16[304,128]{1,0:T(8,128)(2,1)} %get-tuple-element.73), channel_id=1, source_target_pairs={{0,16},{16,32},{32,48},{48,64},{64,80},{80,96},{96,112},{1,17},{17... | collective-permute-start | bytes 233480 | tf_op jit(solution)/shard_map/ppermute | solution.py:439
  68.4 1.4 pad_maximum_fusion.1
  69.8 2.3 %copy.90 = bf16[3,3,4,64,2,128]{5,4,3,2,1,0:T(2,128)(2,1)} copy(bf16[3,3,4,64,2,128]{5,3,1,0,2,4:T(8,128)(2,1)S(1)} %pad_maximum_fusion.1) | data formatting | bytes 2359296 | tf_op jit(solution)/shard_map/stack | solution.py:419
  72.0 3.2 %reshape.89.w3 = bf16[9,256,256]{2,1,0:T(8,128)(2,1)S(1)} reshape(bf16[3,3,4,64,2,128]{5,4,3,2,1,0:T(2,128)(2,1)} %copy.90) | data formatting | bytes 2359296 | tf_op jit(solution)/shard_map/reshape | solution.py:432
  75.3 1.2 copy-done.1
  76.5 1.0 copy-done.3
  77.4 7.9 %backward.1 = bf16[16,176,128]{2,1,0:T(8,128)(2,1)} custom-call(bf16[304,128]{1,0:T(8,128)(2,1)} %collective-permute-done.6.before, bf16[4,8,16,128]{3,2,1,0:T(8,128)(2,1)S(1)} %constant_dynamic-update-slice_fusion.middle, bf16[304,128]{1,0:T(8,128)(2,1)} %collective-permute-done.7.after, bf16[48,128]{1,0:T(8,128)(2,1)S(1)} %bitcast.95, ...), custom_call_target="tpu_custom_call" | custom-call | tf_op jit(solution)/shard_map/backward/pallas_call | solution.py:383
  85.3 5.9 %all-to-all-start.1 = ((bf16[16,176,128]{2,1,0:T(8,128)(2,1)}), bf16[16,176,128]{2,1,0:T(8,128)(2,1)S(1)}, u32[]{:S(2)}, u32[]{:S(2)}) async-start(bf16[16,176,128]{2,1,0:T(8,128)(2,1)} %backward.1), calls=%async_computation.1 | async-start | bytes 1441792 | tf_op jit(solution)/shard_map/all_to_all | solution.py:473
  91.2 13.7 %all-to-all-done.1 = bf16[16,176,128]{2,1,0:T(8,128)(2,1)S(1)} async-done(((bf16[16,176,128]{2,1,0:T(8,128)(2,1)}), bf16[16,176,128]{2,1,0:T(8,128)(2,1)S(1)}, u32[]{:S(2)}, u32[]{:S(2)}) %all-to-all-start.1) | async-done | bytes 720928 | tf_op jit(solution)/shard_map/all_to_all | solution.py:473
  105.0 23.7 %all-gather = bf16[1408,128]{1,0:T(8,128)(2,1)S(1)} all-gather(bf16[176,128]{1,0:T(8,128)(2,1)S(1)} %reduce_sum.21), channel_id=2, replica_groups=mesh['gy'=8,'gz'=16] {'gy'}, dimensions={0}, use_global_device_ids=true | all-gather | bytes 405504 | tf_op jit(solution)/shard_map/all_gather | solution.py:477
  129.9 27.2 %all-gather.2 = bf16[16,45,128]{2,1,0:T(8,128)(2,1)S(1)} all-gather(bf16[1,45,128]{2,1,0:T(8,128)(2,1)S(1)} %fusion.2), channel_id=3, replica_groups=mesh['gy'=8,'gz'=16] {'gz'}, dimensions={0}, use_global_device_ids=true | all-gather | bytes 195840 | tf_op jit(solution)/shard_map/all_gather | solution.py:484
  160.0 1.1 copy.92
  (79 shorter events, 8.8 us)
Async XLA Ops:
  0.6 19.4 %copy-start.6 = (bf16[27,64,32]{1,2,0:T(8,128)(2,1)S(1)}, bf16[27,64,32]{1,2,0:T(8,128)(2,1)}, u32[]{:S(2)}) copy-start(bf16[27,64,32]{1,2,0:T(8,128)(2,1)} %param.12) | copy-start | bytes 331780
  1.6 21.9 %collective-permute-start.1 = (bf16[8,32,128]{2,1,0:T(8,128)(2,1)S(1)}, bf16[8,32,128]{2,1,0:T(8,128)(2,1)S(1)}, u32[]{:S(2)}, u32[]{:S(2)}) collective-permute-start(bf16[8,32,128]{2,1,0:T(8,128)(2,1)S(1)} %bitcast.102), channel_id=1, source_target_pairs={{1,0},{2,1},{3,2},{4,3},{5,4},{6,5},{7,6},{8,7},{9,8},{10,9},{11,1... | collective-permute-start | bytes 196616 | tf_op jit(solution)/shard_map/ppermute | solution.py:439
  4.9 18.5 %collective-permute-start = (bf16[8,32,128]{2,1,0:T(8,128)(2,1)S(1)}, bf16[8,32,128]{2,1,0:T(8,128)(2,1)S(1)}, u32[]{:S(2)}, u32[]{:S(2)}) collective-permute-start(bf16[8,32,128]{2,1,0:T(8,128)(2,1)S(1)} %bitcast.103), channel_id=1, source_target_pairs={{0,1},{1,2},{2,3},{3,4},{4,5},{5,6},{6,7},{7,8},{8,9},{9,10},{10,1... | collective-permute-start | bytes 196616 | tf_op jit(solution)/shard_map/ppermute | solution.py:439
  11.1 26.0 %all-to-all-start = ((bf16[16,2,192]{2,1,0:T(2,128)(2,1)}), bf16[16,2,192]{2,1,0:T(2,128)(2,1)S(1)}, u32[]{:S(2)}, u32[]{:S(2)}) async-start(bf16[16,2,192]{2,1,0:T(2,128)(2,1)} %reshape.107), calls=%async_computation | async-start | bytes 32768 | tf_op jit(solution)/shard_map/all_to_all | solution.py:456
  20.2 1.0 copy-start.5
  23.2 6.4 %copy-start.7 = (f32[64]{0:T(128)S(1)}, f32[64]{0:T(128)}, u32[]{:S(2)}) copy-start(f32[64]{0:T(128)} %param.13) | copy-start | bytes 772
  23.2 6.5 %copy-start.8 = (f32[32]{0:T(128)S(1)}, f32[32]{0:T(128)}, u32[]{:S(2)}) copy-start(f32[32]{0:T(128)} %param.11) | copy-start | bytes 388
  23.6 13.7 %collective-permute-start.3 = (bf16[8,96,128]{2,1,0:T(8,128)(2,1)S(1)}, bf16[8,96,128]{2,1,0:T(8,128)(2,1)S(1)}, u32[]{:S(2)}, u32[]{:S(2)}) collective-permute-start(bf16[8,96,128]{2,1,0:T(8,128)(2,1)S(1)} %maximum_maximum_fusion.mid), channel_id=1, source_target_pairs={{16,0},{32,16},{48,32},{64,48},{80,64},{96,80},{112,96},{17,1},{33... | collective-permute-start | bytes 589832 | tf_op jit(solution)/shard_map/ppermute | solution.py:439
  24.9 12.4 %collective-permute-start.2 = (bf16[8,96,128]{2,1,0:T(8,128)(2,1)S(1)}, bf16[8,96,128]{2,1,0:T(8,128)(2,1)S(1)}, u32[]{:S(2)}, u32[]{:S(2)}) collective-permute-start(bf16[8,96,128]{2,1,0:T(8,128)(2,1)S(1)} %maximum_maximum_fusion.mid), channel_id=1, source_target_pairs={{0,16},{16,32},{32,48},{48,64},{64,80},{80,96},{96,112},{1,17},{17... | collective-permute-start | bytes 589832 | tf_op jit(solution)/shard_map/ppermute | solution.py:439
  33.5 3.8 %copy-start.4 = (bf16[256,512]{1,0:T(8,128)(2,1)S(1)}, bf16[256,512]{1,0:T(8,128)(2,1)}, u32[]{:S(2)}) copy-start(bf16[256,512]{1,0:T(8,128)(2,1)} %constant.28.clone.pick) | copy-start | bytes 786436
  47.7 1.0 copy-start
  48.7 0.7 copy-start.2
  49.4 7.5 %collective-permute-start.4 = (bf16[4,2,16,128]{3,2,1,0:T(8,128)(2,1)S(1)}, bf16[4,2,16,128]{3,2,1,0:T(8,128)(2,1)S(1)}, u32[]{:S(2)}, u32[]{:S(2)}) collective-permute-start(bf16[4,2,16,128]{3,2,1,0:T(8,128)(2,1)S(1)} %get-tuple-element.65), channel_id=1, source_target_pairs={{0,1},{1,2},{2,3},{3,4},{4,5},{5,6},{6,7},{7,8},{8,9},{9,10},{10,1... | collective-permute-start | bytes 98312 | tf_op jit(solution)/shard_map/ppermute | solution.py:439
  54.9 6.7 %collective-permute-start.5 = (bf16[4,2,16,128]{3,2,1,0:T(8,128)(2,1)S(1)}, bf16[4,2,16,128]{3,2,1,0:T(8,128)(2,1)S(1)}, u32[]{:S(2)}, u32[]{:S(2)}) collective-permute-start(bf16[4,2,16,128]{3,2,1,0:T(8,128)(2,1)S(1)} %get-tuple-element.64), channel_id=1, source_target_pairs={{1,0},{2,1},{3,2},{4,3},{5,4},{6,5},{7,6},{8,7},{9,8},{10,9},{11,1... | collective-permute-start | bytes 98312 | tf_op jit(solution)/shard_map/ppermute | solution.py:439
  62.3 12.9 %collective-permute-start.7 = (bf16[304,128]{1,0:T(8,128)(2,1)}, bf16[304,128]{1,0:T(8,128)(2,1)}, u32[]{:S(2)}, u32[]{:S(2)}) collective-permute-start(bf16[304,128]{1,0:T(8,128)(2,1)} %get-tuple-element.72), channel_id=1, source_target_pairs={{16,0},{32,16},{48,32},{64,48},{80,64},{96,80},{112,96},{17,1},{33... | collective-permute-start | bytes 233480 | tf_op jit(solution)/shard_map/ppermute | solution.py:439
  63.6 11.6 %collective-permute-start.6 = (bf16[304,128]{1,0:T(8,128)(2,1)}, bf16[304,128]{1,0:T(8,128)(2,1)}, u32[]{:S(2)}, u32[]{:S(2)}) collective-permute-start(bf16[304,128]{1,0:T(8,128)(2,1)} %get-tuple-element.73), channel_id=1, source_target_pairs={{0,16},{16,32},{32,48},{48,64},{64,80},{80,96},{96,112},{1,17},{17... | collective-permute-start | bytes 233480 | tf_op jit(solution)/shard_map/ppermute | solution.py:439
  72.0 3.2 %copy-start.9 = (f32[128]{0:T(128)S(1)}, f32[128]{0:T(128)}, u32[]{:S(2)}) copy-start(f32[128]{0:T(128)} %param.15) | copy-start | bytes 1540
  75.2 1.2 copy-start.1
  76.5 1.0 copy-start.3
  85.3 19.6 %all-to-all-start.1 = ((bf16[16,176,128]{2,1,0:T(8,128)(2,1)}), bf16[16,176,128]{2,1,0:T(8,128)(2,1)S(1)}, u32[]{:S(2)}, u32[]{:S(2)}) async-start(bf16[16,176,128]{2,1,0:T(8,128)(2,1)} %backward.1), calls=%async_computation.1 | async-start | bytes 1441792 | tf_op jit(solution)/shard_map/all_to_all | solution.py:473

commit v2 on v1

--- a/solution.py
+++ b/solution.py
@@ -14,7 +14,7 @@
 PAIRS = ((0, 1), (2, 3), (-3, -2), (4, 5), (-1, 6))
 VMEM = pl.BlockSpec(memory_space=pltpu.VMEM)
 SMEM = pl.BlockSpec(memory_space=pltpu.SMEM)
-LIMIT = 48 * 1024 * 1024
+LIMIT = 24 * 1024 * 1024
 
 
 def dot(a, b):
@@ -57,10 +57,14 @@
 
 
 def forward_kernel(
-    place, top, mid, bot, pick, w1, b1, w2, b2,
-    hidden2, ratio2, patches1, ratio1, fields,
-    left, field, first, spread, pre2, second,
+    place, top, mid, bot, cot, pick, k1, b1, k2, b2,
+    hidden2, to_next, to_previous, ratio2, patches1, ratio1, fields, w2,
+    w1, left, field, first, spread, pre2, second,
 ):
+    lay_weights1(k1, w1)
+    lay_weights2(k2, w2)
+    bias1 = jnp.concatenate([b1[...]] * 8, axis=1)
+    bias2 = jnp.concatenate([b2[...]] * 4, axis=1)
     base_y, base_z, size_y, size_z = place[0], place[1], place[2], place[3]
 
     def inside(offset_y, offset_z, scale):
@@ -111,7 +115,7 @@
 
     def block1(yw, carry):
         stack = field[pl.ds(2 * yw, 4)].reshape(256, 640)
-        pre = dot_tn(stack, w1[...]) + b1[...]
+        pre = dot_tn(stack, w1[...]) + bias1
         e = exps(pre)
         total = e[:, :128] + e[:, 128:]
         total = total + roll(total, 64, 1)
@@ -155,7 +159,7 @@
             axis=1,
         ).reshape(1024, 512)
         term = dot(block, w2[dy]).reshape(8, 4, 32, 256)
-        pre2[...] = term + b2[...] if dy == 0 else pre2[...] + term
+        pre2[...] = term + bias2 if dy == 0 else pre2[...] + term
 
     half = lane((16, 128)) < 64
 
@@ -180,22 +184,72 @@
         return carry
 
     lax.fori_loop(0, 4, block2, 0)
-
-
-def run_forward(place, pieces, pick, w1, b1, w2, b2):
+    to_next[0:128] = hidden2[:, 0:2].reshape(128, 128)
+    to_previous[0:128] = hidden2[:, 2:4].reshape(128, 128)
+    own = cot[...].astype(F32).T.astype(BF16)
+    to_next[128:144] = own
+    to_previous[128:144] = own
+
+
+def lay_weights1(taps, out):
+    group = lane((16, 128)) // 32
+    zero = jnp.zeros((16, 128), F32)
+    for py in range(4):
+        for px in range(4):
+            at = (py * 4 + px) * 16
+            for qy in range(2):
+                dy = py - qy
+                sides = [
+                    taps[(px - qx) * 3 + dy] if 0 <= dy < 3 and 0 <= px - qx < 3 else zero for qx in range(2)
+                ]
+                value = jnp.where(group == 0, sides[0], sides[1])
+                shifted = jnp.where(group == 2, roll(sides[0], 4, 0), roll(sides[1], 4, 0))
+                out[at : at + 16, qy * 128 : qy * 128 + 128] = jnp.where(group < 2, value, shifted).astype(BF16)
+
+
+def lay_weights2(taps, out):
+    zero = jnp.zeros((32, 64), BF16)
+    for dy in range(3):
+        out[dy, 384:512, 0:128] = jnp.zeros((128, 128), BF16)
+        out[dy, 0:128, 128:256] = jnp.zeros((128, 128), BF16)
+        for dz in range(3):
+            for px in range(4):
+                sides = [taps[(px - qx) * 9 + dy * 3 + dz] if 0 <= px - qx < 3 else zero for qx in range(2)]
+                tile = jnp.concatenate(sides, axis=1)
+                for qz in range(2):
+                    at = (dz + qz) * 128 + px * 32
+                    out[dy, at : at + 32, qz * 128 : qz * 128 + 128] = tile
+
+
+def lay_weights3(taps, out):
+    zero = jnp.zeros((64, 128), BF16)
+    for tap in range(9):
+        out[tap, 192:256, 0:128] = zero
+        out[tap, 0:64, 128:256] = zero
+        for dx in range(3):
+            value = taps[dx * 9 + tap]
+            out[tap, dx * 64 : dx * 64 + 64, 0:128] = value
+            out[tap, dx * 64 + 64 : dx * 64 + 128, 128:256] = value
+
+
+def run_forward(*operands):
     return pl.pallas_call(
         forward_kernel,
         name="forward",
         out_shape=(
             jax.ShapeDtypeStruct((4, 4, 16, 128), BF16),
+            jax.ShapeDtypeStruct((144, 128), BF16),
+            jax.ShapeDtypeStruct((144, 128), BF16),
             jax.ShapeDtypeStruct((8, 4, 32, 256), F32),
             jax.ShapeDtypeStruct((6, 6, 32, 128), BF16),
             jax.ShapeDtypeStruct((4, 256, 256), F32),
             jax.ShapeDtypeStruct((10, 64, 256), BF16),
+            jax.ShapeDtypeStruct((3, 512, 256), BF16),
         ),
-        in_specs=[SMEM] + [VMEM] * 8,
-        out_specs=(VMEM,) * 5,
+        in_specs=[SMEM] + [VMEM] * (len(operands) - 1),
+        out_specs=(VMEM,) * 8,
         scratch_shapes=[
+            pltpu.VMEM((256, 256), BF16),
             pltpu.VMEM((22, 80, 256), BF16),
             pltpu.VMEM((22, 64, 640), BF16),
             pltpu.VMEM((10, 10, 80, 128), F32),
@@ -204,16 +258,44 @@
             pltpu.VMEM((4, 32, 128), F32),
         ],
         compiler_params=pltpu.CompilerParams(vmem_limit_bytes=LIMIT),
-    )(place, *pieces, pick, w1, b1, w2, b2)
+    )(*operands)
+
+
+def weave_kernel(lower, hidden2, upper, to_next, to_previous):
+    for target, first_row in ((to_next, 0), (to_previous, 2)):
+        for y in range(2):
+            row, at = first_row + y, y * 128
+            target[at : at + 32] = lower[row * 32 : row * 32 + 32]
+            target[at + 32 : at + 96] = hidden2[row].reshape(64, 128)
+            target[at + 96 : at + 128] = upper[row * 32 : row * 32 + 32]
+        target[256:272] = lower[128:144]
+        target[288:304] = upper[128:144]
+
+
+def run_weave(lower, hidden2, upper, own_cot):
+    def kernel(lower, hidden2, upper, own_cot, to_next, to_previous):
+        weave_kernel(lower, hidden2, upper, to_next, to_previous)
+        to_next[272:288] = own_cot[128:144]
+        to_previous[272:288] = own_cot[128:144]
+
+    return pl.pallas_call(
+        kernel,
+        name="weave",
+        out_shape=(jax.ShapeDtypeStruct((304, 128), BF16),) * 2,
+        in_specs=[VMEM] * 4,
+        out_specs=(VMEM,) * 2,
+    )(lower, hidden2, upper, own_cot)
 
 
 def backward_kernel(
     groups,
-    before, middle, after, own_cot, w3, b3, w2, ratio2, patches1, ratio1, fields,
+    before, lower, middle, upper, after, own_cot, k3, b3, w2, ratio2, patches1, ratio1, fields,
     packed,
-    patches2, pre3, delta3, patch2, grad2, delta2, patch1, grad1, delta1,
+    w3, patches2, pre3, delta3, patch2, grad2, delta2, patch1, grad1, delta1,
 ):
     wide = 128 // groups
+    lay_weights3(k3, w3)
+    bias3_in = jnp.concatenate([b3[...]] * 2, axis=1)
     half = lane((16, 128)) < 64
 
     def lay(y, source):
@@ -227,17 +309,21 @@
         lay(y, lambda z: before[(y * 8 + z) * 16 : (y * 8 + z + 1) * 16])
         lay(y + 6, lambda z: after[(y * 8 + z) * 16 : (y * 8 + z + 1) * 16])
 
-    def lay_middle(y, carry):
-        lay(y + 2, lambda z: middle[y, z])
-        return carry
-
-    lax.fori_loop(0, 4, lay_middle, 0)
+    def pick_middle(y, z):
+        if z < 2:
+            return lower[(y * 2 + z) * 16 : (y * 2 + z + 1) * 16]
+        if z < 6:
+            return middle[y, z - 2]
+        return upper[(y * 2 + z - 6) * 16 : (y * 2 + z - 5) * 16]
+
+    for y in range(4):
+        lay(y + 2, functools.partial(pick_middle, y))
 
     for tap in range(9):
         dy, dz = tap // 3, tap % 3
         block = patches2[dy : dy + 6, dz : dz + 6].reshape(576, 256)
         term = dot(block, w3[tap]).reshape(6, 6, 16, 256)
-        pre3[...] = term + b3[...] if tap == 0 else pre3[...] + term
+        pre3[...] = term + bias3_in if tap == 0 else pre3[...] + term
 
     for wy in range(3):
         for wz in range(3):
@@ -247,7 +333,7 @@
             total = total[:, :128] + total[:, 128:]
             mean = total * 0.125
             if wy == 1:
-                cot = own_cot[wz * 16 : wz * 16 + 16]
+                cot = (lower, own_cot, upper)[wz][128:144]
             else:
                 cot = (before if wy == 0 else after)[256 + wz * 16 : 272 + wz * 16]
             share = cot.astype(F32) * (0.125 / mean)
@@ -302,7 +388,8 @@
     bias2 = own2.astype(F32).sum(axis=0, keepdims=True)
     bias2 = bias2[:, :128] + bias2[:, 128:]
     bias2 = bias2 + roll(bias2, 64, 1)
-    kernel2 = []
+    low_lane = lane((32, 128)) < 64
+    taps = [None] * 27
     for dy in range(3):
         block = jnp.concatenate(
             [
@@ -311,14 +398,18 @@
             ],
             axis=1,
         ).reshape(256, 512)
-        full = dot_tn(own2, block)
+        full = dot_tn(block, own2)
         for dz in range(3):
-            lanes0 = full[:, dz * 128 : dz * 128 + 128]
-            lanes1 = full[:, dz * 128 + 128 : dz * 128 + 256]
-            one = lanes0[:64] + lanes1[128:192]
-            two = lanes0[64:128] + lanes1[192:256]
-            kernel2.append(one + roll(two, 96, 1))
-    kernel2 = jnp.concatenate(kernel2, axis=0).reshape(groups, 576 // groups, 128)
+            rows = full[dz * 128 : dz * 128 + 128, :128] + full[dz * 128 + 128 : dz * 128 + 256, 128:]
+            for dx in range(3):
+                taps[dx * 9 + dy * 3 + dz] = rows[dx * 32 : dx * 32 + 32] + roll(
+                    rows[dx * 32 + 32 : dx * 32 + 64], 64, 1
+                )
+    kernel2 = [
+        jnp.where(low_lane, taps[2 * m], roll(taps[2 * m + 1], 64, 1) if 2 * m + 1 < 27 else 0.0)
+        for m in range(14)
+    ]
+    kernel2 = jnp.concatenate(kernel2, axis=0).reshape(groups, 448 // groups, 128)
 
     for dy in range(3):
         block = delta2[2 - dy : 6 - dy].reshape(512, 256)
@@ -359,26 +450,29 @@
         full = term if full is None else full + term
     full = full.reshape(4, 4, 16, 256)
     kernel1 = []
+    group1 = lane((16, 128)) // 32
     for dy in range(3):
         rows = full[dy, :, :, :128] + full[dy + 1, :, :, 128:]
+        pieces = []
         for dx in range(3):
             value = rows[dx] + roll(rows[dx + 1], 96, 1)
-            kernel1.append(value + roll(roll(value, 12, 0), 64, 1))
-    kernel1 = jnp.concatenate(kernel1, axis=0).reshape(groups, 144 // groups, 128)
+            value = value + roll(roll(value, 12, 0), 64, 1)
+            pieces.append(roll(value, 32 * dx, 1) if dx else value)
+        kernel1.append(jnp.where(group1 == 0, pieces[0], jnp.where(group1 == 1, pieces[1], pieces[2])))
+    kernel1 = jnp.concatenate(kernel1, axis=0).reshape(groups, 48 // groups, 128)
 
     feature_rows = jnp.concatenate([features, jnp.zeros((112, 128), F32)], axis=0).T
     feature_rows = feature_rows.reshape(groups, wide, 128)
-    low_lane = lane((1, 128)) < 64
-    biases = jnp.concatenate([bias3, jnp.where(low_lane, bias2, bias1)], axis=0)
+    biases = jnp.concatenate([bias3, jnp.where(lane((1, 128)) < 64, bias2, bias1)], axis=0)
     biases = jnp.broadcast_to(biases[None], (groups, 2, 128))
-    rows = 14 * wide + 720 // groups + wide + 2
+    rows = 15 * wide + 496 // groups + 2
     fill = packed.shape[1] - rows
     pieces = kernel3 + [feature_rows, kernel2, kernel1, biases, jnp.zeros((groups, fill, 128), F32)]
     packed[...] = jnp.concatenate(pieces, axis=1).astype(BF16)
 
 
 def run_backward(groups, *operands):
-    rows = 14 * (128 // groups) + 720 // groups + 128 // groups + 2
+    rows = 15 * (128 // groups) + 496 // groups + 2
     rows = -(-rows // 16) * 16
     return pl.pallas_call(
         functools.partial(backward_kernel, groups),
@@ -387,6 +481,7 @@
         in_specs=[VMEM] * len(operands),
         out_specs=VMEM,
         scratch_shapes=[
+            pltpu.VMEM((9, 256, 256), BF16),
             pltpu.VMEM((8, 8, 16, 256), BF16),
             pltpu.VMEM((6, 6, 16, 256), F32),
             pltpu.VMEM((6, 6, 16, 256), BF16),
@@ -412,24 +507,32 @@
     return out.reshape(256, 512).astype(jnp.bfloat16)
 
 
-def spread_taps(taps, axis, out_axis):
-    pads = [[(0, 0)] * taps.ndim for _ in range(2)]
-    pads[0][axis] = (0, 1)
-    pads[1][axis] = (1, 0)
-    return jnp.stack([jnp.pad(taps, pads[0]), jnp.pad(taps, pads[1])], axis=out_axis)
-
-
-def weights(kernel1, kernel2, kernel3):
-    k1 = kernel1.reshape(3, 3, 3, 32, 4).transpose(1, 0, 2, 4, 3)
-    k1 = spread_taps(k1, 1, 4)
-    k1 = spread_taps(k1, 2, 4)
-    k1 = spread_taps(k1, 0, 4)
-    k2 = kernel2.reshape(3, 3, 3, 64, 32).transpose(1, 2, 0, 4, 3)
-    k2 = spread_taps(k2, 2, 4)
-    k2 = spread_taps(k2, 1, 4)
-    k3 = kernel3.reshape(3, 3, 3, 128, 64).transpose(1, 2, 0, 4, 3)
-    k3 = spread_taps(k3, 2, 4)
-    return k1.reshape(256, 256), k2.reshape(3, 512, 256), k3.reshape(9, 256, 256)
+def unpack_kernel(rest, grad1, grad2):
+    groups, rows = rest.shape[0], rest.shape[1]
+    rows2 = 448 // groups
+    whole = rest[...].astype(F32)
+    grad = whole[:, :rows2].reshape(14, 32, 128)
+    for tap in range(27):
+        grad2[tap] = grad[tap // 2, :, (tap % 2) * 64 : (tap % 2) * 64 + 64]
+    grad = whole[:, rows2:].reshape(3, 16, 128)
+    for dy in range(3):
+        for dz in range(3):
+            for dx in range(3):
+                grad1[dx * 9 + dy * 3 + dz] = grad[dy, dz * 4 : dz * 4 + 4, dx * 32 : dx * 32 + 32]
+
+
+def run_unpack(rest):
+    return pl.pallas_call(
+        unpack_kernel,
+        name="unpack",
+        out_shape=(jax.ShapeDtypeStruct((27, 4, 32), F32), jax.ShapeDtypeStruct((27, 32, 64), F32)),
+        in_specs=[VMEM],
+        out_specs=(VMEM, VMEM),
+    )(rest)
+
+
+def spread_to_all(value, axis):
+    return lax.all_to_all(jnp.broadcast_to(value[None], (lax.axis_size(axis),) + value.shape), axis, 0, 0, tiled=True)
 
 
 def both_ways(to_next, to_previous, axis):
@@ -450,45 +553,37 @@
     strip = jnp.concatenate([lower[:, 4:], tile, upper[:, :28], jnp.zeros((8, 8, 128), BF16)], axis=1)
     top, bottom = both_ways(strip, strip, "gy")
 
-    w1, w2, w3 = weights(kernel1, kernel2, kernel3)
-    cot = jnp.pad(cotangent[:, 0], ((0, 0), (1, 1), (0, 0)))
-    cot = jnp.stack([cot[:, d : d + size_z] for d in range(3)], axis=2)
-    cot = lax.all_to_all(cot.transpose(1, 0, 2, 3), "gz", 0, 0, tiled=True)
-    cot = cot.reshape(128, 3, 16).transpose(1, 2, 0).reshape(48, 128)
-
-    hidden2, ratio2, patches1, ratio1, fields = run_forward(
-        place, (top, strip, bottom), jnp.asarray(pick_matrix()), w1,
-        jnp.tile(bias1, 8)[None], w2, jnp.tile(bias2, 4)[None],
+    cot = lax.all_to_all(cotangent[:, 0].transpose(1, 0, 2), "gz", 0, 0, tiled=True).reshape(128, 16)
+    k1 = kernel1.transpose(0, 2, 1).reshape(9, 12, 32).astype(F32)
+    k1 = jnp.tile(jnp.pad(k1, ((0, 0), (0, 4), (0, 0))), (1, 1, 4))
+    k2, k3 = kernel2.transpose(0, 2, 1), kernel3.transpose(0, 2, 1)
+
+    hidden2, to_next, to_previous, ratio2, patches1, ratio1, fields, w2 = run_forward(
+        place, top, strip, bottom, cot, jnp.asarray(pick_matrix()), k1, bias1[None], k2, bias2[None]
     )
-    lower, upper = both_ways(hidden2[:, 0:2], hidden2[:, 2:4], "gz")
-    middle = jnp.concatenate([lower, hidden2, upper], axis=1)
-    before, after = both_ways(
-        jnp.concatenate([middle[0:2].reshape(256, 128), cot], axis=0),
-        jnp.concatenate([middle[2:4].reshape(256, 128), cot], axis=0),
-        "gy",
-    )
+    lower, upper = both_ways(to_next, to_previous, "gz")
+    row_next, row_previous = run_weave(lower, hidden2, upper, to_next)
+    before, after = both_ways(row_next, row_previous, "gy")
     packed = run_backward(
-        size_z, before, middle, after, cot, w3, jnp.tile(bias3, 2)[None], w2, ratio2, patches1, ratio1, fields
+        size_z, before, lower, hidden2, upper, after, to_next, k3, bias3[None], w2, ratio2, patches1, ratio1, fields
     )
     packed = lax.all_to_all(packed, "gz", 0, 0, tiled=True)
     at = 14 * wide
     features = packed[:, at : at + wide, :16].transpose(1, 0, 2)[:, None]
     partial = packed.astype(F32).sum(axis=0).astype(BF16)
-    total = lax.all_gather(partial, "gy", axis=0).astype(F32).sum(axis=0)
-    rows2, rows1 = 576 // size_z, 144 // size_z
+    total = spread_to_all(partial, "gy").astype(F32).sum(axis=0)
+    at = at + wide
+    last = at + 496 // size_z
+    grad1, grad2 = run_unpack(spread_to_all(total[at:last].astype(BF16), "gz"))
     low = total[: 9 * wide].reshape(3, 3, wide, 2, 64)
     high = total[9 * wide : 14 * wide].reshape(5, wide, 2, 64).transpose(0, 2, 1, 3)
     high = high.reshape(10, wide, 64)[:9].reshape(3, 3, wide, 1, 64)
     grad3 = jnp.concatenate([low, high], axis=3).transpose(3, 0, 1, 2, 4).reshape(27, wide, 64)
-    at = at + wide
-    rest = lax.all_gather(total[at : at + rows2 + rows1].astype(BF16), "gz", axis=0).astype(F32)
-    grad2 = rest[:, :rows2].reshape(3, 3, 64, 4, 32)[:, :, :, :3]
-    grad2 = grad2.transpose(3, 0, 1, 2, 4).reshape(27, 64, 32)
-    grad1 = rest[:, rows2:].reshape(3, 3, 4, 4, 128)[:, :, :3, :, :32]
-    grad1 = grad1.transpose(1, 0, 2, 4, 3).reshape(27, 32, 4)
-    at = at + rows2 + rows1
-    shift3 = lax.dynamic_slice_in_dim(total[at], place_z * wide, wide, 0)
-    return features, grad1, total[at + 1, 64:96], grad2, total[at + 1, :64], grad3, shift3
+    shift3 = lax.dynamic_slice_in_dim(total[last], place_z * wide, wide, 0)
+    return (
+        features, grad1.transpose(0, 2, 1), total[last + 1, 64:96], grad2.transpose(0, 2, 1),
+        total[last + 1, :64], grad3, shift3,
+    )
 
 
 def solution(mesh):

time: 165 us -> 137 us (0.83); the launches traced: 162 us -> 136 us
  blocking collectives: 50.9 us -> 22.5 us
  starting transfers between devices: 40.6 us -> 50.7 us
  local copies, waits for them, and re-layouts: 28.6 us -> 22.8 us
  other arithmetic: 3.64 us -> 0.94 us
    all_gather x2 -> x0, blocking collectives: 50.9 us -> none  [the longest x1 27.2 us: shards(): lax.all_gather(total[at:at + rows2 + rows1].astype(BF16), 'gz', axis=0)]
    all_to_all x0 -> x1, blocking collectives: none -> 22.5 us  [shards(): packed = lax.all_to_all(packed, 'gz', 0, 0, tiled=True)]
    all_to_all x2 -> x3, starting transfers between devices: 13.8 us -> 24.3 us  [the longest x2 16.6 us: spread_to_all(): lax.all_to_all(jnp.broadcast_to(value[None], (lax.axis_size(axis),) + val...]
    unnamed x27 -> x60, local copies, waits for them, and re-layouts: 6.9 us -> 16.2 us
    another operation x15 -> x2, local copies, waits for them, and re-layouts: 8.53 us -> 0.86 us  [shards(): k1 = jnp.tile(jnp.pad(k1, ((0, 0), (0, 4), (0, 0))), (1, 1, 4))]
    reshape x5 -> x0, local copies, waits for them, and re-layouts: 7.65 us -> none  [the longest x1 3.62 us: weights(): k2.reshape(3, 512, 256)]
    pallas_call x0 -> x2, Pallas kernels: none -> 3.36 us  [the longest x1 1.78 us: run_unpack(): pl.pallas_call(unpack_kernel, name='unpack', out_shape=(jax.ShapeDtypeStr...]
    another operation x6 -> x0, other arithmetic: 2.51 us -> none  [spread_taps(): jnp.stack([jnp.pad(taps, pads[0]), jnp.pad(taps, pads[1])], axis=out_axis)]
  transfers between devices with their start and end apart: 10 -> 11, of which waited for: 2 -> 8; matrix products, arithmetic and copies ran while one was open for 13% -> 3% of each run, Pallas kernels for 0% -> 0%
where the time goes in v2:
time: 137 us; the launch traced here: 136 us
  starting transfers between devices  50.7 us (37%)
  local copies, waits for them, and re-layouts  22.8 us (17%)
  blocking collectives  22.5 us (16%)
  Pallas kernels  19.6 us (14%)
  waiting for transfers between devices  18.5 us (14%)
    all_to_all x1, blocking collectives, shards(): packed = lax.all_to_all(packed, 'gz', 0, 0, tiled=True)  22.5 us
    ppermute x4, starting transfers between devices, both_ways(): lax.ppermute(to_next, axis, forth)  19 us
    all_to_all x2, starting transfers between devices, spread_to_all(): lax.all_to_all(jnp.broadcast_to(value[None], (lax.axis_size(axis),) + val...  16.6 us
    unnamed x60, local copies, waits for them, and re-layouts  16.2 us
    all_to_all x2, waiting for transfers between devices, spread_to_all(): lax.all_to_all(jnp.broadcast_to(value[None], (lax.axis_size(axis),) + val...  11.4 us
    pallas_call x1, Pallas kernels, run_forward(): pl.pallas_call(forward_kernel, name='forward', out_shape=(jax.ShapeDtypeS...  10.6 us
    all_to_all x1, starting transfers between devices, shards(): lax.all_to_all(cotangent[:, 0].transpose(1, 0, 2), 'gz', 0, 0, tiled=True)  7.68 us
    ppermute x4, starting transfers between devices, both_ways(): lax.ppermute(to_previous, axis, back)  7.42 us
  transfers between devices with their start and end apart: 11, of which 8 were waited for; matrix products, arithmetic and copies ran while one was open for 3% of the time, Pallas kernels for 0%

profile of v2, /device:TPU:1, one launch (start us, length us, event | category | flops | bytes accessed | tf_op | source)
XLA Modules:
  0.0 136.0 jit_solution(2270102128124804279)
XLA Ops:
  0.6 0.9 copy.34
  1.5 6.0 %collective-permute-start = (bf16[8,32,128]{2,1,0:T(8,128)(2,1)S(1)}, bf16[8,32,128]{2,1,0:T(8,128)(2,1)S(1)}, u32[]{:S(2)}, u32[]{:S(2)}) collective-permute-start(bf16[8,32,128]{2,1,0:T(8,128)(2,1)S(1)} %bitcast.43), channel_id=1, source_target_pairs={{0,1},{1,2},{2,3},{3,4},{4,5},{5,6},{6,7},{7,8},{8,9},{9,10},{10,1... | collective-permute-start | bytes 196616 | tf_op jit(solution)/shard_map/ppermute | solution.py:542
  7.6 1.9 %collective-permute-start.1 = (bf16[8,32,128]{2,1,0:T(8,128)(2,1)S(1)}, bf16[8,32,128]{2,1,0:T(8,128)(2,1)S(1)}, u32[]{:S(2)}, u32[]{:S(2)}) collective-permute-start(bf16[8,32,128]{2,1,0:T(8,128)(2,1)S(1)} %bitcast.44), channel_id=1, source_target_pairs={{1,0},{2,1},{3,2},{4,3},{5,4},{6,5},{7,6},{8,7},{9,8},{10,9},{11,1... | collective-permute-start | bytes 196616 | tf_op jit(solution)/shard_map/ppermute | solution.py:542
  10.2 7.7 %all-to-all-start = ((bf16[16,8,16]{2,1,0:T(8,128)(2,1)}), bf16[16,8,16]{2,1,0:T(8,128)(2,1)S(1)}, u32[]{:S(2)}, u32[]{:S(2)}) async-start(bf16[16,8,16]{2,1,0:T(8,128)(2,1)} %bitcast.35), calls=%async_computation | async-start | bytes 65536 | tf_op jit(solution)/shard_map/all_to_all | solution.py:556
  18.1 1.3 collective-permute-start.3
  19.4 4.2 %collective-permute-start.2 = (bf16[8,96,128]{2,1,0:T(8,128)(2,1)S(1)}, bf16[8,96,128]{2,1,0:T(8,128)(2,1)S(1)}, u32[]{:S(2)}, u32[]{:S(2)}) collective-permute-start(bf16[8,96,128]{2,1,0:T(8,128)(2,1)S(1)} %maximum_maximum_fusion.mid), channel_id=1, source_target_pairs={{0,16},{16,32},{32,48},{48,64},{64,80},{80,96},{96,112},{1,17},{17... | collective-permute-start | bytes 589832 | tf_op jit(solution)/shard_map/ppermute | solution.py:542
  24.3 0.8 tile.10.k1
  25.1 1.7 %collective-permute-done.3.bot = bf16[8,96,128]{2,1,0:T(8,128)(2,1)S(1)} collective-permute-done((bf16[8,96,128]{2,1,0:T(8,128)(2,1)S(1)}, bf16[8,96,128]{2,1,0:T(8,128)(2,1)S(1)}, u32[]{:S(2)}, u32[]{:S(2)}) %collective-permute-start.3) | collective-permute-done | bytes 196640 | tf_op jit(solution)/shard_map/ppermute | solution.py:542
  29.0 0.9 copy-done.5
  29.9 0.9 copy-done.8
  30.9 0.9 copy-done.9
  31.8 0.9 copy-done.11
  32.7 0.9 copy-done.13
  33.7 10.6 %forward.1 = (bf16[4,4,16,128]{3,2,1,0:T(8,128)(2,1)S(1)}, bf16[144,128]{1,0:T(8,128)(2,1)S(1)}, bf16[144,128]{1,0:T(8,128)(2,1)S(1)}, f32[8,4,32,256]{3,2,1,0:T...) custom-call(s32[4]{0:T(128)S(1)} %copy-done.20, ...), custom_call_target="tpu_custom_call" | custom-call | tf_op jit(solution)/shard_map/forward/pallas_call | solution.py:236
  46.3 2.9 %collective-permute-start.5 = (bf16[144,128]{1,0:T(8,128)(2,1)S(1)}, bf16[144,128]{1,0:T(8,128)(2,1)S(1)}, u32[]{:S(2)}, u32[]{:S(2)}) collective-permute-start(bf16[144,128]{1,0:T(8,128)(2,1)S(1)} %get-tuple-element.21), channel_id=1, source_target_pairs={{1,0},{2,1},{3,2},{4,3},{5,4},{6,5},{7,6},{8,7},{9,8},{10,9},{11,1... | collective-permute-start | bytes 110600 | tf_op jit(solution)/shard_map/ppermute | solution.py:542
  49.2 4.7 %collective-permute-start.4 = (bf16[144,128]{1,0:T(8,128)(2,1)S(1)}, bf16[144,128]{1,0:T(8,128)(2,1)S(1)}, u32[]{:S(2)}, u32[]{:S(2)}) collective-permute-start(bf16[144,128]{1,0:T(8,128)(2,1)S(1)} %get-tuple-element.19.own_cot), channel_id=1, source_target_pairs={{0,1},{1,2},{2,3},{3,4},{4,5},{5,6},{6,7},{7,8},{8,9},{9,10},{10,1... | collective-permute-start | bytes 110600 | tf_op jit(solution)/shard_map/ppermute | solution.py:542
  54.0 1.0 collective-permute-done.4.lower
  55.6 1.6 %weave.1 = (bf16[304,128]{1,0:T(8,128)(2,1)}, bf16[304,128]{1,0:T(8,128)(2,1)}) custom-call(bf16[144,128]{1,0:T(8,128)(2,1)} %copy-done.18, bf16[4,4,16,128]{3,2,1,0:T(8,128)(2,1)} %copy-done.6, bf16[144,128]{1,0:T(8,128)(2,1)} %copy-done.16, bf16[144,128]{1,0:T(8,128)(2,1)} %copy-done.14), custom_call_target="tpu_custom_call" | custom-call | tf_op jit(solution)/shard_map/weave/pallas_call | solution.py:281
  57.2 4.1 %collective-permute-start.6 = (bf16[304,128]{1,0:T(8,128)(2,1)}, bf16[304,128]{1,0:T(8,128)(2,1)S(1)}, u32[]{:S(2)}, u32[]{:S(2)}) collective-permute-start(bf16[304,128]{1,0:T(8,128)(2,1)} %get-tuple-element.22), channel_id=1, source_target_pairs={{0,16},{16,32},{32,48},{48,64},{64,80},{80,96},{96,112},{1,17},{17... | collective-permute-start | bytes 233480 | tf_op jit(solution)/shard_map/ppermute | solution.py:542
  61.3 1.3 collective-permute-start.7
  63.0 3.8 %collective-permute-done.7.after = bf16[304,128]{1,0:T(8,128)(2,1)S(1)} collective-permute-done((bf16[304,128]{1,0:T(8,128)(2,1)}, bf16[304,128]{1,0:T(8,128)(2,1)S(1)}, u32[]{:S(2)}, u32[]{:S(2)}) %collective-permute-start.7) | collective-permute-done | bytes 77856 | tf_op jit(solution)/shard_map/ppermute | solution.py:542
  67.5 1.0 copy-done.2
  68.5 1.0 copy-done.4
  70.9 5.7 %backward.1 = bf16[16,160,128]{2,1,0:T(8,128)(2,1)S(1)} custom-call(bf16[304,128]{1,0:T(8,128)(2,1)S(1)} %collective-permute-done.6.before, bf16[144,128]{1,0:T(8,128)(2,1)S(1)} %copy-done.19, bf16[4,4,16,128]{3,2,1,0:T(8,128)(2,1)S(1)} %copy-done.7, bf16[144,128]{1,0:T(8,128)(2,1)S(1)} %copy-done.17, bf16[304,128]{1,0:T(8,128)(2,1)S(1)} %collective-permute-done.7.after, ...), custom_call_target="tpu_custom_call" | custom-call | tf_op jit(solution)/shard_map/backward/pallas_call | solution.py:477
  76.7 22.5 %all_to_all.20 = bf16[16,160,128]{2,1,0:T(8,128)(2,1)S(1)} all-to-all(bf16[16,160,128]{2,1,0:T(8,128)(2,1)S(1)} %backward.1), channel_id=1, replica_groups=mesh['gy'=8,'gz'=16] {'gz'}, dimensions={0} | all-to-all | bytes 1310720 | tf_op jit(solution)/shard_map/all_to_all | solution.py:570
  99.3 0.8 broadcast_in_dim.32
  100.0 10.9 %all-to-all-start.2 = ((bf16[8,160,128]{2,1,0:T(8,128)(2,1)}), bf16[8,160,128]{2,1,0:T(8,128)(2,1)S(1)}, u32[]{:S(2)}, u32[]{:S(2)}) async-start(bf16[8,160,128]{2,1,0:T(8,128)(2,1)} %broadcast_in_dim.32), calls=%async_computation.2 | async-start | bytes 655360 | tf_op jit(solution)/shard_map/all_to_all | solution.py:535
  111.6 5.8 %all-to-all-done.2 = bf16[8,160,128]{2,1,0:T(8,128)(2,1)S(1)} async-done(((bf16[8,160,128]{2,1,0:T(8,128)(2,1)}), bf16[8,160,128]{2,1,0:T(8,128)(2,1)S(1)}, u32[]{:S(2)}, u32[]{:S(2)}) %all-to-all-start.2) | async-done | bytes 327712 | tf_op jit(solution)/shard_map/all_to_all | solution.py:535
  120.2 5.7 %all-to-all-start.3 = ((bf16[16,31,128]{2,1,0:T(8,128)(2,1)}), bf16[16,31,128]{2,1,0:T(8,128)(2,1)S(1)}, u32[]{:S(2)}, u32[]{:S(2)}) async-start(bf16[16,31,128]{2,1,0:T(8,128)(2,1)} %broadcast_in_dim.33), calls=%async_computation.3 | async-start | bytes 262144 | tf_op jit(solution)/shard_map/all_to_all | solution.py:535
  126.0 0.8 copy-done.26
  128.0 5.6 %all-to-all-done.3.rest = bf16[16,31,128]{2,1,0:T(8,128)(2,1)S(1)} async-done(((bf16[16,31,128]{2,1,0:T(8,128)(2,1)}), bf16[16,31,128]{2,1,0:T(8,128)(2,1)S(1)}, u32[]{:S(2)}, u32[]{:S(2)}) %all-to-all-start.3) | async-done | bytes 127008 | tf_op jit(solution)/shard_map/all_to_all | solution.py:535
  134.2 1.8 %unpack.1 = (f32[27,4,32]{2,1,0:T(4,128)}, f32[27,32,64]{2,1,0:T(8,128)}) custom-call(bf16[16,31,128]{2,1,0:T(8,128)(2,1)} %copy-done.24), custom_call_target="tpu_custom_call" | custom-call | tf_op jit(solution)/shard_map/unpack/pallas_call | solution.py:525
  (84 shorter events, 14.6 us)
Async XLA Ops:
  0.6 8.9 %copy-start.27 = (bf16[8,1,16,16]{3,2,1,0:T(8,128)(2,1)S(1)}, bf16[8,1,16,16]{3,2,1,0:T(8,128)(2,1)}, u32[]{:S(2)}) copy-start(bf16[8,1,16,16]{3,2,1,0:T(8,128)(2,1)} %param.16) | copy-start | bytes 12292
  1.5 16.4 %collective-permute-start = (bf16[8,32,128]{2,1,0:T(8,128)(2,1)S(1)}, bf16[8,32,128]{2,1,0:T(8,128)(2,1)S(1)}, u32[]{:S(2)}, u32[]{:S(2)}) collective-permute-start(bf16[8,32,128]{2,1,0:T(8,128)(2,1)S(1)} %bitcast.43), channel_id=1, source_target_pairs={{0,1},{1,2},{2,3},{3,4},{4,5},{5,6},{6,7},{7,8},{8,9},{9,10},{10,1... | collective-permute-start | bytes 196616 | tf_op jit(solution)/shard_map/ppermute | solution.py:542
  7.6 10.4 %collective-permute-start.1 = (bf16[8,32,128]{2,1,0:T(8,128)(2,1)S(1)}, bf16[8,32,128]{2,1,0:T(8,128)(2,1)S(1)}, u32[]{:S(2)}, u32[]{:S(2)}) collective-permute-start(bf16[8,32,128]{2,1,0:T(8,128)(2,1)S(1)} %bitcast.44), channel_id=1, source_target_pairs={{1,0},{2,1},{3,2},{4,3},{5,4},{6,5},{7,6},{8,7},{9,8},{10,9},{11,1... | collective-permute-start | bytes 196616 | tf_op jit(solution)/shard_map/ppermute | solution.py:542
  10.2 7.7 %copy-start.28 = (bf16[27,32,4]{1,2,0:T(4,128)(2,1)S(1)}, bf16[27,32,4]{1,2,0:T(4,128)(2,1)}, u32[]{:S(2)}) copy-start(bf16[27,32,4]{1,2,0:T(4,128)(2,1)} %param.10) | copy-start | bytes 20740
  10.2 15.0 %all-to-all-start = ((bf16[16,8,16]{2,1,0:T(8,128)(2,1)}), bf16[16,8,16]{2,1,0:T(8,128)(2,1)S(1)}, u32[]{:S(2)}, u32[]{:S(2)}) async-start(bf16[16,8,16]{2,1,0:T(8,128)(2,1)} %bitcast.35), calls=%async_computation | async-start | bytes 65536 | tf_op jit(solution)/shard_map/all_to_all | solution.py:556
  18.1 8.7 %collective-permute-start.3 = (bf16[8,96,128]{2,1,0:T(8,128)(2,1)S(1)}, bf16[8,96,128]{2,1,0:T(8,128)(2,1)S(1)}, u32[]{:S(2)}, u32[]{:S(2)}) collective-permute-start(bf16[8,96,128]{2,1,0:T(8,128)(2,1)S(1)} %maximum_maximum_fusion.mid), channel_id=1, source_target_pairs={{16,0},{32,16},{48,32},{64,48},{80,64},{96,80},{112,96},{17,1},{33... | collective-permute-start | bytes 589832 | tf_op jit(solution)/shard_map/ppermute | solution.py:542
  19.4 8.3 %collective-permute-start.2 = (bf16[8,96,128]{2,1,0:T(8,128)(2,1)S(1)}, bf16[8,96,128]{2,1,0:T(8,128)(2,1)S(1)}, u32[]{:S(2)}, u32[]{:S(2)}) collective-permute-start(bf16[8,96,128]{2,1,0:T(8,128)(2,1)S(1)} %maximum_maximum_fusion.mid), channel_id=1, source_target_pairs={{0,16},{16,32},{32,48},{48,64},{64,80},{80,96},{96,112},{1,17},{17... | collective-permute-start | bytes 589832 | tf_op jit(solution)/shard_map/ppermute | solution.py:542
  29.0 0.9 copy-start.5
  29.9 0.9 copy-start.8
  30.9 0.9 copy-start.9
  31.8 0.9 copy-start.11
  32.7 0.9 copy-start.13
  33.7 33.2 %copy-start = (bf16[27,128,64]{1,2,0:T(8,128)(2,1)S(1)}, bf16[27,128,64]{1,2,0:T(8,128)(2,1)}, u32[]{:S(2)}) copy-start(bf16[27,128,64]{1,2,0:T(8,128)(2,1)} %param.14) | copy-start | bytes 1327108
  44.2 0.7 copy-start.1
  45.0 0.7 copy-start.3
  46.3 8.7 %copy-start.14 = (bf16[144,128]{1,0:T(8,128)(2,1)}, bf16[144,128]{1,0:T(8,128)(2,1)S(1)}, u32[]{:S(2)}) copy-start(bf16[144,128]{1,0:T(8,128)(2,1)S(1)} %get-tuple-element.19.own_cot) | copy-start | bytes 110596
  46.3 7.6 %collective-permute-start.5 = (bf16[144,128]{1,0:T(8,128)(2,1)S(1)}, bf16[144,128]{1,0:T(8,128)(2,1)S(1)}, u32[]{:S(2)}, u32[]{:S(2)}) collective-permute-start(bf16[144,128]{1,0:T(8,128)(2,1)S(1)} %get-tuple-element.21), channel_id=1, source_target_pairs={{1,0},{2,1},{3,2},{4,3},{5,4},{6,5},{7,6},{8,7},{9,8},{10,9},{11,1... | collective-permute-start | bytes 110600 | tf_op jit(solution)/shard_map/ppermute | solution.py:542
  49.2 5.7 %collective-permute-start.4 = (bf16[144,128]{1,0:T(8,128)(2,1)S(1)}, bf16[144,128]{1,0:T(8,128)(2,1)S(1)}, u32[]{:S(2)}, u32[]{:S(2)}) collective-permute-start(bf16[144,128]{1,0:T(8,128)(2,1)S(1)} %get-tuple-element.19.own_cot), channel_id=1, source_target_pairs={{0,1},{1,2},{2,3},{3,4},{4,5},{5,6},{6,7},{7,8},{8,9},{9,10},{10,1... | collective-permute-start | bytes 110600 | tf_op jit(solution)/shard_map/ppermute | solution.py:542
  53.9 1.0 copy-start.16
  55.6 11.2 %copy-start.7 = (bf16[4,4,16,128]{3,2,1,0:T(8,128)(2,1)S(1)}, bf16[4,4,16,128]{3,2,1,0:T(8,128)(2,1)}, u32[]{:S(2)}) copy-start(bf16[4,4,16,128]{3,2,1,0:T(8,128)(2,1)} %copy-done.6) | copy-start | bytes 196612
  55.6 11.2 %copy-start.15 = (bf16[144,128]{1,0:T(8,128)(2,1)S(1)}, bf16[144,128]{1,0:T(8,128)(2,1)}, u32[]{:S(2)}) copy-start(bf16[144,128]{1,0:T(8,128)(2,1)} %copy-done.14) | copy-start | bytes 110596
  57.2 5.9 %collective-permute-start.6 = (bf16[304,128]{1,0:T(8,128)(2,1)}, bf16[304,128]{1,0:T(8,128)(2,1)S(1)}, u32[]{:S(2)}, u32[]{:S(2)}) collective-permute-start(bf16[304,128]{1,0:T(8,128)(2,1)} %get-tuple-element.22), channel_id=1, source_target_pairs={{0,16},{16,32},{32,48},{48,64},{64,80},{80,96},{96,112},{1,17},{17... | collective-permute-start | bytes 233480 | tf_op jit(solution)/shard_map/ppermute | solution.py:542
  61.3 5.5 %collective-permute-start.7 = (bf16[304,128]{1,0:T(8,128)(2,1)}, bf16[304,128]{1,0:T(8,128)(2,1)S(1)}, u32[]{:S(2)}, u32[]{:S(2)}) collective-permute-start(bf16[304,128]{1,0:T(8,128)(2,1)} %get-tuple-element.23), channel_id=1, source_target_pairs={{16,0},{32,16},{48,32},{64,48},{80,64},{96,80},{112,96},{17,1},{33... | collective-permute-start | bytes 233480 | tf_op jit(solution)/shard_map/ppermute | solution.py:542
  67.5 1.0 copy-start.2
  68.4 1.0 copy-start.4
  69.4 0.8 copy-start.17
  70.2 0.8 copy-start.19
  100.0 17.3 %all-to-all-start.2 = ((bf16[8,160,128]{2,1,0:T(8,128)(2,1)}), bf16[8,160,128]{2,1,0:T(8,128)(2,1)S(1)}, u32[]{:S(2)}, u32[]{:S(2)}) async-start(bf16[8,160,128]{2,1,0:T(8,128)(2,1)} %broadcast_in_dim.32), calls=%async_computation.2 | async-start | bytes 655360 | tf_op jit(solution)/shard_map/all_to_all | solution.py:535
  117.4 1.1 copy-start.25
  118.6 0.8 slice-start
  120.2 13.4 %all-to-all-start.3 = ((bf16[16,31,128]{2,1,0:T(8,128)(2,1)}), bf16[16,31,128]{2,1,0:T(8,128)(2,1)S(1)}, u32[]{:S(2)}, u32[]{:S(2)}) async-start(bf16[16,31,128]{2,1,0:T(8,128)(2,1)} %broadcast_in_dim.33), calls=%async_computation.3 | async-start | bytes 262144 | tf_op jit(solution)/shard_map/all_to_all | solution.py:535
  125.9 0.9 copy-start.26
  (9 other events, 5.9 us)

commit v3 on v2

--- a/solution.py
+++ b/solution.py
@@ -13,7 +13,7 @@
 SLOPE = 0.3
 PAIRS = ((0, 1), (2, 3), (-3, -2), (4, 5), (-1, 6))
 VMEM = pl.BlockSpec(memory_space=pltpu.VMEM)
-SMEM = pl.BlockSpec(memory_space=pltpu.SMEM)
+HBM = pl.BlockSpec(memory_space=pltpu.HBM)
 LIMIT = 24 * 1024 * 1024
 
 
@@ -56,16 +56,40 @@
     return jnp.where(rows == count - 1, 0.0, roll(value, count - 1, 0))
 
 
-def forward_kernel(
-    place, top, mid, bot, cot, pick, k1, b1, k2, b2,
-    hidden2, to_next, to_previous, ratio2, patches1, ratio1, fields, w2,
-    w1, left, field, first, spread, pre2, second,
-):
+def fetch(sources, targets, sems):
+    copies = [
+        pltpu.make_async_copy(source, target, sems.at[k])
+        for k, (source, target) in enumerate(zip(sources, targets))
+    ]
+    for copy in copies:
+        copy.start()
+    return copies
+
+
+def landing(operands):
+    return [pltpu.VMEM(x.shape, x.dtype) for x in operands]
+
+
+def forward_kernel(*refs):
+    sources, refs = refs[:9], refs[9:]
+    (to_next, to_previous, *kept_out), refs = refs[:9], refs[9:]
+    (top, mid, bot, cot, pick, k1, b1, k2, b2), refs = refs[:9], refs[9:]
+    kept, refs = refs[:7], refs[7:]
+    hidden2, own_cot, ratio2, patches1, ratio1, fields, w2 = kept
+    w1, left, field, first, spread, pre2, second, in_sems, out_sems = refs
+    copies = fetch(sources, (top, mid, bot, cot, pick, k1, b1, k2, b2), in_sems)
+    leaving = [pltpu.make_async_copy(kept[k], kept_out[k], out_sems.at[k]) for k in range(7)]
+    for k in range(5, 9):
+        copies[k].wait()
     lay_weights1(k1, w1)
     lay_weights2(k2, w2)
+    leaving[6].start()
+    for k in range(5):
+        copies[k].wait()
     bias1 = jnp.concatenate([b1[...]] * 8, axis=1)
     bias2 = jnp.concatenate([b2[...]] * 4, axis=1)
-    base_y, base_z, size_y, size_z = place[0], place[1], place[2], place[3]
+    base_y, base_z = lax.axis_index("gy"), lax.axis_index("gz")
+    size_y, size_z = lax.axis_size("gy"), lax.axis_size("gz")
 
     def inside(offset_y, offset_z, scale):
         row = base_y * (4 // scale) + offset_y
@@ -110,6 +134,7 @@
 
     lax.fori_loop(0, 11, sift, 0)
     fields[...] = field[6:16, :, :256]
+    leaving[5].start()
     first[:, :, 0:8] = jnp.zeros((10, 10, 8, 128), F32)
     first[:, :, 72:80] = jnp.zeros((10, 10, 8, 128), F32)
 
@@ -136,6 +161,7 @@
         return carry
 
     lax.fori_loop(0, 10, block1, 0)
+    leaving[4].start()
 
     group1 = lane((32, 128)) // 32
 
@@ -149,6 +175,7 @@
 
     lax.fori_loop(0, 10, frame, 0)
     patches1[...] = spread[2:8, 2:8]
+    leaving[3].start()
 
     for dy in range(3):
         block = jnp.concatenate(
@@ -184,11 +211,17 @@
         return carry
 
     lax.fori_loop(0, 4, block2, 0)
+    leaving[0].start()
+    leaving[2].start()
     to_next[0:128] = hidden2[:, 0:2].reshape(128, 128)
     to_previous[0:128] = hidden2[:, 2:4].reshape(128, 128)
     own = cot[...].astype(F32).T.astype(BF16)
     to_next[128:144] = own
     to_previous[128:144] = own
+    own_cot[...] = own
+    leaving[1].start()
+    for copy in leaving:
+        copy.wait()
 
 
 def lay_weights1(taps, out):
@@ -233,22 +266,24 @@
 
 
 def run_forward(*operands):
+    kept = (
+        jax.ShapeDtypeStruct((4, 4, 16, 128), BF16),
+        jax.ShapeDtypeStruct((16, 128), BF16),
+        jax.ShapeDtypeStruct((8, 4, 32, 256), F32),
+        jax.ShapeDtypeStruct((6, 6, 32, 128), BF16),
+        jax.ShapeDtypeStruct((4, 256, 256), F32),
+        jax.ShapeDtypeStruct((10, 64, 256), BF16),
+        jax.ShapeDtypeStruct((3, 512, 256), BF16),
+    )
     return pl.pallas_call(
         forward_kernel,
         name="forward",
-        out_shape=(
-            jax.ShapeDtypeStruct((4, 4, 16, 128), BF16),
-            jax.ShapeDtypeStruct((144, 128), BF16),
-            jax.ShapeDtypeStruct((144, 128), BF16),
-            jax.ShapeDtypeStruct((8, 4, 32, 256), F32),
-            jax.ShapeDtypeStruct((6, 6, 32, 128), BF16),
-            jax.ShapeDtypeStruct((4, 256, 256), F32),
-            jax.ShapeDtypeStruct((10, 64, 256), BF16),
-            jax.ShapeDtypeStruct((3, 512, 256), BF16),
-        ),
-        in_specs=[SMEM] + [VMEM] * (len(operands) - 1),
-        out_specs=(VMEM,) * 8,
-        scratch_shapes=[
+        out_shape=(jax.ShapeDtypeStruct((144, 128), BF16),) * 2 + kept,
+        in_specs=[HBM] * len(operands),
+        out_specs=(VMEM,) * 2 + (HBM,) * 7,
+        scratch_shapes=landing(operands)
+        + landing(kept)
+        + [
             pltpu.VMEM((256, 256), BF16),
             pltpu.VMEM((22, 80, 256), BF16),
             pltpu.VMEM((22, 64, 640), BF16),
@@ -256,45 +291,53 @@
             pltpu.VMEM((10, 10, 32, 128), BF16),
             pltpu.VMEM((8, 4, 32, 256), F32),
             pltpu.VMEM((4, 32, 128), F32),
+            pltpu.SemaphoreType.DMA((9,)),
+            pltpu.SemaphoreType.DMA((7,)),
         ],
         compiler_params=pltpu.CompilerParams(vmem_limit_bytes=LIMIT),
     )(*operands)
 
 
-def weave_kernel(lower, hidden2, upper, to_next, to_previous):
+def weave_kernel(lower, hidden2, upper, own_cot, to_next, to_previous, sems):
+    pairs = []
     for target, first_row in ((to_next, 0), (to_previous, 2)):
         for y in range(2):
             row, at = first_row + y, y * 128
-            target[at : at + 32] = lower[row * 32 : row * 32 + 32]
-            target[at + 32 : at + 96] = hidden2[row].reshape(64, 128)
-            target[at + 96 : at + 128] = upper[row * 32 : row * 32 + 32]
-        target[256:272] = lower[128:144]
-        target[288:304] = upper[128:144]
-
-
-def run_weave(lower, hidden2, upper, own_cot):
-    def kernel(lower, hidden2, upper, own_cot, to_next, to_previous):
-        weave_kernel(lower, hidden2, upper, to_next, to_previous)
-        to_next[272:288] = own_cot[128:144]
-        to_previous[272:288] = own_cot[128:144]
-
+            pairs.append((lower.at[pl.ds(row * 32, 32)], target.at[pl.ds(at, 32)]))
+            for z in range(4):
+                pairs.append((hidden2.at[row, z], target.at[pl.ds(at + 32 + 16 * z, 16)]))
+            pairs.append((upper.at[pl.ds(row * 32, 32)], target.at[pl.ds(at + 96, 32)]))
+        pairs.append((lower.at[pl.ds(128, 16)], target.at[pl.ds(256, 16)]))
+        pairs.append((own_cot, target.at[pl.ds(272, 16)]))
+        pairs.append((upper.at[pl.ds(128, 16)], target.at[pl.ds(288, 16)]))
+    for copy in fetch(*zip(*pairs), sems):
+        copy.wait()
+
+
+def run_weave(*operands):
     return pl.pallas_call(
-        kernel,
+        weave_kernel,
         name="weave",
         out_shape=(jax.ShapeDtypeStruct((304, 128), BF16),) * 2,
-        in_specs=[VMEM] * 4,
-        out_specs=(VMEM,) * 2,
-    )(lower, hidden2, upper, own_cot)
-
-
-def backward_kernel(
-    groups,
-    before, lower, middle, upper, after, own_cot, k3, b3, w2, ratio2, patches1, ratio1, fields,
-    packed,
-    w3, patches2, pre3, delta3, patch2, grad2, delta2, patch1, grad1, delta1,
-):
+        in_specs=[HBM] * 4,
+        out_specs=(HBM,) * 2,
+        scratch_shapes=[pltpu.SemaphoreType.DMA((30,))],
+    )(*operands)
+
+
+def backward_kernel(*refs):
+    sources, packed, refs = refs[:13], refs[13], refs[14:]
+    landed, refs = refs[:13], refs[13:]
+    k3, b3, lower, middle, upper, own_cot, before, after, ratio2, w2, patches1, ratio1, fields = landed
+    w3, patches2, pre3, delta3, patch2, grad2, delta2, patch1, grad1, delta1, turned, in_sems = refs
+    copies = fetch(sources, landed, in_sems)
+    rows_y, groups = packed.shape[0], packed.shape[1]
     wide = 128 // groups
+    for k in range(2):
+        copies[k].wait()
     lay_weights3(k3, w3)
+    for k in range(2, 8):
+        copies[k].wait()
     bias3_in = jnp.concatenate([b3[...]] * 2, axis=1)
     half = lane((16, 128)) < 64
 
@@ -333,7 +376,7 @@
             total = total[:, :128] + total[:, 128:]
             mean = total * 0.125
             if wy == 1:
-                cot = (lower, own_cot, upper)[wz][128:144]
+                cot = own_cot[...] if wz == 1 else (lower if wz == 0 else upper)[128:144]
             else:
                 cot = (before if wy == 0 else after)[256 + wz * 16 : 272 + wz * 16]
             share = cot.astype(F32) * (0.125 / mean)
@@ -379,6 +422,7 @@
             grad2[y, z, pl.ds(0, 16, stride=2), :] = jnp.where(half, swapped, x)
             grad2[y, z, pl.ds(1, 16, stride=2), :] = jnp.where(half, x, swapped)
 
+    copies[8].wait()
     for y in range(6):
         value = grad2[(y + 1) // 2]
         value = jnp.concatenate([value, value], axis=2)
@@ -388,7 +432,8 @@
     bias2 = own2.astype(F32).sum(axis=0, keepdims=True)
     bias2 = bias2[:, :128] + bias2[:, 128:]
     bias2 = bias2 + roll(bias2, 64, 1)
-    low_lane = lane((32, 128)) < 64
+    copies[9].wait()
+    copies[10].wait()
     taps = [None] * 27
     for dy in range(3):
         block = jnp.concatenate(
@@ -405,12 +450,6 @@
                 taps[dx * 9 + dy * 3 + dz] = rows[dx * 32 : dx * 32 + 32] + roll(
                     rows[dx * 32 + 32 : dx * 32 + 64], 64, 1
                 )
-    kernel2 = [
-        jnp.where(low_lane, taps[2 * m], roll(taps[2 * m + 1], 64, 1) if 2 * m + 1 < 27 else 0.0)
-        for m in range(14)
-    ]
-    kernel2 = jnp.concatenate(kernel2, axis=0).reshape(groups, 448 // groups, 128)
-
     for dy in range(3):
         block = delta2[2 - dy : 6 - dy].reshape(512, 256)
         term = dot_nt(block, w2[dy]).reshape(4, 4, 32, 512)
@@ -423,6 +462,9 @@
         value = jnp.where(group == which, value, 0.0)
         value = value + roll(value, 32, 1)
         return value + roll(value, 64, 1)
+
+    copies[11].wait()
+    copies[12].wait()
 
     def gather1(y, carry):
         for z, (zo_a, pz_a, zo_b, pz_b) in enumerate(((0, 3, 1, 1), (1, 2, 2, 0), (1, 3, 2, 1), (2, 2, 3, 0))):
@@ -450,37 +492,49 @@
         full = term if full is None else full + term
     full = full.reshape(4, 4, 16, 256)
     kernel1 = []
-    group1 = lane((16, 128)) // 32
     for dy in range(3):
         rows = full[dy, :, :, :128] + full[dy + 1, :, :, 128:]
-        pieces = []
         for dx in range(3):
             value = rows[dx] + roll(rows[dx + 1], 96, 1)
-            value = value + roll(roll(value, 12, 0), 64, 1)
-            pieces.append(roll(value, 32 * dx, 1) if dx else value)
-        kernel1.append(jnp.where(group1 == 0, pieces[0], jnp.where(group1 == 1, pieces[1], pieces[2])))
-    kernel1 = jnp.concatenate(kernel1, axis=0).reshape(groups, 48 // groups, 128)
-
-    feature_rows = jnp.concatenate([features, jnp.zeros((112, 128), F32)], axis=0).T
-    feature_rows = feature_rows.reshape(groups, wide, 128)
-    biases = jnp.concatenate([bias3, jnp.where(lane((1, 128)) < 64, bias2, bias1)], axis=0)
-    biases = jnp.broadcast_to(biases[None], (groups, 2, 128))
-    rows = 15 * wide + 496 // groups + 2
-    fill = packed.shape[1] - rows
-    pieces = kernel3 + [feature_rows, kernel2, kernel1, biases, jnp.zeros((groups, fill, 128), F32)]
-    packed[...] = jnp.concatenate(pieces, axis=1).astype(BF16)
-
-
-def run_backward(groups, *operands):
-    rows = 15 * (128 // groups) + 496 // groups + 2
-    rows = -(-rows // 16) * 16
+            kernel1.append(value + roll(roll(value, 12, 0), 64, 1))
+
+    biases = jnp.concatenate(
+        [bias3, jnp.where(lane((1, 128)) < 64, bias2, bias1), jnp.zeros((14, 128), F32)], axis=0
+    )
+    shared = jnp.concatenate(taps + kernel1 + [biases], axis=0)
+    count = rows_y * groups
+    shared = shared.reshape(rows_y, groups, 1024 // count, 128)
+
+    turned[...] = jnp.concatenate([features, jnp.zeros((112, 128), F32)], axis=0).T
+    feature_rows = turned[pl.ds(0, 16, stride=8), :]
+    for c in range(1, 8):
+        feature_rows = feature_rows + roll(turned[pl.ds(c, 16, stride=8), :], 16 * c, 1)
+    feature_rows = feature_rows.reshape(groups, wide // 8, 128)
+
+    kernel3 = jnp.concatenate(kernel3, axis=1)
+    share = 14 * wide // rows_y
+    used = 1024 // count + share + wide // 8
+    fill = jnp.zeros((groups, packed.shape[2] - used, 128), F32)
+    for a in range(rows_y):
+        own = kernel3[:, a * share : a * share + share]
+        packed[a] = jnp.concatenate([shared[a], own, feature_rows, fill], axis=1).astype(BF16)
+
+
+def packed_rows(rows_y, groups):
+    wide = 128 // groups
+    used = 1024 // (rows_y * groups) + 14 * wide // rows_y + wide // 8
+    return -(-used // 8) * 8
+
+
+def run_backward(rows_y, groups, *operands):
     return pl.pallas_call(
-        functools.partial(backward_kernel, groups),
+        backward_kernel,
         name="backward",
-        out_shape=jax.ShapeDtypeStruct((groups, rows, 128), BF16),
-        in_specs=[VMEM] * len(operands),
+        out_shape=jax.ShapeDtypeStruct((rows_y, groups, packed_rows(rows_y, groups), 128), BF16),
+        in_specs=[HBM] * len(operands),
         out_specs=VMEM,
-        scratch_shapes=[
+        scratch_shapes=landing(operands)
+        + [
             pltpu.VMEM((9, 256, 256), BF16),
             pltpu.VMEM((8, 8, 16, 256), BF16),
             pltpu.VMEM((6, 6, 16, 256), F32),
@@ -491,9 +545,116 @@
             pltpu.VMEM((4, 4, 32, 512), F32),
             pltpu.VMEM((4, 64, 128), F32),
             pltpu.VMEM((4, 256, 256), BF16),
+            pltpu.VMEM((128, 128), F32),
+            pltpu.SemaphoreType.DMA((13,)),
         ],
         compiler_params=pltpu.CompilerParams(vmem_limit_bytes=LIMIT),
     )(*operands)
+
+
+def sum_kernel(source, to_column, to_all, features, landed, shown, sems):
+    rows_y = to_column.shape[0]
+    count, shared = to_all.shape[0], to_all.shape[1]
+    groups = count // rows_y
+    wide = 128 // groups
+    share = 14 * wide // rows_y
+    parts = sems.shape[0] - 1
+    size = count // parts
+    copies = fetch(
+        [source.at[pl.ds(k * size, size)] for k in range(parts)],
+        [landed.at[pl.ds(k * size, size)] for k in range(parts)],
+        sems,
+    )
+    total = None
+    for k in range(parts):
+        copies[k].wait()
+        term = landed[k * size : k * size + size].astype(F32).sum(axis=0)
+        total = term if total is None else total + term
+    total = total.astype(BF16).astype(F32)
+    to_all[...] = jnp.broadcast_to(total[None, :shared], to_all.shape).astype(BF16)
+    fill = jnp.zeros((to_column.shape[1] - share, 128), F32)
+    column = jnp.concatenate([total[shared : shared + share], fill], axis=0)
+    to_column[...] = jnp.broadcast_to(column[None], to_column.shape).astype(BF16)
+    own = landed[pl.ds(lax.axis_index("gy") * groups, groups)].astype(F32)
+    for c in range(wide):
+        shown[c] = own[:, shared + share + c // 8, (c % 8) * 16 : (c % 8) * 16 + 16].astype(BF16)
+    last = pltpu.make_async_copy(shown, features, sems.at[parts])
+    last.start()
+    last.wait()
+
+
+def run_sum(received, rows_y, groups):
+    count, wide = rows_y * groups, 128 // groups
+    share = -(-(14 * wide // rows_y) // 16) * 16
+    return pl.pallas_call(
+        sum_kernel,
+        name="sum",
+        out_shape=(
+            jax.ShapeDtypeStruct((rows_y, share, 128), BF16),
+            jax.ShapeDtypeStruct((count, 1024 // count, 128), BF16),
+            jax.ShapeDtypeStruct((wide, groups, 16), BF16),
+        ),
+        in_specs=[HBM],
+        out_specs=(VMEM, VMEM, HBM),
+        scratch_shapes=[
+            pltpu.VMEM(received.shape, BF16),
+            pltpu.VMEM((wide, groups, 16), BF16),
+            pltpu.SemaphoreType.DMA((5,)),
+        ],
+    )(received)
+
+
+def unpack_kernel(column_in, shared_in, grad1, grad2, grad3, shift1, shift2, shift3, column, shared, lines, sems):
+    copies = fetch((column_in, shared_in), (column, shared), sems)
+    rows_y, count = column.shape[0], shared.shape[0]
+    wide = grad3.shape[1]
+    share = 14 * wide // rows_y
+    copies[0].wait()
+    for a in range(rows_y):
+        lines[a * share : a * share + share] = column[a].astype(F32)[:share]
+    for tap in range(9):
+        low = lines[tap * wide : tap * wide + wide]
+        grad3[tap] = low[:, :64]
+        grad3[9 + tap] = low[:, 64:]
+        at = (9 + tap // 2) * wide
+        grad3[18 + tap] = lines[at : at + wide][:, (tap % 2) * 64 : (tap % 2) * 64 + 64]
+    copies[1].wait()
+    rows = shared[...].astype(F32).reshape(1024, 128)
+    for tap in range(27):
+        grad2[tap] = rows[tap * 32 : tap * 32 + 32, :64]
+    for dy in range(3):
+        for dx in range(3):
+            at = 864 + (dy * 3 + dx) * 16
+            for dz in range(3):
+                grad1[dx * 9 + dy * 3 + dz] = rows[at + dz * 4 : at + dz * 4 + 4, :32]
+    biases = rows[1008:1016]
+    shift1[...] = biases[1:2, 64:96]
+    shift2[...] = biases[1:2, :64]
+    place = lax.axis_index("gz")
+    shift3[...] = roll(biases, lax.rem(128 - place * wide, 128), 1)[0:1, :wide]
+
+
+def run_unpack(column, shared, wide):
+    return pl.pallas_call(
+        unpack_kernel,
+        name="unpack",
+        out_shape=(
+            jax.ShapeDtypeStruct((27, 4, 32), F32),
+            jax.ShapeDtypeStruct((27, 32, 64), F32),
+            jax.ShapeDtypeStruct((27, wide, 64), F32),
+            jax.ShapeDtypeStruct((1, 32), F32),
+            jax.ShapeDtypeStruct((1, 64), F32),
+            jax.ShapeDtypeStruct((1, wide), F32),
+        ),
+        in_specs=[HBM] * 2,
+        out_specs=(VMEM,) * 6,
+        scratch_shapes=[
+            pltpu.VMEM(column.shape, BF16),
+            pltpu.VMEM(shared.shape, BF16),
+            pltpu.VMEM((14 * wide, 128), F32),
+            pltpu.SemaphoreType.DMA((2,)),
+        ],
+    )(column, shared)
 
 
 def pick_matrix():
@@ -507,34 +668,6 @@
     return out.reshape(256, 512).astype(jnp.bfloat16)
 
 
-def unpack_kernel(rest, grad1, grad2):
-    groups, rows = rest.shape[0], rest.shape[1]
-    rows2 = 448 // groups
-    whole = rest[...].astype(F32)
-    grad = whole[:, :rows2].reshape(14, 32, 128)
-    for tap in range(27):
-        grad2[tap] = grad[tap // 2, :, (tap % 2) * 64 : (tap % 2) * 64 + 64]
-    grad = whole[:, rows2:].reshape(3, 16, 128)
-    for dy in range(3):
-        for dz in range(3):
-            for dx in range(3):
-                grad1[dx * 9 + dy * 3 + dz] = grad[dy, dz * 4 : dz * 4 + 4, dx * 32 : dx * 32 + 32]
-
-
-def run_unpack(rest):
-    return pl.pallas_call(
-        unpack_kernel,
-        name="unpack",
-        out_shape=(jax.ShapeDtypeStruct((27, 4, 32), F32), jax.ShapeDtypeStruct((27, 32, 64), F32)),
-        in_specs=[VMEM],
-        out_specs=(VMEM, VMEM),
-    )(rest)
-
-
-def spread_to_all(value, axis):
-    return lax.all_to_all(jnp.broadcast_to(value[None], (lax.axis_size(axis),) + value.shape), axis, 0, 0, tiled=True)
-
-
 def both_ways(to_next, to_previous, axis):
     devices = lax.axis_size(axis)
     forth = [(i, i + 1) for i in range(devices - 1)]
@@ -544,45 +677,37 @@
 
 def shards(universe, kernel1, bias1, kernel2, bias2, kernel3, bias3, cotangent):
     size_y, size_z = lax.axis_size("gy"), lax.axis_size("gz")
-    place_y, place_z = lax.axis_index("gy"), lax.axis_index("gz")
     wide = 128 // size_z
-    place = jnp.stack([place_y, place_z, jnp.int32(size_y), jnp.int32(size_z)]).astype(jnp.int32)
 
     tile = universe.transpose(1, 2, 0, 3).reshape(8, 32, 128)
     lower, upper = both_ways(tile, tile, "gz")
     strip = jnp.concatenate([lower[:, 4:], tile, upper[:, :28], jnp.zeros((8, 8, 128), BF16)], axis=1)
     top, bottom = both_ways(strip, strip, "gy")
 
+    cotangent, strip = lax.optimization_barrier((cotangent, strip))
     cot = lax.all_to_all(cotangent[:, 0].transpose(1, 0, 2), "gz", 0, 0, tiled=True).reshape(128, 16)
     k1 = kernel1.transpose(0, 2, 1).reshape(9, 12, 32).astype(F32)
     k1 = jnp.tile(jnp.pad(k1, ((0, 0), (0, 4), (0, 0))), (1, 1, 4))
     k2, k3 = kernel2.transpose(0, 2, 1), kernel3.transpose(0, 2, 1)
 
-    hidden2, to_next, to_previous, ratio2, patches1, ratio1, fields, w2 = run_forward(
-        place, top, strip, bottom, cot, jnp.asarray(pick_matrix()), k1, bias1[None], k2, bias2[None]
+    to_next, to_previous, hidden2, own_cot, ratio2, patches1, ratio1, fields, w2 = run_forward(
+        top, strip, bottom, cot, jnp.asarray(pick_matrix()), k1, bias1[None], k2, bias2[None]
     )
     lower, upper = both_ways(to_next, to_previous, "gz")
-    row_next, row_previous = run_weave(lower, hidden2, upper, to_next)
+    row_next, row_previous = run_weave(lower, hidden2, upper, own_cot)
     before, after = both_ways(row_next, row_previous, "gy")
     packed = run_backward(
-        size_z, before, lower, hidden2, upper, after, to_next, k3, bias3[None], w2, ratio2, patches1, ratio1, fields
+        size_y, size_z,
+        k3, bias3[None], lower, hidden2, upper, own_cot, before, after, ratio2, w2, patches1, ratio1, fields,
     )
-    packed = lax.all_to_all(packed, "gz", 0, 0, tiled=True)
-    at = 14 * wide
-    features = packed[:, at : at + wide, :16].transpose(1, 0, 2)[:, None]
-    partial = packed.astype(F32).sum(axis=0).astype(BF16)
-    total = spread_to_all(partial, "gy").astype(F32).sum(axis=0)
-    at = at + wide
-    last = at + 496 // size_z
-    grad1, grad2 = run_unpack(spread_to_all(total[at:last].astype(BF16), "gz"))
-    low = total[: 9 * wide].reshape(3, 3, wide, 2, 64)
-    high = total[9 * wide : 14 * wide].reshape(5, wide, 2, 64).transpose(0, 2, 1, 3)
-    high = high.reshape(10, wide, 64)[:9].reshape(3, 3, wide, 1, 64)
-    grad3 = jnp.concatenate([low, high], axis=3).transpose(3, 0, 1, 2, 4).reshape(27, wide, 64)
-    shift3 = lax.dynamic_slice_in_dim(total[last], place_z * wide, wide, 0)
+    packed = packed.reshape((size_y * size_z,) + packed.shape[2:])
+    packed = lax.all_to_all(packed, ("gy", "gz"), 0, 0, tiled=True)
+    to_column, to_all, features = run_sum(packed, size_y, size_z)
+    to_column = lax.all_to_all(to_column, "gy", 0, 0, tiled=True)
+    to_all = lax.all_to_all(to_all, ("gy", "gz"), 0, 0, tiled=True)
+    grad1, grad2, grad3, shift1, shift2, shift3 = run_unpack(to_column, to_all, wide)
     return (
-        features, grad1.transpose(0, 2, 1), total[last + 1, 64:96], grad2.transpose(0, 2, 1),
-        total[last + 1, :64], grad3, shift3,
+        features[:, None], grad1.transpose(0, 2, 1), shift1[0], grad2.transpose(0, 2, 1), shift2[0], grad3, shift3[0]
     )
 
 

time: 137 us -> 152 us (1.11)
  blocking collectives: 22.5 us -> 54.8 us
  starting transfers between devices: 50.7 us -> 28.9 us
  Pallas kernels: 19.6 us -> 29.5 us
  local copies, waits for them, and re-layouts: 22.8 us -> 16 us
  waiting for transfers between devices: 18.5 us -> 20.4 us
    all_to_all x1 -> x3, blocking collectives: 22.5 us -> 54.8 us  [the longest x1 28.6 us: shards(): packed = lax.all_to_all(packed, ('gy', 'gz'), 0, 0, tiled=True)]
    all_to_all x2 -> x0, starting transfers between devices: 16.6 us -> none  [spread_to_all(): lax.all_to_all(jnp.broadcast_to(value[None], (lax.axis_size(axis),) + val...]
    all_to_all x2 -> x0, waiting for transfers between devices: 11.4 us -> none  [spread_to_all(): lax.all_to_all(jnp.broadcast_to(value[None], (lax.axis_size(axis),) + val...]
    pallas_call x2 -> x3, Pallas kernels: 7.3 us -> 15.7 us  [the longest x1 6.92 us: run_backward(): pl.pallas_call(backward_kernel, name='backward', out_shape=jax.ShapeDtype...]
    ppermute x4, waiting for transfers between devices: 5.45 us -> 13.5 us  [both_ways(): lax.ppermute(to_previous, axis, back)]
    all_to_all x1, waiting for transfers between devices: 0.06 us -> 6.42 us  [shards(): lax.all_to_all(cotangent[:, 0].transpose(1, 0, 2), 'gz', 0, 0, tiled=True)]
    ppermute x4, starting transfers between devices: 19 us -> 16.3 us  [both_ways(): lax.ppermute(to_next, axis, forth)]
    unnamed x60 -> x50, local copies, waits for them, and re-layouts: 16.2 us -> 13.5 us
  transfers between devices with their start and end apart: 11 -> 9, of which waited for: 8 -> 5; matrix products, arithmetic and copies ran while one was open for 3% -> 1% of each run, Pallas kernels for 0% -> 0%
where the time goes in v3:
time: 152 us; the launch traced here: 151 us
  blocking collectives  54.8 us (36%)
  Pallas kernels  29.5 us (19%)
  starting transfers between devices  28.9 us (19%)
  waiting for transfers between devices  20.4 us (13%)
  local copies, waits for them, and re-layouts  16 us (11%)
    all_to_all x1, blocking collectives, shards(): packed = lax.all_to_all(packed, ('gy', 'gz'), 0, 0, tiled=True)  28.6 us
    all_to_all x1, blocking collectives, shards(): to_all = lax.all_to_all(to_all, ('gy', 'gz'), 0, 0, tiled=True)  17.1 us
    ppermute x4, starting transfers between devices, both_ways(): lax.ppermute(to_next, axis, forth)  16.3 us
    ppermute x4, waiting for transfers between devices, both_ways(): lax.ppermute(to_previous, axis, back)  13.5 us
    unnamed x50, local copies, waits for them, and re-layouts  13.5 us
    pallas_call x1, Pallas kernels, run_forward(): pl.pallas_call(forward_kernel, name='forward', out_shape=(jax.ShapeDtypeS...  12 us
    all_to_all x1, blocking collectives, shards(): to_column = lax.all_to_all(to_column, 'gy', 0, 0, tiled=True)  9.06 us
    pallas_call x1, Pallas kernels, run_backward(): pl.pallas_call(backward_kernel, name='backward', out_shape=jax.ShapeDtype...  6.92 us
  transfers between devices with their start and end apart: 9, of which 5 were waited for; matrix products, arithmetic and copies ran while one was open for 1% of the time, Pallas kernels for 0%

profile of v3, /device:TPU:1, one launch (start us, length us, event | category | flops | bytes accessed | tf_op | source)
XLA Modules:
  0.0 150.5 jit_solution(13454626741121147692)
XLA Ops:
  0.6 0.9 copy.19
  1.5 6.0 %collective-permute-start = (bf16[8,32,128]{2,1,0:T(8,128)(2,1)S(1)}, bf16[8,32,128]{2,1,0:T(8,128)(2,1)S(1)}, u32[]{:S(2)}, u32[]{:S(2)}) collective-permute-start(bf16[8,32,128]{2,1,0:T(8,128)(2,1)S(1)} %bitcast.31), channel_id=1, source_target_pairs={{0,1},{1,2},{2,3},{3,4},{4,5},{5,6},{6,7},{7,8},{8,9},{9,10},{10,1... | collective-permute-start | bytes 196616 | tf_op jit(solution)/shard_map/ppermute | solution.py:675
  7.6 1.9 %collective-permute-start.1 = (bf16[8,32,128]{2,1,0:T(8,128)(2,1)S(1)}, bf16[8,32,128]{2,1,0:T(8,128)(2,1)S(1)}, u32[]{:S(2)}, u32[]{:S(2)}) collective-permute-start(bf16[8,32,128]{2,1,0:T(8,128)(2,1)S(1)} %bitcast.32), channel_id=1, source_target_pairs={{1,0},{2,1},{3,2},{4,3},{5,4},{6,5},{7,6},{8,7},{9,8},{10,9},{11,1... | collective-permute-start | bytes 196616 | tf_op jit(solution)/shard_map/ppermute | solution.py:675
  9.6 5.0 %collective-permute-done.1 = bf16[8,32,128]{2,1,0:T(8,128)(2,1)S(1)} collective-permute-done((bf16[8,32,128]{2,1,0:T(8,128)(2,1)S(1)}, bf16[8,32,128]{2,1,0:T(8,128)(2,1)S(1)}, u32[]{:S(2)}, u32[]{:S(2)}) %collective-permute-start.1) | collective-permute-done | bytes 65568 | tf_op jit(solution)/shard_map/ppermute | solution.py:675
  14.8 1.3 collective-permute-start.3
  16.1 4.2 %collective-permute-start.2 = (bf16[8,96,128]{2,1,0:T(8,128)(2,1)S(1)}, bf16[8,96,128]{2,1,0:T(8,128)(2,1)S(1)}, u32[]{:S(2)}, u32[]{:S(2)}) collective-permute-start(bf16[8,96,128]{2,1,0:T(8,128)(2,1)S(1)} %maximum_maximum_fusion.refs_1_), channel_id=1, source_target_pairs={{0,16},{16,32},{32,48},{48,64},{64,80},{80,96},{96,112},{1,17},{17... | collective-permute-start | bytes 589832 | tf_op jit(solution)/shard_map/ppermute | solution.py:675
  21.0 6.2 %all-to-all-start = ((bf16[16,8,16]{2,1,0:T(8,128)(2,1)}), bf16[16,8,16]{2,1,0:T(8,128)(2,1)S(1)}, u32[]{:S(2)}, u32[]{:S(2)}) async-start(bf16[16,8,16]{2,1,0:T(8,128)(2,1)} %bitcast.22), calls=%async_computation | async-start | bytes 65536 | tf_op jit(solution)/shard_map/all_to_all | solution.py:688
  27.2 0.8 tile.10.refs_5_
  28.0 6.4 %all-to-all-done = bf16[16,8,16]{2,1,0:T(8,128)(2,1)S(1)} async-done(((bf16[16,8,16]{2,1,0:T(8,128)(2,1)}), bf16[16,8,16]{2,1,0:T(8,128)(2,1)S(1)}, u32[]{:S(2)}, u32[]{:S(2)}) %all-to-all-start) | async-done | bytes 4128 | tf_op jit(solution)/shard_map/all_to_all | solution.py:688
  36.4 0.9 copy-done.5
  37.3 0.9 copy-done.8
  38.3 0.9 copy-done.9
  39.2 0.9 copy-done.11
  40.1 0.9 copy-done.13
  41.1 12.0 %forward.1 = (bf16[144,128]{1,0:T(8,128)(2,1)S(1)}, bf16[144,128]{1,0:T(8,128)(2,1)S(1)}, bf16[4,4,16,128]{3,2,1,0:T(8,128)(2,1)S(1)}, bf16[16,128]{1,0:T(8,128)...) custom-call(bf16[8,96,128]{2,1,0:T(8,128)(2,1)S(1)} %copy-done.13, ...), custom_call_target="tpu_custom_call" | custom-call | tf_op jit(solution)/shard_map/forward/pallas_call | solution.py:278
  55.1 2.5 %collective-permute-start.4 = (bf16[144,128]{1,0:T(8,128)(2,1)S(1)}, bf16[144,128]{1,0:T(8,128)(2,1)S(1)}, u32[]{:S(2)}, u32[]{:S(2)}) collective-permute-start(bf16[144,128]{1,0:T(8,128)(2,1)S(1)} %get-tuple-element.31), channel_id=1, source_target_pairs={{0,1},{1,2},{2,3},{3,4},{4,5},{5,6},{6,7},{7,8},{8,9},{9,10},{10,1... | collective-permute-start | bytes 110600 | tf_op jit(solution)/shard_map/ppermute | solution.py:675
  57.7 1.9 %collective-permute-start.5 = (bf16[144,128]{1,0:T(8,128)(2,1)S(1)}, bf16[144,128]{1,0:T(8,128)(2,1)S(1)}, u32[]{:S(2)}, u32[]{:S(2)}) collective-permute-start(bf16[144,128]{1,0:T(8,128)(2,1)S(1)} %get-tuple-element.33), channel_id=1, source_target_pairs={{1,0},{2,1},{3,2},{4,3},{5,4},{6,5},{7,6},{8,7},{9,8},{10,9},{11,1... | collective-permute-start | bytes 110600 | tf_op jit(solution)/shard_map/ppermute | solution.py:675
  59.6 4.8 %collective-permute-done.5.upper.refs_4_ = bf16[144,128]{1,0:T(8,128)(2,1)S(1)} collective-permute-done((bf16[144,128]{1,0:T(8,128)(2,1)S(1)}, bf16[144,128]{1,0:T(8,128)(2,1)S(1)}, u32[]{:S(2)}, u32[]{:S(2)}) %collective-permute-start.5) | collective-permute-done | bytes 36896 | tf_op jit(solution)/shard_map/ppermute | solution.py:675
  65.1 6.1 %weave.1 = (bf16[304,128]{1,0:T(8,128)(2,1)}, bf16[304,128]{1,0:T(8,128)(2,1)}) custom-call(bf16[144,128]{1,0:T(8,128)(2,1)} %copy-done.14, bf16[4,4,16,128]{3,2,1,0:T(8,128)(2,1)} %copy-done.6, bf16[144,128]{1,0:T(8,128)(2,1)} %copy-done.16, bf16[16,128]{1,0:T(8,128)(2,1)} %copy-done.18), custom_call_target="tpu_custom_call" | custom-call | tf_op jit(solution)/shard_map/weave/pallas_call | solution.py:318
  71.2 3.5 %collective-permute-start.6 = (bf16[304,128]{1,0:T(8,128)(2,1)}, bf16[304,128]{1,0:T(8,128)(2,1)S(1)}, u32[]{:S(2)}, u32[]{:S(2)}) collective-permute-start(bf16[304,128]{1,0:T(8,128)(2,1)} %get-tuple-element.35), channel_id=1, source_target_pairs={{0,16},{16,32},{32,48},{48,64},{64,80},{80,96},{96,112},{1,17},{17... | collective-permute-start | bytes 233480 | tf_op jit(solution)/shard_map/ppermute | solution.py:675
  74.7 1.3 collective-permute-start.7
  76.5 3.6 %collective-permute-done.7.refs_7_ = bf16[304,128]{1,0:T(8,128)(2,1)S(1)} collective-permute-done((bf16[304,128]{1,0:T(8,128)(2,1)}, bf16[304,128]{1,0:T(8,128)(2,1)S(1)}, u32[]{:S(2)}, u32[]{:S(2)}) %collective-permute-start.7) | collective-permute-done | bytes 77856 | tf_op jit(solution)/shard_map/ppermute | solution.py:675
  80.8 1.0 copy-done.2
  81.7 1.0 copy-done.4
  82.7 0.8 copy-done.15
  83.5 0.8 copy-done.17
  84.2 6.9 %backward.1 = bf16[8,16,24,128]{3,2,1,0:T(8,128)(2,1)S(1)} custom-call(bf16[27,64,128]{2,1,0:T(8,128)(2,1)S(1)} %bitcast.25, f32[1,128]{1,0:T(1,128)S(1)} %bitcast.30, bf16[144,128]{1,0:T(8,128)(2,1)S(1)} %copy-done.15, bf16[4,4,16,128]{3,2,1,0:T(8,128)(2,1)S(1)} %copy-done.7, bf16[144,128]{1,0:T(8,128)(2,1)S(1)} %copy-done.17, ...), custom_call_target="tpu_custom_call" | custom-call | tf_op jit(solution)/shard_map/backward/pallas_call | solution.py:530
  91.2 28.6 %all_to_all.20.source = bf16[128,24,128]{2,1,0:T(8,128)(2,1)} all-to-all(bf16[128,24,128]{2,1,0:T(8,128)(2,1)S(1)} %bitcast.24), channel_id=1, replica_groups=mesh['gy'=8,'gz'=16] {'gy','gz'}, dimensions={0} | all-to-all | bytes 1572864 | tf_op jit(solution)/shard_map/all_to_all | solution.py:704
  119.8 2.7 %sum.1 = (bf16[8,16,128]{2,1,0:T(8,128)(2,1)}, bf16[128,8,128]{2,1,0:T(8,128)(2,1)}, bf16[8,16,16]{2,1,0:T(8,128)(2,1)}) custom-call(bf16[128,24,128]{2,1,0:T(8,128)(2,1)} %all_to_all.20.source), custom_call_target="tpu_custom_call" | custom-call | tf_op jit(solution)/shard_map/sum/pallas_call | solution.py:589
  122.5 9.1 %all_to_all.21.column_in = bf16[8,16,128]{2,1,0:T(8,128)(2,1)} all-to-all(bf16[8,16,128]{2,1,0:T(8,128)(2,1)} %get-tuple-element.43), channel_id=1, replica_groups=mesh['gy'=8,'gz'=16] {'gy'}, dimensions={0} | all-to-all | bytes 65536 | tf_op jit(solution)/shard_map/all_to_all | solution.py:706
  131.5 17.1 %all_to_all.22.shared_in = bf16[128,8,128]{2,1,0:T(8,128)(2,1)} all-to-all(bf16[128,8,128]{2,1,0:T(8,128)(2,1)} %get-tuple-element.44), channel_id=1, replica_groups=mesh['gy'=8,'gz'=16] {'gy','gz'}, dimensions={0} | all-to-all | bytes 524288 | tf_op jit(solution)/shard_map/all_to_all | solution.py:707
  148.7 1.8 %unpack.1 = (f32[27,4,32]{2,1,0:T(4,128)}, f32[27,32,64]{2,1,0:T(8,128)}, f32[27,8,64]{2,1,0:T(8,128)}, f32[1,32]{1,0:T(1,128)}, f32[1,64]{1,0:T(1,128)}, /*index=5*/f32[1,8]{1,0:T(1,128)}) custom-call(bf16[8,16,128]{2,1,0:T(8,128)(2,1)} %all_to_all.21.column_in, bf16[128,8,128]{2,1,0:T(8,128)(2,1)} %all_to_all.22.shared_in), custom_call_target="tpu_custom_call" | custom-call | tf_op jit(solution)/shard_map/unpack/pallas_call | solution.py:638
  (54 shorter events, 6.8 us)
Async XLA Ops:
  1.5 8.1 %collective-permute-start = (bf16[8,32,128]{2,1,0:T(8,128)(2,1)S(1)}, bf16[8,32,128]{2,1,0:T(8,128)(2,1)S(1)}, u32[]{:S(2)}, u32[]{:S(2)}) collective-permute-start(bf16[8,32,128]{2,1,0:T(8,128)(2,1)S(1)} %bitcast.31), channel_id=1, source_target_pairs={{0,1},{1,2},{2,3},{3,4},{4,5},{5,6},{6,7},{7,8},{8,9},{9,10},{10,1... | collective-permute-start | bytes 196616 | tf_op jit(solution)/shard_map/ppermute | solution.py:675
  7.6 7.1 %collective-permute-start.1 = (bf16[8,32,128]{2,1,0:T(8,128)(2,1)S(1)}, bf16[8,32,128]{2,1,0:T(8,128)(2,1)S(1)}, u32[]{:S(2)}, u32[]{:S(2)}) collective-permute-start(bf16[8,32,128]{2,1,0:T(8,128)(2,1)S(1)} %bitcast.32), channel_id=1, source_target_pairs={{1,0},{2,1},{3,2},{4,3},{5,4},{6,5},{7,6},{8,7},{9,8},{10,9},{11,1... | collective-permute-start | bytes 196616 | tf_op jit(solution)/shard_map/ppermute | solution.py:675
  14.7 5.6 %copy-start.24 = (bf16[27,32,4]{1,2,0:T(4,128)(2,1)S(1)}, bf16[27,32,4]{1,2,0:T(4,128)(2,1)}, u32[]{:S(2)}) copy-start(bf16[27,32,4]{1,2,0:T(4,128)(2,1)} %param.10) | copy-start | bytes 20740
  14.8 5.5 %copy-start.23 = (bf16[8,1,16,16]{3,2,1,0:T(8,128)(2,1)S(1)}, bf16[8,1,16,16]{3,2,1,0:T(8,128)(2,1)}, u32[]{:S(2)}) copy-start(bf16[8,1,16,16]{3,2,1,0:T(8,128)(2,1)} %param.16) | copy-start | bytes 12292
  14.8 19.6 %collective-permute-start.3 = (bf16[8,96,128]{2,1,0:T(8,128)(2,1)S(1)}, bf16[8,96,128]{2,1,0:T(8,128)(2,1)S(1)}, u32[]{:S(2)}, u32[]{:S(2)}) collective-permute-start(bf16[8,96,128]{2,1,0:T(8,128)(2,1)S(1)} %maximum_maximum_fusion.refs_1_), channel_id=1, source_target_pairs={{16,0},{32,16},{48,32},{64,48},{80,64},{96,80},{112,96},{17,1},{33... | collective-permute-start | bytes 589832 | tf_op jit(solution)/shard_map/ppermute | solution.py:675
  16.1 19.0 %collective-permute-start.2 = (bf16[8,96,128]{2,1,0:T(8,128)(2,1)S(1)}, bf16[8,96,128]{2,1,0:T(8,128)(2,1)S(1)}, u32[]{:S(2)}, u32[]{:S(2)}) collective-permute-start(bf16[8,96,128]{2,1,0:T(8,128)(2,1)S(1)} %maximum_maximum_fusion.refs_1_), channel_id=1, source_target_pairs={{0,16},{16,32},{32,48},{48,64},{64,80},{80,96},{96,112},{1,17},{17... | collective-permute-start | bytes 589832 | tf_op jit(solution)/shard_map/ppermute | solution.py:675
  21.0 13.5 %all-to-all-start = ((bf16[16,8,16]{2,1,0:T(8,128)(2,1)}), bf16[16,8,16]{2,1,0:T(8,128)(2,1)S(1)}, u32[]{:S(2)}, u32[]{:S(2)}) async-start(bf16[16,8,16]{2,1,0:T(8,128)(2,1)} %bitcast.22), calls=%async_computation | async-start | bytes 65536 | tf_op jit(solution)/shard_map/all_to_all | solution.py:688
  34.4 0.7 copy-start.10
  35.1 0.7 copy-start.12
  35.8 0.7 copy-start.20
  35.8 0.7 copy-start.21
  36.4 0.9 copy-start.5
  37.3 0.9 copy-start.8
  38.3 0.9 copy-start.9
  39.2 0.9 copy-start.11
  40.1 0.9 copy-start.13
  41.1 39.0 %copy-start = (bf16[27,128,64]{1,2,0:T(8,128)(2,1)S(1)}, bf16[27,128,64]{1,2,0:T(8,128)(2,1)}, u32[]{:S(2)}) copy-start(bf16[27,128,64]{1,2,0:T(8,128)(2,1)} %param.14) | copy-start | bytes 1327108
  53.1 0.7 copy-start.1
  53.8 0.7 copy-start.3
  55.1 9.3 %copy-start.18 = (bf16[16,128]{1,0:T(8,128)(2,1)}, bf16[16,128]{1,0:T(8,128)(2,1)S(1)}, u32[]{:S(2)}) copy-start(bf16[16,128]{1,0:T(8,128)(2,1)S(1)} %get-tuple-element.34.own_cot.refs_5_) | copy-start | bytes 12292
  55.1 4.5 %collective-permute-start.4 = (bf16[144,128]{1,0:T(8,128)(2,1)S(1)}, bf16[144,128]{1,0:T(8,128)(2,1)S(1)}, u32[]{:S(2)}, u32[]{:S(2)}) collective-permute-start(bf16[144,128]{1,0:T(8,128)(2,1)S(1)} %get-tuple-element.31), channel_id=1, source_target_pairs={{0,1},{1,2},{2,3},{3,4},{4,5},{5,6},{6,7},{7,8},{8,9},{9,10},{10,1... | collective-permute-start | bytes 110600 | tf_op jit(solution)/shard_map/ppermute | solution.py:675
  57.7 6.8 %collective-permute-start.5 = (bf16[144,128]{1,0:T(8,128)(2,1)S(1)}, bf16[144,128]{1,0:T(8,128)(2,1)S(1)}, u32[]{:S(2)}, u32[]{:S(2)}) collective-permute-start(bf16[144,128]{1,0:T(8,128)(2,1)S(1)} %get-tuple-element.33), channel_id=1, source_target_pairs={{1,0},{2,1},{3,2},{4,3},{5,4},{6,5},{7,6},{8,7},{9,8},{10,9},{11,1... | collective-permute-start | bytes 110600 | tf_op jit(solution)/shard_map/ppermute | solution.py:675
  59.6 4.8 %copy-start.14 = (bf16[144,128]{1,0:T(8,128)(2,1)}, bf16[144,128]{1,0:T(8,128)(2,1)S(1)}, u32[]{:S(2)}) copy-start(bf16[144,128]{1,0:T(8,128)(2,1)S(1)} %collective-permute-done.4.lower.refs_2_) | copy-start | bytes 110596
  65.1 15.0 %copy-start.7 = (bf16[4,4,16,128]{3,2,1,0:T(8,128)(2,1)S(1)}, bf16[4,4,16,128]{3,2,1,0:T(8,128)(2,1)}, u32[]{:S(2)}) copy-start(bf16[4,4,16,128]{3,2,1,0:T(8,128)(2,1)} %copy-done.6) | copy-start | bytes 196612
  71.2 5.3 %collective-permute-start.6 = (bf16[304,128]{1,0:T(8,128)(2,1)}, bf16[304,128]{1,0:T(8,128)(2,1)S(1)}, u32[]{:S(2)}, u32[]{:S(2)}) collective-permute-start(bf16[304,128]{1,0:T(8,128)(2,1)} %get-tuple-element.35), channel_id=1, source_target_pairs={{0,16},{16,32},{32,48},{48,64},{64,80},{80,96},{96,112},{1,17},{17... | collective-permute-start | bytes 233480 | tf_op jit(solution)/shard_map/ppermute | solution.py:675
  74.7 5.4 %collective-permute-start.7 = (bf16[304,128]{1,0:T(8,128)(2,1)}, bf16[304,128]{1,0:T(8,128)(2,1)S(1)}, u32[]{:S(2)}, u32[]{:S(2)}) collective-permute-start(bf16[304,128]{1,0:T(8,128)(2,1)} %get-tuple-element.36), channel_id=1, source_target_pairs={{16,0},{32,16},{48,32},{64,48},{80,64},{96,80},{112,96},{17,1},{33... | collective-permute-start | bytes 233480 | tf_op jit(solution)/shard_map/ppermute | solution.py:675
  80.1 0.7 copy-start.19
  80.1 0.7 copy-start.22
  80.8 1.0 copy-start.2
  81.7 1.0 copy-start.4
  82.7 0.8 copy-start.15
  83.5 0.8 copy-start.17
  (2 other events, 1.2 us)

commit v4 on v2

--- a/solution.py
+++ b/solution.py
@@ -13,7 +13,6 @@
 SLOPE = 0.3
 PAIRS = ((0, 1), (2, 3), (-3, -2), (4, 5), (-1, 6))
 VMEM = pl.BlockSpec(memory_space=pltpu.VMEM)
-SMEM = pl.BlockSpec(memory_space=pltpu.SMEM)
 LIMIT = 24 * 1024 * 1024
 
 
@@ -56,16 +55,16 @@
     return jnp.where(rows == count - 1, 0.0, roll(value, count - 1, 0))
 
 
-def forward_kernel(
-    place, top, mid, bot, cot, pick, k1, b1, k2, b2,
-    hidden2, to_next, to_previous, ratio2, patches1, ratio1, fields, w2,
-    w1, left, field, first, spread, pre2, second,
-):
+def forward_kernel(*refs):
+    (top, mid, bot, cot, pick, k1, b1, k2, b2), refs = refs[:9], refs[9:]
+    (to_next, to_previous, hidden2, own_cot, ratio2, patches1, ratio1, fields, w2), refs = refs[:9], refs[9:]
+    w1, left, field, first, spread, pre2, second = refs
     lay_weights1(k1, w1)
     lay_weights2(k2, w2)
     bias1 = jnp.concatenate([b1[...]] * 8, axis=1)
     bias2 = jnp.concatenate([b2[...]] * 4, axis=1)
-    base_y, base_z, size_y, size_z = place[0], place[1], place[2], place[3]
+    base_y, base_z = lax.axis_index("gy"), lax.axis_index("gz")
+    size_y, size_z = lax.axis_size("gy"), lax.axis_size("gz")
 
     def inside(offset_y, offset_z, scale):
         row = base_y * (4 // scale) + offset_y
@@ -189,18 +188,24 @@
     own = cot[...].astype(F32).T.astype(BF16)
     to_next[128:144] = own
     to_previous[128:144] = own
+    own_cot[...] = own
 
 
 def lay_weights1(taps, out):
     group = lane((16, 128)) // 32
     zero = jnp.zeros((16, 128), F32)
+    wide = []
+    for k in range(9):
+        pieces = [taps[3 * k + dz].astype(F32) for dz in range(3)] + [jnp.zeros((4, 32), F32)]
+        rows = jnp.concatenate(pieces, axis=0)
+        wide.append(jnp.concatenate([rows] * 4, axis=1))
     for py in range(4):
         for px in range(4):
             at = (py * 4 + px) * 16
             for qy in range(2):
                 dy = py - qy
                 sides = [
-                    taps[(px - qx) * 3 + dy] if 0 <= dy < 3 and 0 <= px - qx < 3 else zero for qx in range(2)
+                    wide[(px - qx) * 3 + dy] if 0 <= dy < 3 and 0 <= px - qx < 3 else zero for qx in range(2)
                 ]
                 value = jnp.where(group == 0, sides[0], sides[1])
                 shifted = jnp.where(group == 2, roll(sides[0], 4, 0), roll(sides[1], 4, 0))
@@ -233,21 +238,21 @@
 
 
 def run_forward(*operands):
+    kept = (
+        jax.ShapeDtypeStruct((4, 4, 16, 128), BF16),
+        jax.ShapeDtypeStruct((16, 128), BF16),
+        jax.ShapeDtypeStruct((8, 4, 32, 256), F32),
+        jax.ShapeDtypeStruct((6, 6, 32, 128), BF16),
+        jax.ShapeDtypeStruct((4, 256, 256), F32),
+        jax.ShapeDtypeStruct((10, 64, 256), BF16),
+        jax.ShapeDtypeStruct((3, 512, 256), BF16),
+    )
     return pl.pallas_call(
         forward_kernel,
         name="forward",
-        out_shape=(
-            jax.ShapeDtypeStruct((4, 4, 16, 128), BF16),
-            jax.ShapeDtypeStruct((144, 128), BF16),
-            jax.ShapeDtypeStruct((144, 128), BF16),
-            jax.ShapeDtypeStruct((8, 4, 32, 256), F32),
-            jax.ShapeDtypeStruct((6, 6, 32, 128), BF16),
-            jax.ShapeDtypeStruct((4, 256, 256), F32),
-            jax.ShapeDtypeStruct((10, 64, 256), BF16),
-            jax.ShapeDtypeStruct((3, 512, 256), BF16),
-        ),
-        in_specs=[SMEM] + [VMEM] * (len(operands) - 1),
-        out_specs=(VMEM,) * 8,
+        out_shape=(jax.ShapeDtypeStruct((144, 128), BF16),) * 2 + kept,
+        in_specs=[VMEM] * len(operands),
+        out_specs=(VMEM,) * 9,
         scratch_shapes=[
             pltpu.VMEM((256, 256), BF16),
             pltpu.VMEM((22, 80, 256), BF16),
@@ -261,7 +266,7 @@
     )(*operands)
 
 
-def weave_kernel(lower, hidden2, upper, to_next, to_previous):
+def weave_kernel(lower, hidden2, upper, own_cot, to_next, to_previous):
     for target, first_row in ((to_next, 0), (to_previous, 2)):
         for y in range(2):
             row, at = first_row + y, y * 128
@@ -269,30 +274,27 @@
             target[at + 32 : at + 96] = hidden2[row].reshape(64, 128)
             target[at + 96 : at + 128] = upper[row * 32 : row * 32 + 32]
         target[256:272] = lower[128:144]
+        target[272:288] = own_cot[...]
         target[288:304] = upper[128:144]
 
 
-def run_weave(lower, hidden2, upper, own_cot):
-    def kernel(lower, hidden2, upper, own_cot, to_next, to_previous):
-        weave_kernel(lower, hidden2, upper, to_next, to_previous)
-        to_next[272:288] = own_cot[128:144]
-        to_previous[272:288] = own_cot[128:144]
-
+def run_weave(*operands):
     return pl.pallas_call(
-        kernel,
+        weave_kernel,
         name="weave",
         out_shape=(jax.ShapeDtypeStruct((304, 128), BF16),) * 2,
         in_specs=[VMEM] * 4,
         out_specs=(VMEM,) * 2,
-    )(lower, hidden2, upper, own_cot)
-
-
-def backward_kernel(
-    groups,
-    before, lower, middle, upper, after, own_cot, k3, b3, w2, ratio2, patches1, ratio1, fields,
-    packed,
-    w3, patches2, pre3, delta3, patch2, grad2, delta2, patch1, grad1, delta1,
-):
+        compiler_params=pltpu.CompilerParams(vmem_limit_bytes=LIMIT),
+    )(*operands)
+
+
+def backward_kernel(*refs):
+    (k3, b3, lower, middle, upper, own_cot, before, after, ratio2, w2, patches1, ratio1, fields), refs = (
+        refs[:13], refs[13:],
+    )
+    packed, w3, patches2, pre3, delta3, patch2, grad2, delta2, patch1, grad1, delta1, turned = refs
+    groups = packed.shape[0]
     wide = 128 // groups
     lay_weights3(k3, w3)
     bias3_in = jnp.concatenate([b3[...]] * 2, axis=1)
@@ -333,7 +335,7 @@
             total = total[:, :128] + total[:, 128:]
             mean = total * 0.125
             if wy == 1:
-                cot = (lower, own_cot, upper)[wz][128:144]
+                cot = own_cot[...] if wz == 1 else (lower if wz == 0 else upper)[128:144]
             else:
                 cot = (before if wy == 0 else after)[256 + wz * 16 : 272 + wz * 16]
             share = cot.astype(F32) * (0.125 / mean)
@@ -388,7 +390,6 @@
     bias2 = own2.astype(F32).sum(axis=0, keepdims=True)
     bias2 = bias2[:, :128] + bias2[:, 128:]
     bias2 = bias2 + roll(bias2, 64, 1)
-    low_lane = lane((32, 128)) < 64
     taps = [None] * 27
     for dy in range(3):
         block = jnp.concatenate(
@@ -405,12 +406,6 @@
                 taps[dx * 9 + dy * 3 + dz] = rows[dx * 32 : dx * 32 + 32] + roll(
                     rows[dx * 32 + 32 : dx * 32 + 64], 64, 1
                 )
-    kernel2 = [
-        jnp.where(low_lane, taps[2 * m], roll(taps[2 * m + 1], 64, 1) if 2 * m + 1 < 27 else 0.0)
-        for m in range(14)
-    ]
-    kernel2 = jnp.concatenate(kernel2, axis=0).reshape(groups, 448 // groups, 128)
-
     for dy in range(3):
         block = delta2[2 - dy : 6 - dy].reshape(512, 256)
         term = dot_nt(block, w2[dy]).reshape(4, 4, 32, 512)
@@ -423,6 +418,7 @@
         value = jnp.where(group == which, value, 0.0)
         value = value + roll(value, 32, 1)
         return value + roll(value, 64, 1)
+
 
     def gather1(y, carry):
         for z, (zo_a, pz_a, zo_b, pz_b) in enumerate(((0, 3, 1, 1), (1, 2, 2, 0), (1, 3, 2, 1), (2, 2, 3, 0))):
@@ -459,25 +455,37 @@
             value = value + roll(roll(value, 12, 0), 64, 1)
             pieces.append(roll(value, 32 * dx, 1) if dx else value)
         kernel1.append(jnp.where(group1 == 0, pieces[0], jnp.where(group1 == 1, pieces[1], pieces[2])))
-    kernel1 = jnp.concatenate(kernel1, axis=0).reshape(groups, 48 // groups, 128)
-
-    feature_rows = jnp.concatenate([features, jnp.zeros((112, 128), F32)], axis=0).T
-    feature_rows = feature_rows.reshape(groups, wide, 128)
-    biases = jnp.concatenate([bias3, jnp.where(lane((1, 128)) < 64, bias2, bias1)], axis=0)
-    biases = jnp.broadcast_to(biases[None], (groups, 2, 128))
-    rows = 15 * wide + 496 // groups + 2
-    fill = packed.shape[1] - rows
-    pieces = kernel3 + [feature_rows, kernel2, kernel1, biases, jnp.zeros((groups, fill, 128), F32)]
-    packed[...] = jnp.concatenate(pieces, axis=1).astype(BF16)
+
+    low_lane = lane((32, 128)) < 64
+    kernel2 = [
+        jnp.where(low_lane, taps[2 * m], roll(taps[2 * m + 1], 64, 1) if 2 * m + 1 < 27 else 0.0)
+        for m in range(14)
+    ]
+    biases = jnp.concatenate(
+        [bias3, jnp.where(lane((1, 128)) < 64, bias2, bias1), jnp.zeros((14, 128), F32)], axis=0
+    )
+    shared = jnp.concatenate(kernel2 + kernel1 + [biases], axis=0).reshape(groups, 512 // groups, 128)
+
+    turned[...] = jnp.concatenate([features, jnp.zeros((112, 128), F32)], axis=0).T
+    feature_rows = turned[pl.ds(0, 16, stride=8), :]
+    for c in range(1, 8):
+        feature_rows = feature_rows + roll(turned[pl.ds(c, 16, stride=8), :], 16 * c, 1)
+    feature_rows = feature_rows.reshape(groups, wide // 8, 128)
+
+    fill = jnp.zeros((groups, packed.shape[1] - 512 // groups - 14 * wide - wide // 8, 128), F32)
+    packed[...] = jnp.concatenate([shared] + kernel3 + [feature_rows, fill], axis=1).astype(BF16)
+
+
+def packed_rows(groups):
+    wide = 128 // groups
+    return -(-(512 // groups + 14 * wide + wide // 8) // 8) * 8
 
 
 def run_backward(groups, *operands):
-    rows = 15 * (128 // groups) + 496 // groups + 2
-    rows = -(-rows // 16) * 16
     return pl.pallas_call(
-        functools.partial(backward_kernel, groups),
+        backward_kernel,
         name="backward",
-        out_shape=jax.ShapeDtypeStruct((groups, rows, 128), BF16),
+        out_shape=jax.ShapeDtypeStruct((groups, packed_rows(groups), 128), BF16),
         in_specs=[VMEM] * len(operands),
         out_specs=VMEM,
         scratch_shapes=[
@@ -491,9 +499,111 @@
             pltpu.VMEM((4, 4, 32, 512), F32),
             pltpu.VMEM((4, 64, 128), F32),
             pltpu.VMEM((4, 256, 256), BF16),
+            pltpu.VMEM((128, 128), F32),
         ],
         compiler_params=pltpu.CompilerParams(vmem_limit_bytes=LIMIT),
     )(*operands)
+
+
+def sum_kernel(received, to_column, features):
+    groups, rows = received.shape[0], to_column.shape[1]
+    wide = 128 // groups
+    own = received[:, rows : rows + wide // 8].astype(F32)
+    for c in range(wide):
+        features[c] = own[:, c // 8, (c % 8) * 16 : (c % 8) * 16 + 16].astype(BF16)
+    total = received[:, :rows].astype(F32).sum(axis=0)
+    to_column[...] = jnp.broadcast_to(total[None], to_column.shape).astype(BF16)
+
+
+def run_sum(received, rows_y):
+    groups = received.shape[0]
+    wide = 128 // groups
+    return pl.pallas_call(
+        sum_kernel,
+        name="sum",
+        out_shape=(
+            jax.ShapeDtypeStruct((rows_y, 512 // groups + 14 * wide, 128), BF16),
+            jax.ShapeDtypeStruct((wide, groups, 16), BF16),
+        ),
+        in_specs=[VMEM],
+        out_specs=(VMEM, VMEM),
+        compiler_params=pltpu.CompilerParams(vmem_limit_bytes=LIMIT),
+    )(received)
+
+
+def share_kernel(column, to_all):
+    total = column[:, : to_all.shape[1]].astype(F32).sum(axis=0)
+    to_all[...] = jnp.broadcast_to(total[None], to_all.shape).astype(BF16)
+
+
+def run_share(column, groups):
+    return pl.pallas_call(
+        share_kernel,
+        name="share",
+        out_shape=jax.ShapeDtypeStruct((groups, 512 // groups, 128), BF16),
+        in_specs=[VMEM],
+        out_specs=VMEM,
+        compiler_params=pltpu.CompilerParams(vmem_limit_bytes=LIMIT),
+    )(column)
+
+
+def third_kernel(column, grad3):
+    wide = grad3.shape[1]
+    first = column.shape[1] - 14 * wide
+    lines = column[:, first:].astype(F32).sum(axis=0)
+    for tap in range(9):
+        low = lines[tap * wide : tap * wide + wide]
+        grad3[tap] = low[:, :64]
+        grad3[9 + tap] = low[:, 64:]
+        at = (9 + tap // 2) * wide
+        grad3[18 + tap] = lines[at : at + wide][:, (tap % 2) * 64 : (tap % 2) * 64 + 64]
+
+
+def run_third(column, wide):
+    return pl.pallas_call(
+        third_kernel,
+        name="third",
+        out_shape=jax.ShapeDtypeStruct((27, wide, 64), F32),
+        in_specs=[VMEM],
+        out_specs=VMEM,
+        compiler_params=pltpu.CompilerParams(vmem_limit_bytes=LIMIT),
+    )(column)
+
+
+def unpack_kernel(shared, grad1, grad2, shift1, shift2, shift3):
+    wide = shift3.shape[1]
+    rows = shared[...].astype(F32).reshape(512, 128)
+    for tap in range(27):
+        at = (tap // 2) * 32
+        grad2[tap] = rows[at : at + 32, (tap % 2) * 64 : (tap % 2) * 64 + 64]
+    for dy in range(3):
+        for dz in range(3):
+            at = 448 + dy * 16 + dz * 4
+            for dx in range(3):
+                grad1[dx * 9 + dy * 3 + dz] = rows[at : at + 4, dx * 32 : dx * 32 + 32]
+    biases = rows[496:504]
+    shift1[...] = biases[1:2, 64:96]
+    shift2[...] = biases[1:2, :64]
+    place = lax.axis_index("gz")
+    shift3[...] = roll(biases, lax.rem(128 - place * wide, 128), 1)[0:1, :wide]
+
+
+def run_unpack(shared):
+    wide = 128 // shared.shape[0]
+    return pl.pallas_call(
+        unpack_kernel,
+        name="unpack",
+        out_shape=(
+            jax.ShapeDtypeStruct((27, 4, 32), F32),
+            jax.ShapeDtypeStruct((27, 32, 64), F32),
+            jax.ShapeDtypeStruct((1, 32), F32),
+            jax.ShapeDtypeStruct((1, 64), F32),
+            jax.ShapeDtypeStruct((1, wide), F32),
+        ),
+        in_specs=[VMEM],
+        out_specs=(VMEM,) * 5,
+        compiler_params=pltpu.CompilerParams(vmem_limit_bytes=LIMIT),
+    )(shared)
 
 
 def pick_matrix():
@@ -507,34 +617,6 @@
     return out.reshape(256, 512).astype(jnp.bfloat16)
 
 
-def unpack_kernel(rest, grad1, grad2):
-    groups, rows = rest.shape[0], rest.shape[1]
-    rows2 = 448 // groups
-    whole = rest[...].astype(F32)
-    grad = whole[:, :rows2].reshape(14, 32, 128)
-    for tap in range(27):
-        grad2[tap] = grad[tap // 2, :, (tap % 2) * 64 : (tap % 2) * 64 + 64]
-    grad = whole[:, rows2:].reshape(3, 16, 128)
-    for dy in range(3):
-        for dz in range(3):
-            for dx in range(3):
-                grad1[dx * 9 + dy * 3 + dz] = grad[dy, dz * 4 : dz * 4 + 4, dx * 32 : dx * 32 + 32]
-
-
-def run_unpack(rest):
-    return pl.pallas_call(
-        unpack_kernel,
-        name="unpack",
-        out_shape=(jax.ShapeDtypeStruct((27, 4, 32), F32), jax.ShapeDtypeStruct((27, 32, 64), F32)),
-        in_specs=[VMEM],
-        out_specs=(VMEM, VMEM),
-    )(rest)
-
-
-def spread_to_all(value, axis):
-    return lax.all_to_all(jnp.broadcast_to(value[None], (lax.axis_size(axis),) + value.shape), axis, 0, 0, tiled=True)
-
-
 def both_ways(to_next, to_previous, axis):
     devices = lax.axis_size(axis)
     forth = [(i, i + 1) for i in range(devices - 1)]
@@ -544,9 +626,7 @@
 
 def shards(universe, kernel1, bias1, kernel2, bias2, kernel3, bias3, cotangent):
     size_y, size_z = lax.axis_size("gy"), lax.axis_size("gz")
-    place_y, place_z = lax.axis_index("gy"), lax.axis_index("gz")
     wide = 128 // size_z
-    place = jnp.stack([place_y, place_z, jnp.int32(size_y), jnp.int32(size_z)]).astype(jnp.int32)
 
     tile = universe.transpose(1, 2, 0, 3).reshape(8, 32, 128)
     lower, upper = both_ways(tile, tile, "gz")
@@ -554,35 +634,27 @@
     top, bottom = both_ways(strip, strip, "gy")
 
     cot = lax.all_to_all(cotangent[:, 0].transpose(1, 0, 2), "gz", 0, 0, tiled=True).reshape(128, 16)
-    k1 = kernel1.transpose(0, 2, 1).reshape(9, 12, 32).astype(F32)
-    k1 = jnp.tile(jnp.pad(k1, ((0, 0), (0, 4), (0, 0))), (1, 1, 4))
+    k1 = kernel1.transpose(0, 2, 1)
     k2, k3 = kernel2.transpose(0, 2, 1), kernel3.transpose(0, 2, 1)
 
-    hidden2, to_next, to_previous, ratio2, patches1, ratio1, fields, w2 = run_forward(
-        place, top, strip, bottom, cot, jnp.asarray(pick_matrix()), k1, bias1[None], k2, bias2[None]
+    to_next, to_previous, hidden2, own_cot, ratio2, patches1, ratio1, fields, w2 = run_forward(
+        top, strip, bottom, cot, jnp.asarray(pick_matrix()), k1, bias1[None], k2, bias2[None]
     )
     lower, upper = both_ways(to_next, to_previous, "gz")
-    row_next, row_previous = run_weave(lower, hidden2, upper, to_next)
+    row_next, row_previous = run_weave(lower, hidden2, upper, own_cot)
     before, after = both_ways(row_next, row_previous, "gy")
     packed = run_backward(
-        size_z, before, lower, hidden2, upper, after, to_next, k3, bias3[None], w2, ratio2, patches1, ratio1, fields
+        size_z,
+        k3, bias3[None], lower, hidden2, upper, own_cot, before, after, ratio2, w2, patches1, ratio1, fields,
     )
     packed = lax.all_to_all(packed, "gz", 0, 0, tiled=True)
-    at = 14 * wide
-    features = packed[:, at : at + wide, :16].transpose(1, 0, 2)[:, None]
-    partial = packed.astype(F32).sum(axis=0).astype(BF16)
-    total = spread_to_all(partial, "gy").astype(F32).sum(axis=0)
-    at = at + wide
-    last = at + 496 // size_z
-    grad1, grad2 = run_unpack(spread_to_all(total[at:last].astype(BF16), "gz"))
-    low = total[: 9 * wide].reshape(3, 3, wide, 2, 64)
-    high = total[9 * wide : 14 * wide].reshape(5, wide, 2, 64).transpose(0, 2, 1, 3)
-    high = high.reshape(10, wide, 64)[:9].reshape(3, 3, wide, 1, 64)
-    grad3 = jnp.concatenate([low, high], axis=3).transpose(3, 0, 1, 2, 4).reshape(27, wide, 64)
-    shift3 = lax.dynamic_slice_in_dim(total[last], place_z * wide, wide, 0)
+    column, features = run_sum(packed, size_y)
+    column = lax.all_to_all(column, "gy", 0, 0, tiled=True)
+    shared = lax.all_to_all(run_share(column, size_z), "gz", 0, 0, tiled=True)
+    grad3 = run_third(column, wide)
+    grad1, grad2, shift1, shift2, shift3 = run_unpack(shared)
     return (
-        features, grad1.transpose(0, 2, 1), total[last + 1, 64:96], grad2.transpose(0, 2, 1),
-        total[last + 1, :64], grad3, shift3,
+        features[:, None], grad1.transpose(0, 2, 1), shift1[0], grad2.transpose(0, 2, 1), shift2[0], grad3, shift3[0]
     )
 
 

time: 137 us -> 118 us (0.86)
  blocking collectives: 22.5 us -> 46.7 us
  starting transfers between devices: 50.7 us -> 28.2 us
  local copies, waits for them, and re-layouts: 22.8 us -> 2.31 us
  waiting for transfers between devices: 18.5 us -> 20.7 us
    all_to_all x0 -> x2, blocking collectives: none -> 27.2 us  [the longest x1 13.9 us: shards(): column = lax.all_to_all(column, 'gy', 0, 0, tiled=True)]
    all_to_all x3 -> x1, starting transfers between devices: 24.3 us -> 5.36 us  [shards(): shared = lax.all_to_all(run_share(column, size_z), 'gz', 0, 0, tiled=True)]
    unnamed x60 -> x17, local copies, waits for them, and re-layouts: 16.2 us -> 1.32 us
    ppermute x4, waiting for transfers between devices: 5.45 us -> 13.6 us  [both_ways(): lax.ppermute(to_previous, axis, back)]
    all_to_all x3 -> x1, waiting for transfers between devices: 11.4 us -> 6.99 us  [shards(): shared = lax.all_to_all(run_share(column, size_z), 'gz', 0, 0, tiled=True)]
    all_to_all x1, blocking collectives: 22.5 us -> 19.5 us  [shards(): packed = lax.all_to_all(packed, 'gz', 0, 0, tiled=True)]
    ppermute x4, starting transfers between devices: 19 us -> 16.3 us  [both_ways(): lax.ppermute(to_next, axis, forth)]
    ppermute x4, waiting for transfers between devices: 1.65 us -> 0.13 us  [both_ways(): lax.ppermute(to_next, axis, forth)]
  transfers between devices with their start and end apart: 11 -> 9, of which waited for: 8 -> 5; matrix products, arithmetic and copies ran while one was open for 3% -> 0% of each run, Pallas kernels for 0% -> 1%
where the time goes in v4:
time: 118 us
  blocking collectives  46.7 us (40%)
  starting transfers between devices  28.2 us (24%)
  waiting for transfers between devices  20.7 us (18%)
  Pallas kernels  18.9 us (16%)
  local copies, waits for them, and re-layouts  2.31 us (2%)
    all_to_all x1, blocking collectives, shards(): packed = lax.all_to_all(packed, 'gz', 0, 0, tiled=True)  19.5 us
    ppermute x4, starting transfers between devices, both_ways(): lax.ppermute(to_next, axis, forth)  16.3 us
    all_to_all x1, blocking collectives, shards(): column = lax.all_to_all(column, 'gy', 0, 0, tiled=True)  13.9 us
    ppermute x4, waiting for transfers between devices, both_ways(): lax.ppermute(to_previous, axis, back)  13.6 us
    all_to_all x1, blocking collectives, shards(): lax.all_to_all(cotangent[:, 0].transpose(1, 0, 2), 'gz', 0, 0, tiled=True)  13.3 us
    pallas_call x1, Pallas kernels, run_forward(): pl.pallas_call(forward_kernel, name='forward', out_shape=(jax.ShapeDtypeS...  10 us
    all_to_all x1, waiting for transfers between devices, shards(): shared = lax.all_to_all(run_share(column, size_z), 'gz', 0, 0, tiled=True)  6.99 us
    ppermute x4, starting transfers between devices, both_ways(): lax.ppermute(to_previous, axis, back)  6.56 us
  transfers between devices with their start and end apart: 9, of which 5 were waited for; matrix products, arithmetic and copies ran while one was open for 0% of the time, Pallas kernels for 1%

profile of v4, /device:TPU:1, one launch (start us, length us, event | category | flops | bytes accessed | tf_op | source)
XLA Modules:
  0.0 117.7 jit_solution(14913147449756269398)
XLA Ops:
  0.6 0.9 copy.19
  1.5 6.0 %collective-permute-start = (bf16[8,32,128]{2,1,0:T(8,128)(2,1)S(1)}, bf16[8,32,128]{2,1,0:T(8,128)(2,1)S(1)}, u32[]{:S(2)}, u32[]{:S(2)}) collective-permute-start(bf16[8,32,128]{2,1,0:T(8,128)(2,1)S(1)} %bitcast.30), channel_id=1, source_target_pairs={{0,1},{1,2},{2,3},{3,4},{4,5},{5,6},{6,7},{7,8},{8,9},{9,10},{10,1... | collective-permute-start | bytes 196616 | tf_op jit(solution)/shard_map/ppermute | solution.py:624
  7.6 1.9 %collective-permute-start.1 = (bf16[8,32,128]{2,1,0:T(8,128)(2,1)S(1)}, bf16[8,32,128]{2,1,0:T(8,128)(2,1)S(1)}, u32[]{:S(2)}, u32[]{:S(2)}) collective-permute-start(bf16[8,32,128]{2,1,0:T(8,128)(2,1)S(1)} %bitcast.31), channel_id=1, source_target_pairs={{1,0},{2,1},{3,2},{4,3},{5,4},{6,5},{7,6},{8,7},{9,8},{10,9},{11,1... | collective-permute-start | bytes 196616 | tf_op jit(solution)/shard_map/ppermute | solution.py:624
  9.5 0.1 pad.3.clone
  9.6 0.0 collective-permute-done
  9.6 5.0 %collective-permute-done.1 = bf16[8,32,128]{2,1,0:T(8,128)(2,1)S(1)} collective-permute-done((bf16[8,32,128]{2,1,0:T(8,128)(2,1)S(1)}, bf16[8,32,128]{2,1,0:T(8,128)(2,1)S(1)}, u32[]{:S(2)}, u32[]{:S(2)}) %collective-permute-start.1) | collective-permute-done | bytes 65568 | tf_op jit(solution)/shard_map/ppermute | solution.py:624
  14.7 0.1 maximum_maximum_fusion.refs_1_
  14.8 1.4 %collective-permute-start.3 = (bf16[8,96,128]{2,1,0:T(8,128)(2,1)S(1)}, bf16[8,96,128]{2,1,0:T(8,128)(2,1)S(1)}, u32[]{:S(2)}, u32[]{:S(2)}) collective-permute-start(bf16[8,96,128]{2,1,0:T(8,128)(2,1)S(1)} %maximum_maximum_fusion.refs_1_), channel_id=1, source_target_pairs={{16,0},{32,16},{48,32},{64,48},{80,64},{96,80},{112,96},{17,1},{33... | collective-permute-start | bytes 589832 | tf_op jit(solution)/shard_map/ppermute | solution.py:624
  16.2 4.2 %collective-permute-start.2 = (bf16[8,96,128]{2,1,0:T(8,128)(2,1)S(1)}, bf16[8,96,128]{2,1,0:T(8,128)(2,1)S(1)}, u32[]{:S(2)}, u32[]{:S(2)}) collective-permute-start(bf16[8,96,128]{2,1,0:T(8,128)(2,1)S(1)} %maximum_maximum_fusion.refs_1_), channel_id=1, source_target_pairs={{0,16},{16,32},{32,48},{48,64},{64,80},{80,96},{96,112},{1,17},{17... | collective-permute-start | bytes 589832 | tf_op jit(solution)/shard_map/ppermute | solution.py:624
  20.4 0.0 copy-start.3
  20.4 13.3 %all_to_all.20 = bf16[16,8,16]{2,1,0:T(8,128)(2,1)S(1)} all-to-all(bf16[16,8,16]{2,1,0:T(8,128)(2,1)S(1)} %bitcast.33), channel_id=1, replica_groups=mesh['gy'=8,'gz'=16] {'gz'}, dimensions={0} | all-to-all | bytes 8192 | tf_op jit(solution)/shard_map/all_to_all | solution.py:636
  33.7 0.0 copy-start.5
  33.8 0.6 copy-done.4
  34.4 0.0 copy-done.5
  34.4 10.0 %forward.1 = (bf16[144,128]{1,0:T(8,128)(2,1)S(1)}, bf16[144,128]{1,0:T(8,128)(2,1)S(1)}, bf16[4,4,16,128]{3,2,1,0:T(8,128)(2,1)S(1)}, bf16[16,128]{1,0:T(8,128)...) custom-call(bf16[8,96,128]{2,1,0:T(8,128)(2,1)S(1)} %collective-perm, ...), custom_call_target="tpu_custom_call" | custom-call | tf_op jit(solution)/shard_map/forward/pallas_call | solution.py:250
  44.4 2.5 %collective-permute-start.4 = (bf16[144,128]{1,0:T(8,128)(2,1)S(1)}, bf16[144,128]{1,0:T(8,128)(2,1)S(1)}, u32[]{:S(2)}, u32[]{:S(2)}) collective-permute-start(bf16[144,128]{1,0:T(8,128)(2,1)S(1)} %get-tuple-element.25), channel_id=1, source_target_pairs={{0,1},{1,2},{2,3},{3,4},{4,5},{5,6},{6,7},{7,8},{8,9},{9,10},{10,1... | collective-permute-start | bytes 110600 | tf_op jit(solution)/shard_map/ppermute | solution.py:624
  47.0 1.9 %collective-permute-start.5 = (bf16[144,128]{1,0:T(8,128)(2,1)S(1)}, bf16[144,128]{1,0:T(8,128)(2,1)S(1)}, u32[]{:S(2)}, u32[]{:S(2)}) collective-permute-start(bf16[144,128]{1,0:T(8,128)(2,1)S(1)} %get-tuple-element.27), channel_id=1, source_target_pairs={{1,0},{2,1},{3,2},{4,3},{5,4},{6,5},{7,6},{8,7},{9,8},{10,9},{11,1... | collective-permute-start | bytes 110600 | tf_op jit(solution)/shard_map/ppermute | solution.py:624
  48.9 4.8 %collective-permute-done.5.upper.refs_4_ = bf16[144,128]{1,0:T(8,128)(2,1)S(1)} collective-permute-done((bf16[144,128]{1,0:T(8,128)(2,1)S(1)}, bf16[144,128]{1,0:T(8,128)(2,1)S(1)}, u32[]{:S(2)}, u32[]{:S(2)}) %collective-permute-start.5) | collective-permute-done | bytes 36896 | tf_op jit(solution)/shard_map/ppermute | solution.py:624
  53.8 3.5 %collective-permute-start.6 = (bf16[304,128]{1,0:T(8,128)(2,1)S(1)}, bf16[304,128]{1,0:T(8,128)(2,1)S(1)}, u32[]{:S(2)}, u32[]{:S(2)}) collective-permute-start(bf16[304,128]{1,0:T(8,128)(2,1)S(1)} %get-tuple-element.29), channel_id=1, source_target_pairs={{0,16},{16,32},{32,48},{48,64},{64,80},{80,96},{96,112},{1,17},{17... | collective-permute-start | bytes 233480 | tf_op jit(solution)/shard_map/ppermute | solution.py:624
  57.3 1.3 %collective-permute-start.7 = (bf16[304,128]{1,0:T(8,128)(2,1)S(1)}, bf16[304,128]{1,0:T(8,128)(2,1)S(1)}, u32[]{:S(2)}, u32[]{:S(2)}) collective-permute-start(bf16[304,128]{1,0:T(8,128)(2,1)S(1)} %get-tuple-element.30), channel_id=1, source_target_pairs={{16,0},{32,16},{48,32},{64,48},{80,64},{96,80},{112,96},{17,1},{33... | collective-permute-start | bytes 233480 | tf_op jit(solution)/shard_map/ppermute | solution.py:624
  58.6 0.1 collective-permute-done.6.refs_6_
  58.8 3.7 %collective-permute-done.7.refs_7_ = bf16[304,128]{1,0:T(8,128)(2,1)S(1)} collective-permute-done((bf16[304,128]{1,0:T(8,128)(2,1)S(1)}, bf16[304,128]{1,0:T(8,128)(2,1)S(1)}, u32[]{:S(2)}, u32[]{:S(2)}) %collective-permute-start.7) | collective-permute-done | bytes 77856 | tf_op jit(solution)/shard_map/ppermute | solution.py:624
  62.5 0.7 copy-done.6
  63.1 5.8 %backward.1 = bf16[16,152,128]{2,1,0:T(8,128)(2,1)S(1)} custom-call(bf16[27,64,128]{2,1,0:T(8,128)(2,1)S(1)} %bitcast.23, f32[1,128]{1,0:T(1,128)S(1)} %bitcast.29, bf16[144,128]{1,0:T(8,128)(2,1)S(1)} %collective-permute-done.4.lower.refs_2_, bf16[4,4,16,128]{3,2,1,0:T(8,128)(2,1)S(1)} %get-tuple-element.26.hidden2.refs_3_, ...), custom_call_target="tpu_custom_call" | custom-call | tf_op jit(solution)/shard_map/backward/pallas_call | solution.py:485
  68.9 19.5 %all_to_all.21.received = bf16[16,152,128]{2,1,0:T(8,128)(2,1)S(1)} all-to-all(bf16[16,152,128]{2,1,0:T(8,128)(2,1)S(1)} %backward.1), channel_id=1, replica_groups=mesh['gy'=8,'gz'=16] {'gz'}, dimensions={0} | all-to-all | bytes 1245184 | tf_op jit(solution)/shard_map/all_to_all | solution.py:650
  88.4 0.7 sum.1
  89.1 13.9 %all_to_all.22.column = bf16[8,144,128]{2,1,0:T(8,128)(2,1)S(1)} all-to-all(bf16[8,144,128]{2,1,0:T(8,128)(2,1)S(1)} %get-tuple-element.37), channel_id=1, replica_groups=mesh['gy'=8,'gz'=16] {'gy'}, dimensions={0} | all-to-all | bytes 589824 | tf_op jit(solution)/shard_map/all_to_all | solution.py:652
  103.1 0.7 share.1
  103.7 5.4 %all-to-all-start.3 = ((bf16[16,32,128]{2,1,0:T(8,128)(2,1)}), bf16[16,32,128]{2,1,0:T(8,128)(2,1)S(1)}, u32[]{:S(2)}, u32[]{:S(2)}) async-start(bf16[16,32,128]{2,1,0:T(8,128)(2,1)} %share.1), calls=%async_computation.3 | async-start | bytes 262144 | tf_op jit(solution)/shard_map/all_to_all | solution.py:653
  109.1 0.7 third.1
  109.8 7.0 %all-to-all-done.3.shared = bf16[16,32,128]{2,1,0:T(8,128)(2,1)S(1)} async-done(((bf16[16,32,128]{2,1,0:T(8,128)(2,1)}), bf16[16,32,128]{2,1,0:T(8,128)(2,1)S(1)}, u32[]{:S(2)}, u32[]{:S(2)}) %all-to-all-start.3) | async-done | bytes 131104 | tf_op jit(solution)/shard_map/all_to_all | solution.py:653
  116.8 0.9 unpack.1
  (18 shorter events, 0.1 us)
Async XLA Ops:
  1.5 8.1 %collective-permute-start = (bf16[8,32,128]{2,1,0:T(8,128)(2,1)S(1)}, bf16[8,32,128]{2,1,0:T(8,128)(2,1)S(1)}, u32[]{:S(2)}, u32[]{:S(2)}) collective-permute-start(bf16[8,32,128]{2,1,0:T(8,128)(2,1)S(1)} %bitcast.30), channel_id=1, source_target_pairs={{0,1},{1,2},{2,3},{3,4},{4,5},{5,6},{6,7},{7,8},{8,9},{9,10},{10,1... | collective-permute-start | bytes 196616 | tf_op jit(solution)/shard_map/ppermute | solution.py:624
  7.6 7.1 %collective-permute-start.1 = (bf16[8,32,128]{2,1,0:T(8,128)(2,1)S(1)}, bf16[8,32,128]{2,1,0:T(8,128)(2,1)S(1)}, u32[]{:S(2)}, u32[]{:S(2)}) collective-permute-start(bf16[8,32,128]{2,1,0:T(8,128)(2,1)S(1)} %bitcast.31), channel_id=1, source_target_pairs={{1,0},{2,1},{3,2},{4,3},{5,4},{6,5},{7,6},{8,7},{9,8},{10,9},{11,1... | collective-permute-start | bytes 196616 | tf_op jit(solution)/shard_map/ppermute | solution.py:624
  9.6 10.8 %copy-start.7 = (bf16[8,1,16,16]{3,2,1,0:T(8,128)(2,1)S(1)}, bf16[8,1,16,16]{3,2,1,0:T(8,128)(2,1)}, u32[]{:S(2)}) copy-start(bf16[8,1,16,16]{3,2,1,0:T(8,128)(2,1)} %param.16) | copy-start | bytes 12292
  14.7 19.1 %copy-start.1 = (bf16[256,512]{1,0:T(8,128)(2,1)S(1)}, bf16[256,512]{1,0:T(8,128)(2,1)}, u32[]{:S(2)}) copy-start(bf16[256,512]{1,0:T(8,128)(2,1)} %constant.4.clone.refs_4_) | copy-start | bytes 786436
  14.7 19.1 %copy-start.2 = (bf16[27,64,32]{1,2,0:T(8,128)(2,1)S(1)}, bf16[27,64,32]{1,2,0:T(8,128)(2,1)}, u32[]{:S(2)}) copy-start(bf16[27,64,32]{1,2,0:T(8,128)(2,1)} %param.12) | copy-start | bytes 331780
  14.8 18.9 %collective-permute-start.3 = (bf16[8,96,128]{2,1,0:T(8,128)(2,1)S(1)}, bf16[8,96,128]{2,1,0:T(8,128)(2,1)S(1)}, u32[]{:S(2)}, u32[]{:S(2)}) collective-permute-start(bf16[8,96,128]{2,1,0:T(8,128)(2,1)S(1)} %maximum_maximum_fusion.refs_1_), channel_id=1, source_target_pairs={{16,0},{32,16},{48,32},{64,48},{80,64},{96,80},{112,96},{17,1},{33... | collective-permute-start | bytes 589832 | tf_op jit(solution)/shard_map/ppermute | solution.py:624
  16.2 17.5 %collective-permute-start.2 = (bf16[8,96,128]{2,1,0:T(8,128)(2,1)S(1)}, bf16[8,96,128]{2,1,0:T(8,128)(2,1)S(1)}, u32[]{:S(2)}, u32[]{:S(2)}) collective-permute-start(bf16[8,96,128]{2,1,0:T(8,128)(2,1)S(1)} %maximum_maximum_fusion.refs_1_), channel_id=1, source_target_pairs={{0,16},{16,32},{32,48},{48,64},{64,80},{80,96},{96,112},{1,17},{17... | collective-permute-start | bytes 589832 | tf_op jit(solution)/shard_map/ppermute | solution.py:624
  20.4 13.3 %copy-start.3 = (bf16[27,32,4]{1,2,0:T(4,128)(2,1)S(1)}, bf16[27,32,4]{1,2,0:T(4,128)(2,1)}, u32[]{:S(2)}) copy-start(bf16[27,32,4]{1,2,0:T(4,128)(2,1)} %param.10) | copy-start | bytes 20740
  33.7 0.7 copy-start.4
  33.7 0.7 copy-start.5
  34.4 28.1 %copy-start = (bf16[27,128,64]{1,2,0:T(8,128)(2,1)S(1)}, bf16[27,128,64]{1,2,0:T(8,128)(2,1)}, u32[]{:S(2)}) copy-start(bf16[27,128,64]{1,2,0:T(8,128)(2,1)} %param.14) | copy-start | bytes 1327108
  44.4 4.5 %collective-permute-start.4 = (bf16[144,128]{1,0:T(8,128)(2,1)S(1)}, bf16[144,128]{1,0:T(8,128)(2,1)S(1)}, u32[]{:S(2)}, u32[]{:S(2)}) collective-permute-start(bf16[144,128]{1,0:T(8,128)(2,1)S(1)} %get-tuple-element.25), channel_id=1, source_target_pairs={{0,1},{1,2},{2,3},{3,4},{4,5},{5,6},{6,7},{7,8},{8,9},{9,10},{10,1... | collective-permute-start | bytes 110600 | tf_op jit(solution)/shard_map/ppermute | solution.py:624
  47.0 6.8 %collective-permute-start.5 = (bf16[144,128]{1,0:T(8,128)(2,1)S(1)}, bf16[144,128]{1,0:T(8,128)(2,1)S(1)}, u32[]{:S(2)}, u32[]{:S(2)}) collective-permute-start(bf16[144,128]{1,0:T(8,128)(2,1)S(1)} %get-tuple-element.27), channel_id=1, source_target_pairs={{1,0},{2,1},{3,2},{4,3},{5,4},{6,5},{7,6},{8,7},{9,8},{10,9},{11,1... | collective-permute-start | bytes 110600 | tf_op jit(solution)/shard_map/ppermute | solution.py:624
  53.8 5.0 %collective-permute-start.6 = (bf16[304,128]{1,0:T(8,128)(2,1)S(1)}, bf16[304,128]{1,0:T(8,128)(2,1)S(1)}, u32[]{:S(2)}, u32[]{:S(2)}) collective-permute-start(bf16[304,128]{1,0:T(8,128)(2,1)S(1)} %get-tuple-element.29), channel_id=1, source_target_pairs={{0,16},{16,32},{32,48},{48,64},{64,80},{80,96},{96,112},{1,17},{17... | collective-permute-start | bytes 233480 | tf_op jit(solution)/shard_map/ppermute | solution.py:624
  57.3 5.1 %collective-permute-start.7 = (bf16[304,128]{1,0:T(8,128)(2,1)S(1)}, bf16[304,128]{1,0:T(8,128)(2,1)S(1)}, u32[]{:S(2)}, u32[]{:S(2)}) collective-permute-start(bf16[304,128]{1,0:T(8,128)(2,1)S(1)} %get-tuple-element.30), channel_id=1, source_target_pairs={{16,0},{32,16},{48,32},{64,48},{80,64},{96,80},{112,96},{17,1},{33... | collective-permute-start | bytes 233480 | tf_op jit(solution)/shard_map/ppermute | solution.py:624
  62.5 0.7 copy-start.6
  103.7 13.1 %all-to-all-start.3 = ((bf16[16,32,128]{2,1,0:T(8,128)(2,1)}), bf16[16,32,128]{2,1,0:T(8,128)(2,1)S(1)}, u32[]{:S(2)}, u32[]{:S(2)}) async-start(bf16[16,32,128]{2,1,0:T(8,128)(2,1)} %share.1), calls=%async_computation.3 | async-start | bytes 262144 | tf_op jit(solution)/shard_map/all_to_all | solution.py:653

commit v5 on v4

--- a/solution.py
+++ b/solution.py
@@ -293,7 +293,7 @@
     (k3, b3, lower, middle, upper, own_cot, before, after, ratio2, w2, patches1, ratio1, fields), refs = (
         refs[:13], refs[13:],
     )
-    packed, w3, patches2, pre3, delta3, patch2, grad2, delta2, patch1, grad1, delta1, turned = refs
+    packed3, packed, w3, patches2, pre3, delta3, patch2, grad2, delta2, patch1, grad1, delta1, turned = refs
     groups = packed.shape[0]
     wide = 128 // groups
     lay_weights3(k3, w3)
@@ -366,6 +366,14 @@
         other = roll(high[2 * m + 1], 64, 1) if 2 * m + 1 < 9 else jnp.zeros((128, 128), F32)
         paired.append(jnp.where(first_half, high[2 * m], other))
     kernel3 = [piece.reshape(groups, wide, 128) for piece in low + paired]
+
+    turned[...] = jnp.concatenate([features, jnp.zeros((112, 128), F32)], axis=0).T
+    feature_rows = turned[pl.ds(0, 16, stride=8), :]
+    for c in range(1, 8):
+        feature_rows = feature_rows + roll(turned[pl.ds(c, 16, stride=8), :], 16 * c, 1)
+    feature_rows = feature_rows.reshape(groups, wide // 8, 128)
+    fill = jnp.zeros((groups, packed3.shape[1] - 14 * wide - wide // 8, 128), F32)
+    packed3[...] = jnp.concatenate(kernel3 + [feature_rows, fill], axis=1).astype(BF16)
 
     for tap in range(9):
         dy, dz = tap // 3, tap % 3
@@ -464,30 +472,21 @@
     biases = jnp.concatenate(
         [bias3, jnp.where(lane((1, 128)) < 64, bias2, bias1), jnp.zeros((14, 128), F32)], axis=0
     )
-    shared = jnp.concatenate(kernel2 + kernel1 + [biases], axis=0).reshape(groups, 512 // groups, 128)
-
-    turned[...] = jnp.concatenate([features, jnp.zeros((112, 128), F32)], axis=0).T
-    feature_rows = turned[pl.ds(0, 16, stride=8), :]
-    for c in range(1, 8):
-        feature_rows = feature_rows + roll(turned[pl.ds(c, 16, stride=8), :], 16 * c, 1)
-    feature_rows = feature_rows.reshape(groups, wide // 8, 128)
-
-    fill = jnp.zeros((groups, packed.shape[1] - 512 // groups - 14 * wide - wide // 8, 128), F32)
-    packed[...] = jnp.concatenate([shared] + kernel3 + [feature_rows, fill], axis=1).astype(BF16)
-
-
-def packed_rows(groups):
+    shared = jnp.concatenate(kernel2 + kernel1 + [biases], axis=0)
+    packed[...] = shared.reshape(groups, 512 // groups, 128).astype(BF16)
+
+
+def run_backward(groups, *operands):
     wide = 128 // groups
-    return -(-(512 // groups + 14 * wide + wide // 8) // 8) * 8
-
-
-def run_backward(groups, *operands):
     return pl.pallas_call(
         backward_kernel,
         name="backward",
-        out_shape=jax.ShapeDtypeStruct((groups, packed_rows(groups), 128), BF16),
+        out_shape=(
+            jax.ShapeDtypeStruct((groups, -(-(14 * wide + wide // 8) // 8) * 8, 128), BF16),
+            jax.ShapeDtypeStruct((groups, 512 // groups, 128), BF16),
+        ),
         in_specs=[VMEM] * len(operands),
-        out_specs=VMEM,
+        out_specs=(VMEM, VMEM),
         scratch_shapes=[
             pltpu.VMEM((9, 256, 256), BF16),
             pltpu.VMEM((8, 8, 16, 256), BF16),
@@ -522,7 +521,7 @@
         sum_kernel,
         name="sum",
         out_shape=(
-            jax.ShapeDtypeStruct((rows_y, 512 // groups + 14 * wide, 128), BF16),
+            jax.ShapeDtypeStruct((rows_y, 14 * wide, 128), BF16),
             jax.ShapeDtypeStruct((wide, groups, 16), BF16),
         ),
         in_specs=[VMEM],
@@ -531,26 +530,25 @@
     )(received)
 
 
-def share_kernel(column, to_all):
-    total = column[:, : to_all.shape[1]].astype(F32).sum(axis=0)
-    to_all[...] = jnp.broadcast_to(total[None], to_all.shape).astype(BF16)
-
-
-def run_share(column, groups):
+def share_kernel(parts, to_each):
+    total = parts[...].astype(F32).sum(axis=0)
+    to_each[...] = jnp.broadcast_to(total[None], to_each.shape).astype(BF16)
+
+
+def run_share(parts, count):
     return pl.pallas_call(
         share_kernel,
         name="share",
-        out_shape=jax.ShapeDtypeStruct((groups, 512 // groups, 128), BF16),
+        out_shape=jax.ShapeDtypeStruct((count,) + parts.shape[1:], BF16),
         in_specs=[VMEM],
         out_specs=VMEM,
         compiler_params=pltpu.CompilerParams(vmem_limit_bytes=LIMIT),
-    )(column)
+    )(parts)
 
 
 def third_kernel(column, grad3):
     wide = grad3.shape[1]
-    first = column.shape[1] - 14 * wide
-    lines = column[:, first:].astype(F32).sum(axis=0)
+    lines = column[...].astype(F32).sum(axis=0)
     for tap in range(9):
         low = lines[tap * wide : tap * wide + wide]
         grad3[tap] = low[:, :64]
@@ -631,9 +629,10 @@
     tile = universe.transpose(1, 2, 0, 3).reshape(8, 32, 128)
     lower, upper = both_ways(tile, tile, "gz")
     strip = jnp.concatenate([lower[:, 4:], tile, upper[:, :28], jnp.zeros((8, 8, 128), BF16)], axis=1)
+    cot = lax.all_to_all(cotangent[:, 0].transpose(1, 0, 2), "gz", 0, 0, tiled=True).reshape(128, 16)
+    strip, cot = lax.optimization_barrier((strip, cot))
     top, bottom = both_ways(strip, strip, "gy")
 
-    cot = lax.all_to_all(cotangent[:, 0].transpose(1, 0, 2), "gz", 0, 0, tiled=True).reshape(128, 16)
     k1 = kernel1.transpose(0, 2, 1)
     k2, k3 = kernel2.transpose(0, 2, 1), kernel3.transpose(0, 2, 1)
 
@@ -643,15 +642,17 @@
     lower, upper = both_ways(to_next, to_previous, "gz")
     row_next, row_previous = run_weave(lower, hidden2, upper, own_cot)
     before, after = both_ways(row_next, row_previous, "gy")
-    packed = run_backward(
+    packed3, packed = run_backward(
         size_z,
         k3, bias3[None], lower, hidden2, upper, own_cot, before, after, ratio2, w2, patches1, ratio1, fields,
     )
     packed = lax.all_to_all(packed, "gz", 0, 0, tiled=True)
-    column, features = run_sum(packed, size_y)
-    column = lax.all_to_all(column, "gy", 0, 0, tiled=True)
-    shared = lax.all_to_all(run_share(column, size_z), "gz", 0, 0, tiled=True)
-    grad3 = run_third(column, wide)
+    packed3 = lax.all_to_all(packed3, "gz", 0, 0, tiled=True)
+    shared = lax.all_to_all(run_share(packed, size_y), "gy", 0, 0, tiled=True)
+    column, features = run_sum(packed3, size_y)
+    shared, column = lax.optimization_barrier((shared, column))
+    shared = lax.all_to_all(run_share(shared, size_z), "gz", 0, 0, tiled=True)
+    grad3 = run_third(lax.all_to_all(column, "gy", 0, 0, tiled=True), wide)
     grad1, grad2, shift1, shift2, shift3 = run_unpack(shared)
     return (
         features[:, None], grad1.transpose(0, 2, 1), shift1[0], grad2.transpose(0, 2, 1), shift2[0], grad3, shift3[0]

time: 118 us -> 142 us (1.20)
  starting transfers between devices: 28.2 us -> 50.8 us
  blocking collectives: 46.7 us -> 26.9 us
  waiting for transfers between devices: 20.7 us -> 39.6 us
    all_to_all x1 -> x4, starting transfers between devices: 5.36 us -> 26.6 us  [the longest x1 11.6 us: shards(): shared = lax.all_to_all(run_share(packed, size_y), 'gy', 0, 0, tiled=True)]
    all_to_all x1 -> x4, waiting for transfers between devices: 6.99 us -> 27 us  [the longest x1 10.4 us: shards(): packed3 = lax.all_to_all(packed3, 'gz', 0, 0, tiled=True)]
    all_to_all x2 -> x1, blocking collectives: 27.2 us -> 12.7 us  [shards(): shared = lax.all_to_all(run_share(shared, size_z), 'gz', 0, 0, tiled=True)]
    all_to_all x1, blocking collectives: 19.5 us -> 14.1 us  [shards(): packed = lax.all_to_all(packed, 'gz', 0, 0, tiled=True)]
    ppermute x4, waiting for transfers between devices: 13.6 us -> 11.6 us  [both_ways(): lax.ppermute(to_previous, axis, back)]
    ppermute x4, starting transfers between devices: 16.3 us -> 17.8 us  [both_ways(): lax.ppermute(to_next, axis, forth)]
  transfers between devices with their start and end apart: 9 -> 12, of which waited for: 5 -> 9; matrix products, arithmetic and copies ran while one was open for 0% -> 1% of each run, Pallas kernels for 1% -> 2%
where the time goes in v5:
time: 142 us; the launch traced here: 141 us
  starting transfers between devices  50.8 us (36%)
  waiting for transfers between devices  39.6 us (28%)
  blocking collectives  26.9 us (19%)
  Pallas kernels  19.6 us (14%)
  local copies, waits for them, and re-layouts  2.95 us (2%)
    ppermute x4, starting transfers between devices, both_ways(): lax.ppermute(to_next, axis, forth)  17.8 us
    all_to_all x1, blocking collectives, shards(): packed = lax.all_to_all(packed, 'gz', 0, 0, tiled=True)  14.1 us
    all_to_all x1, blocking collectives, shards(): shared = lax.all_to_all(run_share(shared, size_z), 'gz', 0, 0, tiled=True)  12.7 us
    ppermute x4, waiting for transfers between devices, both_ways(): lax.ppermute(to_previous, axis, back)  11.6 us
    all_to_all x1, starting transfers between devices, shards(): shared = lax.all_to_all(run_share(packed, size_y), 'gy', 0, 0, tiled=True)  11.6 us
    all_to_all x1, waiting for transfers between devices, shards(): packed3 = lax.all_to_all(packed3, 'gz', 0, 0, tiled=True)  10.4 us
    pallas_call x1, Pallas kernels, run_forward(): pl.pallas_call(forward_kernel, name='forward', out_shape=(jax.ShapeDtypeS...  10.1 us
    all_to_all x1, starting transfers between devices, shards(): lax.all_to_all(cotangent[:, 0].transpose(1, 0, 2), 'gz', 0, 0, tiled=True)  7.55 us
  transfers between devices with their start and end apart: 12, of which 9 were waited for; matrix products, arithmetic and copies ran while one was open for 1% of the time, Pallas kernels for 2%

profile of v5, /device:TPU:1, one launch (start us, length us, event | category | flops | bytes accessed | tf_op | source)
XLA Modules:
  0.0 140.7 jit_solution(2820215401032266107)
XLA Ops:
  0.6 0.9 copy.19
  1.5 6.0 %collective-permute-start = (bf16[8,32,128]{2,1,0:T(8,128)(2,1)S(1)}, bf16[8,32,128]{2,1,0:T(8,128)(2,1)S(1)}, u32[]{:S(2)}, u32[]{:S(2)}) collective-permute-start(bf16[8,32,128]{2,1,0:T(8,128)(2,1)S(1)} %bitcast.30), channel_id=1, source_target_pairs={{0,1},{1,2},{2,3},{3,4},{4,5},{5,6},{6,7},{7,8},{8,9},{9,10},{10,1... | collective-permute-start | bytes 196616 | tf_op jit(solution)/shard_map/ppermute | solution.py:622
  7.6 1.9 %collective-permute-start.1 = (bf16[8,32,128]{2,1,0:T(8,128)(2,1)S(1)}, bf16[8,32,128]{2,1,0:T(8,128)(2,1)S(1)}, u32[]{:S(2)}, u32[]{:S(2)}) collective-permute-start(bf16[8,32,128]{2,1,0:T(8,128)(2,1)S(1)} %bitcast.31), channel_id=1, source_target_pairs={{1,0},{2,1},{3,2},{4,3},{5,4},{6,5},{7,6},{8,7},{9,8},{10,9},{11,1... | collective-permute-start | bytes 196616 | tf_op jit(solution)/shard_map/ppermute | solution.py:622
  9.5 0.6 copy.23
  10.2 7.6 %all-to-all-start = ((bf16[16,8,16]{2,1,0:T(8,128)(2,1)}), bf16[16,8,16]{2,1,0:T(8,128)(2,1)S(1)}, u32[]{:S(2)}, u32[]{:S(2)}) async-start(bf16[16,8,16]{2,1,0:T(8,128)(2,1)} %bitcast.21), calls=%async_computation | async-start | bytes 65536 | tf_op jit(solution)/shard_map/all_to_all | solution.py:632
  18.0 7.0 %all-to-all-done = bf16[16,8,16]{2,1,0:T(8,128)(2,1)S(1)} async-done(((bf16[16,8,16]{2,1,0:T(8,128)(2,1)}), bf16[16,8,16]{2,1,0:T(8,128)(2,1)S(1)}, u32[]{:S(2)}, u32[]{:S(2)}) %all-to-all-start) | async-done | bytes 4128 | tf_op jit(solution)/shard_map/all_to_all | solution.py:632
  25.0 1.3 collective-permute-start.3
  26.3 4.2 %collective-permute-start.2 = (bf16[8,96,128]{2,1,0:T(8,128)(2,1)S(1)}, bf16[8,96,128]{2,1,0:T(8,128)(2,1)S(1)}, u32[]{:S(2)}, u32[]{:S(2)}) collective-permute-start(bf16[8,96,128]{2,1,0:T(8,128)(2,1)S(1)} %maximum_maximum_fusion.refs_1_), channel_id=1, source_target_pairs={{0,16},{16,32},{32,48},{48,64},{64,80},{80,96},{96,112},{1,17},{17... | collective-permute-start | bytes 589832 | tf_op jit(solution)/shard_map/ppermute | solution.py:622
  30.5 2.9 %collective-permute-done.3.refs_2_ = bf16[8,96,128]{2,1,0:T(8,128)(2,1)S(1)} collective-permute-done((bf16[8,96,128]{2,1,0:T(8,128)(2,1)S(1)}, bf16[8,96,128]{2,1,0:T(8,128)(2,1)S(1)}, u32[]{:S(2)}, u32[]{:S(2)}) %collective-permute-start.3) | collective-permute-done | bytes 196640 | tf_op jit(solution)/shard_map/ppermute | solution.py:622
  33.4 0.9 collective-permute-done.2.refs_0_
  34.3 0.6 copy-done.4
  34.9 10.1 %forward.1 = (bf16[144,128]{1,0:T(8,128)(2,1)S(1)}, bf16[144,128]{1,0:T(8,128)(2,1)S(1)}, bf16[4,4,16,128]{3,2,1,0:T(8,128)(2,1)S(1)}, bf16[16,128]{1,0:T(8,128)...) custom-call(bf16[8,96,128]{2,1,0:T(8,128)(2,1)S(1)} %collective-perm, ...), custom_call_target="tpu_custom_call" | custom-call | tf_op jit(solution)/shard_map/forward/pallas_call | solution.py:250
  45.0 3.5 %collective-permute-start.4 = (bf16[144,128]{1,0:T(8,128)(2,1)S(1)}, bf16[144,128]{1,0:T(8,128)(2,1)S(1)}, u32[]{:S(2)}, u32[]{:S(2)}) collective-permute-start(bf16[144,128]{1,0:T(8,128)(2,1)S(1)} %get-tuple-element.33), channel_id=1, source_target_pairs={{0,1},{1,2},{2,3},{3,4},{4,5},{5,6},{6,7},{7,8},{8,9},{9,10},{10,1... | collective-permute-start | bytes 110600 | tf_op jit(solution)/shard_map/ppermute | solution.py:622
  48.5 1.9 %collective-permute-start.5 = (bf16[144,128]{1,0:T(8,128)(2,1)S(1)}, bf16[144,128]{1,0:T(8,128)(2,1)S(1)}, u32[]{:S(2)}, u32[]{:S(2)}) collective-permute-start(bf16[144,128]{1,0:T(8,128)(2,1)S(1)} %get-tuple-element.35), channel_id=1, source_target_pairs={{1,0},{2,1},{3,2},{4,3},{5,4},{6,5},{7,6},{8,7},{9,8},{10,9},{11,1... | collective-permute-start | bytes 110600 | tf_op jit(solution)/shard_map/ppermute | solution.py:622
  50.4 4.8 %collective-permute-done.5.upper.refs_4_ = bf16[144,128]{1,0:T(8,128)(2,1)S(1)} collective-permute-done((bf16[144,128]{1,0:T(8,128)(2,1)S(1)}, bf16[144,128]{1,0:T(8,128)(2,1)S(1)}, u32[]{:S(2)}, u32[]{:S(2)}) %collective-permute-start.5) | collective-permute-done | bytes 36896 | tf_op jit(solution)/shard_map/ppermute | solution.py:622
  55.3 4.1 %collective-permute-start.6 = (bf16[304,128]{1,0:T(8,128)(2,1)S(1)}, bf16[304,128]{1,0:T(8,128)(2,1)S(1)}, u32[]{:S(2)}, u32[]{:S(2)}) collective-permute-start(bf16[304,128]{1,0:T(8,128)(2,1)S(1)} %get-tuple-element.37), channel_id=1, source_target_pairs={{0,16},{16,32},{32,48},{48,64},{64,80},{80,96},{96,112},{1,17},{17... | collective-permute-start | bytes 233480 | tf_op jit(solution)/shard_map/ppermute | solution.py:622
  59.4 1.3 collective-permute-start.7
  60.8 3.9 %collective-permute-done.7.refs_7_ = bf16[304,128]{1,0:T(8,128)(2,1)S(1)} collective-permute-done((bf16[304,128]{1,0:T(8,128)(2,1)S(1)}, bf16[304,128]{1,0:T(8,128)(2,1)S(1)}, u32[]{:S(2)}, u32[]{:S(2)}) %collective-permute-start.7) | collective-permute-done | bytes 77856 | tf_op jit(solution)/shard_map/ppermute | solution.py:622
  64.7 0.7 copy-done.6
  65.4 6.5 %backward.1 = (bf16[16,120,128]{2,1,0:T(8,128)(2,1)}, bf16[16,32,128]{2,1,0:T(8,128)(2,1)S(1)}) custom-call(bf16[27,64,128]{2,1,0:T(8,128)(2,1)S(1)} %bitcast.23, f32[1,128]{1,0:T(1,128)S(1)} %bitcast.29, bf16[144,128]{1,0:T(8,128)(2,1)S(1)} %collective-permute-done.4.lower.refs_2_, bf16[4,4,16,128]{3,2,1,0:T(8,128)(2,1)S(1)} %get-tuple-element.34.hidden2.refs_3_, ...), custom_call_target="tpu_custom_call" | custom-call | tf_op jit(solution)/shard_map/backward/pallas_call | solution.py:481
  71.8 14.1 %all_to_all.30.parts = bf16[16,32,128]{2,1,0:T(8,128)(2,1)S(1)} all-to-all(bf16[16,32,128]{2,1,0:T(8,128)(2,1)S(1)} %get-tuple-element.46), channel_id=1, replica_groups=mesh['gy'=8,'gz'=16] {'gz'}, dimensions={0} | all-to-all | bytes 262144 | tf_op jit(solution)/shard_map/all_to_all | solution.py:649
  86.0 4.0 %all-to-all-start.1 = ((bf16[16,120,128]{2,1,0:T(8,128)(2,1)}), bf16[16,120,128]{2,1,0:T(8,128)(2,1)S(1)}, u32[]{:S(2)}, u32[]{:S(2)}) async-start(bf16[16,120,128]{2,1,0:T(8,128)(2,1)} %get-tuple-element.44), calls=%async_computation.1 | async-start | bytes 983040 | tf_op jit(solution)/shard_map/all_to_all | solution.py:650
  90.0 0.7 share.2
  90.6 10.4 %all-to-all-done.1.received = bf16[16,120,128]{2,1,0:T(8,128)(2,1)S(1)} async-done(((bf16[16,120,128]{2,1,0:T(8,128)(2,1)}), bf16[16,120,128]{2,1,0:T(8,128)(2,1)S(1)}, u32[]{:S(2)}, u32[]{:S(2)}) %all-to-all-start.1) | async-done | bytes 491552 | tf_op jit(solution)/shard_map/all_to_all | solution.py:650
  101.0 11.6 %all-to-all-start.3 = ((bf16[8,32,128]{2,1,0:T(8,128)(2,1)}), bf16[8,32,128]{2,1,0:T(8,128)(2,1)S(1)}, u32[]{:S(2)}, u32[]{:S(2)}) async-start(bf16[8,32,128]{2,1,0:T(8,128)(2,1)} %share.2), calls=%async_computation.3 | async-start | bytes 131072 | tf_op jit(solution)/shard_map/all_to_all | solution.py:651
  112.6 0.8 sum.1
  113.4 4.4 %all-to-all-done.3.parts = bf16[8,32,128]{2,1,0:T(8,128)(2,1)S(1)} async-done(((bf16[8,32,128]{2,1,0:T(8,128)(2,1)}), bf16[8,32,128]{2,1,0:T(8,128)(2,1)S(1)}, u32[]{:S(2)}, u32[]{:S(2)}) %all-to-all-start.3) | async-done | bytes 65568 | tf_op jit(solution)/shard_map/all_to_all | solution.py:651
  117.8 12.7 %all_to_all.31.shared = bf16[16,32,128]{2,1,0:T(8,128)(2,1)S(1)} all-to-all(bf16[16,32,128]{2,1,0:T(8,128)(2,1)S(1)} %share.3), channel_id=1, replica_groups=mesh['gy'=8,'gz'=16] {'gz'}, dimensions={0} | all-to-all | bytes 262144 | tf_op jit(solution)/shard_map/all_to_all | solution.py:654
  130.6 3.4 %all-to-all-start.5 = ((bf16[8,112,128]{2,1,0:T(8,128)(2,1)}), bf16[8,112,128]{2,1,0:T(8,128)(2,1)S(1)}, u32[]{:S(2)}, u32[]{:S(2)}) async-start(bf16[8,112,128]{2,1,0:T(8,128)(2,1)} %get-tuple-element.53), calls=%async_computation.5 | async-start | bytes 458752 | tf_op jit(solution)/shard_map/all_to_all | solution.py:655
  134.0 0.9 unpack.1
  134.8 5.1 %all-to-all-done.5.column = bf16[8,112,128]{2,1,0:T(8,128)(2,1)S(1)} async-done(((bf16[8,112,128]{2,1,0:T(8,128)(2,1)}), bf16[8,112,128]{2,1,0:T(8,128)(2,1)S(1)}, u32[]{:S(2)}, u32[]{:S(2)}) %all-to-all-start.5) | async-done | bytes 229408 | tf_op jit(solution)/shard_map/all_to_all | solution.py:655
  140.0 0.7 third.1
  (24 shorter events, 0.4 us)
Async XLA Ops:
  0.6 8.9 %copy-start.7 = (bf16[8,1,16,16]{3,2,1,0:T(8,128)(2,1)S(1)}, bf16[8,1,16,16]{3,2,1,0:T(8,128)(2,1)}, u32[]{:S(2)}) copy-start(bf16[8,1,16,16]{3,2,1,0:T(8,128)(2,1)} %param.16) | copy-start | bytes 12292
  1.5 16.3 %collective-permute-start = (bf16[8,32,128]{2,1,0:T(8,128)(2,1)S(1)}, bf16[8,32,128]{2,1,0:T(8,128)(2,1)S(1)}, u32[]{:S(2)}, u32[]{:S(2)}) collective-permute-start(bf16[8,32,128]{2,1,0:T(8,128)(2,1)S(1)} %bitcast.30), channel_id=1, source_target_pairs={{0,1},{1,2},{2,3},{3,4},{4,5},{5,6},{6,7},{7,8},{8,9},{9,10},{10,1... | collective-permute-start | bytes 196616 | tf_op jit(solution)/shard_map/ppermute | solution.py:622
  7.6 10.2 %collective-permute-start.1 = (bf16[8,32,128]{2,1,0:T(8,128)(2,1)S(1)}, bf16[8,32,128]{2,1,0:T(8,128)(2,1)S(1)}, u32[]{:S(2)}, u32[]{:S(2)}) collective-permute-start(bf16[8,32,128]{2,1,0:T(8,128)(2,1)S(1)} %bitcast.31), channel_id=1, source_target_pairs={{1,0},{2,1},{3,2},{4,3},{5,4},{6,5},{7,6},{8,7},{9,8},{10,9},{11,1... | collective-permute-start | bytes 196616 | tf_op jit(solution)/shard_map/ppermute | solution.py:622
  10.2 14.9 %all-to-all-start = ((bf16[16,8,16]{2,1,0:T(8,128)(2,1)}), bf16[16,8,16]{2,1,0:T(8,128)(2,1)S(1)}, u32[]{:S(2)}, u32[]{:S(2)}) async-start(bf16[16,8,16]{2,1,0:T(8,128)(2,1)} %bitcast.21), calls=%async_computation | async-start | bytes 65536 | tf_op jit(solution)/shard_map/all_to_all | solution.py:632
  17.8 16.5 %copy-start.1 = (bf16[256,512]{1,0:T(8,128)(2,1)S(1)}, bf16[256,512]{1,0:T(8,128)(2,1)}, u32[]{:S(2)}) copy-start(bf16[256,512]{1,0:T(8,128)(2,1)} %constant.4.clone.refs_4_) | copy-start | bytes 786436
  17.8 16.4 %copy-start.2 = (bf16[27,64,32]{1,2,0:T(8,128)(2,1)S(1)}, bf16[27,64,32]{1,2,0:T(8,128)(2,1)}, u32[]{:S(2)}) copy-start(bf16[27,64,32]{1,2,0:T(8,128)(2,1)} %param.12) | copy-start | bytes 331780
  17.8 16.4 %copy-start.3 = (bf16[27,32,4]{1,2,0:T(4,128)(2,1)S(1)}, bf16[27,32,4]{1,2,0:T(4,128)(2,1)}, u32[]{:S(2)}) copy-start(bf16[27,32,4]{1,2,0:T(4,128)(2,1)} %param.10) | copy-start | bytes 20740
  25.0 8.4 %collective-permute-start.3 = (bf16[8,96,128]{2,1,0:T(8,128)(2,1)S(1)}, bf16[8,96,128]{2,1,0:T(8,128)(2,1)S(1)}, u32[]{:S(2)}, u32[]{:S(2)}) collective-permute-start(bf16[8,96,128]{2,1,0:T(8,128)(2,1)S(1)} %maximum_maximum_fusion.refs_1_), channel_id=1, source_target_pairs={{16,0},{32,16},{48,32},{64,48},{80,64},{96,80},{112,96},{17,1},{33... | collective-permute-start | bytes 589832 | tf_op jit(solution)/shard_map/ppermute | solution.py:622
  26.3 7.9 %collective-permute-start.2 = (bf16[8,96,128]{2,1,0:T(8,128)(2,1)S(1)}, bf16[8,96,128]{2,1,0:T(8,128)(2,1)S(1)}, u32[]{:S(2)}, u32[]{:S(2)}) collective-permute-start(bf16[8,96,128]{2,1,0:T(8,128)(2,1)S(1)} %maximum_maximum_fusion.refs_1_), channel_id=1, source_target_pairs={{0,16},{16,32},{32,48},{48,64},{64,80},{80,96},{96,112},{1,17},{17... | collective-permute-start | bytes 589832 | tf_op jit(solution)/shard_map/ppermute | solution.py:622
  34.2 0.7 copy-start.4
  34.2 0.7 copy-start.5
  34.9 29.8 %copy-start = (bf16[27,128,64]{1,2,0:T(8,128)(2,1)S(1)}, bf16[27,128,64]{1,2,0:T(8,128)(2,1)}, u32[]{:S(2)}) copy-start(bf16[27,128,64]{1,2,0:T(8,128)(2,1)} %param.14) | copy-start | bytes 1327108
  45.0 5.4 %collective-permute-start.4 = (bf16[144,128]{1,0:T(8,128)(2,1)S(1)}, bf16[144,128]{1,0:T(8,128)(2,1)S(1)}, u32[]{:S(2)}, u32[]{:S(2)}) collective-permute-start(bf16[144,128]{1,0:T(8,128)(2,1)S(1)} %get-tuple-element.33), channel_id=1, source_target_pairs={{0,1},{1,2},{2,3},{3,4},{4,5},{5,6},{6,7},{7,8},{8,9},{9,10},{10,1... | collective-permute-start | bytes 110600 | tf_op jit(solution)/shard_map/ppermute | solution.py:622
  48.5 6.8 %collective-permute-start.5 = (bf16[144,128]{1,0:T(8,128)(2,1)S(1)}, bf16[144,128]{1,0:T(8,128)(2,1)S(1)}, u32[]{:S(2)}, u32[]{:S(2)}) collective-permute-start(bf16[144,128]{1,0:T(8,128)(2,1)S(1)} %get-tuple-element.35), channel_id=1, source_target_pairs={{1,0},{2,1},{3,2},{4,3},{5,4},{6,5},{7,6},{8,7},{9,8},{10,9},{11,1... | collective-permute-start | bytes 110600 | tf_op jit(solution)/shard_map/ppermute | solution.py:622
  55.3 5.5 %collective-permute-start.6 = (bf16[304,128]{1,0:T(8,128)(2,1)S(1)}, bf16[304,128]{1,0:T(8,128)(2,1)S(1)}, u32[]{:S(2)}, u32[]{:S(2)}) collective-permute-start(bf16[304,128]{1,0:T(8,128)(2,1)S(1)} %get-tuple-element.37), channel_id=1, source_target_pairs={{0,16},{16,32},{32,48},{48,64},{64,80},{80,96},{96,112},{1,17},{17... | collective-permute-start | bytes 233480 | tf_op jit(solution)/shard_map/ppermute | solution.py:622
  59.4 5.3 %collective-permute-start.7 = (bf16[304,128]{1,0:T(8,128)(2,1)S(1)}, bf16[304,128]{1,0:T(8,128)(2,1)S(1)}, u32[]{:S(2)}, u32[]{:S(2)}) collective-permute-start(bf16[304,128]{1,0:T(8,128)(2,1)S(1)} %get-tuple-element.38), channel_id=1, source_target_pairs={{16,0},{32,16},{48,32},{64,48},{80,64},{96,80},{112,96},{17,1},{33... | collective-permute-start | bytes 233480 | tf_op jit(solution)/shard_map/ppermute | solution.py:622
  64.7 0.7 copy-start.6
  86.0 15.0 %all-to-all-start.1 = ((bf16[16,120,128]{2,1,0:T(8,128)(2,1)}), bf16[16,120,128]{2,1,0:T(8,128)(2,1)S(1)}, u32[]{:S(2)}, u32[]{:S(2)}) async-start(bf16[16,120,128]{2,1,0:T(8,128)(2,1)} %get-tuple-element.44), calls=%async_computation.1 | async-start | bytes 983040 | tf_op jit(solution)/shard_map/all_to_all | solution.py:650
  101.0 16.8 %all-to-all-start.3 = ((bf16[8,32,128]{2,1,0:T(8,128)(2,1)}), bf16[8,32,128]{2,1,0:T(8,128)(2,1)S(1)}, u32[]{:S(2)}, u32[]{:S(2)}) async-start(bf16[8,32,128]{2,1,0:T(8,128)(2,1)} %share.2), calls=%async_computation.3 | async-start | bytes 131072 | tf_op jit(solution)/shard_map/all_to_all | solution.py:651
  130.6 9.4 %all-to-all-start.5 = ((bf16[8,112,128]{2,1,0:T(8,128)(2,1)}), bf16[8,112,128]{2,1,0:T(8,128)(2,1)S(1)}, u32[]{:S(2)}, u32[]{:S(2)}) async-start(bf16[8,112,128]{2,1,0:T(8,128)(2,1)} %get-tuple-element.53), calls=%async_computation.5 | async-start | bytes 458752 | tf_op jit(solution)/shard_map/all_to_all | solution.py:655

commit v6 on v4

--- a/solution.py
+++ b/solution.py
@@ -1,8 +1,8 @@
 import functools
+import math
 
 import jax
 import jax.numpy as jnp
-import numpy as np
 from jax import lax
 from jax.experimental import pallas as pl
 from jax.experimental.pallas import tpu as pltpu
@@ -11,6 +11,7 @@
 F32 = jnp.float32
 BF16 = jnp.bfloat16
 SLOPE = 0.3
+TWO_LOG2_E = 2.0 / math.log(2.0)
 PAIRS = ((0, 1), (2, 3), (-3, -2), (4, 5), (-1, 6))
 VMEM = pl.BlockSpec(memory_space=pltpu.VMEM)
 LIMIT = 24 * 1024 * 1024
@@ -33,7 +34,8 @@
 
 
 def exps(pre):
-    return jnp.exp(2.0 * jnp.maximum(pre, SLOPE * pre))
+    scaled = pre * TWO_LOG2_E
+    return jnp.exp2(jnp.maximum(scaled, SLOPE * scaled))
 
 
 def rounded(value):
@@ -55,14 +57,47 @@
     return jnp.where(rows == count - 1, 0.0, roll(value, count - 1, 0))
 
 
-def forward_kernel(*refs):
-    (top, mid, bot, cot, pick, k1, b1, k2, b2), refs = refs[:9], refs[9:]
-    (to_next, to_previous, hidden2, own_cot, ratio2, patches1, ratio1, fields, w2), refs = refs[:9], refs[9:]
-    w1, left, field, first, spread, pre2, second = refs
+def weights_kernel(k1, b1, k2, b2, k3, b3, w1, w2, w3, biases, pick):
     lay_weights1(k1, w1)
     lay_weights2(k2, w2)
-    bias1 = jnp.concatenate([b1[...]] * 8, axis=1)
-    bias2 = jnp.concatenate([b2[...]] * 4, axis=1)
+    lay_weights3(k3, w3)
+    rows = [
+        jnp.concatenate([b1[...]] * 8, axis=1),
+        jnp.concatenate([b2[...]] * 4, axis=1),
+        jnp.concatenate([b3[...]] * 2, axis=1),
+    ]
+    biases[...] = jnp.concatenate(rows + [jnp.zeros((5, 256), F32)], axis=0)
+    for px in range(4):
+        row = lax.broadcasted_iota(jnp.int32, (256, 128), 0)
+        col = lax.broadcasted_iota(jnp.int32, (256, 128), 1)
+        same = row // 128 == col // 64
+        hit = (row % 128) == 2 * (col % 64) - 1 + px
+        pick[:, px * 128 : px * 128 + 128] = jnp.where(same & hit, 1.0, 0.0).astype(BF16)
+
+
+def run_weights(*operands):
+    return pl.pallas_call(
+        weights_kernel,
+        name="weights",
+        out_shape=(
+            jax.ShapeDtypeStruct((256, 256), BF16),
+            jax.ShapeDtypeStruct((3, 512, 256), BF16),
+            jax.ShapeDtypeStruct((9, 256, 256), BF16),
+            jax.ShapeDtypeStruct((8, 256), F32),
+            jax.ShapeDtypeStruct((256, 512), BF16),
+        ),
+        in_specs=[VMEM] * 6,
+        out_specs=(VMEM,) * 5,
+        compiler_params=pltpu.CompilerParams(vmem_limit_bytes=LIMIT),
+    )(*operands)
+
+
+def forward_kernel(
+    top, mid, bot, cot, w1, w2, biases, pick,
+    to_next, to_previous, hidden2, own_cot, ratio2, patches1, ratio1, fields,
+    left, field, turned, first, spread, pre2, second,
+):
+    bias1, bias2 = biases[0:1], biases[1:2]
     base_y, base_z = lax.axis_index("gy"), lax.axis_index("gz")
     size_y, size_z = lax.axis_size("gy"), lax.axis_size("gz")
 
@@ -100,21 +135,24 @@
     def sift(step, carry):
         block = left[pl.ds(2 * step, 2)].reshape(160, 256)
         out = dot(block, pick[...]).astype(BF16).reshape(2, 5, 16, 512)
-        for px in range(4):
-            for k in range(5):
-                field[pl.ds(2 * step, 2), px * 16 : px * 16 + 16, k * 128 : k * 128 + 128] = out[
-                    :, k, :, px * 128 : px * 128 + 128
-                ]
+        for parity in range(2):
+            for px in range(4):
+                at = (parity * 4 + px) * 16
+                for k in range(5):
+                    field[step, at : at + 16, k * 128 : k * 128 + 128] = out[
+                        parity, k, :, px * 128 : px * 128 + 128
+                    ]
+        turned[step] = field[step].T
         return carry
 
     lax.fori_loop(0, 11, sift, 0)
-    fields[...] = field[6:16, :, :256]
+    fields[...] = field[3:8, :, :256]
     first[:, :, 0:8] = jnp.zeros((10, 10, 8, 128), F32)
     first[:, :, 72:80] = jnp.zeros((10, 10, 8, 128), F32)
 
     def block1(yw, carry):
-        stack = field[pl.ds(2 * yw, 4)].reshape(256, 640)
-        pre = dot_tn(stack, w1[...]) + bias1
+        stack = jnp.concatenate([turned[yw], turned[yw + 1]], axis=1)
+        pre = dot(stack, w1[...]) + bias1
         e = exps(pre)
         total = e[:, :128] + e[:, 128:]
         total = total + roll(total, 64, 1)
@@ -238,25 +276,25 @@
 
 
 def run_forward(*operands):
-    kept = (
-        jax.ShapeDtypeStruct((4, 4, 16, 128), BF16),
-        jax.ShapeDtypeStruct((16, 128), BF16),
-        jax.ShapeDtypeStruct((8, 4, 32, 256), F32),
-        jax.ShapeDtypeStruct((6, 6, 32, 128), BF16),
-        jax.ShapeDtypeStruct((4, 256, 256), F32),
-        jax.ShapeDtypeStruct((10, 64, 256), BF16),
-        jax.ShapeDtypeStruct((3, 512, 256), BF16),
-    )
     return pl.pallas_call(
         forward_kernel,
         name="forward",
-        out_shape=(jax.ShapeDtypeStruct((144, 128), BF16),) * 2 + kept,
+        out_shape=(
+            jax.ShapeDtypeStruct((144, 128), BF16),
+            jax.ShapeDtypeStruct((144, 128), BF16),
+            jax.ShapeDtypeStruct((4, 4, 16, 128), BF16),
+            jax.ShapeDtypeStruct((16, 128), BF16),
+            jax.ShapeDtypeStruct((8, 4, 32, 256), F32),
+            jax.ShapeDtypeStruct((6, 6, 32, 128), BF16),
+            jax.ShapeDtypeStruct((4, 256, 256), F32),
+            jax.ShapeDtypeStruct((5, 128, 256), BF16),
+        ),
         in_specs=[VMEM] * len(operands),
-        out_specs=(VMEM,) * 9,
+        out_specs=(VMEM,) * 8,
         scratch_shapes=[
-            pltpu.VMEM((256, 256), BF16),
             pltpu.VMEM((22, 80, 256), BF16),
-            pltpu.VMEM((22, 64, 640), BF16),
+            pltpu.VMEM((11, 128, 640), BF16),
+            pltpu.VMEM((11, 640, 128), BF16),
             pltpu.VMEM((10, 10, 80, 128), F32),
             pltpu.VMEM((10, 10, 32, 128), BF16),
             pltpu.VMEM((8, 4, 32, 256), F32),
@@ -289,70 +327,44 @@
     )(*operands)
 
 
-def backward_kernel(*refs):
-    (k3, b3, lower, middle, upper, own_cot, before, after, ratio2, w2, patches1, ratio1, fields), refs = (
-        refs[:13], refs[13:],
-    )
-    packed, w3, patches2, pre3, delta3, patch2, grad2, delta2, patch1, grad1, delta1, turned = refs
+def lay_patches2(rows, target):
+    half = lane((16, 128)) < 64
+    swapped = roll(rows.astype(F32), 64, 1)
+    target[...] = jnp.concatenate(
+        [jnp.where(half, down(swapped), swapped), jnp.where(half, swapped, up(swapped))], axis=1
+    ).astype(BF16)
+
+
+def pool3(pre, cot):
+    e = exps(pre)
+    total = e[0, 0] + e[0, 1] + e[1, 0] + e[1, 1]
+    total = total[:, :128] + total[:, 128:]
+    mean = total * 0.125
+    share = cot.astype(F32) * (0.125 / mean)
+    share = jnp.concatenate([share, share], axis=1)
+    return mean, (jnp.where(pre > 0, 1.0, SLOPE) * (e * share)).astype(BF16)
+
+
+def own_kernel(hidden2, own_cot, w3, biases, packed, shift3, patches2, pre3, turned):
     groups = packed.shape[0]
     wide = 128 // groups
-    lay_weights3(k3, w3)
-    bias3_in = jnp.concatenate([b3[...]] * 2, axis=1)
-    half = lane((16, 128)) < 64
-
-    def lay(y, source):
-        for z in range(8):
-            swapped = roll(source(z).astype(F32), 64, 1)
-            patches2[y, z] = jnp.concatenate(
-                [jnp.where(half, down(swapped), swapped), jnp.where(half, swapped, up(swapped))], axis=1
-            ).astype(BF16)
-
-    for y in range(2):
-        lay(y, lambda z: before[(y * 8 + z) * 16 : (y * 8 + z + 1) * 16])
-        lay(y + 6, lambda z: after[(y * 8 + z) * 16 : (y * 8 + z + 1) * 16])
-
-    def pick_middle(y, z):
-        if z < 2:
-            return lower[(y * 2 + z) * 16 : (y * 2 + z + 1) * 16]
-        if z < 6:
-            return middle[y, z - 2]
-        return upper[(y * 2 + z - 6) * 16 : (y * 2 + z - 5) * 16]
-
     for y in range(4):
-        lay(y + 2, functools.partial(pick_middle, y))
-
+        for z in range(4):
+            lay_patches2(hidden2[y, z], patches2.at[y, z])
     for tap in range(9):
         dy, dz = tap // 3, tap % 3
-        block = patches2[dy : dy + 6, dz : dz + 6].reshape(576, 256)
-        term = dot(block, w3[tap]).reshape(6, 6, 16, 256)
-        pre3[...] = term + bias3_in if tap == 0 else pre3[...] + term
-
-    for wy in range(3):
-        for wz in range(3):
-            pre = pre3[2 * wy : 2 * wy + 2, 2 * wz : 2 * wz + 2]
-            e = exps(pre)
-            total = e[0, 0] + e[0, 1] + e[1, 0] + e[1, 1]
-            total = total[:, :128] + total[:, 128:]
-            mean = total * 0.125
-            if wy == 1:
-                cot = own_cot[...] if wz == 1 else (lower if wz == 0 else upper)[128:144]
-            else:
-                cot = (before if wy == 0 else after)[256 + wz * 16 : 272 + wz * 16]
-            share = cot.astype(F32) * (0.125 / mean)
-            share = jnp.concatenate([share, share], axis=1)
-            delta3[2 * wy : 2 * wy + 2, 2 * wz : 2 * wz + 2] = (
-                jnp.where(pre > 0, 1.0, SLOPE) * (e * share)
-            ).astype(BF16)
-            if wy == 1 and wz == 1:
-                features = rounded(jnp.log(mean) * 0.5)
-
-    own3 = delta3[2:4, 2:4].reshape(64, 256)
+        block = patches2[dy : dy + 2, dz : dz + 2].reshape(64, 256)
+        term = dot(block, w3[tap])
+        pre3[...] = term + biases[2:3] if tap == 0 else pre3[...] + term
+    mean, delta = pool3(pre3[...].reshape(2, 2, 16, 256), own_cot[...])
+    features = rounded(jnp.log(mean) * 0.5)
+    own3 = delta.reshape(64, 256)
     bias3 = own3.astype(F32).sum(axis=0, keepdims=True)
-    bias3 = bias3[:, :128] + bias3[:, 128:]
+    shift3[...] = bias3[:, :128] + bias3[:, 128:]
     low, high = [], []
     for tap in range(9):
         dy, dz = tap // 3, tap % 3
-        block = patches2[dy + 2 : dy + 4, dz + 2 : dz + 4].reshape(64, 256)
+        block = patches2[dy : dy + 2, dz : dz + 2].reshape(64, 256)
         full = dot_tn(own3, block)
         one = full[:128]
         low_lanes, high_lanes = roll(full[128:, :128], 64, 1), roll(full[128:, 128:], 64, 1)
@@ -366,6 +378,76 @@
         other = roll(high[2 * m + 1], 64, 1) if 2 * m + 1 < 9 else jnp.zeros((128, 128), F32)
         paired.append(jnp.where(first_half, high[2 * m], other))
     kernel3 = [piece.reshape(groups, wide, 128) for piece in low + paired]
+
+    turned[...] = jnp.concatenate([features, jnp.zeros((112, 128), F32)], axis=0).T
+    feature_rows = turned[pl.ds(0, 16, stride=8), :]
+    for c in range(1, 8):
+        feature_rows = feature_rows + roll(turned[pl.ds(c, 16, stride=8), :], 16 * c, 1)
+    feature_rows = feature_rows.reshape(groups, wide // 8, 128)
+    fill = jnp.zeros((groups, packed.shape[1] - 14 * wide - wide // 8, 128), F32)
+    packed[...] = jnp.concatenate(kernel3 + [feature_rows, fill], axis=1).astype(BF16)
+
+
+def run_own(groups, *operands):
+    wide = 128 // groups
+    return pl.pallas_call(
+        own_kernel,
+        name="own",
+        out_shape=(
+            jax.ShapeDtypeStruct((groups, -(-(14 * wide + wide // 8) // 8) * 8, 128), BF16),
+            jax.ShapeDtypeStruct((1, 128), F32),
+        ),
+        in_specs=[VMEM] * len(operands),
+        out_specs=(VMEM,) * 2,
+        scratch_shapes=[
+            pltpu.VMEM((4, 4, 16, 256), BF16),
+            pltpu.VMEM((64, 256), F32),
+            pltpu.VMEM((128, 128), F32),
+        ],
+        compiler_params=pltpu.CompilerParams(vmem_limit_bytes=LIMIT),
+        cost_estimate=pl.CostEstimate(flops=150000000, bytes_accessed=4000000, transcendentals=20000),
+    )(*operands)
+
+
+def backward_kernel(
+    before, lower, middle, upper, after, own_cot, w3, biases, w2, ratio2, patches1, ratio1, fields, packed3, shift3,
+    packed, patches2, pre3, delta3, patch2, grad2, delta2, patch1, grad1, delta1,
+):
+    groups = packed.shape[0]
+    half = lane((16, 128)) < 64
+
+    def lay(y, source):
+        for z in range(8):
+            lay_patches2(source(z), patches2.at[y, z])
+
+    for y in range(2):
+        lay(y, lambda z: before[(y * 8 + z) * 16 : (y * 8 + z + 1) * 16])
+        lay(y + 6, lambda z: after[(y * 8 + z) * 16 : (y * 8 + z + 1) * 16])
+
+    def pick_middle(y, z):
+        if z < 2:
+            return lower[(y * 2 + z) * 16 : (y * 2 + z + 1) * 16]
+        if z < 6:
+            return middle[y, z - 2]
+        return upper[(y * 2 + z - 6) * 16 : (y * 2 + z - 5) * 16]
+
+    for y in range(4):
+        lay(y + 2, functools.partial(pick_middle, y))
+
+    for tap in range(9):
+        dy, dz = tap // 3, tap % 3
+        block = patches2[dy : dy + 6, dz : dz + 6].reshape(576, 256)
+        term = dot(block, w3[tap]).reshape(6, 6, 16, 256)
+        pre3[...] = term + biases[2:3] if tap == 0 else pre3[...] + term
+
+    for wy in range(3):
+        for wz in range(3):
+            pre = pre3[2 * wy : 2 * wy + 2, 2 * wz : 2 * wz + 2]
+            if wy == 1:
+                cot = own_cot[...] if wz == 1 else (lower if wz == 0 else upper)[128:144]
+            else:
+                cot = (before if wy == 0 else after)[256 + wz * 16 : 272 + wz * 16]
+            delta3[2 * wy : 2 * wy + 2, 2 * wz : 2 * wz + 2] = pool3(pre, cot)[1]
 
     for tap in range(9):
         dy, dz = tap // 3, tap % 3
@@ -442,7 +524,7 @@
     bias1 = bias1 + roll(bias1, 32, 1)
     full = None
     for yw in range(4):
-        term = dot(fields[2 * yw : 2 * yw + 4].reshape(256, 256), delta1[yw])
+        term = dot(fields[yw : yw + 2].reshape(256, 256), delta1[yw])
         full = term if full is None else full + term
     full = full.reshape(4, 4, 16, 256)
     kernel1 = []
@@ -461,35 +543,23 @@
         jnp.where(low_lane, taps[2 * m], roll(taps[2 * m + 1], 64, 1) if 2 * m + 1 < 27 else 0.0)
         for m in range(14)
     ]
-    biases = jnp.concatenate(
-        [bias3, jnp.where(lane((1, 128)) < 64, bias2, bias1), jnp.zeros((14, 128), F32)], axis=0
+    shifts = jnp.concatenate(
+        [shift3[...], jnp.where(lane((1, 128)) < 64, bias2, bias1), jnp.zeros((14, 128), F32)], axis=0
     )
-    shared = jnp.concatenate(kernel2 + kernel1 + [biases], axis=0).reshape(groups, 512 // groups, 128)
-
-    turned[...] = jnp.concatenate([features, jnp.zeros((112, 128), F32)], axis=0).T
-    feature_rows = turned[pl.ds(0, 16, stride=8), :]
-    for c in range(1, 8):
-        feature_rows = feature_rows + roll(turned[pl.ds(c, 16, stride=8), :], 16 * c, 1)
-    feature_rows = feature_rows.reshape(groups, wide // 8, 128)
-
-    fill = jnp.zeros((groups, packed.shape[1] - 512 // groups - 14 * wide - wide // 8, 128), F32)
-    packed[...] = jnp.concatenate([shared] + kernel3 + [feature_rows, fill], axis=1).astype(BF16)
-
-
-def packed_rows(groups):
-    wide = 128 // groups
-    return -(-(512 // groups + 14 * wide + wide // 8) // 8) * 8
+    shared = jnp.concatenate(kernel2 + kernel1 + [shifts], axis=0)
+    rows = 512 // groups
+    packed[:, :rows] = shared.reshape(groups, rows, 128).astype(BF16)
+    packed[:, rows:] = packed3[...]
 
 
 def run_backward(groups, *operands):
     return pl.pallas_call(
         backward_kernel,
         name="backward",
-        out_shape=jax.ShapeDtypeStruct((groups, packed_rows(groups), 128), BF16),
+        out_shape=jax.ShapeDtypeStruct((groups, 512 // groups + operands[-2].shape[1], 128), BF16),
         in_specs=[VMEM] * len(operands),
         out_specs=VMEM,
         scratch_shapes=[
-            pltpu.VMEM((9, 256, 256), BF16),
             pltpu.VMEM((8, 8, 16, 256), BF16),
             pltpu.VMEM((6, 6, 16, 256), F32),
             pltpu.VMEM((6, 6, 16, 256), BF16),
@@ -499,7 +569,6 @@
             pltpu.VMEM((4, 4, 32, 512), F32),
             pltpu.VMEM((4, 64, 128), F32),
             pltpu.VMEM((4, 256, 256), BF16),
-            pltpu.VMEM((128, 128), F32),
         ],
         compiler_params=pltpu.CompilerParams(vmem_limit_bytes=LIMIT),
     )(*operands)
@@ -606,17 +675,6 @@
     )(shared)
 
 
-def pick_matrix():
-    out = np.zeros((2, 128, 4, 2, 64), np.float32)
-    for px in range(4):
-        for w in range(64):
-            x = 2 * w - 1 + px
-            if 0 <= x < 128:
-                for h in range(2):
-                    out[h, x, px, h, w] = 1
-    return out.reshape(256, 512).astype(jnp.bfloat16)
-
-
 def both_ways(to_next, to_previous, axis):
     devices = lax.axis_size(axis)
     forth = [(i, i + 1) for i in range(devices - 1)]
@@ -629,23 +687,25 @@
     wide = 128 // size_z
 
     tile = universe.transpose(1, 2, 0, 3).reshape(8, 32, 128)
+    cot = lax.all_to_all(cotangent[:, 0].transpose(1, 0, 2), "gz", 0, 0, tiled=True).reshape(128, 16)
+    tile, cot = lax.optimization_barrier((tile, cot))
     lower, upper = both_ways(tile, tile, "gz")
     strip = jnp.concatenate([lower[:, 4:], tile, upper[:, :28], jnp.zeros((8, 8, 128), BF16)], axis=1)
     top, bottom = both_ways(strip, strip, "gy")
 
-    cot = lax.all_to_all(cotangent[:, 0].transpose(1, 0, 2), "gz", 0, 0, tiled=True).reshape(128, 16)
-    k1 = kernel1.transpose(0, 2, 1)
-    k2, k3 = kernel2.transpose(0, 2, 1), kernel3.transpose(0, 2, 1)
-
-    to_next, to_previous, hidden2, own_cot, ratio2, patches1, ratio1, fields, w2 = run_forward(
-        top, strip, bottom, cot, jnp.asarray(pick_matrix()), k1, bias1[None], k2, bias2[None]
+    k1, k2, k3 = kernel1.transpose(0, 2, 1), kernel2.transpose(0, 2, 1), kernel3.transpose(0, 2, 1)
+    w1, w2, w3, biases, pick = run_weights(k1, bias1[None], k2, bias2[None], k3, bias3[None])
+    to_next, to_previous, hidden2, own_cot, ratio2, patches1, ratio1, fields = run_forward(
+        top, strip, bottom, cot, w1, w2, biases, pick
     )
     lower, upper = both_ways(to_next, to_previous, "gz")
+    packed3, shift3 = run_own(size_z, hidden2, own_cot, w3, biases)
     row_next, row_previous = run_weave(lower, hidden2, upper, own_cot)
     before, after = both_ways(row_next, row_previous, "gy")
     packed = run_backward(
         size_z,
-        k3, bias3[None], lower, hidden2, upper, own_cot, before, after, ratio2, w2, patches1, ratio1, fields,
+        before, lower, hidden2, upper, after, own_cot, w3, biases, w2, ratio2, patches1, ratio1, fields,
+        packed3, shift3,
     )
     packed = lax.all_to_all(packed, "gz", 0, 0, tiled=True)
     column, features = run_sum(packed, size_y)

time: 118 us -> 126 us (1.068)
  blocking collectives: 46.7 us -> 37.8 us
  waiting for transfers between devices: 20.7 us -> 26 us
  local copies, waits for them, and re-layouts: 2.31 us -> 7.03 us
  starting transfers between devices: 28.2 us -> 32.9 us
  Pallas kernels: 18.9 us -> 20.4 us
    all_to_all x1 -> x0, blocking collectives: 13.3 us -> none  [shards(): lax.all_to_all(cotangent[:, 0].transpose(1, 0, 2), 'gz', 0, 0, tiled=True)]
    all_to_all x0 -> x1, starting transfers between devices: none -> 8.45 us  [shards(): lax.all_to_all(cotangent[:, 0].transpose(1, 0, 2), 'gz', 0, 0, tiled=True)]
    all_to_all x0 -> x1, waiting for transfers between devices: none -> 6.41 us  [shards(): lax.all_to_all(cotangent[:, 0].transpose(1, 0, 2), 'gz', 0, 0, tiled=True)]
    unnamed x17 -> x13, local copies, waits for them, and re-layouts: 1.32 us -> 6.03 us
    ppermute x4, starting transfers between devices: 16.3 us -> 12.5 us  [both_ways(): lax.ppermute(to_next, axis, forth)]
    all_to_all x1, blocking collectives: 13.9 us -> 17.6 us  [shards(): column = lax.all_to_all(column, 'gy', 0, 0, tiled=True)]
    pallas_call x0 -> x2, Pallas kernels: none -> 1.72 us  [the longest x1 1.3 us: run_own(): pl.pallas_call(own_kernel, name='own', out_shape=(jax.ShapeDtypeStruct((g...]
  transfers between devices with their start and end apart: 9 -> 10, of which waited for: 5 -> 5; matrix products, arithmetic and copies ran while one was open for 0% -> 1% of each run, Pallas kernels for 1% -> 2%
where the time goes in v6:
time: 126 us; the launch traced here: 125 us
  blocking collectives  37.8 us (30%)
  starting transfers between devices  32.9 us (26%)
  waiting for transfers between devices  26 us (21%)
  Pallas kernels  20.4 us (16%)
  local copies, waits for them, and re-layouts  7.03 us (6%)
    all_to_all x1, blocking collectives, shards(): packed = lax.all_to_all(packed, 'gz', 0, 0, tiled=True)  20.2 us
    all_to_all x1, blocking collectives, shards(): column = lax.all_to_all(column, 'gy', 0, 0, tiled=True)  17.6 us
    ppermute x4, waiting for transfers between devices, both_ways(): lax.ppermute(to_previous, axis, back)  12.6 us
    ppermute x4, starting transfers between devices, both_ways(): lax.ppermute(to_next, axis, forth)  12.5 us
    pallas_call x1, Pallas kernels, run_forward(): pl.pallas_call(forward_kernel, name='forward', out_shape=(jax.ShapeDtypeS...  10.3 us
    all_to_all x1, starting transfers between devices, shards(): lax.all_to_all(cotangent[:, 0].transpose(1, 0, 2), 'gz', 0, 0, tiled=True)  8.45 us
    all_to_all x1, waiting for transfers between devices, shards(): shared = lax.all_to_all(run_share(column, size_z), 'gz', 0, 0, tiled=True)  6.99 us
    ppermute x4, starting transfers between devices, both_ways(): lax.ppermute(to_previous, axis, back)  6.6 us
  transfers between devices with their start and end apart: 10, of which 5 were waited for; matrix products, arithmetic and copies ran while one was open for 1% of the time, Pallas kernels for 2%

profile of v6, /device:TPU:1, one launch (start us, length us, event | category | flops | bytes accessed | tf_op | source)
XLA Modules:
  0.0 125.0 jit_solution(5635176982714249744)
XLA Ops:
  0.6 1.4 %copy.22 = bf16[8,1,16,16]{3,0,2,1:T(8,128)(2,1)} copy(bf16[8,1,16,16]{3,2,1,0:T(8,128)(2,1)} %param.15) | data formatting | bytes 8192 | tf_op args[7]
  2.0 8.4 %all-to-all-start = ((bf16[16,8,16]{2,1,0:T(8,128)(2,1)}), bf16[16,8,16]{2,1,0:T(8,128)(2,1)S(1)}, u32[]{:S(2)}, u32[]{:S(2)}) async-start(bf16[16,8,16]{2,1,0:T(8,128)(2,1)} %bitcast.21), calls=%async_computation | async-start | bytes 65536 | tf_op jit(solution)/shard_map/all_to_all | solution.py:690
  10.5 0.9 copy.18
  11.4 6.4 %all-to-all-done = bf16[16,8,16]{2,1,0:T(8,128)(2,1)S(1)} async-done(((bf16[16,8,16]{2,1,0:T(8,128)(2,1)}), bf16[16,8,16]{2,1,0:T(8,128)(2,1)S(1)}, u32[]{:S(2)}, u32[]{:S(2)}) %all-to-all-start) | async-done | bytes 4128 | tf_op jit(solution)/shard_map/all_to_all | solution.py:690
  17.8 2.5 %collective-permute-start = (bf16[8,32,128]{2,1,0:T(8,128)(2,1)S(1)}, bf16[8,32,128]{2,1,0:T(8,128)(2,1)S(1)}, u32[]{:S(2)}, u32[]{:S(2)}) collective-permute-start(bf16[8,32,128]{2,1,0:T(8,128)(2,1)S(1)} %bitcast.30), channel_id=1, source_target_pairs={{0,1},{1,2},{2,3},{3,4},{4,5},{5,6},{6,7},{7,8},{8,9},{9,10},{10,1... | collective-permute-start | bytes 196616 | tf_op jit(solution)/shard_map/ppermute | solution.py:682
  20.3 1.9 %collective-permute-start.1 = (bf16[8,32,128]{2,1,0:T(8,128)(2,1)S(1)}, bf16[8,32,128]{2,1,0:T(8,128)(2,1)S(1)}, u32[]{:S(2)}, u32[]{:S(2)}) collective-permute-start(bf16[8,32,128]{2,1,0:T(8,128)(2,1)S(1)} %bitcast.31), channel_id=1, source_target_pairs={{1,0},{2,1},{3,2},{4,3},{5,4},{6,5},{7,6},{8,7},{9,8},{10,9},{11,1... | collective-permute-start | bytes 196616 | tf_op jit(solution)/shard_map/ppermute | solution.py:682
  22.3 5.0 %collective-permute-done.1 = bf16[8,32,128]{2,1,0:T(8,128)(2,1)S(1)} collective-permute-done((bf16[8,32,128]{2,1,0:T(8,128)(2,1)S(1)}, bf16[8,32,128]{2,1,0:T(8,128)(2,1)S(1)}, u32[]{:S(2)}, u32[]{:S(2)}) %collective-permute-start.1) | collective-permute-done | bytes 65568 | tf_op jit(solution)/shard_map/ppermute | solution.py:682
  27.5 1.3 %collective-permute-start.3 = (bf16[8,96,128]{2,1,0:T(8,128)(2,1)S(1)}, bf16[8,96,128]{2,1,0:T(8,128)(2,1)S(1)}, u32[]{:S(2)}, u32[]{:S(2)}) collective-permute-start(bf16[8,96,128]{2,1,0:T(8,128)(2,1)S(1)} %maximum_maximum_fusion.mid), channel_id=1, source_target_pairs={{16,0},{32,16},{48,32},{64,48},{80,64},{96,80},{112,96},{17,1},{33... | collective-permute-start | bytes 589832 | tf_op jit(solution)/shard_map/ppermute | solution.py:682
  28.8 4.2 %collective-permute-start.2 = (bf16[8,96,128]{2,1,0:T(8,128)(2,1)S(1)}, bf16[8,96,128]{2,1,0:T(8,128)(2,1)S(1)}, u32[]{:S(2)}, u32[]{:S(2)}) collective-permute-start(bf16[8,96,128]{2,1,0:T(8,128)(2,1)S(1)} %maximum_maximum_fusion.mid), channel_id=1, source_target_pairs={{0,16},{16,32},{32,48},{48,64},{64,80},{80,96},{96,112},{1,17},{17... | collective-permute-start | bytes 589832 | tf_op jit(solution)/shard_map/ppermute | solution.py:682
  33.0 1.0 copy-done
  34.0 0.9 copy-done.1
  34.9 0.7 copy-done.2
  35.7 0.7 copy-done.3
  36.3 0.7 copy-done.4
  37.0 0.7 copy-done.5
  38.1 10.3 %forward.1 = (bf16[144,128]{1,0:T(8,128)(2,1)S(1)}, bf16[144,128]{1,0:T(8,128)(2,1)S(1)}, bf16[4,4,16,128]{3,2,1,0:T(8,128)(2,1)S(1)}, bf16[16,128]{1,0:T(8,128)...) custom-call(bf16[8,96,128]{2,1,0:T(8,128)(2,1)S(1)} %collective-perm, ...), custom_call_target="tpu_custom_call" | custom-call | tf_op jit(solution)/shard_map/forward/pallas_call | solution.py:279
  48.4 2.2 %collective-permute-start.4 = (bf16[144,128]{1,0:T(8,128)(2,1)S(1)}, bf16[144,128]{1,0:T(8,128)(2,1)S(1)}, u32[]{:S(2)}, u32[]{:S(2)}) collective-permute-start(bf16[144,128]{1,0:T(8,128)(2,1)S(1)} %get-tuple-element.39), channel_id=1, source_target_pairs={{0,1},{1,2},{2,3},{3,4},{4,5},{5,6},{6,7},{7,8},{8,9},{9,10},{10,1... | collective-permute-start | bytes 110600 | tf_op jit(solution)/shard_map/ppermute | solution.py:682
  50.6 2.1 %collective-permute-start.5 = (bf16[144,128]{1,0:T(8,128)(2,1)S(1)}, bf16[144,128]{1,0:T(8,128)(2,1)S(1)}, u32[]{:S(2)}, u32[]{:S(2)}) collective-permute-start(bf16[144,128]{1,0:T(8,128)(2,1)S(1)} %get-tuple-element.41), channel_id=1, source_target_pairs={{1,0},{2,1},{3,2},{4,3},{5,4},{6,5},{7,6},{8,7},{9,8},{10,9},{11,1... | collective-permute-start | bytes 110600 | tf_op jit(solution)/shard_map/ppermute | solution.py:682
  52.7 5.0 %collective-permute-done.5.upper = bf16[144,128]{1,0:T(8,128)(2,1)S(1)} collective-permute-done((bf16[144,128]{1,0:T(8,128)(2,1)S(1)}, bf16[144,128]{1,0:T(8,128)(2,1)S(1)}, u32[]{:S(2)}, u32[]{:S(2)}) %collective-permute-start.5) | collective-permute-done | bytes 36896 | tf_op jit(solution)/shard_map/ppermute | solution.py:682
  57.8 3.5 %collective-permute-start.6 = (bf16[304,128]{1,0:T(8,128)(2,1)S(1)}, bf16[304,128]{1,0:T(8,128)(2,1)S(1)}, u32[]{:S(2)}, u32[]{:S(2)}) collective-permute-start(bf16[304,128]{1,0:T(8,128)(2,1)S(1)} %get-tuple-element.43), channel_id=1, source_target_pairs={{0,16},{16,32},{32,48},{48,64},{64,80},{80,96},{96,112},{1,17},{17... | collective-permute-start | bytes 233480 | tf_op jit(solution)/shard_map/ppermute | solution.py:682
  61.3 1.3 %collective-permute-start.7 = (bf16[304,128]{1,0:T(8,128)(2,1)S(1)}, bf16[304,128]{1,0:T(8,128)(2,1)S(1)}, u32[]{:S(2)}, u32[]{:S(2)}) collective-permute-start(bf16[304,128]{1,0:T(8,128)(2,1)S(1)} %get-tuple-element.44), channel_id=1, source_target_pairs={{16,0},{32,16},{48,32},{64,48},{80,64},{96,80},{112,96},{17,1},{33... | collective-permute-start | bytes 233480 | tf_op jit(solution)/shard_map/ppermute | solution.py:682
  62.6 1.3 %own.1 = (bf16[16,120,128]{2,1,0:T(8,128)(2,1)S(1)}, f32[1,128]{1,0:T(1,128)S(1)}) custom-call(bf16[4,4,16,128]{3,2,1,0:T(8,128)(2,1)S(1)} %get-tuple-element.40.hidden2.middle, bf16[16,128]{1,0:T(8,128)(2,1)S(1)} %get-tuple-element.42.own_cot, bf16[9,256,256]{2,1,0:T(8,128)(2,1)S(1)} %get-tuple-element.45.w3, f32[8,256]{1,0:T(8,128)S(1)} %get-tuple-element.37.biases), custom_call_target="tpu_custom_call" | custom-call | flops 150000000 | bytes 4000000 | tf_op jit(solution)/shard_map/own/pallas_call | solution.py:393
  63.9 2.5 %collective-permute-done.7.after = bf16[304,128]{1,0:T(8,128)(2,1)S(1)} collective-permute-done((bf16[304,128]{1,0:T(8,128)(2,1)S(1)}, bf16[304,128]{1,0:T(8,128)(2,1)S(1)}, u32[]{:S(2)}, u32[]{:S(2)}) %collective-permute-start.7) | collective-permute-done | bytes 77856 | tf_op jit(solution)/shard_map/ppermute | solution.py:682
  66.5 5.4 %backward.1 = bf16[16,152,128]{2,1,0:T(8,128)(2,1)S(1)} custom-call(bf16[304,128]{1,0:T(8,128)(2,1)S(1)} %collective-permute-done.6.before, bf16[144,128]{1,0:T(8,128)(2,1)S(1)} %collective-permute-done.4.lower, bf16[4,4,16,128]{3,2,1,0:T(8,128)(2,1)S(1)} %get-tuple-element.40.hidden2.middle, bf16[144,128]{1,0:T(8,128)(2,1)S(1)} %collective-permute-done.5.upper, ...), custom_call_target="tpu_custom_call" | custom-call | tf_op jit(solution)/shard_map/backward/pallas_call | solution.py:556
  71.9 20.2 %all_to_all.20.received = bf16[16,152,128]{2,1,0:T(8,128)(2,1)S(1)} all-to-all(bf16[16,152,128]{2,1,0:T(8,128)(2,1)S(1)} %backward.1), channel_id=1, replica_groups=mesh['gy'=8,'gz'=16] {'gz'}, dimensions={0} | all-to-all | bytes 1245184 | tf_op jit(solution)/shard_map/all_to_all | solution.py:710
  92.1 0.7 sum.1
  92.8 17.6 %all_to_all.21.column = bf16[8,144,128]{2,1,0:T(8,128)(2,1)S(1)} all-to-all(bf16[8,144,128]{2,1,0:T(8,128)(2,1)S(1)} %get-tuple-element.53), channel_id=1, replica_groups=mesh['gy'=8,'gz'=16] {'gy'}, dimensions={0} | all-to-all | bytes 589824 | tf_op jit(solution)/shard_map/all_to_all | solution.py:712
  110.4 0.7 share.1
  111.0 5.4 %all-to-all-start.3 = ((bf16[16,32,128]{2,1,0:T(8,128)(2,1)}), bf16[16,32,128]{2,1,0:T(8,128)(2,1)S(1)}, u32[]{:S(2)}, u32[]{:S(2)}) async-start(bf16[16,32,128]{2,1,0:T(8,128)(2,1)} %share.1), calls=%async_computation.3 | async-start | bytes 262144 | tf_op jit(solution)/shard_map/all_to_all | solution.py:713
  116.4 0.7 third.1
  117.2 7.0 %all-to-all-done.3.shared = bf16[16,32,128]{2,1,0:T(8,128)(2,1)S(1)} async-done(((bf16[16,32,128]{2,1,0:T(8,128)(2,1)}), bf16[16,32,128]{2,1,0:T(8,128)(2,1)S(1)}, u32[]{:S(2)}, u32[]{:S(2)}) %all-to-all-start.3) | async-done | bytes 131104 | tf_op jit(solution)/shard_map/all_to_all | solution.py:713
  124.1 0.9 unpack.1
  (17 shorter events, 0.7 us)
Async XLA Ops:
  2.0 15.8 %all-to-all-start = ((bf16[16,8,16]{2,1,0:T(8,128)(2,1)}), bf16[16,8,16]{2,1,0:T(8,128)(2,1)S(1)}, u32[]{:S(2)}, u32[]{:S(2)}) async-start(bf16[16,8,16]{2,1,0:T(8,128)(2,1)} %bitcast.21), calls=%async_computation | async-start | bytes 65536 | tf_op jit(solution)/shard_map/all_to_all | solution.py:690
  17.8 4.6 %collective-permute-start = (bf16[8,32,128]{2,1,0:T(8,128)(2,1)S(1)}, bf16[8,32,128]{2,1,0:T(8,128)(2,1)S(1)}, u32[]{:S(2)}, u32[]{:S(2)}) collective-permute-start(bf16[8,32,128]{2,1,0:T(8,128)(2,1)S(1)} %bitcast.30), channel_id=1, source_target_pairs={{0,1},{1,2},{2,3},{3,4},{4,5},{5,6},{6,7},{7,8},{8,9},{9,10},{10,1... | collective-permute-start | bytes 196616 | tf_op jit(solution)/shard_map/ppermute | solution.py:682
  20.3 7.1 %collective-permute-start.1 = (bf16[8,32,128]{2,1,0:T(8,128)(2,1)S(1)}, bf16[8,32,128]{2,1,0:T(8,128)(2,1)S(1)}, u32[]{:S(2)}, u32[]{:S(2)}) collective-permute-start(bf16[8,32,128]{2,1,0:T(8,128)(2,1)S(1)} %bitcast.31), channel_id=1, source_target_pairs={{1,0},{2,1},{3,2},{4,3},{5,4},{6,5},{7,6},{8,7},{9,8},{10,9},{11,1... | collective-permute-start | bytes 196616 | tf_op jit(solution)/shard_map/ppermute | solution.py:682
  27.5 10.6 %collective-permute-start.3 = (bf16[8,96,128]{2,1,0:T(8,128)(2,1)S(1)}, bf16[8,96,128]{2,1,0:T(8,128)(2,1)S(1)}, u32[]{:S(2)}, u32[]{:S(2)}) collective-permute-start(bf16[8,96,128]{2,1,0:T(8,128)(2,1)S(1)} %maximum_maximum_fusion.mid), channel_id=1, source_target_pairs={{16,0},{32,16},{48,32},{64,48},{80,64},{96,80},{112,96},{17,1},{33... | collective-permute-start | bytes 589832 | tf_op jit(solution)/shard_map/ppermute | solution.py:682
  28.8 9.3 %collective-permute-start.2 = (bf16[8,96,128]{2,1,0:T(8,128)(2,1)S(1)}, bf16[8,96,128]{2,1,0:T(8,128)(2,1)S(1)}, u32[]{:S(2)}, u32[]{:S(2)}) collective-permute-start(bf16[8,96,128]{2,1,0:T(8,128)(2,1)S(1)} %maximum_maximum_fusion.mid), channel_id=1, source_target_pairs={{0,16},{16,32},{32,48},{48,64},{64,80},{80,96},{96,112},{1,17},{17... | collective-permute-start | bytes 589832 | tf_op jit(solution)/shard_map/ppermute | solution.py:682
  33.0 1.0 copy-start
  34.0 0.9 copy-start.1
  34.9 0.7 copy-start.2
  35.7 0.7 copy-start.3
  36.3 0.7 copy-start.4
  37.0 0.7 copy-start.5
  48.4 4.4 %collective-permute-start.4 = (bf16[144,128]{1,0:T(8,128)(2,1)S(1)}, bf16[144,128]{1,0:T(8,128)(2,1)S(1)}, u32[]{:S(2)}, u32[]{:S(2)}) collective-permute-start(bf16[144,128]{1,0:T(8,128)(2,1)S(1)} %get-tuple-element.39), channel_id=1, source_target_pairs={{0,1},{1,2},{2,3},{3,4},{4,5},{5,6},{6,7},{7,8},{8,9},{9,10},{10,1... | collective-permute-start | bytes 110600 | tf_op jit(solution)/shard_map/ppermute | solution.py:682
  50.6 7.1 %collective-permute-start.5 = (bf16[144,128]{1,0:T(8,128)(2,1)S(1)}, bf16[144,128]{1,0:T(8,128)(2,1)S(1)}, u32[]{:S(2)}, u32[]{:S(2)}) collective-permute-start(bf16[144,128]{1,0:T(8,128)(2,1)S(1)} %get-tuple-element.41), channel_id=1, source_target_pairs={{1,0},{2,1},{3,2},{4,3},{5,4},{6,5},{7,6},{8,7},{9,8},{10,9},{11,1... | collective-permute-start | bytes 110600 | tf_op jit(solution)/shard_map/ppermute | solution.py:682
  57.8 6.1 %collective-permute-start.6 = (bf16[304,128]{1,0:T(8,128)(2,1)S(1)}, bf16[304,128]{1,0:T(8,128)(2,1)S(1)}, u32[]{:S(2)}, u32[]{:S(2)}) collective-permute-start(bf16[304,128]{1,0:T(8,128)(2,1)S(1)} %get-tuple-element.43), channel_id=1, source_target_pairs={{0,16},{16,32},{32,48},{48,64},{64,80},{80,96},{96,112},{1,17},{17... | collective-permute-start | bytes 233480 | tf_op jit(solution)/shard_map/ppermute | solution.py:682
  61.3 5.2 %collective-permute-start.7 = (bf16[304,128]{1,0:T(8,128)(2,1)S(1)}, bf16[304,128]{1,0:T(8,128)(2,1)S(1)}, u32[]{:S(2)}, u32[]{:S(2)}) collective-permute-start(bf16[304,128]{1,0:T(8,128)(2,1)S(1)} %get-tuple-element.44), channel_id=1, source_target_pairs={{16,0},{32,16},{48,32},{64,48},{80,64},{96,80},{112,96},{17,1},{33... | collective-permute-start | bytes 233480 | tf_op jit(solution)/shard_map/ppermute | solution.py:682
  111.0 13.1 %all-to-all-start.3 = ((bf16[16,32,128]{2,1,0:T(8,128)(2,1)}), bf16[16,32,128]{2,1,0:T(8,128)(2,1)S(1)}, u32[]{:S(2)}, u32[]{:S(2)}) async-start(bf16[16,32,128]{2,1,0:T(8,128)(2,1)} %share.1), calls=%async_computation.3 | async-start | bytes 262144 | tf_op jit(solution)/shard_map/all_to_all | solution.py:713

commit v7 on v6

--- a/solution.py
+++ b/solution.py
@@ -57,16 +57,7 @@
     return jnp.where(rows == count - 1, 0.0, roll(value, count - 1, 0))
 
 
-def weights_kernel(k1, b1, k2, b2, k3, b3, w1, w2, w3, biases, pick):
-    lay_weights1(k1, w1)
-    lay_weights2(k2, w2)
-    lay_weights3(k3, w3)
-    rows = [
-        jnp.concatenate([b1[...]] * 8, axis=1),
-        jnp.concatenate([b2[...]] * 4, axis=1),
-        jnp.concatenate([b3[...]] * 2, axis=1),
-    ]
-    biases[...] = jnp.concatenate(rows + [jnp.zeros((5, 256), F32)], axis=0)
+def lay_pick(pick):
     for px in range(4):
         row = lax.broadcasted_iota(jnp.int32, (256, 128), 0)
         col = lax.broadcasted_iota(jnp.int32, (256, 128), 1)
@@ -75,29 +66,16 @@
         pick[:, px * 128 : px * 128 + 128] = jnp.where(same & hit, 1.0, 0.0).astype(BF16)
 
 
-def run_weights(*operands):
-    return pl.pallas_call(
-        weights_kernel,
-        name="weights",
-        out_shape=(
-            jax.ShapeDtypeStruct((256, 256), BF16),
-            jax.ShapeDtypeStruct((3, 512, 256), BF16),
-            jax.ShapeDtypeStruct((9, 256, 256), BF16),
-            jax.ShapeDtypeStruct((8, 256), F32),
-            jax.ShapeDtypeStruct((256, 512), BF16),
-        ),
-        in_specs=[VMEM] * 6,
-        out_specs=(VMEM,) * 5,
-        compiler_params=pltpu.CompilerParams(vmem_limit_bytes=LIMIT),
-    )(*operands)
-
-
 def forward_kernel(
-    top, mid, bot, cot, w1, w2, biases, pick,
-    to_next, to_previous, hidden2, own_cot, ratio2, patches1, ratio1, fields,
-    left, field, turned, first, spread, pre2, second,
+    top, mid, bot, cot, k1, b1, k2, b2,
+    to_next, to_previous, hidden2, own_cot, ratio2, patches1, ratio1, fields, w2,
+    w1, pick, left, field, turned, pre1, first, spread, pre2, second,
 ):
-    bias1, bias2 = biases[0:1], biases[1:2]
+    lay_weights1(k1, w1)
+    lay_weights2(k2, w2)
+    lay_pick(pick)
+    bias1 = jnp.concatenate([b1[...]] * 8, axis=1)
+    bias2 = jnp.concatenate([b2[...]] * 4, axis=1)
     base_y, base_z = lax.axis_index("gy"), lax.axis_index("gz")
     size_y, size_z = lax.axis_size("gy"), lax.axis_size("gz")
 
@@ -152,24 +130,23 @@
 
     def block1(yw, carry):
         stack = jnp.concatenate([turned[yw], turned[yw + 1]], axis=1)
-        pre = dot(stack, w1[...]) + bias1
-        e = exps(pre)
-        total = e[:, :128] + e[:, 128:]
-        total = total + roll(total, 64, 1)
-        total = total + roll(total, 32, 1)
-        mean = total * 0.125
-        pooled = rounded(jnp.log(mean) * 0.5)
+        pre1[...] = dot(stack, w1[...])
+        place = jnp.where((yw >= 3) & (yw < 7), yw - 3, 4)
         for k, pair in enumerate(PAIRS):
             for h, zw in enumerate(pair):
                 at = k * 128 + h * 64
-                first[yw, zw + 3, 8:72] = pooled[at : at + 64] * inside(yw - 3, zw, 1)
-
-        @pl.when((yw >= 3) & (yw < 7))
-        def _():
-            share = 0.125 / mean[:256]
-            share = jnp.concatenate([share, share], axis=1)
-            ratio1[yw - 3] = jnp.where(pre[:256] > 0, 1.0, SLOPE) * (e[:256] * share)
-
+                pre = pre1[at : at + 64] + bias1
+                e = exps(pre)
+                total = e[:, :128] + e[:, 128:]
+                total = total + roll(total, 64, 1)
+                total = total + roll(total, 32, 1)
+                mean = total * 0.125
+                pooled = rounded(jnp.log(mean) * 0.5)
+                first[yw, zw + 3, 8:72] = pooled * inside(yw - 3, zw, 1)
+                if k < 2:
+                    share = 0.125 / mean
+                    share = jnp.concatenate([share, share], axis=1)
+                    ratio1[place, at : at + 64] = jnp.where(pre > 0, 1.0, SLOPE) * (e * share)
         return carry
 
     lax.fori_loop(0, 10, block1, 0)
@@ -187,34 +164,27 @@
     lax.fori_loop(0, 10, frame, 0)
     patches1[...] = spread[2:8, 2:8]
 
-    for dy in range(3):
-        block = jnp.concatenate(
-            [
-                jnp.concatenate([spread[dy : dy + 8, 2 * zo + pz] for pz in range(4)], axis=2)[:, None]
-                for zo in range(4)
-            ],
-            axis=1,
-        ).reshape(1024, 512)
-        term = dot(block, w2[dy]).reshape(8, 4, 32, 256)
-        pre2[...] = term + bias2 if dy == 0 else pre2[...] + term
-
     half = lane((16, 128)) < 64
 
     def block2(yp, carry):
-        pre = pre2[pl.ds(2 * yp, 2)]
-        e = exps(pre)
-        both = e[0] + e[1]
-        total = (both[:, :, :128] + both[:, :, 128:]).reshape(128, 128)
-        total = total + roll(total, 64, 1)
-        mean = total * 0.125
-        pooled = rounded(jnp.log(mean) * 0.5).reshape(4, 32, 128)
-        share = (0.125 / mean).reshape(4, 32, 128)
-        share = jnp.concatenate([share, share], axis=2)
-        scaled = jnp.where(pre > 0, 1.0, SLOPE) * (e * share[None])
+        columns = []
         for zo in range(4):
+            tiles = [spread[pl.ds(2 * yp + dy, 2), 2 * zo + pz] for dy in range(3) for pz in range(4)]
+            columns.append(jnp.concatenate(tiles, axis=2)[:, None])
+        block = jnp.concatenate(columns, axis=1).reshape(256, 1536)
+        pre2[...] = dot(block, w2[...].reshape(1536, 256)).reshape(2, 4, 32, 256)
+        for zo in range(4):
+            pre = pre2[:, zo] + bias2
+            e = exps(pre)
+            both = e[0] + e[1]
+            total = both[:, :128] + both[:, 128:]
+            total = total + roll(total, 64, 1)
+            mean = total * 0.125
             ok = inside(yp - 1, zo - 1, 2)
-            ratio2[pl.ds(2 * yp, 2), zo] = scaled[:, zo] * ok
-            second[zo] = pooled[zo] * ok
+            share = (0.125 * ok) / mean
+            share = jnp.concatenate([share, share], axis=1)
+            ratio2[pl.ds(2 * yp, 2), zo] = jnp.where(pre > 0, 1.0, SLOPE) * (e * share[None])
+            second[zo] = rounded(jnp.log(mean) * 0.5) * ok
             even = second[zo, pl.ds(0, 16, stride=2), :]
             odd = second[zo, pl.ds(1, 16, stride=2), :]
             hidden2[yp, zo] = jnp.where(half, even, odd).astype(BF16)
@@ -286,18 +256,22 @@
             jax.ShapeDtypeStruct((16, 128), BF16),
             jax.ShapeDtypeStruct((8, 4, 32, 256), F32),
             jax.ShapeDtypeStruct((6, 6, 32, 128), BF16),
-            jax.ShapeDtypeStruct((4, 256, 256), F32),
+            jax.ShapeDtypeStruct((5, 256, 256), F32),
             jax.ShapeDtypeStruct((5, 128, 256), BF16),
+            jax.ShapeDtypeStruct((3, 512, 256), BF16),
         ),
         in_specs=[VMEM] * len(operands),
-        out_specs=(VMEM,) * 8,
+        out_specs=(VMEM,) * 9,
         scratch_shapes=[
+            pltpu.VMEM((256, 256), BF16),
+            pltpu.VMEM((256, 512), BF16),
             pltpu.VMEM((22, 80, 256), BF16),
             pltpu.VMEM((11, 128, 640), BF16),
             pltpu.VMEM((11, 640, 128), BF16),
+            pltpu.VMEM((640, 256), F32),
             pltpu.VMEM((10, 10, 80, 128), F32),
             pltpu.VMEM((10, 10, 32, 128), BF16),
-            pltpu.VMEM((8, 4, 32, 256), F32),
+            pltpu.VMEM((2, 4, 32, 256), F32),
             pltpu.VMEM((4, 32, 128), F32),
         ],
         compiler_params=pltpu.CompilerParams(vmem_limit_bytes=LIMIT),
@@ -345,9 +319,11 @@
     return mean, (jnp.where(pre > 0, 1.0, SLOPE) * (e * share)).astype(BF16)
 
 
-def own_kernel(hidden2, own_cot, w3, biases, packed, shift3, patches2, pre3, turned):
+def own_kernel(hidden2, own_cot, k3, b3, packed, shift3, w3, wide3, patches2, pre3, turned):
     groups = packed.shape[0]
     wide = 128 // groups
+    lay_weights3(k3, w3)
+    wide3[...] = jnp.concatenate([b3[...]] * 2, axis=1)
     for y in range(4):
         for z in range(4):
             lay_patches2(hidden2[y, z], patches2.at[y, z])
@@ -355,7 +331,7 @@
         dy, dz = tap // 3, tap % 3
         block = patches2[dy : dy + 2, dz : dz + 2].reshape(64, 256)
         term = dot(block, w3[tap])
-        pre3[...] = term + biases[2:3] if tap == 0 else pre3[...] + term
+        pre3[...] = term + wide3[...] if tap == 0 else pre3[...] + term
     mean, delta = pool3(pre3[...].reshape(2, 2, 16, 256), own_cot[...])
     features = rounded(jnp.log(mean) * 0.5)
     own3 = delta.reshape(64, 256)
@@ -396,9 +372,11 @@
         out_shape=(
             jax.ShapeDtypeStruct((groups, -(-(14 * wide + wide // 8) // 8) * 8, 128), BF16),
             jax.ShapeDtypeStruct((1, 128), F32),
+            jax.ShapeDtypeStruct((9, 256, 256), BF16),
+            jax.ShapeDtypeStruct((1, 256), F32),
         ),
         in_specs=[VMEM] * len(operands),
-        out_specs=(VMEM,) * 2,
+        out_specs=(VMEM,) * 4,
         scratch_shapes=[
             pltpu.VMEM((4, 4, 16, 256), BF16),
             pltpu.VMEM((64, 256), F32),
@@ -410,8 +388,8 @@
 
 
 def backward_kernel(
-    before, lower, middle, upper, after, own_cot, w3, biases, w2, ratio2, patches1, ratio1, fields, packed3, shift3,
-    packed, patches2, pre3, delta3, patch2, grad2, delta2, patch1, grad1, delta1,
+    before, lower, middle, upper, after, own_cot, w3, bias3, w2, ratio2, patches1, ratio1, fields, packed3, shift3,
+    packed, patches2, pre3, delta3, patch2, grad2, delta2, patch1, beside, grad1, delta1,
 ):
     groups = packed.shape[0]
     half = lane((16, 128)) < 64
@@ -434,11 +412,11 @@
     for y in range(4):
         lay(y + 2, functools.partial(pick_middle, y))
 
-    for tap in range(9):
-        dy, dz = tap // 3, tap % 3
-        block = patches2[dy : dy + 6, dz : dz + 6].reshape(576, 256)
-        term = dot(block, w3[tap]).reshape(6, 6, 16, 256)
-        pre3[...] = term + biases[2:3] if tap == 0 else pre3[...] + term
+    for dy in range(3):
+        blocks = [patches2[dy : dy + 6, dz : dz + 6].reshape(576, 256) for dz in range(3)]
+        weights = w3[3 * dy : 3 * dy + 3].reshape(768, 256)
+        term = dot(jnp.concatenate(blocks, axis=1), weights).reshape(6, 6, 16, 256)
+        pre3[...] = term + bias3[...] if dy == 0 else pre3[...] + term
 
     for wy in range(3):
         for wz in range(3):
@@ -449,11 +427,11 @@
                 cot = (before if wy == 0 else after)[256 + wz * 16 : 272 + wz * 16]
             delta3[2 * wy : 2 * wy + 2, 2 * wz : 2 * wz + 2] = pool3(pre, cot)[1]
 
-    for tap in range(9):
-        dy, dz = tap // 3, tap % 3
-        block = delta3[2 - dy : 6 - dy, 2 - dz : 6 - dz].reshape(256, 256)
-        term = dot_nt(block, w3[tap]).reshape(4, 4, 16, 256)
-        patch2[...] = term if tap == 0 else patch2[...] + term
+    for dy in range(3):
+        blocks = [delta3[2 - dy : 6 - dy, 2 - dz : 6 - dz].reshape(256, 256) for dz in range(3)]
+        weights = jnp.concatenate([w3[3 * dy + dz] for dz in range(3)], axis=1)
+        term = dot_nt(jnp.concatenate(blocks, axis=1), weights).reshape(4, 4, 16, 256)
+        patch2[...] = term if dy == 0 else patch2[...] + term
 
     for y in range(4):
         for z in range(4):
@@ -488,10 +466,16 @@
                 taps[dx * 9 + dy * 3 + dz] = rows[dx * 32 : dx * 32 + 32] + roll(
                     rows[dx * 32 + 32 : dx * 32 + 64], 64, 1
                 )
-    for dy in range(3):
-        block = delta2[2 - dy : 6 - dy].reshape(512, 256)
-        term = dot_nt(block, w2[dy]).reshape(4, 4, 32, 512)
-        patch1[...] = term if dy == 0 else patch1[...] + term
+    def g1(columns, lanes, rows):
+        blocks = [delta2[2 - dy : 6 - dy, columns, :, lanes].reshape(-1, lanes.stop - lanes.start) for dy in range(3)]
+        weights = jnp.concatenate([w2[dy, rows, lanes] for dy in range(3)], axis=1)
+        return dot_nt(jnp.concatenate(blocks, axis=1), weights)
+
+    patch1[...] = g1(slice(1, 3), slice(0, 256), slice(0, 512)).reshape(4, 2, 32, 512)
+    below = g1(slice(0, 1), slice(128, 256), slice(384, 512)).reshape(4, 32, 128)
+    above = g1(slice(3, 4), slice(0, 128), slice(0, 128)).reshape(4, 32, 128)
+    beside[0] = below
+    beside[1] = above
 
     low_half = lane((32, 128)) < 64
     group = lane((32, 128)) // 32
@@ -503,11 +487,13 @@
 
 
     def gather1(y, carry):
-        for z, (zo_a, pz_a, zo_b, pz_b) in enumerate(((0, 3, 1, 1), (1, 2, 2, 0), (1, 3, 2, 1), (2, 2, 3, 0))):
-            value = (
-                patch1[y, zo_a, :, pz_a * 128 : pz_a * 128 + 128]
-                + patch1[y, zo_b, :, pz_b * 128 : pz_b * 128 + 128]
-            )
+        def part(zo, pz):
+            return patch1[y, zo, :, pz * 128 : pz * 128 + 128]
+
+        sums = (
+            beside[0, y] + part(0, 1), part(0, 2) + part(1, 0), part(0, 3) + part(1, 1), part(1, 2) + beside[1, y],
+        )
+        for z, value in enumerate(sums):
             value = rounded(value + roll(jnp.where(low_half, up(value), down(value)), 64, 1))
             grad1[z, pl.ds(0, 32, stride=2), :] = widen(value, 1)
             grad1[z, pl.ds(1, 32, stride=2), :] = widen(value, 2)
@@ -566,7 +552,8 @@
             pltpu.VMEM((4, 4, 16, 256), F32),
             pltpu.VMEM((4, 4, 32, 128), F32),
             pltpu.VMEM((6, 4, 32, 256), BF16),
-            pltpu.VMEM((4, 4, 32, 512), F32),
+            pltpu.VMEM((4, 2, 32, 512), F32),
+            pltpu.VMEM((2, 4, 32, 128), F32),
             pltpu.VMEM((4, 64, 128), F32),
             pltpu.VMEM((4, 256, 256), BF16),
         ],
@@ -688,23 +675,21 @@
 
     tile = universe.transpose(1, 2, 0, 3).reshape(8, 32, 128)
     cot = lax.all_to_all(cotangent[:, 0].transpose(1, 0, 2), "gz", 0, 0, tiled=True).reshape(128, 16)
-    tile, cot = lax.optimization_barrier((tile, cot))
     lower, upper = both_ways(tile, tile, "gz")
     strip = jnp.concatenate([lower[:, 4:], tile, upper[:, :28], jnp.zeros((8, 8, 128), BF16)], axis=1)
     top, bottom = both_ways(strip, strip, "gy")
 
     k1, k2, k3 = kernel1.transpose(0, 2, 1), kernel2.transpose(0, 2, 1), kernel3.transpose(0, 2, 1)
-    w1, w2, w3, biases, pick = run_weights(k1, bias1[None], k2, bias2[None], k3, bias3[None])
-    to_next, to_previous, hidden2, own_cot, ratio2, patches1, ratio1, fields = run_forward(
-        top, strip, bottom, cot, w1, w2, biases, pick
+    to_next, to_previous, hidden2, own_cot, ratio2, patches1, ratio1, fields, w2 = run_forward(
+        top, strip, bottom, cot, k1, bias1[None], k2, bias2[None]
     )
     lower, upper = both_ways(to_next, to_previous, "gz")
-    packed3, shift3 = run_own(size_z, hidden2, own_cot, w3, biases)
+    packed3, shift3, w3, wide3 = run_own(size_z, hidden2, own_cot, k3, bias3[None])
     row_next, row_previous = run_weave(lower, hidden2, upper, own_cot)
     before, after = both_ways(row_next, row_previous, "gy")
     packed = run_backward(
         size_z,
-        before, lower, hidden2, upper, after, own_cot, w3, biases, w2, ratio2, patches1, ratio1, fields,
+        before, lower, hidden2, upper, after, own_cot, w3, wide3, w2, ratio2, patches1, ratio1, fields,
         packed3, shift3,
     )
     packed = lax.all_to_all(packed, "gz", 0, 0, tiled=True)

time: 126 us -> 121 us (0.960)
  blocking collectives: 37.8 us -> 46.7 us
  waiting for transfers between devices: 26 us -> 19.4 us
  starting transfers between devices: 32.9 us -> 28.1 us
  local copies, waits for them, and re-layouts: 7.03 us -> 4.81 us
    all_to_all x0 -> x1, blocking collectives: none -> 13.3 us  [shards(): lax.all_to_all(cotangent[:, 0].transpose(1, 0, 2), 'gz', 0, 0, tiled=True)]
    all_to_all x1 -> x0, starting transfers between devices: 8.45 us -> none  [shards(): lax.all_to_all(cotangent[:, 0].transpose(1, 0, 2), 'gz', 0, 0, tiled=True)]
    all_to_all x1 -> x0, waiting for transfers between devices: 6.41 us -> none  [shards(): lax.all_to_all(cotangent[:, 0].transpose(1, 0, 2), 'gz', 0, 0, tiled=True)]
    ppermute x4, starting transfers between devices: 12.5 us -> 16.3 us  [both_ways(): lax.ppermute(to_next, axis, forth)]
    all_to_all x1, blocking collectives: 17.6 us -> 13.9 us  [shards(): column = lax.all_to_all(column, 'gy', 0, 0, tiled=True)]
    unnamed x13, local copies, waits for them, and re-layouts: 6.03 us -> 3.77 us
  transfers between devices with their start and end apart: 10 -> 9, of which waited for: 5 -> 4; matrix products, arithmetic and copies ran while one was open for 1% -> 1% of each run, Pallas kernels for 2% -> 2%
where the time goes in v7:
time: 121 us; the launch traced here: 120 us
  blocking collectives  46.7 us (39%)
  starting transfers between devices  28.1 us (23%)
  Pallas kernels  20.3 us (17%)
  waiting for transfers between devices  19.4 us (16%)
  local copies, waits for them, and re-layouts  4.81 us (4%)
    all_to_all x1, blocking collectives, shards(): packed = lax.all_to_all(packed, 'gz', 0, 0, tiled=True)  19.5 us
    ppermute x4, starting transfers between devices, both_ways(): lax.ppermute(to_next, axis, forth)  16.3 us
    all_to_all x1, blocking collectives, shards(): column = lax.all_to_all(column, 'gy', 0, 0, tiled=True)  13.9 us
    all_to_all x1, blocking collectives, shards(): lax.all_to_all(cotangent[:, 0].transpose(1, 0, 2), 'gz', 0, 0, tiled=True)  13.3 us
    ppermute x4, waiting for transfers between devices, both_ways(): lax.ppermute(to_previous, axis, back)  12.4 us
    pallas_call x1, Pallas kernels, run_forward(): pl.pallas_call(forward_kernel, name='forward', out_shape=(jax.ShapeDtypeS...  10.9 us
    all_to_all x1, waiting for transfers between devices, shards(): shared = lax.all_to_all(run_share(column, size_z), 'gz', 0, 0, tiled=True)  6.99 us
    ppermute x4, starting transfers between devices, both_ways(): lax.ppermute(to_previous, axis, back)  6.43 us
  transfers between devices with their start and end apart: 9, of which 4 were waited for; matrix products, arithmetic and copies ran while one was open for 1% of the time, Pallas kernels for 2%

profile of v7, /device:TPU:1, one launch (start us, length us, event | category | flops | bytes accessed | tf_op | source)
XLA Modules:
  0.0 120.2 jit_solution(8715455885400309024)
XLA Ops:
  0.7 0.9 copy.18
  1.6 6.0 %collective-permute-start = (bf16[8,32,128]{2,1,0:T(8,128)(2,1)S(1)}, bf16[8,32,128]{2,1,0:T(8,128)(2,1)S(1)}, u32[]{:S(2)}, u32[]{:S(2)}) collective-permute-start(bf16[8,32,128]{2,1,0:T(8,128)(2,1)S(1)} %bitcast.30), channel_id=1, source_target_pairs={{0,1},{1,2},{2,3},{3,4},{4,5},{5,6},{6,7},{7,8},{8,9},{9,10},{10,1... | collective-permute-start | bytes 196616 | tf_op jit(solution)/shard_map/ppermute | solution.py:669
  7.7 1.9 %collective-permute-start.1 = (bf16[8,32,128]{2,1,0:T(8,128)(2,1)S(1)}, bf16[8,32,128]{2,1,0:T(8,128)(2,1)S(1)}, u32[]{:S(2)}, u32[]{:S(2)}) collective-permute-start(bf16[8,32,128]{2,1,0:T(8,128)(2,1)S(1)} %bitcast.31), channel_id=1, source_target_pairs={{1,0},{2,1},{3,2},{4,3},{5,4},{6,5},{7,6},{8,7},{9,8},{10,9},{11,1... | collective-permute-start | bytes 196616 | tf_op jit(solution)/shard_map/ppermute | solution.py:669
  9.6 0.1 pad.3.clone
  9.7 5.0 %collective-permute-done.1 = bf16[8,32,128]{2,1,0:T(8,128)(2,1)S(1)} collective-permute-done((bf16[8,32,128]{2,1,0:T(8,128)(2,1)S(1)}, bf16[8,32,128]{2,1,0:T(8,128)(2,1)S(1)}, u32[]{:S(2)}, u32[]{:S(2)}) %collective-permute-start.1) | collective-permute-done | bytes 65568 | tf_op jit(solution)/shard_map/ppermute | solution.py:669
  14.7 0.1 maximum_maximum_fusion.mid
  14.8 1.3 %collective-permute-start.3 = (bf16[8,96,128]{2,1,0:T(8,128)(2,1)S(1)}, bf16[8,96,128]{2,1,0:T(8,128)(2,1)S(1)}, u32[]{:S(2)}, u32[]{:S(2)}) collective-permute-start(bf16[8,96,128]{2,1,0:T(8,128)(2,1)S(1)} %maximum_maximum_fusion.mid), channel_id=1, source_target_pairs={{16,0},{32,16},{48,32},{64,48},{80,64},{96,80},{112,96},{17,1},{33... | collective-permute-start | bytes 589832 | tf_op jit(solution)/shard_map/ppermute | solution.py:669
  16.1 4.2 %collective-permute-start.2 = (bf16[8,96,128]{2,1,0:T(8,128)(2,1)S(1)}, bf16[8,96,128]{2,1,0:T(8,128)(2,1)S(1)}, u32[]{:S(2)}, u32[]{:S(2)}) collective-permute-start(bf16[8,96,128]{2,1,0:T(8,128)(2,1)S(1)} %maximum_maximum_fusion.mid), channel_id=1, source_target_pairs={{0,16},{16,32},{32,48},{48,64},{64,80},{80,96},{96,112},{1,17},{17... | collective-permute-start | bytes 589832 | tf_op jit(solution)/shard_map/ppermute | solution.py:669
  20.3 0.8 copy.22
  21.1 13.3 %all_to_all.20 = bf16[16,8,16]{2,1,0:T(8,128)(2,1)S(1)} all-to-all(bf16[16,8,16]{2,1,0:T(8,128)(2,1)S(1)} %bitcast.33), channel_id=1, replica_groups=mesh['gy'=8,'gz'=16] {'gz'}, dimensions={0} | all-to-all | bytes 8192 | tf_op jit(solution)/shard_map/all_to_all | solution.py:677
  34.4 0.0 collective-permute-done.3.bot
  34.4 0.9 copy-done
  35.3 0.7 copy-done.1
  36.1 0.7 copy-done.2
  36.7 0.7 copy-done.3
  37.4 10.9 %forward.1 = (bf16[144,128]{1,0:T(8,128)(2,1)S(1)}, bf16[144,128]{1,0:T(8,128)(2,1)S(1)}, bf16[4,4,16,128]{3,2,1,0:T(8,128)(2,1)S(1)}, bf16[16,128]{1,0:T(8,128)...) custom-call(bf16[8,96,128]{2,1,0:T(8,128)(2,1)S(1)} %collective-perm, ...), custom_call_target="tpu_custom_call" | custom-call | tf_op jit(solution)/shard_map/forward/pallas_call | solution.py:249
  48.3 2.5 %collective-permute-start.4 = (bf16[144,128]{1,0:T(8,128)(2,1)S(1)}, bf16[144,128]{1,0:T(8,128)(2,1)S(1)}, u32[]{:S(2)}, u32[]{:S(2)}) collective-permute-start(bf16[144,128]{1,0:T(8,128)(2,1)S(1)} %get-tuple-element.29), channel_id=1, source_target_pairs={{0,1},{1,2},{2,3},{3,4},{4,5},{5,6},{6,7},{7,8},{8,9},{9,10},{10,1... | collective-permute-start | bytes 110600 | tf_op jit(solution)/shard_map/ppermute | solution.py:669
  50.8 1.9 %collective-permute-start.5 = (bf16[144,128]{1,0:T(8,128)(2,1)S(1)}, bf16[144,128]{1,0:T(8,128)(2,1)S(1)}, u32[]{:S(2)}, u32[]{:S(2)}) collective-permute-start(bf16[144,128]{1,0:T(8,128)(2,1)S(1)} %get-tuple-element.31), channel_id=1, source_target_pairs={{1,0},{2,1},{3,2},{4,3},{5,4},{6,5},{7,6},{8,7},{9,8},{10,9},{11,1... | collective-permute-start | bytes 110600 | tf_op jit(solution)/shard_map/ppermute | solution.py:669
  52.8 4.8 %collective-permute-done.5.upper = bf16[144,128]{1,0:T(8,128)(2,1)S(1)} collective-permute-done((bf16[144,128]{1,0:T(8,128)(2,1)S(1)}, bf16[144,128]{1,0:T(8,128)(2,1)S(1)}, u32[]{:S(2)}, u32[]{:S(2)}) %collective-permute-start.5) | collective-permute-done | bytes 36896 | tf_op jit(solution)/shard_map/ppermute | solution.py:669
  57.6 3.5 %collective-permute-start.6 = (bf16[304,128]{1,0:T(8,128)(2,1)S(1)}, bf16[304,128]{1,0:T(8,128)(2,1)S(1)}, u32[]{:S(2)}, u32[]{:S(2)}) collective-permute-start(bf16[304,128]{1,0:T(8,128)(2,1)S(1)} %get-tuple-element.33), channel_id=1, source_target_pairs={{0,16},{16,32},{32,48},{48,64},{64,80},{80,96},{96,112},{1,17},{17... | collective-permute-start | bytes 233480 | tf_op jit(solution)/shard_map/ppermute | solution.py:669
  61.2 1.3 %collective-permute-start.7 = (bf16[304,128]{1,0:T(8,128)(2,1)S(1)}, bf16[304,128]{1,0:T(8,128)(2,1)S(1)}, u32[]{:S(2)}, u32[]{:S(2)}) collective-permute-start(bf16[304,128]{1,0:T(8,128)(2,1)S(1)} %get-tuple-element.34), channel_id=1, source_target_pairs={{16,0},{32,16},{48,32},{64,48},{80,64},{96,80},{112,96},{17,1},{33... | collective-permute-start | bytes 233480 | tf_op jit(solution)/shard_map/ppermute | solution.py:669
  62.5 1.3 %own.1 = (bf16[16,120,128]{2,1,0:T(8,128)(2,1)S(1)}, f32[1,128]{1,0:T(1,128)S(1)}, bf16[9,256,256]{2,1,0:T(8,128)(2,1)S(1)}, f32[1,256]{1,0:T(1,128)S(1)}) custom-call(bf16[4,4,16,128]{3,2,1,0:T(8,128)(2,1)S(1)} %get-tuple-element.30.hidden2.middle, bf16[16,128]{1,0:T(8,128)(2,1)S(1)} %get-tuple-element.32.own_cot, bf16[27,64,128]{2,1,0:T(8,128)(2,1)S(1)} %bitcast.28, ...), custom_call_target="tpu_custom_call" | custom-call | flops 150000000 | bytes 4000000 | tf_op jit(solution)/shard_map/own/pallas_call | solution.py:369
  63.8 2.5 %collective-permute-done.7.after = bf16[304,128]{1,0:T(8,128)(2,1)S(1)} collective-permute-done((bf16[304,128]{1,0:T(8,128)(2,1)S(1)}, bf16[304,128]{1,0:T(8,128)(2,1)S(1)}, u32[]{:S(2)}, u32[]{:S(2)}) %collective-permute-start.7) | collective-permute-done | bytes 77856 | tf_op jit(solution)/shard_map/ppermute | solution.py:669
  66.3 5.0 %backward.1 = bf16[16,152,128]{2,1,0:T(8,128)(2,1)S(1)} custom-call(bf16[304,128]{1,0:T(8,128)(2,1)S(1)} %collective-permute-done.6.before, bf16[144,128]{1,0:T(8,128)(2,1)S(1)} %collective-permute-done.4.lower, bf16[4,4,16,128]{3,2,1,0:T(8,128)(2,1)S(1)} %get-tuple-element.30.hidden2.middle, bf16[144,128]{1,0:T(8,128)(2,1)S(1)} %collective-permute-done.5.upper, ...), custom_call_target="tpu_custom_call" | custom-call | tf_op jit(solution)/shard_map/backward/pallas_call | solution.py:542
  71.4 19.5 %all_to_all.21.received = bf16[16,152,128]{2,1,0:T(8,128)(2,1)S(1)} all-to-all(bf16[16,152,128]{2,1,0:T(8,128)(2,1)S(1)} %backward.1), channel_id=1, replica_groups=mesh['gy'=8,'gz'=16] {'gz'}, dimensions={0} | all-to-all | bytes 1245184 | tf_op jit(solution)/shard_map/all_to_all | solution.py:695
  90.8 0.7 sum.1
  91.6 13.9 %all_to_all.22.column = bf16[8,144,128]{2,1,0:T(8,128)(2,1)S(1)} all-to-all(bf16[8,144,128]{2,1,0:T(8,128)(2,1)S(1)} %get-tuple-element.45), channel_id=1, replica_groups=mesh['gy'=8,'gz'=16] {'gy'}, dimensions={0} | all-to-all | bytes 589824 | tf_op jit(solution)/shard_map/all_to_all | solution.py:697
  105.5 0.7 share.1
  106.2 5.4 %all-to-all-start.3 = ((bf16[16,32,128]{2,1,0:T(8,128)(2,1)}), bf16[16,32,128]{2,1,0:T(8,128)(2,1)S(1)}, u32[]{:S(2)}, u32[]{:S(2)}) async-start(bf16[16,32,128]{2,1,0:T(8,128)(2,1)} %share.1), calls=%async_computation.3 | async-start | bytes 262144 | tf_op jit(solution)/shard_map/all_to_all | solution.py:698
  111.5 0.7 third.1
  112.3 7.0 %all-to-all-done.3.shared = bf16[16,32,128]{2,1,0:T(8,128)(2,1)S(1)} async-done(((bf16[16,32,128]{2,1,0:T(8,128)(2,1)}), bf16[16,32,128]{2,1,0:T(8,128)(2,1)S(1)}, u32[]{:S(2)}, u32[]{:S(2)}) %all-to-all-start.3) | async-done | bytes 131104 | tf_op jit(solution)/shard_map/all_to_all | solution.py:698
  119.3 0.9 unpack.1
  (15 shorter events, 0.1 us)
Async XLA Ops:
  0.6 61.9 %copy-start.5 = (f32[128]{0:T(128)S(1)}, f32[128]{0:T(128)}, u32[]{:S(2)}) copy-start(f32[128]{0:T(128)} %param.14) | copy-start | bytes 1540
  0.6 61.9 %copy-start.4 = (bf16[27,128,64]{1,2,0:T(8,128)(2,1)S(1)}, bf16[27,128,64]{1,2,0:T(8,128)(2,1)}, u32[]{:S(2)}) copy-start(bf16[27,128,64]{1,2,0:T(8,128)(2,1)} %param.13) | copy-start | bytes 1327108
  1.6 8.1 %collective-permute-start = (bf16[8,32,128]{2,1,0:T(8,128)(2,1)S(1)}, bf16[8,32,128]{2,1,0:T(8,128)(2,1)S(1)}, u32[]{:S(2)}, u32[]{:S(2)}) collective-permute-start(bf16[8,32,128]{2,1,0:T(8,128)(2,1)S(1)} %bitcast.30), channel_id=1, source_target_pairs={{0,1},{1,2},{2,3},{3,4},{4,5},{5,6},{6,7},{7,8},{8,9},{9,10},{10,1... | collective-permute-start | bytes 196616 | tf_op jit(solution)/shard_map/ppermute | solution.py:669
  7.7 7.1 %collective-permute-start.1 = (bf16[8,32,128]{2,1,0:T(8,128)(2,1)S(1)}, bf16[8,32,128]{2,1,0:T(8,128)(2,1)S(1)}, u32[]{:S(2)}, u32[]{:S(2)}) collective-permute-start(bf16[8,32,128]{2,1,0:T(8,128)(2,1)S(1)} %bitcast.31), channel_id=1, source_target_pairs={{1,0},{2,1},{3,2},{4,3},{5,4},{6,5},{7,6},{8,7},{9,8},{10,9},{11,1... | collective-permute-start | bytes 196616 | tf_op jit(solution)/shard_map/ppermute | solution.py:669
  14.8 19.5 %collective-permute-start.3 = (bf16[8,96,128]{2,1,0:T(8,128)(2,1)S(1)}, bf16[8,96,128]{2,1,0:T(8,128)(2,1)S(1)}, u32[]{:S(2)}, u32[]{:S(2)}) collective-permute-start(bf16[8,96,128]{2,1,0:T(8,128)(2,1)S(1)} %maximum_maximum_fusion.mid), channel_id=1, source_target_pairs={{16,0},{32,16},{48,32},{64,48},{80,64},{96,80},{112,96},{17,1},{33... | collective-permute-start | bytes 589832 | tf_op jit(solution)/shard_map/ppermute | solution.py:669
  16.1 18.2 %collective-permute-start.2 = (bf16[8,96,128]{2,1,0:T(8,128)(2,1)S(1)}, bf16[8,96,128]{2,1,0:T(8,128)(2,1)S(1)}, u32[]{:S(2)}, u32[]{:S(2)}) collective-permute-start(bf16[8,96,128]{2,1,0:T(8,128)(2,1)S(1)} %maximum_maximum_fusion.mid), channel_id=1, source_target_pairs={{0,16},{16,32},{32,48},{48,64},{64,80},{80,96},{96,112},{1,17},{17... | collective-permute-start | bytes 589832 | tf_op jit(solution)/shard_map/ppermute | solution.py:669
  34.4 0.9 copy-start
  35.3 0.7 copy-start.1
  36.1 0.7 copy-start.2
  36.7 0.7 copy-start.3
  48.3 4.5 %collective-permute-start.4 = (bf16[144,128]{1,0:T(8,128)(2,1)S(1)}, bf16[144,128]{1,0:T(8,128)(2,1)S(1)}, u32[]{:S(2)}, u32[]{:S(2)}) collective-permute-start(bf16[144,128]{1,0:T(8,128)(2,1)S(1)} %get-tuple-element.29), channel_id=1, source_target_pairs={{0,1},{1,2},{2,3},{3,4},{4,5},{5,6},{6,7},{7,8},{8,9},{9,10},{10,1... | collective-permute-start | bytes 110600 | tf_op jit(solution)/shard_map/ppermute | solution.py:669
  50.8 6.8 %collective-permute-start.5 = (bf16[144,128]{1,0:T(8,128)(2,1)S(1)}, bf16[144,128]{1,0:T(8,128)(2,1)S(1)}, u32[]{:S(2)}, u32[]{:S(2)}) collective-permute-start(bf16[144,128]{1,0:T(8,128)(2,1)S(1)} %get-tuple-element.31), channel_id=1, source_target_pairs={{1,0},{2,1},{3,2},{4,3},{5,4},{6,5},{7,6},{8,7},{9,8},{10,9},{11,1... | collective-permute-start | bytes 110600 | tf_op jit(solution)/shard_map/ppermute | solution.py:669
  57.6 6.2 %collective-permute-start.6 = (bf16[304,128]{1,0:T(8,128)(2,1)S(1)}, bf16[304,128]{1,0:T(8,128)(2,1)S(1)}, u32[]{:S(2)}, u32[]{:S(2)}) collective-permute-start(bf16[304,128]{1,0:T(8,128)(2,1)S(1)} %get-tuple-element.33), channel_id=1, source_target_pairs={{0,16},{16,32},{32,48},{48,64},{64,80},{80,96},{96,112},{1,17},{17... | collective-permute-start | bytes 233480 | tf_op jit(solution)/shard_map/ppermute | solution.py:669
  61.2 5.1 %collective-permute-start.7 = (bf16[304,128]{1,0:T(8,128)(2,1)S(1)}, bf16[304,128]{1,0:T(8,128)(2,1)S(1)}, u32[]{:S(2)}, u32[]{:S(2)}) collective-permute-start(bf16[304,128]{1,0:T(8,128)(2,1)S(1)} %get-tuple-element.34), channel_id=1, source_target_pairs={{16,0},{32,16},{48,32},{64,48},{80,64},{96,80},{112,96},{17,1},{33... | collective-permute-start | bytes 233480 | tf_op jit(solution)/shard_map/ppermute | solution.py:669
  106.2 13.1 %all-to-all-start.3 = ((bf16[16,32,128]{2,1,0:T(8,128)(2,1)}), bf16[16,32,128]{2,1,0:T(8,128)(2,1)S(1)}, u32[]{:S(2)}, u32[]{:S(2)}) async-start(bf16[16,32,128]{2,1,0:T(8,128)(2,1)} %share.1), calls=%async_computation.3 | async-start | bytes 262144 | tf_op jit(solution)/shard_map/all_to_all | solution.py:698

commit v8 on v7

--- a/solution.py
+++ b/solution.py
@@ -67,15 +67,15 @@
 
 
 def forward_kernel(
-    top, mid, bot, cot, k1, b1, k2, b2,
-    to_next, to_previous, hidden2, own_cot, ratio2, patches1, ratio1, fields, w2,
+    top, mid, bot, k1, k2, biases,
+    to_next, to_previous, hidden2, ratio2, patches1, ratio1, fields, w2,
     w1, pick, left, field, turned, pre1, first, spread, pre2, second,
 ):
     lay_weights1(k1, w1)
     lay_weights2(k2, w2)
     lay_pick(pick)
-    bias1 = jnp.concatenate([b1[...]] * 8, axis=1)
-    bias2 = jnp.concatenate([b2[...]] * 4, axis=1)
+    bias1 = jnp.concatenate([biases[0:1, :32]] * 8, axis=1)
+    bias2 = jnp.concatenate([biases[1:2, :64]] * 4, axis=1)
     base_y, base_z = lax.axis_index("gy"), lax.axis_index("gz")
     size_y, size_z = lax.axis_size("gy"), lax.axis_size("gz")
 
@@ -94,62 +94,61 @@
             pieces.append(jnp.concatenate([rows[a : a + 16], rows[b : b + 16]], axis=1))
         left[target] = jnp.concatenate(pieces, axis=0).astype(BF16)
 
-    def lay_top(step, carry):
+    def lay_both(step, carry):
+        lay(mid, step, step + 7)
+        lay(mid, step + 4, step + 11)
+        return carry
+
+    def lay_ends(step, carry):
         lay(top, step + 1, step)
-        return carry
-
-    def lay_mid(step, carry):
-        lay(mid, step, step + 7)
-        return carry
-
-    def lay_bot(step, carry):
         lay(bot, step, step + 15)
         return carry
 
-    lax.fori_loop(0, 7, lay_top, 0)
-    lax.fori_loop(0, 8, lay_mid, 0)
-    lax.fori_loop(0, 7, lay_bot, 0)
-
-    def sift(step, carry):
-        block = left[pl.ds(2 * step, 2)].reshape(160, 256)
-        out = dot(block, pick[...]).astype(BF16).reshape(2, 5, 16, 512)
-        for parity in range(2):
+    lax.fori_loop(0, 4, lay_both, 0)
+    lax.fori_loop(0, 7, lay_ends, 0)
+
+    for part in range(2):
+        block = left[part * 11 : part * 11 + 11].reshape(880, 256)
+        out = dot(block, pick[...]).astype(BF16).reshape(11, 5, 16, 512)
+        for step in range(11):
+            row = part * 11 + step
             for px in range(4):
-                at = (parity * 4 + px) * 16
+                at = (row % 2 * 4 + px) * 16
                 for k in range(5):
-                    field[step, at : at + 16, k * 128 : k * 128 + 128] = out[
-                        parity, k, :, px * 128 : px * 128 + 128
+                    field[row // 2, at : at + 16, k * 128 : k * 128 + 128] = out[
+                        step, k, :, px * 128 : px * 128 + 128
                     ]
-        turned[step] = field[step].T
-        return carry
-
-    lax.fori_loop(0, 11, sift, 0)
+    for pair in range(11):
+        turned[pair] = field[pair].T
     fields[...] = field[3:8, :, :256]
     first[:, :, 0:8] = jnp.zeros((10, 10, 8, 128), F32)
     first[:, :, 72:80] = jnp.zeros((10, 10, 8, 128), F32)
 
-    def block1(yw, carry):
-        stack = jnp.concatenate([turned[yw], turned[yw + 1]], axis=1)
-        pre1[...] = dot(stack, w1[...])
-        place = jnp.where((yw >= 3) & (yw < 7), yw - 3, 4)
-        for k, pair in enumerate(PAIRS):
-            for h, zw in enumerate(pair):
-                at = k * 128 + h * 64
-                pre = pre1[at : at + 64] + bias1
-                e = exps(pre)
-                total = e[:, :128] + e[:, 128:]
-                total = total + roll(total, 64, 1)
-                total = total + roll(total, 32, 1)
-                mean = total * 0.125
-                pooled = rounded(jnp.log(mean) * 0.5)
-                first[yw, zw + 3, 8:72] = pooled * inside(yw - 3, zw, 1)
-                if k < 2:
-                    share = 0.125 / mean
-                    share = jnp.concatenate([share, share], axis=1)
-                    ratio1[place, at : at + 64] = jnp.where(pre > 0, 1.0, SLOPE) * (e * share)
+    def block1(step, carry):
+        for part in range(2):
+            stack = jnp.concatenate([turned[2 * step + part], turned[2 * step + part + 1]], axis=1)
+            pre1[part] = dot(stack, w1[...])
+        for part in range(2):
+            yw = 2 * step + part
+            place = jnp.where((yw >= 3) & (yw < 7), yw - 3, 4)
+            for k, pair in enumerate(PAIRS):
+                for h, zw in enumerate(pair):
+                    at = k * 128 + h * 64
+                    pre = pre1[part, at : at + 64] + bias1
+                    e = exps(pre)
+                    total = e[:, :128] + e[:, 128:]
+                    total = total + roll(total, 64, 1)
+                    total = total + roll(total, 32, 1)
+                    mean = total * 0.125
+                    pooled = rounded(jnp.log(mean) * 0.5)
+                    first[yw, zw + 3, 8:72] = pooled * inside(yw - 3, zw, 1)
+                    if k < 2:
+                        share = 0.125 / mean
+                        share = jnp.concatenate([share, share], axis=1)
+                        ratio1[place, at : at + 64] = jnp.where(pre > 0, 1.0, SLOPE) * (e * share)
         return carry
 
-    lax.fori_loop(0, 10, block1, 0)
+    lax.fori_loop(0, 5, block1, 0)
 
     group1 = lane((32, 128)) // 32
 
@@ -166,37 +165,39 @@
 
     half = lane((16, 128)) < 64
 
-    def block2(yp, carry):
-        columns = []
-        for zo in range(4):
-            tiles = [spread[pl.ds(2 * yp + dy, 2), 2 * zo + pz] for dy in range(3) for pz in range(4)]
-            columns.append(jnp.concatenate(tiles, axis=2)[:, None])
-        block = jnp.concatenate(columns, axis=1).reshape(256, 1536)
-        pre2[...] = dot(block, w2[...].reshape(1536, 256)).reshape(2, 4, 32, 256)
-        for zo in range(4):
-            pre = pre2[:, zo] + bias2
-            e = exps(pre)
-            both = e[0] + e[1]
-            total = both[:, :128] + both[:, 128:]
-            total = total + roll(total, 64, 1)
-            mean = total * 0.125
-            ok = inside(yp - 1, zo - 1, 2)
-            share = (0.125 * ok) / mean
-            share = jnp.concatenate([share, share], axis=1)
-            ratio2[pl.ds(2 * yp, 2), zo] = jnp.where(pre > 0, 1.0, SLOPE) * (e * share[None])
-            second[zo] = rounded(jnp.log(mean) * 0.5) * ok
-            even = second[zo, pl.ds(0, 16, stride=2), :]
-            odd = second[zo, pl.ds(1, 16, stride=2), :]
-            hidden2[yp, zo] = jnp.where(half, even, odd).astype(BF16)
+    def block2(step, carry):
+        for part in range(2):
+            yp = 2 * step + part
+            columns = []
+            for zo in range(4):
+                tiles = [spread[pl.ds(2 * yp + dy, 2), 2 * zo + pz] for dy in range(3) for pz in range(4)]
+                columns.append(jnp.concatenate(tiles, axis=2)[:, None])
+            block = jnp.concatenate(columns, axis=1).reshape(256, 1536)
+            pre2[part] = dot(block, w2[...].reshape(1536, 256)).reshape(2, 4, 32, 256)
+        for part in range(2):
+            yp = 2 * step + part
+            for zo in range(4):
+                pre = pre2[part, :, zo] + bias2
+                e = exps(pre)
+                both = e[0] + e[1]
+                total = both[:, :128] + both[:, 128:]
+                total = total + roll(total, 64, 1)
+                mean = total * 0.125
+                ok = inside(yp - 1, zo - 1, 2)
+                share = (0.125 * ok) / mean
+                share = jnp.concatenate([share, share], axis=1)
+                ratio2[pl.ds(2 * yp, 2), zo] = jnp.where(pre > 0, 1.0, SLOPE) * (e * share[None])
+                second[part, zo] = rounded(jnp.log(mean) * 0.5) * ok
+        for part in range(2):
+            for zo in range(4):
+                even = second[part, zo, pl.ds(0, 16, stride=2), :]
+                odd = second[part, zo, pl.ds(1, 16, stride=2), :]
+                hidden2[2 * step + part, zo] = jnp.where(half, even, odd).astype(BF16)
         return carry
 
-    lax.fori_loop(0, 4, block2, 0)
-    to_next[0:128] = hidden2[:, 0:2].reshape(128, 128)
-    to_previous[0:128] = hidden2[:, 2:4].reshape(128, 128)
-    own = cot[...].astype(F32).T.astype(BF16)
-    to_next[128:144] = own
-    to_previous[128:144] = own
-    own_cot[...] = own
+    lax.fori_loop(0, 2, block2, 0)
+    to_next[...] = hidden2[:, 0:2].reshape(128, 128)
+    to_previous[...] = hidden2[:, 2:4].reshape(128, 128)
 
 
 def lay_weights1(taps, out):
@@ -221,14 +222,14 @@
 
 
 def lay_weights2(taps, out):
-    zero = jnp.zeros((32, 64), BF16)
+    zero = jnp.zeros((32, 64), F32)
     for dy in range(3):
         out[dy, 384:512, 0:128] = jnp.zeros((128, 128), BF16)
         out[dy, 0:128, 128:256] = jnp.zeros((128, 128), BF16)
         for dz in range(3):
             for px in range(4):
                 sides = [taps[(px - qx) * 9 + dy * 3 + dz] if 0 <= px - qx < 3 else zero for qx in range(2)]
-                tile = jnp.concatenate(sides, axis=1)
+                tile = jnp.concatenate(sides, axis=1).astype(BF16)
                 for qz in range(2):
                     at = (dz + qz) * 128 + px * 32
                     out[dy, at : at + 32, qz * 128 : qz * 128 + 128] = tile
@@ -250,10 +251,9 @@
         forward_kernel,
         name="forward",
         out_shape=(
-            jax.ShapeDtypeStruct((144, 128), BF16),
-            jax.ShapeDtypeStruct((144, 128), BF16),
+            jax.ShapeDtypeStruct((128, 128), BF16),
+            jax.ShapeDtypeStruct((128, 128), BF16),
             jax.ShapeDtypeStruct((4, 4, 16, 128), BF16),
-            jax.ShapeDtypeStruct((16, 128), BF16),
             jax.ShapeDtypeStruct((8, 4, 32, 256), F32),
             jax.ShapeDtypeStruct((6, 6, 32, 128), BF16),
             jax.ShapeDtypeStruct((5, 256, 256), F32),
@@ -261,42 +261,72 @@
             jax.ShapeDtypeStruct((3, 512, 256), BF16),
         ),
         in_specs=[VMEM] * len(operands),
-        out_specs=(VMEM,) * 9,
+        out_specs=(VMEM,) * 8,
+        cost_estimate=pl.CostEstimate(flops=5000000000, bytes_accessed=8000000, transcendentals=8000000),
         scratch_shapes=[
             pltpu.VMEM((256, 256), BF16),
             pltpu.VMEM((256, 512), BF16),
             pltpu.VMEM((22, 80, 256), BF16),
             pltpu.VMEM((11, 128, 640), BF16),
             pltpu.VMEM((11, 640, 128), BF16),
-            pltpu.VMEM((640, 256), F32),
+            pltpu.VMEM((2, 640, 256), F32),
             pltpu.VMEM((10, 10, 80, 128), F32),
             pltpu.VMEM((10, 10, 32, 128), BF16),
-            pltpu.VMEM((2, 4, 32, 256), F32),
-            pltpu.VMEM((4, 32, 128), F32),
+            pltpu.VMEM((2, 2, 4, 32, 256), F32),
+            pltpu.VMEM((2, 4, 32, 128), F32),
         ],
         compiler_params=pltpu.CompilerParams(vmem_limit_bytes=LIMIT),
     )(*operands)
 
 
-def weave_kernel(lower, hidden2, upper, own_cot, to_next, to_previous):
+def deal_kernel(cot, dealt):
+    groups, width = dealt.shape[0], dealt.shape[2]
+    rows = jnp.concatenate([cot[c, 0].astype(F32) for c in range(width // 16)], axis=1)
+    rows = jnp.concatenate([jnp.zeros((1, width), F32), rows, jnp.zeros((1, width), F32)], axis=0)
+    for k in range(groups):
+        dealt[k] = jnp.concatenate([rows[k : k + 3], jnp.zeros((5, width), F32)], axis=0).astype(BF16)
+
+
+def run_deal(cot):
+    wide, _, groups, depth = cot.shape
+    return pl.pallas_call(
+        deal_kernel,
+        name="deal",
+        out_shape=jax.ShapeDtypeStruct((groups, 8, wide * depth), BF16),
+        in_specs=[VMEM],
+        out_specs=VMEM,
+        compiler_params=pltpu.CompilerParams(vmem_limit_bytes=LIMIT),
+    )(cot)
+
+
+def weave_kernel(lower, hidden2, upper, dealt, to_next, to_previous, own_cot):
     for target, first_row in ((to_next, 0), (to_previous, 2)):
         for y in range(2):
             row, at = first_row + y, y * 128
             target[at : at + 32] = lower[row * 32 : row * 32 + 32]
             target[at + 32 : at + 96] = hidden2[row].reshape(64, 128)
             target[at + 96 : at + 128] = upper[row * 32 : row * 32 + 32]
-        target[256:272] = lower[128:144]
-        target[272:288] = own_cot[...]
-        target[288:304] = upper[128:144]
+    groups = dealt.shape[0]
+    wide = 128 // groups
+    row = lax.broadcasted_iota(jnp.int32, (128, 128), 0)
+    col = lax.broadcasted_iota(jnp.int32, (128, 128), 1)
+    order = jnp.where(col == row % groups * wide + row // groups, 1.0, 0.0).astype(BF16)
+    whole = dealt[...].astype(F32)
+    for d in range(3):
+        lines = whole[:, d]
+        stack = jnp.concatenate([lines[:, c * 16 : c * 16 + 16] for c in range(wide)], axis=0).astype(BF16)
+        rows = dot_tn(stack, order).astype(BF16)
+        for target, at in ((to_next, 256), (to_previous, 256), (own_cot, 0)):
+            target[at + 16 * d : at + 16 * d + 16] = rows
 
 
 def run_weave(*operands):
     return pl.pallas_call(
         weave_kernel,
         name="weave",
-        out_shape=(jax.ShapeDtypeStruct((304, 128), BF16),) * 2,
+        out_shape=(jax.ShapeDtypeStruct((304, 128), BF16),) * 2 + (jax.ShapeDtypeStruct((48, 128), BF16),),
         in_specs=[VMEM] * 4,
-        out_specs=(VMEM,) * 2,
+        out_specs=(VMEM,) * 3,
         compiler_params=pltpu.CompilerParams(vmem_limit_bytes=LIMIT),
     )(*operands)
 
@@ -319,11 +349,11 @@
     return mean, (jnp.where(pre > 0, 1.0, SLOPE) * (e * share)).astype(BF16)
 
 
-def own_kernel(hidden2, own_cot, k3, b3, packed, shift3, w3, wide3, patches2, pre3, turned):
+def own_kernel(hidden2, own_cot, k3, biases, packed, shift3, w3, wide3, patches2, pre3, turned):
     groups = packed.shape[0]
     wide = 128 // groups
     lay_weights3(k3, w3)
-    wide3[...] = jnp.concatenate([b3[...]] * 2, axis=1)
+    wide3[...] = jnp.concatenate([biases[2:3]] * 2, axis=1)
     for y in range(4):
         for z in range(4):
             lay_patches2(hidden2[y, z], patches2.at[y, z])
@@ -332,7 +362,7 @@
         block = patches2[dy : dy + 2, dz : dz + 2].reshape(64, 256)
         term = dot(block, w3[tap])
         pre3[...] = term + wide3[...] if tap == 0 else pre3[...] + term
-    mean, delta = pool3(pre3[...].reshape(2, 2, 16, 256), own_cot[...])
+    mean, delta = pool3(pre3[...].reshape(2, 2, 16, 256), own_cot[16:32])
     features = rounded(jnp.log(mean) * 0.5)
     own3 = delta.reshape(64, 256)
     bias3 = own3.astype(F32).sum(axis=0, keepdims=True)
@@ -422,7 +452,7 @@
         for wz in range(3):
             pre = pre3[2 * wy : 2 * wy + 2, 2 * wz : 2 * wz + 2]
             if wy == 1:
-                cot = own_cot[...] if wz == 1 else (lower if wz == 0 else upper)[128:144]
+                cot = own_cot[wz * 16 : wz * 16 + 16]
             else:
                 cot = (before if wy == 0 else after)[256 + wz * 16 : 272 + wz * 16]
             delta3[2 * wy : 2 * wy + 2, 2 * wz : 2 * wz + 2] = pool3(pre, cot)[1]
@@ -674,18 +704,21 @@
     wide = 128 // size_z
 
     tile = universe.transpose(1, 2, 0, 3).reshape(8, 32, 128)
-    cot = lax.all_to_all(cotangent[:, 0].transpose(1, 0, 2), "gz", 0, 0, tiled=True).reshape(128, 16)
+    dealt = lax.all_to_all(run_deal(cotangent), "gz", 0, 0, tiled=True)
+    biases = jnp.stack([jnp.pad(bias1, (0, 96)), jnp.pad(bias2, (0, 64)), bias3])
     lower, upper = both_ways(tile, tile, "gz")
     strip = jnp.concatenate([lower[:, 4:], tile, upper[:, :28], jnp.zeros((8, 8, 128), BF16)], axis=1)
     top, bottom = both_ways(strip, strip, "gy")
 
-    k1, k2, k3 = kernel1.transpose(0, 2, 1), kernel2.transpose(0, 2, 1), kernel3.transpose(0, 2, 1)
-    to_next, to_previous, hidden2, own_cot, ratio2, patches1, ratio1, fields, w2 = run_forward(
-        top, strip, bottom, cot, k1, bias1[None], k2, bias2[None]
+    k1, k2 = kernel1.transpose(0, 2, 1).astype(F32), kernel2.transpose(0, 2, 1).astype(F32)
+    k3 = kernel3.transpose(0, 2, 1)
+    top, dealt = lax.optimization_barrier((top, dealt))
+    to_next, to_previous, hidden2, ratio2, patches1, ratio1, fields, w2 = run_forward(
+        top, strip, bottom, k1, k2, biases
     )
     lower, upper = both_ways(to_next, to_previous, "gz")
-    packed3, shift3, w3, wide3 = run_own(size_z, hidden2, own_cot, k3, bias3[None])
-    row_next, row_previous = run_weave(lower, hidden2, upper, own_cot)
+    row_next, row_previous, own_cot = run_weave(lower, hidden2, upper, dealt)
+    packed3, shift3, w3, wide3 = run_own(size_z, hidden2, own_cot, k3, biases)
     before, after = both_ways(row_next, row_previous, "gy")
     packed = run_backward(
         size_z,

time: 121 us -> 117 us (0.967)
  starting transfers between devices: 28.1 us -> 39.7 us
  blocking collectives: 46.7 us -> 36.7 us
  Pallas kernels: 20.3 us -> 17.1 us
  local copies, waits for them, and re-layouts: 4.81 us -> 1.79 us
  other arithmetic: 0.1 us -> 1.85 us
    all_to_all x1 -> x0, blocking collectives: 13.3 us -> none  [shards(): lax.all_to_all(cotangent[:, 0].transpose(1, 0, 2), 'gz', 0, 0, tiled=True)]
    all_to_all x0 -> x1, starting transfers between devices: none -> 7.89 us  [shards(): dealt = lax.all_to_all(run_deal(cotangent), 'gz', 0, 0, tiled=True)]
    ppermute x4, waiting for transfers between devices: 12.4 us -> 7.47 us  [both_ways(): lax.ppermute(to_previous, axis, back)]
    pallas_call x1, Pallas kernels: 10.9 us -> 6.78 us  [run_forward(): pl.pallas_call(forward_kernel, name='forward', out_shape=(jax.ShapeDtypeS...]
    all_to_all x1, blocking collectives: 13.9 us -> 18.1 us  [shards(): column = lax.all_to_all(column, 'gy', 0, 0, tiled=True)]
    ppermute x4, waiting for transfers between devices: 0.01 us -> 4 us  [both_ways(): lax.ppermute(to_next, axis, forth)]
    unnamed x13 -> x10, local copies, waits for them, and re-layouts: 3.77 us -> 0.77 us
    ppermute x4, starting transfers between devices: 16.3 us -> 18.6 us  [both_ways(): lax.ppermute(to_next, axis, forth)]
  transfers between devices with their start and end apart: 9 -> 10, of which waited for: 4 -> 4; matrix products, arithmetic and copies ran while one was open for 1% -> 2% of each run, Pallas kernels for 2% -> 2%
where the time goes in v8:
time: 117 us; the launch traced here: 116 us
  starting transfers between devices  39.7 us (34%)
  blocking collectives  36.7 us (31%)
  waiting for transfers between devices  18.5 us (16%)
  Pallas kernels  17.1 us (15%)
  other arithmetic  1.85 us (2%)
  local copies, waits for them, and re-layouts  1.79 us (2%)
    all_to_all x1, blocking collectives, shards(): packed = lax.all_to_all(packed, 'gz', 0, 0, tiled=True)  18.6 us
    ppermute x4, starting transfers between devices, both_ways(): lax.ppermute(to_next, axis, forth)  18.6 us
    all_to_all x1, blocking collectives, shards(): column = lax.all_to_all(column, 'gy', 0, 0, tiled=True)  18.1 us
    all_to_all x1, starting transfers between devices, shards(): dealt = lax.all_to_all(run_deal(cotangent), 'gz', 0, 0, tiled=True)  7.89 us
    ppermute x4, starting transfers between devices, both_ways(): lax.ppermute(to_previous, axis, back)  7.83 us
    ppermute x4, waiting for transfers between devices, both_ways(): lax.ppermute(to_previous, axis, back)  7.47 us
    all_to_all x1, waiting for transfers between devices, shards(): shared = lax.all_to_all(run_share(column, size_z), 'gz', 0, 0, tiled=True)  6.99 us
    pallas_call x1, Pallas kernels, run_forward(): pl.pallas_call(forward_kernel, name='forward', out_shape=(jax.ShapeDtypeS...  6.78 us
  transfers between devices with their start and end apart: 10, of which 4 were waited for; matrix products, arithmetic and copies ran while one was open for 2% of the time, Pallas kernels for 2%

profile of v8, /device:TPU:1, one launch (start us, length us, event | category | flops | bytes accessed | tf_op | source)
XLA Modules:
  0.0 116.5 jit_solution(3950641448338259802)
XLA Ops:
  0.7 0.9 copy.15
  1.6 3.3 %collective-permute-start.1 = (bf16[8,32,128]{2,1,0:T(8,128)(2,1)S(1)}, bf16[8,32,128]{2,1,0:T(8,128)(2,1)S(1)}, u32[]{:S(2)}, u32[]{:S(2)}) collective-permute-start(bf16[8,32,128]{2,1,0:T(8,128)(2,1)S(1)} %bitcast.22), channel_id=1, source_target_pairs={{1,0},{2,1},{3,2},{4,3},{5,4},{6,5},{7,6},{8,7},{9,8},{10,9},{11,1... | collective-permute-start | bytes 196616 | tf_op jit(solution)/shard_map/ppermute | solution.py:699
  4.9 4.6 %collective-permute-start = (bf16[8,32,128]{2,1,0:T(8,128)(2,1)S(1)}, bf16[8,32,128]{2,1,0:T(8,128)(2,1)S(1)}, u32[]{:S(2)}, u32[]{:S(2)}) collective-permute-start(bf16[8,32,128]{2,1,0:T(8,128)(2,1)S(1)} %bitcast.23), channel_id=1, source_target_pairs={{0,1},{1,2},{2,3},{3,4},{4,5},{5,6},{6,7},{7,8},{8,9},{9,10},{10,1... | collective-permute-start | bytes 196616 | tf_op jit(solution)/shard_map/ppermute | solution.py:699
  9.6 0.0 copy-start
  9.6 0.7 copy-done
  10.3 0.7 deal.1
  11.0 7.9 %all-to-all-start = ((bf16[16,8,128]{2,1,0:T(8,128)(2,1)}), bf16[16,8,128]{2,1,0:T(8,128)(2,1)S(1)}, u32[]{:S(2)}, u32[]{:S(2)}) async-start(bf16[16,8,128]{2,1,0:T(8,128)(2,1)} %deal.1), calls=%async_computation | async-start | bytes 65536 | tf_op jit(solution)/shard_map/all_to_all | solution.py:707
  18.9 1.0 convert_bitcast_fusion.k2
  19.9 0.8 convert_bitcast_fusion.1.k1
  20.7 0.1 pad.16.clone
  20.8 0.1 maximum_maximum_fusion.mid
  20.9 1.3 %collective-permute-start.3 = (bf16[8,96,128]{2,1,0:T(8,128)(2,1)S(1)}, bf16[8,96,128]{2,1,0:T(8,128)(2,1)S(1)}, u32[]{:S(2)}, u32[]{:S(2)}) collective-permute-start(bf16[8,96,128]{2,1,0:T(8,128)(2,1)S(1)} %maximum_maximum_fusion.mid), channel_id=1, source_target_pairs={{16,0},{32,16},{48,32},{64,48},{80,64},{96,80},{112,96},{17,1},{33... | collective-permute-start | bytes 589832 | tf_op jit(solution)/shard_map/ppermute | solution.py:699
  22.2 4.2 %collective-permute-start.2 = (bf16[8,96,128]{2,1,0:T(8,128)(2,1)S(1)}, bf16[8,96,128]{2,1,0:T(8,128)(2,1)S(1)}, u32[]{:S(2)}, u32[]{:S(2)}) collective-permute-start(bf16[8,96,128]{2,1,0:T(8,128)(2,1)S(1)} %maximum_maximum_fusion.mid), channel_id=1, source_target_pairs={{0,16},{16,32},{32,48},{48,64},{64,80},{80,96},{96,112},{1,17},{17... | collective-permute-start | bytes 589832 | tf_op jit(solution)/shard_map/ppermute | solution.py:699
  26.5 4.0 %collective-permute-done.2.top = bf16[8,96,128]{2,1,0:T(8,128)(2,1)S(1)} collective-permute-done((bf16[8,96,128]{2,1,0:T(8,128)(2,1)S(1)}, bf16[8,96,128]{2,1,0:T(8,128)(2,1)S(1)}, u32[]{:S(2)}, u32[]{:S(2)}) %collective-permute-start.2) | collective-permute-done | bytes 196640 | tf_op jit(solution)/shard_map/ppermute | solution.py:699
  30.5 6.8 %forward.1 = (bf16[128,128]{1,0:T(8,128)(2,1)S(1)}, bf16[128,128]{1,0:T(8,128)(2,1)S(1)}, bf16[4,4,16,128]{3,2,1,0:T(8,128)(2,1)S(1)}, f32[8,4,32,256]{3,2,1,0:T...) custom-call(bf16[8,96,128]{2,1,0:T(8,128)(2,1)S(1)} %collective-perm, ...), custom_call_target="tpu_custom_call" | custom-call | flops 5000000000 | bytes 8000000 | tf_op jit(solution)/shard_map/forward/pallas_call | solution.py:250
  37.2 5.7 %collective-permute-start.4 = (bf16[128,128]{1,0:T(8,128)(2,1)S(1)}, bf16[128,128]{1,0:T(8,128)(2,1)S(1)}, u32[]{:S(2)}, u32[]{:S(2)}) collective-permute-start(bf16[128,128]{1,0:T(8,128)(2,1)S(1)} %get-tuple-element.32), channel_id=1, source_target_pairs={{0,1},{1,2},{2,3},{3,4},{4,5},{5,6},{6,7},{7,8},{8,9},{9,10},{10,1... | collective-permute-start | bytes 98312 | tf_op jit(solution)/shard_map/ppermute | solution.py:699
  42.9 1.9 %collective-permute-start.5 = (bf16[128,128]{1,0:T(8,128)(2,1)S(1)}, bf16[128,128]{1,0:T(8,128)(2,1)S(1)}, u32[]{:S(2)}, u32[]{:S(2)}) collective-permute-start(bf16[128,128]{1,0:T(8,128)(2,1)S(1)} %get-tuple-element.34), channel_id=1, source_target_pairs={{1,0},{2,1},{3,2},{4,3},{5,4},{6,5},{7,6},{8,7},{9,8},{10,9},{11,1... | collective-permute-start | bytes 98312 | tf_op jit(solution)/shard_map/ppermute | solution.py:699
  44.9 4.8 %collective-permute-done.5.upper = bf16[128,128]{1,0:T(8,128)(2,1)S(1)} collective-permute-done((bf16[128,128]{1,0:T(8,128)(2,1)S(1)}, bf16[128,128]{1,0:T(8,128)(2,1)S(1)}, u32[]{:S(2)}, u32[]{:S(2)}) %collective-permute-start.5) | collective-permute-done | bytes 32800 | tf_op jit(solution)/shard_map/ppermute | solution.py:699
  49.7 0.3 weave.1
  49.9 4.1 %collective-permute-start.6 = (bf16[304,128]{1,0:T(8,128)(2,1)S(1)}, bf16[304,128]{1,0:T(8,128)(2,1)S(1)}, u32[]{:S(2)}, u32[]{:S(2)}) collective-permute-start(bf16[304,128]{1,0:T(8,128)(2,1)S(1)} %get-tuple-element.36), channel_id=1, source_target_pairs={{0,16},{16,32},{32,48},{48,64},{64,80},{80,96},{96,112},{1,17},{17... | collective-permute-start | bytes 233480 | tf_op jit(solution)/shard_map/ppermute | solution.py:699
  54.1 1.3 %collective-permute-start.7 = (bf16[304,128]{1,0:T(8,128)(2,1)S(1)}, bf16[304,128]{1,0:T(8,128)(2,1)S(1)}, u32[]{:S(2)}, u32[]{:S(2)}) collective-permute-start(bf16[304,128]{1,0:T(8,128)(2,1)S(1)} %get-tuple-element.37), channel_id=1, source_target_pairs={{16,0},{32,16},{48,32},{64,48},{80,64},{96,80},{112,96},{17,1},{33... | collective-permute-start | bytes 233480 | tf_op jit(solution)/shard_map/ppermute | solution.py:699
  55.4 1.3 %own.1 = (bf16[16,120,128]{2,1,0:T(8,128)(2,1)S(1)}, f32[1,128]{1,0:T(1,128)S(1)}, bf16[9,256,256]{2,1,0:T(8,128)(2,1)S(1)}, f32[1,256]{1,0:T(1,128)S(1)}) custom-call(bf16[4,4,16,128]{3,2,1,0:T(8,128)(2,1)S(1)} %get-tuple-element.33.hidden2.middle, bf16[48,128]{1,0:T(8,128)(2,1)S(1)} %get-tuple-element.38.own_cot, bf16[27,64,128]{2,1,0:T(8,128)(2,1)S(1)} %bitcast.21, ...), custom_call_target="tpu_custom_call" | custom-call | flops 150000000 | bytes 4000000 | tf_op jit(solution)/shard_map/own/pallas_call | solution.py:399
  56.7 2.7 %collective-permute-done.7.after = bf16[304,128]{1,0:T(8,128)(2,1)S(1)} collective-permute-done((bf16[304,128]{1,0:T(8,128)(2,1)S(1)}, bf16[304,128]{1,0:T(8,128)(2,1)S(1)}, u32[]{:S(2)}, u32[]{:S(2)}) %collective-permute-start.7) | collective-permute-done | bytes 77856 | tf_op jit(solution)/shard_map/ppermute | solution.py:699
  59.4 5.0 %backward.1 = bf16[16,152,128]{2,1,0:T(8,128)(2,1)S(1)} custom-call(bf16[304,128]{1,0:T(8,128)(2,1)S(1)} %collective-permute-done.6.before, bf16[128,128]{1,0:T(8,128)(2,1)S(1)} %collective-permute-done.4.lower, bf16[4,4,16,128]{3,2,1,0:T(8,128)(2,1)S(1)} %get-tuple-element.33.hidden2.middle, bf16[128,128]{1,0:T(8,128)(2,1)S(1)} %collective-permute-done.5.upper, ...), custom_call_target="tpu_custom_call" | custom-call | tf_op jit(solution)/shard_map/backward/pallas_call | solution.py:572
  64.4 18.6 %all_to_all.20.received = bf16[16,152,128]{2,1,0:T(8,128)(2,1)S(1)} all-to-all(bf16[16,152,128]{2,1,0:T(8,128)(2,1)S(1)} %backward.1), channel_id=1, replica_groups=mesh['gy'=8,'gz'=16] {'gz'}, dimensions={0} | all-to-all | bytes 1245184 | tf_op jit(solution)/shard_map/all_to_all | solution.py:728
  83.0 0.7 sum.1
  83.8 18.1 %all_to_all.21.column = bf16[8,144,128]{2,1,0:T(8,128)(2,1)S(1)} all-to-all(bf16[8,144,128]{2,1,0:T(8,128)(2,1)S(1)} %get-tuple-element.49), channel_id=1, replica_groups=mesh['gy'=8,'gz'=16] {'gy'}, dimensions={0} | all-to-all | bytes 589824 | tf_op jit(solution)/shard_map/all_to_all | solution.py:730
  101.9 0.7 share.1
  102.5 5.4 %all-to-all-start.3 = ((bf16[16,32,128]{2,1,0:T(8,128)(2,1)}), bf16[16,32,128]{2,1,0:T(8,128)(2,1)S(1)}, u32[]{:S(2)}, u32[]{:S(2)}) async-start(bf16[16,32,128]{2,1,0:T(8,128)(2,1)} %share.1), calls=%async_computation.3 | async-start | bytes 262144 | tf_op jit(solution)/shard_map/all_to_all | solution.py:731
  107.9 0.7 third.1
  108.6 7.0 %all-to-all-done.3.shared = bf16[16,32,128]{2,1,0:T(8,128)(2,1)S(1)} async-done(((bf16[16,32,128]{2,1,0:T(8,128)(2,1)}), bf16[16,32,128]{2,1,0:T(8,128)(2,1)S(1)}, u32[]{:S(2)}, u32[]{:S(2)}) %all-to-all-start.3) | async-done | bytes 131104 | tf_op jit(solution)/shard_map/all_to_all | solution.py:731
  115.6 0.9 unpack.1
  (18 shorter events, 0.1 us)
Async XLA Ops:
  0.6 25.7 %copy-start.3 = (f32[64]{0:T(128)S(1)}, f32[64]{0:T(128)}, u32[]{:S(2)}) copy-start(f32[64]{0:T(128)} %param.12) | copy-start | bytes 772
  0.6 25.7 %copy-start.4 = (f32[32]{0:T(128)S(1)}, f32[32]{0:T(128)}, u32[]{:S(2)}) copy-start(f32[32]{0:T(128)} %param.10) | copy-start | bytes 388
  0.7 25.8 %copy-start.2 = (f32[128]{0:T(128)S(1)}, f32[128]{0:T(128)}, u32[]{:S(2)}) copy-start(f32[128]{0:T(128)} %param.14) | copy-start | bytes 1540
  1.6 19.2 %collective-permute-start.1 = (bf16[8,32,128]{2,1,0:T(8,128)(2,1)S(1)}, bf16[8,32,128]{2,1,0:T(8,128)(2,1)S(1)}, u32[]{:S(2)}, u32[]{:S(2)}) collective-permute-start(bf16[8,32,128]{2,1,0:T(8,128)(2,1)S(1)} %bitcast.22), channel_id=1, source_target_pairs={{1,0},{2,1},{3,2},{4,3},{5,4},{6,5},{7,6},{8,7},{9,8},{10,9},{11,1... | collective-permute-start | bytes 196616 | tf_op jit(solution)/shard_map/ppermute | solution.py:699
  4.9 15.8 %collective-permute-start = (bf16[8,32,128]{2,1,0:T(8,128)(2,1)S(1)}, bf16[8,32,128]{2,1,0:T(8,128)(2,1)S(1)}, u32[]{:S(2)}, u32[]{:S(2)}) collective-permute-start(bf16[8,32,128]{2,1,0:T(8,128)(2,1)S(1)} %bitcast.23), channel_id=1, source_target_pairs={{0,1},{1,2},{2,3},{3,4},{4,5},{5,6},{6,7},{7,8},{8,9},{9,10},{10,1... | collective-permute-start | bytes 196616 | tf_op jit(solution)/shard_map/ppermute | solution.py:699
  9.6 0.8 copy-start
  11.0 15.4 %all-to-all-start = ((bf16[16,8,128]{2,1,0:T(8,128)(2,1)}), bf16[16,8,128]{2,1,0:T(8,128)(2,1)S(1)}, u32[]{:S(2)}, u32[]{:S(2)}) async-start(bf16[16,8,128]{2,1,0:T(8,128)(2,1)} %deal.1), calls=%async_computation | async-start | bytes 65536 | tf_op jit(solution)/shard_map/all_to_all | solution.py:707
  20.9 9.6 %collective-permute-start.3 = (bf16[8,96,128]{2,1,0:T(8,128)(2,1)S(1)}, bf16[8,96,128]{2,1,0:T(8,128)(2,1)S(1)}, u32[]{:S(2)}, u32[]{:S(2)}) collective-permute-start(bf16[8,96,128]{2,1,0:T(8,128)(2,1)S(1)} %maximum_maximum_fusion.mid), channel_id=1, source_target_pairs={{16,0},{32,16},{48,32},{64,48},{80,64},{96,80},{112,96},{17,1},{33... | collective-permute-start | bytes 589832 | tf_op jit(solution)/shard_map/ppermute | solution.py:699
  22.2 8.3 %collective-permute-start.2 = (bf16[8,96,128]{2,1,0:T(8,128)(2,1)S(1)}, bf16[8,96,128]{2,1,0:T(8,128)(2,1)S(1)}, u32[]{:S(2)}, u32[]{:S(2)}) collective-permute-start(bf16[8,96,128]{2,1,0:T(8,128)(2,1)S(1)} %maximum_maximum_fusion.mid), channel_id=1, source_target_pairs={{0,16},{16,32},{32,48},{48,64},{64,80},{80,96},{96,112},{1,17},{17... | collective-permute-start | bytes 589832 | tf_op jit(solution)/shard_map/ppermute | solution.py:699
  26.4 28.9 %copy-start.1 = (bf16[27,128,64]{1,2,0:T(8,128)(2,1)S(1)}, bf16[27,128,64]{1,2,0:T(8,128)(2,1)}, u32[]{:S(2)}) copy-start(bf16[27,128,64]{1,2,0:T(8,128)(2,1)} %param.13) | copy-start | bytes 1327108
  37.2 7.6 %collective-permute-start.4 = (bf16[128,128]{1,0:T(8,128)(2,1)S(1)}, bf16[128,128]{1,0:T(8,128)(2,1)S(1)}, u32[]{:S(2)}, u32[]{:S(2)}) collective-permute-start(bf16[128,128]{1,0:T(8,128)(2,1)S(1)} %get-tuple-element.32), channel_id=1, source_target_pairs={{0,1},{1,2},{2,3},{3,4},{4,5},{5,6},{6,7},{7,8},{8,9},{9,10},{10,1... | collective-permute-start | bytes 98312 | tf_op jit(solution)/shard_map/ppermute | solution.py:699
  42.9 6.7 %collective-permute-start.5 = (bf16[128,128]{1,0:T(8,128)(2,1)S(1)}, bf16[128,128]{1,0:T(8,128)(2,1)S(1)}, u32[]{:S(2)}, u32[]{:S(2)}) collective-permute-start(bf16[128,128]{1,0:T(8,128)(2,1)S(1)} %get-tuple-element.34), channel_id=1, source_target_pairs={{1,0},{2,1},{3,2},{4,3},{5,4},{6,5},{7,6},{8,7},{9,8},{10,9},{11,1... | collective-permute-start | bytes 98312 | tf_op jit(solution)/shard_map/ppermute | solution.py:699
  49.9 6.8 %collective-permute-start.6 = (bf16[304,128]{1,0:T(8,128)(2,1)S(1)}, bf16[304,128]{1,0:T(8,128)(2,1)S(1)}, u32[]{:S(2)}, u32[]{:S(2)}) collective-permute-start(bf16[304,128]{1,0:T(8,128)(2,1)S(1)} %get-tuple-element.36), channel_id=1, source_target_pairs={{0,16},{16,32},{32,48},{48,64},{64,80},{80,96},{96,112},{1,17},{17... | collective-permute-start | bytes 233480 | tf_op jit(solution)/shard_map/ppermute | solution.py:699
  54.1 5.3 %collective-permute-start.7 = (bf16[304,128]{1,0:T(8,128)(2,1)S(1)}, bf16[304,128]{1,0:T(8,128)(2,1)S(1)}, u32[]{:S(2)}, u32[]{:S(2)}) collective-permute-start(bf16[304,128]{1,0:T(8,128)(2,1)S(1)} %get-tuple-element.37), channel_id=1, source_target_pairs={{16,0},{32,16},{48,32},{64,48},{80,64},{96,80},{112,96},{17,1},{33... | collective-permute-start | bytes 233480 | tf_op jit(solution)/shard_map/ppermute | solution.py:699
  102.5 13.1 %all-to-all-start.3 = ((bf16[16,32,128]{2,1,0:T(8,128)(2,1)}), bf16[16,32,128]{2,1,0:T(8,128)(2,1)S(1)}, u32[]{:S(2)}, u32[]{:S(2)}) async-start(bf16[16,32,128]{2,1,0:T(8,128)(2,1)} %share.1), calls=%async_computation.3 | async-start | bytes 262144 | tf_op jit(solution)/shard_map/all_to_all | solution.py:731

commit v9 on v7

--- a/solution.py
+++ b/solution.py
@@ -67,15 +67,15 @@
 
 
 def forward_kernel(
-    top, mid, bot, cot, k1, b1, k2, b2,
+    top, mid, bot, cot, k1, k2, biases,
     to_next, to_previous, hidden2, own_cot, ratio2, patches1, ratio1, fields, w2,
     w1, pick, left, field, turned, pre1, first, spread, pre2, second,
 ):
     lay_weights1(k1, w1)
     lay_weights2(k2, w2)
     lay_pick(pick)
-    bias1 = jnp.concatenate([b1[...]] * 8, axis=1)
-    bias2 = jnp.concatenate([b2[...]] * 4, axis=1)
+    bias1 = jnp.concatenate([biases[0:1, :32]] * 8, axis=1)
+    bias2 = jnp.concatenate([biases[1:2, :64]] * 4, axis=1)
     base_y, base_z = lax.axis_index("gy"), lax.axis_index("gz")
     size_y, size_z = lax.axis_size("gy"), lax.axis_size("gz")
 
@@ -94,87 +94,80 @@
             pieces.append(jnp.concatenate([rows[a : a + 16], rows[b : b + 16]], axis=1))
         left[target] = jnp.concatenate(pieces, axis=0).astype(BF16)
 
-    def lay_top(step, carry):
-        lay(top, step + 1, step)
-        return carry
-
-    def lay_mid(step, carry):
-        lay(mid, step, step + 7)
-        return carry
-
-    def lay_bot(step, carry):
-        lay(bot, step, step + 15)
-        return carry
-
-    lax.fori_loop(0, 7, lay_top, 0)
-    lax.fori_loop(0, 8, lay_mid, 0)
-    lax.fori_loop(0, 7, lay_bot, 0)
-
-    def sift(step, carry):
-        block = left[pl.ds(2 * step, 2)].reshape(160, 256)
-        out = dot(block, pick[...]).astype(BF16).reshape(2, 5, 16, 512)
-        for parity in range(2):
+    for row in range(22):
+        source, index = (top, row + 1) if row < 7 else ((mid, row - 7) if row < 15 else (bot, row - 15))
+        lay(source, index, row)
+
+    for part in range(2):
+        block = left[part * 11 : part * 11 + 11].reshape(880, 256)
+        out = dot(block, pick[...]).astype(BF16).reshape(11, 5, 16, 512)
+        for step in range(11):
+            row = part * 11 + step
             for px in range(4):
-                at = (parity * 4 + px) * 16
+                at = (row % 2 * 4 + px) * 16
                 for k in range(5):
-                    field[step, at : at + 16, k * 128 : k * 128 + 128] = out[
-                        parity, k, :, px * 128 : px * 128 + 128
+                    field[row // 2, at : at + 16, k * 128 : k * 128 + 128] = out[
+                        step, k, :, px * 128 : px * 128 + 128
                     ]
-        turned[step] = field[step].T
-        return carry
-
-    lax.fori_loop(0, 11, sift, 0)
+    for pair in range(11):
+        turned[pair] = field[pair].T
     fields[...] = field[3:8, :, :256]
     first[:, :, 0:8] = jnp.zeros((10, 10, 8, 128), F32)
     first[:, :, 72:80] = jnp.zeros((10, 10, 8, 128), F32)
 
-    def block1(yw, carry):
-        stack = jnp.concatenate([turned[yw], turned[yw + 1]], axis=1)
-        pre1[...] = dot(stack, w1[...])
-        place = jnp.where((yw >= 3) & (yw < 7), yw - 3, 4)
-        for k, pair in enumerate(PAIRS):
-            for h, zw in enumerate(pair):
-                at = k * 128 + h * 64
-                pre = pre1[at : at + 64] + bias1
-                e = exps(pre)
-                total = e[:, :128] + e[:, 128:]
-                total = total + roll(total, 64, 1)
-                total = total + roll(total, 32, 1)
-                mean = total * 0.125
-                pooled = rounded(jnp.log(mean) * 0.5)
-                first[yw, zw + 3, 8:72] = pooled * inside(yw - 3, zw, 1)
-                if k < 2:
-                    share = 0.125 / mean
-                    share = jnp.concatenate([share, share], axis=1)
-                    ratio1[place, at : at + 64] = jnp.where(pre > 0, 1.0, SLOPE) * (e * share)
+    def block1(step, carry):
+        for part in range(5):
+            stack = jnp.concatenate([turned[5 * step + part], turned[5 * step + part + 1]], axis=1)
+            pre1[part] = dot(stack, w1[...])
+        for part in range(5):
+            yw = 5 * step + part
+            place = jnp.where((yw >= 3) & (yw < 7), yw - 3, 4)
+            for k, pair in enumerate(PAIRS):
+                for h, zw in enumerate(pair):
+                    at = k * 128 + h * 64
+                    pre = pre1[part, at : at + 64] + bias1
+                    e = exps(pre)
+                    total = e[:, :128] + e[:, 128:]
+                    total = total + roll(total, 64, 1)
+                    total = total + roll(total, 32, 1)
+                    mean = total * 0.125
+                    pooled = rounded(jnp.log(mean) * 0.5)
+                    first[yw, zw + 3, 8:72] = pooled * inside(yw - 3, zw, 1)
+                    if k < 2:
+                        share = 0.125 / mean
+                        share = jnp.concatenate([share, share], axis=1)
+                        ratio1[place, at : at + 64] = jnp.where(pre > 0, 1.0, SLOPE) * (e * share)
         return carry
 
-    lax.fori_loop(0, 10, block1, 0)
+    lax.fori_loop(0, 2, block1, 0)
 
     group1 = lane((32, 128)) // 32
 
-    def frame(yi, carry):
-        for zi in range(10):
-            part = first[yi, zi, pl.ds(7, 32, stride=2), :]
-            for px in range(1, 4):
-                part = jnp.where(group1 == px, first[yi, zi, pl.ds(7 + px, 32, stride=2), :], part)
-            spread[yi, zi] = part.astype(BF16)
+    def frame(step, carry):
+        for part in range(5):
+            yi = 5 * step + part
+            for zi in range(10):
+                value = first[yi, zi, pl.ds(7, 32, stride=2), :]
+                for px in range(1, 4):
+                    value = jnp.where(group1 == px, first[yi, zi, pl.ds(7 + px, 32, stride=2), :], value)
+                spread[yi, zi] = value.astype(BF16)
         return carry
 
-    lax.fori_loop(0, 10, frame, 0)
+    lax.fori_loop(0, 2, frame, 0)
     patches1[...] = spread[2:8, 2:8]
 
     half = lane((16, 128)) < 64
 
-    def block2(yp, carry):
+    for yp in range(4):
         columns = []
         for zo in range(4):
-            tiles = [spread[pl.ds(2 * yp + dy, 2), 2 * zo + pz] for dy in range(3) for pz in range(4)]
+            tiles = [spread[2 * yp + dy : 2 * yp + dy + 2, 2 * zo + pz] for dy in range(3) for pz in range(4)]
             columns.append(jnp.concatenate(tiles, axis=2)[:, None])
         block = jnp.concatenate(columns, axis=1).reshape(256, 1536)
-        pre2[...] = dot(block, w2[...].reshape(1536, 256)).reshape(2, 4, 32, 256)
+        pre2[yp] = dot(block, w2[...].reshape(1536, 256)).reshape(2, 4, 32, 256)
+    for yp in range(4):
         for zo in range(4):
-            pre = pre2[:, zo] + bias2
+            pre = pre2[yp, :, zo] + bias2
             e = exps(pre)
             both = e[0] + e[1]
             total = both[:, :128] + both[:, 128:]
@@ -183,20 +176,19 @@
             ok = inside(yp - 1, zo - 1, 2)
             share = (0.125 * ok) / mean
             share = jnp.concatenate([share, share], axis=1)
-            ratio2[pl.ds(2 * yp, 2), zo] = jnp.where(pre > 0, 1.0, SLOPE) * (e * share[None])
-            second[zo] = rounded(jnp.log(mean) * 0.5) * ok
-            even = second[zo, pl.ds(0, 16, stride=2), :]
-            odd = second[zo, pl.ds(1, 16, stride=2), :]
+            ratio2[2 * yp : 2 * yp + 2, zo] = jnp.where(pre > 0, 1.0, SLOPE) * (e * share[None])
+            second[yp, zo] = rounded(jnp.log(mean) * 0.5) * ok
+    for yp in range(4):
+        for zo in range(4):
+            even = second[yp, zo, pl.ds(0, 16, stride=2), :]
+            odd = second[yp, zo, pl.ds(1, 16, stride=2), :]
             hidden2[yp, zo] = jnp.where(half, even, odd).astype(BF16)
-        return carry
-
-    lax.fori_loop(0, 4, block2, 0)
-    to_next[0:128] = hidden2[:, 0:2].reshape(128, 128)
-    to_previous[0:128] = hidden2[:, 2:4].reshape(128, 128)
     own = cot[...].astype(F32).T.astype(BF16)
+    own_cot[...] = own
+    to_next[:128] = hidden2[:, 0:2].reshape(128, 128)
+    to_previous[:128] = hidden2[:, 2:4].reshape(128, 128)
     to_next[128:144] = own
     to_previous[128:144] = own
-    own_cot[...] = own
 
 
 def lay_weights1(taps, out):
@@ -221,14 +213,14 @@
 
 
 def lay_weights2(taps, out):
-    zero = jnp.zeros((32, 64), BF16)
+    zero = jnp.zeros((32, 64), F32)
     for dy in range(3):
         out[dy, 384:512, 0:128] = jnp.zeros((128, 128), BF16)
         out[dy, 0:128, 128:256] = jnp.zeros((128, 128), BF16)
         for dz in range(3):
             for px in range(4):
                 sides = [taps[(px - qx) * 9 + dy * 3 + dz] if 0 <= px - qx < 3 else zero for qx in range(2)]
-                tile = jnp.concatenate(sides, axis=1)
+                tile = jnp.concatenate(sides, axis=1).astype(BF16)
                 for qz in range(2):
                     at = (dz + qz) * 128 + px * 32
                     out[dy, at : at + 32, qz * 128 : qz * 128 + 128] = tile
@@ -262,17 +254,18 @@
         ),
         in_specs=[VMEM] * len(operands),
         out_specs=(VMEM,) * 9,
+        cost_estimate=pl.CostEstimate(flops=5000000000, bytes_accessed=8000000, transcendentals=8000000),
         scratch_shapes=[
             pltpu.VMEM((256, 256), BF16),
             pltpu.VMEM((256, 512), BF16),
             pltpu.VMEM((22, 80, 256), BF16),
             pltpu.VMEM((11, 128, 640), BF16),
             pltpu.VMEM((11, 640, 128), BF16),
-            pltpu.VMEM((640, 256), F32),
+            pltpu.VMEM((5, 640, 256), F32),
             pltpu.VMEM((10, 10, 80, 128), F32),
             pltpu.VMEM((10, 10, 32, 128), BF16),
-            pltpu.VMEM((2, 4, 32, 256), F32),
-            pltpu.VMEM((4, 32, 128), F32),
+            pltpu.VMEM((4, 2, 4, 32, 256), F32),
+            pltpu.VMEM((4, 4, 32, 128), F32),
         ],
         compiler_params=pltpu.CompilerParams(vmem_limit_bytes=LIMIT),
     )(*operands)
@@ -319,11 +312,11 @@
     return mean, (jnp.where(pre > 0, 1.0, SLOPE) * (e * share)).astype(BF16)
 
 
-def own_kernel(hidden2, own_cot, k3, b3, packed, shift3, w3, wide3, patches2, pre3, turned):
+def own_kernel(hidden2, own_cot, k3, biases, packed, shift3, w3, wide3, patches2, pre3, turned):
     groups = packed.shape[0]
     wide = 128 // groups
     lay_weights3(k3, w3)
-    wide3[...] = jnp.concatenate([b3[...]] * 2, axis=1)
+    wide3[...] = jnp.concatenate([biases[2:3]] * 2, axis=1)
     for y in range(4):
         for z in range(4):
             lay_patches2(hidden2[y, z], patches2.at[y, z])
@@ -486,7 +479,7 @@
         return value + roll(value, 64, 1)
 
 
-    def gather1(y, carry):
+    for y in range(4):
         def part(zo, pz):
             return patch1[y, zo, :, pz * 128 : pz * 128 + 128]
 
@@ -495,14 +488,11 @@
         )
         for z, value in enumerate(sums):
             value = rounded(value + roll(jnp.where(low_half, up(value), down(value)), 64, 1))
-            grad1[z, pl.ds(0, 32, stride=2), :] = widen(value, 1)
-            grad1[z, pl.ds(1, 32, stride=2), :] = widen(value, 2)
-        value = grad1[...].reshape(256, 128)
+            grad1[y, z, pl.ds(0, 32, stride=2), :] = widen(value, 1)
+            grad1[y, z, pl.ds(1, 32, stride=2), :] = widen(value, 2)
+        value = grad1[y].reshape(256, 128)
         value = jnp.concatenate([value, value], axis=1)
         delta1[y] = (value * ratio1[y]).astype(BF16)
-        return carry
-
-    lax.fori_loop(0, 4, gather1, 0)
 
     bias1 = delta1[...].astype(F32).sum(axis=0).sum(axis=0, keepdims=True)
     bias1 = bias1[:, :128] + bias1[:, 128:]
@@ -554,7 +544,7 @@
             pltpu.VMEM((6, 4, 32, 256), BF16),
             pltpu.VMEM((4, 2, 32, 512), F32),
             pltpu.VMEM((2, 4, 32, 128), F32),
-            pltpu.VMEM((4, 64, 128), F32),
+            pltpu.VMEM((4, 4, 64, 128), F32),
             pltpu.VMEM((4, 256, 256), BF16),
         ],
         compiler_params=pltpu.CompilerParams(vmem_limit_bytes=LIMIT),
@@ -675,17 +665,20 @@
 
     tile = universe.transpose(1, 2, 0, 3).reshape(8, 32, 128)
     cot = lax.all_to_all(cotangent[:, 0].transpose(1, 0, 2), "gz", 0, 0, tiled=True).reshape(128, 16)
+    biases = jnp.stack([jnp.pad(bias1, (0, 96)), jnp.pad(bias2, (0, 64)), bias3])
     lower, upper = both_ways(tile, tile, "gz")
     strip = jnp.concatenate([lower[:, 4:], tile, upper[:, :28], jnp.zeros((8, 8, 128), BF16)], axis=1)
+    strip, kernel1, kernel2 = lax.optimization_barrier((strip, kernel1, kernel2))
     top, bottom = both_ways(strip, strip, "gy")
 
-    k1, k2, k3 = kernel1.transpose(0, 2, 1), kernel2.transpose(0, 2, 1), kernel3.transpose(0, 2, 1)
+    k1, k2 = kernel1.transpose(0, 2, 1).astype(F32), kernel2.transpose(0, 2, 1).astype(F32)
+    k3 = kernel3.transpose(0, 2, 1)
     to_next, to_previous, hidden2, own_cot, ratio2, patches1, ratio1, fields, w2 = run_forward(
-        top, strip, bottom, cot, k1, bias1[None], k2, bias2[None]
+        top, strip, bottom, cot, k1, k2, biases
     )
     lower, upper = both_ways(to_next, to_previous, "gz")
-    packed3, shift3, w3, wide3 = run_own(size_z, hidden2, own_cot, k3, bias3[None])
     row_next, row_previous = run_weave(lower, hidden2, upper, own_cot)
+    packed3, shift3, w3, wide3 = run_own(size_z, hidden2, own_cot, k3, biases)
     before, after = both_ways(row_next, row_previous, "gy")
     packed = run_backward(
         size_z,

time: 121 us -> 117 us (0.967)
  starting transfers between devices: 28.1 us -> 39.7 us
  blocking collectives: 46.7 us -> 36.7 us
  Pallas kernels: 20.3 us -> 16.2 us
  waiting for transfers between devices: 19.4 us -> 17.6 us
  local copies, waits for them, and re-layouts: 4.81 us -> 3.07 us
  other arithmetic: 0.1 us -> 1.76 us
    all_to_all x1 -> x0, blocking collectives: 13.3 us -> none  [shards(): lax.all_to_all(cotangent[:, 0].transpose(1, 0, 2), 'gz', 0, 0, tiled=True)]
    all_to_all x0 -> x1, starting transfers between devices: none -> 7.89 us  [shards(): lax.all_to_all(cotangent[:, 0].transpose(1, 0, 2), 'gz', 0, 0, tiled=True)]
    all_to_all x1, blocking collectives: 13.9 us -> 18.1 us  [shards(): column = lax.all_to_all(column, 'gy', 0, 0, tiled=True)]
    pallas_call x1, Pallas kernels: 10.9 us -> 7.54 us  [run_forward(): pl.pallas_call(forward_kernel, name='forward', out_shape=(jax.ShapeDtypeS...]
    ppermute x4, waiting for transfers between devices: 12.4 us -> 9.72 us  [both_ways(): lax.ppermute(to_previous, axis, back)]
    unnamed x13 -> x5, local copies, waits for them, and re-layouts: 3.77 us -> 1.39 us
    ppermute x4, starting transfers between devices: 16.3 us -> 18.6 us  [both_ways(): lax.ppermute(to_next, axis, forth)]
    ppermute x4, starting transfers between devices: 6.43 us -> 7.83 us  [both_ways(): lax.ppermute(to_previous, axis, back)]
  transfers between devices with their start and end apart: 9 -> 10, of which waited for: 4 -> 5; matrix products, arithmetic and copies ran while one was open for 1% -> 3% of each run, Pallas kernels for 2% -> 2%
where the time goes in v9:
time: 117 us; the launch traced here: 116 us
  starting transfers between devices  39.7 us (34%)
  blocking collectives  36.7 us (31%)
  waiting for transfers between devices  17.6 us (15%)
  Pallas kernels  16.2 us (14%)
  local copies, waits for them, and re-layouts  3.07 us (3%)
  other arithmetic  1.76 us (2%)
    all_to_all x1, blocking collectives, shards(): packed = lax.all_to_all(packed, 'gz', 0, 0, tiled=True)  18.6 us
    ppermute x4, starting transfers between devices, both_ways(): lax.ppermute(to_next, axis, forth)  18.6 us
    all_to_all x1, blocking collectives, shards(): column = lax.all_to_all(column, 'gy', 0, 0, tiled=True)  18.1 us
    ppermute x4, waiting for transfers between devices, both_ways(): lax.ppermute(to_previous, axis, back)  9.72 us
    all_to_all x1, starting transfers between devices, shards(): lax.all_to_all(cotangent[:, 0].transpose(1, 0, 2), 'gz', 0, 0, tiled=True)  7.89 us
    ppermute x4, starting transfers between devices, both_ways(): lax.ppermute(to_previous, axis, back)  7.83 us
    pallas_call x1, Pallas kernels, run_forward(): pl.pallas_call(forward_kernel, name='forward', out_shape=(jax.ShapeDtypeS...  7.54 us
    all_to_all x1, waiting for transfers between devices, shards(): shared = lax.all_to_all(run_share(column, size_z), 'gz', 0, 0, tiled=True)  6.99 us
  transfers between devices with their start and end apart: 10, of which 5 were waited for; matrix products, arithmetic and copies ran while one was open for 3% of the time, Pallas kernels for 2%

profile of v9, /device:TPU:1, one launch (start us, length us, event | category | flops | bytes accessed | tf_op | source)
XLA Modules:
  0.0 115.9 jit_solution(3427310177769594142)
XLA Ops:
  0.6 0.9 copy.18
  1.5 3.3 %collective-permute-start.1 = (bf16[8,32,128]{2,1,0:T(8,128)(2,1)S(1)}, bf16[8,32,128]{2,1,0:T(8,128)(2,1)S(1)}, u32[]{:S(2)}, u32[]{:S(2)}) collective-permute-start(bf16[8,32,128]{2,1,0:T(8,128)(2,1)S(1)} %bitcast.29), channel_id=1, source_target_pairs={{1,0},{2,1},{3,2},{4,3},{5,4},{6,5},{7,6},{8,7},{9,8},{10,9},{11,1... | collective-permute-start | bytes 196616 | tf_op jit(solution)/shard_map/ppermute | solution.py:659
  4.9 4.6 %collective-permute-start = (bf16[8,32,128]{2,1,0:T(8,128)(2,1)S(1)}, bf16[8,32,128]{2,1,0:T(8,128)(2,1)S(1)}, u32[]{:S(2)}, u32[]{:S(2)}) collective-permute-start(bf16[8,32,128]{2,1,0:T(8,128)(2,1)S(1)} %bitcast.30), channel_id=1, source_target_pairs={{0,1},{1,2},{2,3},{3,4},{4,5},{5,6},{6,7},{7,8},{8,9},{9,10},{10,1... | collective-permute-start | bytes 196616 | tf_op jit(solution)/shard_map/ppermute | solution.py:659
  9.5 1.4 %copy.22 = bf16[8,1,16,16]{3,0,2,1:T(8,128)(2,1)} copy(bf16[8,1,16,16]{3,2,1,0:T(8,128)(2,1)} %param.15) | data formatting | bytes 8192 | tf_op args[7]
  10.9 7.9 %all-to-all-start = ((bf16[16,8,16]{2,1,0:T(8,128)(2,1)}), bf16[16,8,16]{2,1,0:T(8,128)(2,1)S(1)}, u32[]{:S(2)}, u32[]{:S(2)}) async-start(bf16[16,8,16]{2,1,0:T(8,128)(2,1)} %bitcast.25), calls=%async_computation | async-start | bytes 65536 | tf_op jit(solution)/shard_map/all_to_all | solution.py:667
  18.8 0.1 pad.16.clone
  18.9 0.7 pad_bitcast_fusion
  19.6 0.7 pad_maximum_fusion.biases
  20.2 0.0 collective-permute-done.1
  20.3 0.1 maximum_maximum_fusion.mid
  20.4 1.3 %collective-permute-start.3 = (bf16[8,96,128]{2,1,0:T(8,128)(2,1)S(1)}, bf16[8,96,128]{2,1,0:T(8,128)(2,1)S(1)}, u32[]{:S(2)}, u32[]{:S(2)}) collective-permute-start(bf16[8,96,128]{2,1,0:T(8,128)(2,1)S(1)} %maximum_maximum_fusion.mid), channel_id=1, source_target_pairs={{16,0},{32,16},{48,32},{64,48},{80,64},{96,80},{112,96},{17,1},{33... | collective-permute-start | bytes 589832 | tf_op jit(solution)/shard_map/ppermute | solution.py:659
  21.7 4.2 %collective-permute-start.2 = (bf16[8,96,128]{2,1,0:T(8,128)(2,1)S(1)}, bf16[8,96,128]{2,1,0:T(8,128)(2,1)S(1)}, u32[]{:S(2)}, u32[]{:S(2)}) collective-permute-start(bf16[8,96,128]{2,1,0:T(8,128)(2,1)S(1)} %maximum_maximum_fusion.mid), channel_id=1, source_target_pairs={{0,16},{16,32},{32,48},{48,64},{64,80},{80,96},{96,112},{1,17},{17... | collective-permute-start | bytes 589832 | tf_op jit(solution)/shard_map/ppermute | solution.py:659
  25.9 1.0 convert_bitcast_fusion.k2
  26.9 2.2 %collective-permute-done.3.bot = bf16[8,96,128]{2,1,0:T(8,128)(2,1)S(1)} collective-permute-done((bf16[8,96,128]{2,1,0:T(8,128)(2,1)S(1)}, bf16[8,96,128]{2,1,0:T(8,128)(2,1)S(1)}, u32[]{:S(2)}, u32[]{:S(2)}) %collective-permute-start.3) | collective-permute-done | bytes 196640 | tf_op jit(solution)/shard_map/ppermute | solution.py:659
  29.1 0.9 collective-permute-done.2.top
  29.9 7.5 %forward.1 = (bf16[144,128]{1,0:T(8,128)(2,1)S(1)}, bf16[144,128]{1,0:T(8,128)(2,1)S(1)}, bf16[4,4,16,128]{3,2,1,0:T(8,128)(2,1)S(1)}, bf16[16,128]{1,0:T(8,128)...) custom-call(bf16[8,96,128]{2,1,0:T(8,128)(2,1)S(1)} %collective-perm, ...), custom_call_target="tpu_custom_call" | custom-call | flops 5000000000 | bytes 8000000 | tf_op jit(solution)/shard_map/forward/pallas_call | solution.py:241
  37.5 5.7 %collective-permute-start.4 = (bf16[144,128]{1,0:T(8,128)(2,1)S(1)}, bf16[144,128]{1,0:T(8,128)(2,1)S(1)}, u32[]{:S(2)}, u32[]{:S(2)}) collective-permute-start(bf16[144,128]{1,0:T(8,128)(2,1)S(1)} %get-tuple-element.35), channel_id=1, source_target_pairs={{0,1},{1,2},{2,3},{3,4},{4,5},{5,6},{6,7},{7,8},{8,9},{9,10},{10,1... | collective-permute-start | bytes 110600 | tf_op jit(solution)/shard_map/ppermute | solution.py:659
  43.2 1.9 %collective-permute-start.5 = (bf16[144,128]{1,0:T(8,128)(2,1)S(1)}, bf16[144,128]{1,0:T(8,128)(2,1)S(1)}, u32[]{:S(2)}, u32[]{:S(2)}) collective-permute-start(bf16[144,128]{1,0:T(8,128)(2,1)S(1)} %get-tuple-element.37), channel_id=1, source_target_pairs={{1,0},{2,1},{3,2},{4,3},{5,4},{6,5},{7,6},{8,7},{9,8},{10,9},{11,1... | collective-permute-start | bytes 110600 | tf_op jit(solution)/shard_map/ppermute | solution.py:659
  45.1 4.8 %collective-permute-done.5.upper = bf16[144,128]{1,0:T(8,128)(2,1)S(1)} collective-permute-done((bf16[144,128]{1,0:T(8,128)(2,1)S(1)}, bf16[144,128]{1,0:T(8,128)(2,1)S(1)}, u32[]{:S(2)}, u32[]{:S(2)}) %collective-permute-start.5) | collective-permute-done | bytes 36896 | tf_op jit(solution)/shard_map/ppermute | solution.py:659
  50.0 4.1 %collective-permute-start.6 = (bf16[304,128]{1,0:T(8,128)(2,1)S(1)}, bf16[304,128]{1,0:T(8,128)(2,1)S(1)}, u32[]{:S(2)}, u32[]{:S(2)}) collective-permute-start(bf16[304,128]{1,0:T(8,128)(2,1)S(1)} %get-tuple-element.39), channel_id=1, source_target_pairs={{0,16},{16,32},{32,48},{48,64},{64,80},{80,96},{96,112},{1,17},{17... | collective-permute-start | bytes 233480 | tf_op jit(solution)/shard_map/ppermute | solution.py:659
  54.1 1.3 %collective-permute-start.7 = (bf16[304,128]{1,0:T(8,128)(2,1)S(1)}, bf16[304,128]{1,0:T(8,128)(2,1)S(1)}, u32[]{:S(2)}, u32[]{:S(2)}) collective-permute-start(bf16[304,128]{1,0:T(8,128)(2,1)S(1)} %get-tuple-element.40), channel_id=1, source_target_pairs={{16,0},{32,16},{48,32},{64,48},{80,64},{96,80},{112,96},{17,1},{33... | collective-permute-start | bytes 233480 | tf_op jit(solution)/shard_map/ppermute | solution.py:659
  55.4 1.3 %own.1 = (bf16[16,120,128]{2,1,0:T(8,128)(2,1)S(1)}, f32[1,128]{1,0:T(1,128)S(1)}, bf16[9,256,256]{2,1,0:T(8,128)(2,1)S(1)}, f32[1,256]{1,0:T(1,128)S(1)}) custom-call(bf16[4,4,16,128]{3,2,1,0:T(8,128)(2,1)S(1)} %get-tuple-element.36.hidden2.middle, bf16[16,128]{1,0:T(8,128)(2,1)S(1)} %get-tuple-element.38.own_cot, bf16[27,64,128]{2,1,0:T(8,128)(2,1)S(1)} %bitcast.28, ...), custom_call_target="tpu_custom_call" | custom-call | flops 150000000 | bytes 4000000 | tf_op jit(solution)/shard_map/own/pallas_call | solution.py:362
  56.7 2.7 %collective-permute-done.7.after = bf16[304,128]{1,0:T(8,128)(2,1)S(1)} collective-permute-done((bf16[304,128]{1,0:T(8,128)(2,1)S(1)}, bf16[304,128]{1,0:T(8,128)(2,1)S(1)}, u32[]{:S(2)}, u32[]{:S(2)}) %collective-permute-start.7) | collective-permute-done | bytes 77856 | tf_op jit(solution)/shard_map/ppermute | solution.py:659
  59.4 4.3 %backward.1 = bf16[16,152,128]{2,1,0:T(8,128)(2,1)S(1)} custom-call(bf16[304,128]{1,0:T(8,128)(2,1)S(1)} %collective-permute-done.6.before, bf16[144,128]{1,0:T(8,128)(2,1)S(1)} %collective-permute-done.4.lower, bf16[4,4,16,128]{3,2,1,0:T(8,128)(2,1)S(1)} %get-tuple-element.36.hidden2.middle, bf16[144,128]{1,0:T(8,128)(2,1)S(1)} %collective-permute-done.5.upper, ...), custom_call_target="tpu_custom_call" | custom-call | tf_op jit(solution)/shard_map/backward/pallas_call | solution.py:532
  63.8 18.6 %all_to_all.20.received = bf16[16,152,128]{2,1,0:T(8,128)(2,1)S(1)} all-to-all(bf16[16,152,128]{2,1,0:T(8,128)(2,1)S(1)} %backward.1), channel_id=1, replica_groups=mesh['gy'=8,'gz'=16] {'gz'}, dimensions={0} | all-to-all | bytes 1245184 | tf_op jit(solution)/shard_map/all_to_all | solution.py:688
  82.4 0.7 sum.1
  83.1 18.1 %all_to_all.21.column = bf16[8,144,128]{2,1,0:T(8,128)(2,1)S(1)} all-to-all(bf16[8,144,128]{2,1,0:T(8,128)(2,1)S(1)} %get-tuple-element.51), channel_id=1, replica_groups=mesh['gy'=8,'gz'=16] {'gy'}, dimensions={0} | all-to-all | bytes 589824 | tf_op jit(solution)/shard_map/all_to_all | solution.py:690
  101.2 0.7 share.1
  101.9 5.4 %all-to-all-start.3 = ((bf16[16,32,128]{2,1,0:T(8,128)(2,1)}), bf16[16,32,128]{2,1,0:T(8,128)(2,1)S(1)}, u32[]{:S(2)}, u32[]{:S(2)}) async-start(bf16[16,32,128]{2,1,0:T(8,128)(2,1)} %share.1), calls=%async_computation.3 | async-start | bytes 262144 | tf_op jit(solution)/shard_map/all_to_all | solution.py:691
  107.3 0.7 third.1
  108.0 7.0 %all-to-all-done.3.shared = bf16[16,32,128]{2,1,0:T(8,128)(2,1)S(1)} async-done(((bf16[16,32,128]{2,1,0:T(8,128)(2,1)}), bf16[16,32,128]{2,1,0:T(8,128)(2,1)S(1)}, u32[]{:S(2)}, u32[]{:S(2)}) %all-to-all-start.3) | async-done | bytes 131104 | tf_op jit(solution)/shard_map/all_to_all | solution.py:691
  115.0 0.9 unpack.1
  (12 shorter events, 0.1 us)
Async XLA Ops:
  0.6 26.2 %copy-start.1 = (bf16[27,32,4]{1,2,0:T(4,128)(2,1)S(1)}, bf16[27,32,4]{1,2,0:T(4,128)(2,1)}, u32[]{:S(2)}) copy-start(bf16[27,32,4]{1,2,0:T(4,128)(2,1)} %param.9) | copy-start | bytes 20740
  1.5 18.7 %collective-permute-start.1 = (bf16[8,32,128]{2,1,0:T(8,128)(2,1)S(1)}, bf16[8,32,128]{2,1,0:T(8,128)(2,1)S(1)}, u32[]{:S(2)}, u32[]{:S(2)}) collective-permute-start(bf16[8,32,128]{2,1,0:T(8,128)(2,1)S(1)} %bitcast.29), channel_id=1, source_target_pairs={{1,0},{2,1},{3,2},{4,3},{5,4},{6,5},{7,6},{8,7},{9,8},{10,9},{11,1... | collective-permute-start | bytes 196616 | tf_op jit(solution)/shard_map/ppermute | solution.py:659
  4.9 15.3 %collective-permute-start = (bf16[8,32,128]{2,1,0:T(8,128)(2,1)S(1)}, bf16[8,32,128]{2,1,0:T(8,128)(2,1)S(1)}, u32[]{:S(2)}, u32[]{:S(2)}) collective-permute-start(bf16[8,32,128]{2,1,0:T(8,128)(2,1)S(1)} %bitcast.30), channel_id=1, source_target_pairs={{0,1},{1,2},{2,3},{3,4},{4,5},{5,6},{6,7},{7,8},{8,9},{9,10},{10,1... | collective-permute-start | bytes 196616 | tf_op jit(solution)/shard_map/ppermute | solution.py:659
  10.9 16.0 %all-to-all-start = ((bf16[16,8,16]{2,1,0:T(8,128)(2,1)}), bf16[16,8,16]{2,1,0:T(8,128)(2,1)S(1)}, u32[]{:S(2)}, u32[]{:S(2)}) async-start(bf16[16,8,16]{2,1,0:T(8,128)(2,1)} %bitcast.25), calls=%async_computation | async-start | bytes 65536 | tf_op jit(solution)/shard_map/all_to_all | solution.py:667
  20.4 8.7 %collective-permute-start.3 = (bf16[8,96,128]{2,1,0:T(8,128)(2,1)S(1)}, bf16[8,96,128]{2,1,0:T(8,128)(2,1)S(1)}, u32[]{:S(2)}, u32[]{:S(2)}) collective-permute-start(bf16[8,96,128]{2,1,0:T(8,128)(2,1)S(1)} %maximum_maximum_fusion.mid), channel_id=1, source_target_pairs={{16,0},{32,16},{48,32},{64,48},{80,64},{96,80},{112,96},{17,1},{33... | collective-permute-start | bytes 589832 | tf_op jit(solution)/shard_map/ppermute | solution.py:659
  21.7 8.3 %collective-permute-start.2 = (bf16[8,96,128]{2,1,0:T(8,128)(2,1)S(1)}, bf16[8,96,128]{2,1,0:T(8,128)(2,1)S(1)}, u32[]{:S(2)}, u32[]{:S(2)}) collective-permute-start(bf16[8,96,128]{2,1,0:T(8,128)(2,1)S(1)} %maximum_maximum_fusion.mid), channel_id=1, source_target_pairs={{0,16},{16,32},{32,48},{48,64},{64,80},{80,96},{96,112},{1,17},{17... | collective-permute-start | bytes 589832 | tf_op jit(solution)/shard_map/ppermute | solution.py:659
  29.9 25.5 %copy-start = (bf16[27,128,64]{1,2,0:T(8,128)(2,1)S(1)}, bf16[27,128,64]{1,2,0:T(8,128)(2,1)}, u32[]{:S(2)}) copy-start(bf16[27,128,64]{1,2,0:T(8,128)(2,1)} %param.13) | copy-start | bytes 1327108
  37.5 7.6 %collective-permute-start.4 = (bf16[144,128]{1,0:T(8,128)(2,1)S(1)}, bf16[144,128]{1,0:T(8,128)(2,1)S(1)}, u32[]{:S(2)}, u32[]{:S(2)}) collective-permute-start(bf16[144,128]{1,0:T(8,128)(2,1)S(1)} %get-tuple-element.35), channel_id=1, source_target_pairs={{0,1},{1,2},{2,3},{3,4},{4,5},{5,6},{6,7},{7,8},{8,9},{9,10},{10,1... | collective-permute-start | bytes 110600 | tf_op jit(solution)/shard_map/ppermute | solution.py:659
  43.2 6.8 %collective-permute-start.5 = (bf16[144,128]{1,0:T(8,128)(2,1)S(1)}, bf16[144,128]{1,0:T(8,128)(2,1)S(1)}, u32[]{:S(2)}, u32[]{:S(2)}) collective-permute-start(bf16[144,128]{1,0:T(8,128)(2,1)S(1)} %get-tuple-element.37), channel_id=1, source_target_pairs={{1,0},{2,1},{3,2},{4,3},{5,4},{6,5},{7,6},{8,7},{9,8},{10,9},{11,1... | collective-permute-start | bytes 110600 | tf_op jit(solution)/shard_map/ppermute | solution.py:659
  50.0 6.8 %collective-permute-start.6 = (bf16[304,128]{1,0:T(8,128)(2,1)S(1)}, bf16[304,128]{1,0:T(8,128)(2,1)S(1)}, u32[]{:S(2)}, u32[]{:S(2)}) collective-permute-start(bf16[304,128]{1,0:T(8,128)(2,1)S(1)} %get-tuple-element.39), channel_id=1, source_target_pairs={{0,16},{16,32},{32,48},{48,64},{64,80},{80,96},{96,112},{1,17},{17... | collective-permute-start | bytes 233480 | tf_op jit(solution)/shard_map/ppermute | solution.py:659
  54.1 5.3 %collective-permute-start.7 = (bf16[304,128]{1,0:T(8,128)(2,1)S(1)}, bf16[304,128]{1,0:T(8,128)(2,1)S(1)}, u32[]{:S(2)}, u32[]{:S(2)}) collective-permute-start(bf16[304,128]{1,0:T(8,128)(2,1)S(1)} %get-tuple-element.40), channel_id=1, source_target_pairs={{16,0},{32,16},{48,32},{64,48},{80,64},{96,80},{112,96},{17,1},{33... | collective-permute-start | bytes 233480 | tf_op jit(solution)/shard_map/ppermute | solution.py:659
  101.9 13.1 %all-to-all-start.3 = ((bf16[16,32,128]{2,1,0:T(8,128)(2,1)}), bf16[16,32,128]{2,1,0:T(8,128)(2,1)S(1)}, u32[]{:S(2)}, u32[]{:S(2)}) async-start(bf16[16,32,128]{2,1,0:T(8,128)(2,1)} %share.1), calls=%async_computation.3 | async-start | bytes 262144 | tf_op jit(solution)/shard_map/all_to_all | solution.py:691

commit v10 on v8

--- a/solution.py
+++ b/solution.py
@@ -38,6 +38,13 @@
     return jnp.exp2(jnp.maximum(scaled, SLOPE * scaled))
 
 
+def pool1(e):
+    total = e[:, :128] + e[:, 128:]
+    total = total + roll(total, 64, 1)
+    total = total + roll(total, 32, 1)
+    return total * 0.125
+
+
 def rounded(value):
     return value.astype(BF16).astype(F32)
 
@@ -67,9 +74,9 @@
 
 
 def forward_kernel(
-    top, mid, bot, k1, k2, biases,
-    to_next, to_previous, hidden2, ratio2, patches1, ratio1, fields, w2,
-    w1, pick, left, field, turned, pre1, first, spread, pre2, second,
+    top, mid, bot, cot, k1, k2, biases,
+    to_next, to_previous, hidden2, own_cot, ratio2, patches1, turned_own, fields, w2, w1,
+    pick, left, field, turned, pre1, first, spread, pre2, second,
 ):
     lay_weights1(k1, w1)
     lay_weights2(k2, w2)
@@ -130,25 +137,16 @@
             pre1[part] = dot(stack, w1[...])
         for part in range(2):
             yw = 2 * step + part
-            place = jnp.where((yw >= 3) & (yw < 7), yw - 3, 4)
             for k, pair in enumerate(PAIRS):
                 for h, zw in enumerate(pair):
                     at = k * 128 + h * 64
-                    pre = pre1[part, at : at + 64] + bias1
-                    e = exps(pre)
-                    total = e[:, :128] + e[:, 128:]
-                    total = total + roll(total, 64, 1)
-                    total = total + roll(total, 32, 1)
-                    mean = total * 0.125
+                    mean = pool1(exps(pre1[part, at : at + 64] + bias1))
                     pooled = rounded(jnp.log(mean) * 0.5)
                     first[yw, zw + 3, 8:72] = pooled * inside(yw - 3, zw, 1)
-                    if k < 2:
-                        share = 0.125 / mean
-                        share = jnp.concatenate([share, share], axis=1)
-                        ratio1[place, at : at + 64] = jnp.where(pre > 0, 1.0, SLOPE) * (e * share)
         return carry
 
     lax.fori_loop(0, 5, block1, 0)
+    turned_own[...] = turned[3:8, :256]
 
     group1 = lane((32, 128)) // 32
 
@@ -196,8 +194,12 @@
         return carry
 
     lax.fori_loop(0, 2, block2, 0)
-    to_next[...] = hidden2[:, 0:2].reshape(128, 128)
-    to_previous[...] = hidden2[:, 2:4].reshape(128, 128)
+    own = cot[...].astype(F32).T.astype(BF16)
+    own_cot[...] = own
+    to_next[:128] = hidden2[:, 0:2].reshape(128, 128)
+    to_previous[:128] = hidden2[:, 2:4].reshape(128, 128)
+    to_next[128:144] = own
+    to_previous[128:144] = own
 
 
 def lay_weights1(taps, out):
@@ -251,20 +253,21 @@
         forward_kernel,
         name="forward",
         out_shape=(
-            jax.ShapeDtypeStruct((128, 128), BF16),
-            jax.ShapeDtypeStruct((128, 128), BF16),
+            jax.ShapeDtypeStruct((144, 128), BF16),
+            jax.ShapeDtypeStruct((144, 128), BF16),
             jax.ShapeDtypeStruct((4, 4, 16, 128), BF16),
+            jax.ShapeDtypeStruct((16, 128), BF16),
             jax.ShapeDtypeStruct((8, 4, 32, 256), F32),
             jax.ShapeDtypeStruct((6, 6, 32, 128), BF16),
-            jax.ShapeDtypeStruct((5, 256, 256), F32),
+            jax.ShapeDtypeStruct((5, 256, 128), BF16),
             jax.ShapeDtypeStruct((5, 128, 256), BF16),
             jax.ShapeDtypeStruct((3, 512, 256), BF16),
+            jax.ShapeDtypeStruct((256, 256), BF16),
         ),
         in_specs=[VMEM] * len(operands),
-        out_specs=(VMEM,) * 8,
+        out_specs=(VMEM,) * 10,
         cost_estimate=pl.CostEstimate(flops=5000000000, bytes_accessed=8000000, transcendentals=8000000),
         scratch_shapes=[
-            pltpu.VMEM((256, 256), BF16),
             pltpu.VMEM((256, 512), BF16),
             pltpu.VMEM((22, 80, 256), BF16),
             pltpu.VMEM((11, 128, 640), BF16),
@@ -279,54 +282,25 @@
     )(*operands)
 
 
-def deal_kernel(cot, dealt):
-    groups, width = dealt.shape[0], dealt.shape[2]
-    rows = jnp.concatenate([cot[c, 0].astype(F32) for c in range(width // 16)], axis=1)
-    rows = jnp.concatenate([jnp.zeros((1, width), F32), rows, jnp.zeros((1, width), F32)], axis=0)
-    for k in range(groups):
-        dealt[k] = jnp.concatenate([rows[k : k + 3], jnp.zeros((5, width), F32)], axis=0).astype(BF16)
-
-
-def run_deal(cot):
-    wide, _, groups, depth = cot.shape
-    return pl.pallas_call(
-        deal_kernel,
-        name="deal",
-        out_shape=jax.ShapeDtypeStruct((groups, 8, wide * depth), BF16),
-        in_specs=[VMEM],
-        out_specs=VMEM,
-        compiler_params=pltpu.CompilerParams(vmem_limit_bytes=LIMIT),
-    )(cot)
-
-
-def weave_kernel(lower, hidden2, upper, dealt, to_next, to_previous, own_cot):
+def weave_kernel(lower, hidden2, upper, own_cot, to_next, to_previous):
     for target, first_row in ((to_next, 0), (to_previous, 2)):
         for y in range(2):
             row, at = first_row + y, y * 128
             target[at : at + 32] = lower[row * 32 : row * 32 + 32]
             target[at + 32 : at + 96] = hidden2[row].reshape(64, 128)
             target[at + 96 : at + 128] = upper[row * 32 : row * 32 + 32]
-    groups = dealt.shape[0]
-    wide = 128 // groups
-    row = lax.broadcasted_iota(jnp.int32, (128, 128), 0)
-    col = lax.broadcasted_iota(jnp.int32, (128, 128), 1)
-    order = jnp.where(col == row % groups * wide + row // groups, 1.0, 0.0).astype(BF16)
-    whole = dealt[...].astype(F32)
-    for d in range(3):
-        lines = whole[:, d]
-        stack = jnp.concatenate([lines[:, c * 16 : c * 16 + 16] for c in range(wide)], axis=0).astype(BF16)
-        rows = dot_tn(stack, order).astype(BF16)
-        for target, at in ((to_next, 256), (to_previous, 256), (own_cot, 0)):
-            target[at + 16 * d : at + 16 * d + 16] = rows
+        target[256:272] = lower[128:144]
+        target[272:288] = own_cot[...]
+        target[288:304] = upper[128:144]
 
 
 def run_weave(*operands):
     return pl.pallas_call(
         weave_kernel,
         name="weave",
-        out_shape=(jax.ShapeDtypeStruct((304, 128), BF16),) * 2 + (jax.ShapeDtypeStruct((48, 128), BF16),),
+        out_shape=(jax.ShapeDtypeStruct((304, 128), BF16),) * 2,
         in_specs=[VMEM] * 4,
-        out_specs=(VMEM,) * 3,
+        out_specs=(VMEM,) * 2,
         compiler_params=pltpu.CompilerParams(vmem_limit_bytes=LIMIT),
     )(*operands)
 
@@ -349,9 +323,22 @@
     return mean, (jnp.where(pre > 0, 1.0, SLOPE) * (e * share)).astype(BF16)
 
 
-def own_kernel(hidden2, own_cot, k3, biases, packed, shift3, w3, wide3, patches2, pre3, turned):
+def own_kernel(
+    hidden2, own_cot, k3, biases, turned_own, w1, packed, shift3, w3, wide3, ratio1, patches2, pre3, turned
+):
     groups = packed.shape[0]
     wide = 128 // groups
+    bias1 = jnp.concatenate([biases[0:1, :32]] * 8, axis=1)
+    for yw in range(4):
+        stack = jnp.concatenate([turned_own[yw], turned_own[yw + 1]], axis=1)
+        ratio1[yw] = dot(stack, w1[...])
+    for yw in range(4):
+        for at in range(0, 256, 64):
+            pre = ratio1[yw, at : at + 64] + bias1
+            e = exps(pre)
+            share = 0.125 / pool1(e)
+            share = jnp.concatenate([share, share], axis=1)
+            ratio1[yw, at : at + 64] = jnp.where(pre > 0, 1.0, SLOPE) * (e * share)
     lay_weights3(k3, w3)
     wide3[...] = jnp.concatenate([biases[2:3]] * 2, axis=1)
     for y in range(4):
@@ -362,7 +349,7 @@
         block = patches2[dy : dy + 2, dz : dz + 2].reshape(64, 256)
         term = dot(block, w3[tap])
         pre3[...] = term + wide3[...] if tap == 0 else pre3[...] + term
-    mean, delta = pool3(pre3[...].reshape(2, 2, 16, 256), own_cot[16:32])
+    mean, delta = pool3(pre3[...].reshape(2, 2, 16, 256), own_cot[...])
     features = rounded(jnp.log(mean) * 0.5)
     own3 = delta.reshape(64, 256)
     bias3 = own3.astype(F32).sum(axis=0, keepdims=True)
@@ -404,9 +391,10 @@
             jax.ShapeDtypeStruct((1, 128), F32),
             jax.ShapeDtypeStruct((9, 256, 256), BF16),
             jax.ShapeDtypeStruct((1, 256), F32),
+            jax.ShapeDtypeStruct((4, 256, 256), F32),
         ),
         in_specs=[VMEM] * len(operands),
-        out_specs=(VMEM,) * 4,
+        out_specs=(VMEM,) * 5,
         scratch_shapes=[
             pltpu.VMEM((4, 4, 16, 256), BF16),
             pltpu.VMEM((64, 256), F32),
@@ -452,7 +440,7 @@
         for wz in range(3):
             pre = pre3[2 * wy : 2 * wy + 2, 2 * wz : 2 * wz + 2]
             if wy == 1:
-                cot = own_cot[wz * 16 : wz * 16 + 16]
+                cot = own_cot[...] if wz == 1 else (lower if wz == 0 else upper)[128:144]
             else:
                 cot = (before if wy == 0 else after)[256 + wz * 16 : 272 + wz * 16]
             delta3[2 * wy : 2 * wy + 2, 2 * wz : 2 * wz + 2] = pool3(pre, cot)[1]
@@ -516,7 +504,7 @@
         return value + roll(value, 64, 1)
 
 
-    def gather1(y, carry):
+    for y in range(4):
         def part(zo, pz):
             return patch1[y, zo, :, pz * 128 : pz * 128 + 128]
 
@@ -525,14 +513,11 @@
         )
         for z, value in enumerate(sums):
             value = rounded(value + roll(jnp.where(low_half, up(value), down(value)), 64, 1))
-            grad1[z, pl.ds(0, 32, stride=2), :] = widen(value, 1)
-            grad1[z, pl.ds(1, 32, stride=2), :] = widen(value, 2)
-        value = grad1[...].reshape(256, 128)
+            grad1[y, z, pl.ds(0, 32, stride=2), :] = widen(value, 1)
+            grad1[y, z, pl.ds(1, 32, stride=2), :] = widen(value, 2)
+        value = grad1[y].reshape(256, 128)
         value = jnp.concatenate([value, value], axis=1)
         delta1[y] = (value * ratio1[y]).astype(BF16)
-        return carry
-
-    lax.fori_loop(0, 4, gather1, 0)
 
     bias1 = delta1[...].astype(F32).sum(axis=0).sum(axis=0, keepdims=True)
     bias1 = bias1[:, :128] + bias1[:, 128:]
@@ -584,7 +569,7 @@
             pltpu.VMEM((6, 4, 32, 256), BF16),
             pltpu.VMEM((4, 2, 32, 512), F32),
             pltpu.VMEM((2, 4, 32, 128), F32),
-            pltpu.VMEM((4, 64, 128), F32),
+            pltpu.VMEM((4, 4, 64, 128), F32),
             pltpu.VMEM((4, 256, 256), BF16),
         ],
         compiler_params=pltpu.CompilerParams(vmem_limit_bytes=LIMIT),
@@ -704,21 +689,23 @@
     wide = 128 // size_z
 
     tile = universe.transpose(1, 2, 0, 3).reshape(8, 32, 128)
-    dealt = lax.all_to_all(run_deal(cotangent), "gz", 0, 0, tiled=True)
-    biases = jnp.stack([jnp.pad(bias1, (0, 96)), jnp.pad(bias2, (0, 64)), bias3])
+    cot = lax.all_to_all(cotangent[:, 0].transpose(1, 0, 2), "gz", 0, 0, tiled=True).reshape(128, 16)
     lower, upper = both_ways(tile, tile, "gz")
     strip = jnp.concatenate([lower[:, 4:], tile, upper[:, :28], jnp.zeros((8, 8, 128), BF16)], axis=1)
+    strip, kernel1, kernel2, bias1, bias2, bias3 = lax.optimization_barrier(
+        (strip, kernel1, kernel2, bias1, bias2, bias3)
+    )
     top, bottom = both_ways(strip, strip, "gy")
+    biases = jnp.stack([jnp.pad(bias1, (0, 96)), jnp.pad(bias2, (0, 64)), bias3])
 
     k1, k2 = kernel1.transpose(0, 2, 1).astype(F32), kernel2.transpose(0, 2, 1).astype(F32)
     k3 = kernel3.transpose(0, 2, 1)
-    top, dealt = lax.optimization_barrier((top, dealt))
-    to_next, to_previous, hidden2, ratio2, patches1, ratio1, fields, w2 = run_forward(
-        top, strip, bottom, k1, k2, biases
+    to_next, to_previous, hidden2, own_cot, ratio2, patches1, turned_own, fields, w2, w1 = run_forward(
+        top, strip, bottom, cot, k1, k2, biases
     )
     lower, upper = both_ways(to_next, to_previous, "gz")
-    row_next, row_previous, own_cot = run_weave(lower, hidden2, upper, dealt)
-    packed3, shift3, w3, wide3 = run_own(size_z, hidden2, own_cot, k3, biases)
+    row_next, row_previous = run_weave(lower, hidden2, upper, own_cot)
+    packed3, shift3, w3, wide3, ratio1 = run_own(size_z, hidden2, own_cot, k3, biases, turned_own, w1)
     before, after = both_ways(row_next, row_previous, "gy")
     packed = run_backward(
         size_z,

time: 117 us -> 114 us (0.974)
  waiting for transfers between devices: 18.5 us -> 16 us
  Pallas kernels: 17.1 us -> 15.9 us
    ppermute x4, waiting for transfers between devices: 4 us -> 0.87 us  [both_ways(): lax.ppermute(to_next, axis, forth)]
    ppermute x4, starting transfers between devices: 18.6 us -> 20 us  [both_ways(): lax.ppermute(to_next, axis, forth)]
    ppermute x4, starting transfers between devices: 7.83 us -> 6.43 us  [both_ways(): lax.ppermute(to_previous, axis, back)]
  transfers between devices with their start and end apart: 10 -> 10, of which waited for: 4 -> 5; matrix products, arithmetic and copies ran while one was open for 2% -> 3% of each run, Pallas kernels for 2% -> 3%
where the time goes in v10:
time: 114 us; the launch traced here: 113 us
  starting transfers between devices  39.4 us (35%)
  blocking collectives  36.7 us (32%)
  waiting for transfers between devices  16 us (14%)
  Pallas kernels  15.9 us (14%)
  local copies, waits for them, and re-layouts  2.41 us (2%)
  other arithmetic  1.85 us (2%)
    ppermute x4, starting transfers between devices, both_ways(): lax.ppermute(to_next, axis, forth)  20 us
    all_to_all x1, blocking collectives, shards(): packed = lax.all_to_all(packed, 'gz', 0, 0, tiled=True)  18.6 us
    all_to_all x1, blocking collectives, shards(): column = lax.all_to_all(column, 'gy', 0, 0, tiled=True)  18.1 us
    ppermute x4, waiting for transfers between devices, both_ways(): lax.ppermute(to_previous, axis, back)  8.14 us
    all_to_all x1, starting transfers between devices, shards(): lax.all_to_all(cotangent[:, 0].transpose(1, 0, 2), 'gz', 0, 0, tiled=True)  7.55 us
    all_to_all x1, waiting for transfers between devices, shards(): shared = lax.all_to_all(run_share(column, size_z), 'gz', 0, 0, tiled=True)  6.99 us
    ppermute x4, starting transfers between devices, both_ways(): lax.ppermute(to_previous, axis, back)  6.43 us
    pallas_call x1, Pallas kernels, run_forward(): pl.pallas_call(forward_kernel, name='forward', out_shape=(jax.ShapeDtypeS...  6.35 us
  transfers between devices with their start and end apart: 10, of which 5 were waited for; matrix products, arithmetic and copies ran while one was open for 3% of the time, Pallas kernels for 3%

profile of v10, /device:TPU:1, one launch (start us, length us, event | category | flops | bytes accessed | tf_op | source)
XLA Modules:
  0.0 113.1 jit_solution(2398667538432451544)
XLA Ops:
  0.7 0.9 copy.18
  1.6 6.0 %collective-permute-start = (bf16[8,32,128]{2,1,0:T(8,128)(2,1)S(1)}, bf16[8,32,128]{2,1,0:T(8,128)(2,1)S(1)}, u32[]{:S(2)}, u32[]{:S(2)}) collective-permute-start(bf16[8,32,128]{2,1,0:T(8,128)(2,1)S(1)} %bitcast.29), channel_id=1, source_target_pairs={{0,1},{1,2},{2,3},{3,4},{4,5},{5,6},{6,7},{7,8},{8,9},{9,10},{10,1... | collective-permute-start | bytes 196616 | tf_op jit(solution)/shard_map/ppermute | solution.py:684
  7.6 1.9 %collective-permute-start.1 = (bf16[8,32,128]{2,1,0:T(8,128)(2,1)S(1)}, bf16[8,32,128]{2,1,0:T(8,128)(2,1)S(1)}, u32[]{:S(2)}, u32[]{:S(2)}) collective-permute-start(bf16[8,32,128]{2,1,0:T(8,128)(2,1)S(1)} %bitcast.30), channel_id=1, source_target_pairs={{1,0},{2,1},{3,2},{4,3},{5,4},{6,5},{7,6},{8,7},{9,8},{10,9},{11,1... | collective-permute-start | bytes 196616 | tf_op jit(solution)/shard_map/ppermute | solution.py:684
  9.6 1.4 %copy.22 = bf16[8,1,16,16]{3,0,2,1:T(8,128)(2,1)} copy(bf16[8,1,16,16]{3,2,1,0:T(8,128)(2,1)} %param.15) | data formatting | bytes 8192 | tf_op args[7]
  10.9 7.6 %all-to-all-start = ((bf16[16,8,16]{2,1,0:T(8,128)(2,1)}), bf16[16,8,16]{2,1,0:T(8,128)(2,1)S(1)}, u32[]{:S(2)}, u32[]{:S(2)}) async-start(bf16[16,8,16]{2,1,0:T(8,128)(2,1)} %bitcast.25), calls=%async_computation | async-start | bytes 65536 | tf_op jit(solution)/shard_map/all_to_all | solution.py:692
  18.5 0.1 pad.16.clone
  18.6 0.0 collective-permute-done
  18.6 0.0 collective-permute-done.1
  18.6 0.1 maximum_maximum_fusion.mid
  18.7 1.3 %collective-permute-start.3 = (bf16[8,96,128]{2,1,0:T(8,128)(2,1)S(1)}, bf16[8,96,128]{2,1,0:T(8,128)(2,1)S(1)}, u32[]{:S(2)}, u32[]{:S(2)}) collective-permute-start(bf16[8,96,128]{2,1,0:T(8,128)(2,1)S(1)} %maximum_maximum_fusion.mid), channel_id=1, source_target_pairs={{16,0},{32,16},{48,32},{64,48},{80,64},{96,80},{112,96},{17,1},{33... | collective-permute-start | bytes 589832 | tf_op jit(solution)/shard_map/ppermute | solution.py:684
  20.0 4.2 %collective-permute-start.2 = (bf16[8,96,128]{2,1,0:T(8,128)(2,1)S(1)}, bf16[8,96,128]{2,1,0:T(8,128)(2,1)S(1)}, u32[]{:S(2)}, u32[]{:S(2)}) collective-permute-start(bf16[8,96,128]{2,1,0:T(8,128)(2,1)S(1)} %maximum_maximum_fusion.mid), channel_id=1, source_target_pairs={{0,16},{16,32},{32,48},{48,64},{64,80},{80,96},{96,112},{1,17},{17... | collective-permute-start | bytes 589832 | tf_op jit(solution)/shard_map/ppermute | solution.py:684
  24.2 0.8 convert_bitcast_fusion.1.k1
  25.0 1.0 convert_bitcast_fusion.k2
  26.0 1.4 %collective-permute-done.3.bot = bf16[8,96,128]{2,1,0:T(8,128)(2,1)S(1)} collective-permute-done((bf16[8,96,128]{2,1,0:T(8,128)(2,1)S(1)}, bf16[8,96,128]{2,1,0:T(8,128)(2,1)S(1)}, u32[]{:S(2)}, u32[]{:S(2)}) %collective-permute-start.3) | collective-permute-done | bytes 196640 | tf_op jit(solution)/shard_map/ppermute | solution.py:684
  27.4 0.9 collective-permute-done.2.top
  28.3 6.4 %forward.1 = (bf16[144,128]{1,0:T(8,128)(2,1)S(1)}, bf16[144,128]{1,0:T(8,128)(2,1)S(1)}, bf16[4,4,16,128]{3,2,1,0:T(8,128)(2,1)S(1)}, bf16[16,128]{1,0:T(8,128)...) custom-call(bf16[8,96,128]{2,1,0:T(8,128)(2,1)S(1)} %collective-perm, ...), custom_call_target="tpu_custom_call" | custom-call | flops 5000000000 | bytes 8000000 | tf_op jit(solution)/shard_map/forward/pallas_call | solution.py:252
  34.6 5.7 %collective-permute-start.4 = (bf16[144,128]{1,0:T(8,128)(2,1)S(1)}, bf16[144,128]{1,0:T(8,128)(2,1)S(1)}, u32[]{:S(2)}, u32[]{:S(2)}) collective-permute-start(bf16[144,128]{1,0:T(8,128)(2,1)S(1)} %get-tuple-element.43), channel_id=1, source_target_pairs={{0,1},{1,2},{2,3},{3,4},{4,5},{5,6},{6,7},{7,8},{8,9},{9,10},{10,1... | collective-permute-start | bytes 110600 | tf_op jit(solution)/shard_map/ppermute | solution.py:684
  40.4 1.9 %collective-permute-start.5 = (bf16[144,128]{1,0:T(8,128)(2,1)S(1)}, bf16[144,128]{1,0:T(8,128)(2,1)S(1)}, u32[]{:S(2)}, u32[]{:S(2)}) collective-permute-start(bf16[144,128]{1,0:T(8,128)(2,1)S(1)} %get-tuple-element.45), channel_id=1, source_target_pairs={{1,0},{2,1},{3,2},{4,3},{5,4},{6,5},{7,6},{8,7},{9,8},{10,9},{11,1... | collective-permute-start | bytes 110600 | tf_op jit(solution)/shard_map/ppermute | solution.py:684
  42.3 4.8 %collective-permute-done.5.upper = bf16[144,128]{1,0:T(8,128)(2,1)S(1)} collective-permute-done((bf16[144,128]{1,0:T(8,128)(2,1)S(1)}, bf16[144,128]{1,0:T(8,128)(2,1)S(1)}, u32[]{:S(2)}, u32[]{:S(2)}) %collective-permute-start.5) | collective-permute-done | bytes 36896 | tf_op jit(solution)/shard_map/ppermute | solution.py:684
  47.2 4.1 %collective-permute-start.6 = (bf16[304,128]{1,0:T(8,128)(2,1)S(1)}, bf16[304,128]{1,0:T(8,128)(2,1)S(1)}, u32[]{:S(2)}, u32[]{:S(2)}) collective-permute-start(bf16[304,128]{1,0:T(8,128)(2,1)S(1)} %get-tuple-element.47), channel_id=1, source_target_pairs={{0,16},{16,32},{32,48},{48,64},{64,80},{80,96},{96,112},{1,17},{17... | collective-permute-start | bytes 233480 | tf_op jit(solution)/shard_map/ppermute | solution.py:684
  51.3 1.3 %collective-permute-start.7 = (bf16[304,128]{1,0:T(8,128)(2,1)S(1)}, bf16[304,128]{1,0:T(8,128)(2,1)S(1)}, u32[]{:S(2)}, u32[]{:S(2)}) collective-permute-start(bf16[304,128]{1,0:T(8,128)(2,1)S(1)} %get-tuple-element.48), channel_id=1, source_target_pairs={{16,0},{32,16},{48,32},{64,48},{80,64},{96,80},{112,96},{17,1},{33... | collective-permute-start | bytes 233480 | tf_op jit(solution)/shard_map/ppermute | solution.py:684
  52.6 2.1 %own.1 = (bf16[16,120,128]{2,1,0:T(8,128)(2,1)S(1)}, f32[1,128]{1,0:T(1,128)S(1)}, bf16[9,256,256]{2,1,0:T(8,128)(2,1)S(1)}, f32[1,256]{1,0:T(1,128)S(1)}, f32[4,256,256]{2,1,0:T(8,128)S(1)}) custom-call(bf16[4,4,16,128]{3,2,1,0:T(8,128)(2,1)S(1)} %get-tuple-element.44.hidden2.middle, bf16[16,128]{1,0:T(8,128)(2,1)S(1)} %get-tuple-element.46.own_cot, ...), custom_call_target="tpu_custom_call" | custom-call | flops 150000000 | bytes 4000000 | tf_op jit(solution)/shard_map/own/pallas_call | solution.py:386
  54.7 1.9 %collective-permute-done.7.after = bf16[304,128]{1,0:T(8,128)(2,1)S(1)} collective-permute-done((bf16[304,128]{1,0:T(8,128)(2,1)S(1)}, bf16[304,128]{1,0:T(8,128)(2,1)S(1)}, u32[]{:S(2)}, u32[]{:S(2)}) %collective-permute-start.7) | collective-permute-done | bytes 77856 | tf_op jit(solution)/shard_map/ppermute | solution.py:684
  56.6 4.4 %backward.1 = bf16[16,152,128]{2,1,0:T(8,128)(2,1)S(1)} custom-call(bf16[304,128]{1,0:T(8,128)(2,1)S(1)} %collective-permute-done.6.before, bf16[144,128]{1,0:T(8,128)(2,1)S(1)} %collective-permute-done.4.lower, bf16[4,4,16,128]{3,2,1,0:T(8,128)(2,1)S(1)} %get-tuple-element.44.hidden2.middle, bf16[144,128]{1,0:T(8,128)(2,1)S(1)} %collective-permute-done.5.upper, ...), custom_call_target="tpu_custom_call" | custom-call | tf_op jit(solution)/shard_map/backward/pallas_call | solution.py:557
  61.0 18.6 %all_to_all.20.received = bf16[16,152,128]{2,1,0:T(8,128)(2,1)S(1)} all-to-all(bf16[16,152,128]{2,1,0:T(8,128)(2,1)S(1)} %backward.1), channel_id=1, replica_groups=mesh['gy'=8,'gz'=16] {'gz'}, dimensions={0} | all-to-all | bytes 1245184 | tf_op jit(solution)/shard_map/all_to_all | solution.py:715
  79.6 0.7 sum.1
  80.3 18.1 %all_to_all.21.column = bf16[8,144,128]{2,1,0:T(8,128)(2,1)S(1)} all-to-all(bf16[8,144,128]{2,1,0:T(8,128)(2,1)S(1)} %get-tuple-element.61), channel_id=1, replica_groups=mesh['gy'=8,'gz'=16] {'gy'}, dimensions={0} | all-to-all | bytes 589824 | tf_op jit(solution)/shard_map/all_to_all | solution.py:717
  98.4 0.7 share.1
  99.1 5.4 %all-to-all-start.3 = ((bf16[16,32,128]{2,1,0:T(8,128)(2,1)}), bf16[16,32,128]{2,1,0:T(8,128)(2,1)S(1)}, u32[]{:S(2)}, u32[]{:S(2)}) async-start(bf16[16,32,128]{2,1,0:T(8,128)(2,1)} %share.1), calls=%async_computation.3 | async-start | bytes 262144 | tf_op jit(solution)/shard_map/all_to_all | solution.py:718
  104.5 0.7 third.1
  105.2 7.0 %all-to-all-done.3.shared = bf16[16,32,128]{2,1,0:T(8,128)(2,1)S(1)} async-done(((bf16[16,32,128]{2,1,0:T(8,128)(2,1)}), bf16[16,32,128]{2,1,0:T(8,128)(2,1)S(1)}, u32[]{:S(2)}, u32[]{:S(2)}) %all-to-all-start.3) | async-done | bytes 131104 | tf_op jit(solution)/shard_map/all_to_all | solution.py:718
  112.2 0.9 unpack.1
  (16 shorter events, 0.1 us)
Async XLA Ops:
  0.6 25.4 %copy-start.1 = (f32[128]{0:T(128)S(1)}, f32[128]{0:T(128)}, u32[]{:S(2)}) copy-start(f32[128]{0:T(128)} %param.14) | copy-start | bytes 1540
  0.6 25.3 %copy-start.2 = (f32[64]{0:T(128)S(1)}, f32[64]{0:T(128)}, u32[]{:S(2)}) copy-start(f32[64]{0:T(128)} %param.12) | copy-start | bytes 772
  0.7 25.3 %copy-start.3 = (f32[32]{0:T(128)S(1)}, f32[32]{0:T(128)}, u32[]{:S(2)}) copy-start(f32[32]{0:T(128)} %param.10) | copy-start | bytes 388
  1.6 17.0 %collective-permute-start = (bf16[8,32,128]{2,1,0:T(8,128)(2,1)S(1)}, bf16[8,32,128]{2,1,0:T(8,128)(2,1)S(1)}, u32[]{:S(2)}, u32[]{:S(2)}) collective-permute-start(bf16[8,32,128]{2,1,0:T(8,128)(2,1)S(1)} %bitcast.29), channel_id=1, source_target_pairs={{0,1},{1,2},{2,3},{3,4},{4,5},{5,6},{6,7},{7,8},{8,9},{9,10},{10,1... | collective-permute-start | bytes 196616 | tf_op jit(solution)/shard_map/ppermute | solution.py:684
  7.6 11.0 %collective-permute-start.1 = (bf16[8,32,128]{2,1,0:T(8,128)(2,1)S(1)}, bf16[8,32,128]{2,1,0:T(8,128)(2,1)S(1)}, u32[]{:S(2)}, u32[]{:S(2)}) collective-permute-start(bf16[8,32,128]{2,1,0:T(8,128)(2,1)S(1)} %bitcast.30), channel_id=1, source_target_pairs={{1,0},{2,1},{3,2},{4,3},{5,4},{6,5},{7,6},{8,7},{9,8},{10,9},{11,1... | collective-permute-start | bytes 196616 | tf_op jit(solution)/shard_map/ppermute | solution.py:684
  10.9 15.1 %all-to-all-start = ((bf16[16,8,16]{2,1,0:T(8,128)(2,1)}), bf16[16,8,16]{2,1,0:T(8,128)(2,1)S(1)}, u32[]{:S(2)}, u32[]{:S(2)}) async-start(bf16[16,8,16]{2,1,0:T(8,128)(2,1)} %bitcast.25), calls=%async_computation | async-start | bytes 65536 | tf_op jit(solution)/shard_map/all_to_all | solution.py:692
  18.7 8.7 %collective-permute-start.3 = (bf16[8,96,128]{2,1,0:T(8,128)(2,1)S(1)}, bf16[8,96,128]{2,1,0:T(8,128)(2,1)S(1)}, u32[]{:S(2)}, u32[]{:S(2)}) collective-permute-start(bf16[8,96,128]{2,1,0:T(8,128)(2,1)S(1)} %maximum_maximum_fusion.mid), channel_id=1, source_target_pairs={{16,0},{32,16},{48,32},{64,48},{80,64},{96,80},{112,96},{17,1},{33... | collective-permute-start | bytes 589832 | tf_op jit(solution)/shard_map/ppermute | solution.py:684
  20.0 8.3 %collective-permute-start.2 = (bf16[8,96,128]{2,1,0:T(8,128)(2,1)S(1)}, bf16[8,96,128]{2,1,0:T(8,128)(2,1)S(1)}, u32[]{:S(2)}, u32[]{:S(2)}) collective-permute-start(bf16[8,96,128]{2,1,0:T(8,128)(2,1)S(1)} %maximum_maximum_fusion.mid), channel_id=1, source_target_pairs={{0,16},{16,32},{32,48},{48,64},{64,80},{80,96},{96,112},{1,17},{17... | collective-permute-start | bytes 589832 | tf_op jit(solution)/shard_map/ppermute | solution.py:684
  28.3 24.3 %copy-start = (bf16[27,128,64]{1,2,0:T(8,128)(2,1)S(1)}, bf16[27,128,64]{1,2,0:T(8,128)(2,1)}, u32[]{:S(2)}) copy-start(bf16[27,128,64]{1,2,0:T(8,128)(2,1)} %param.13) | copy-start | bytes 1327108
  34.6 7.6 %collective-permute-start.4 = (bf16[144,128]{1,0:T(8,128)(2,1)S(1)}, bf16[144,128]{1,0:T(8,128)(2,1)S(1)}, u32[]{:S(2)}, u32[]{:S(2)}) collective-permute-start(bf16[144,128]{1,0:T(8,128)(2,1)S(1)} %get-tuple-element.43), channel_id=1, source_target_pairs={{0,1},{1,2},{2,3},{3,4},{4,5},{5,6},{6,7},{7,8},{8,9},{9,10},{10,1... | collective-permute-start | bytes 110600 | tf_op jit(solution)/shard_map/ppermute | solution.py:684
  40.4 6.8 %collective-permute-start.5 = (bf16[144,128]{1,0:T(8,128)(2,1)S(1)}, bf16[144,128]{1,0:T(8,128)(2,1)S(1)}, u32[]{:S(2)}, u32[]{:S(2)}) collective-permute-start(bf16[144,128]{1,0:T(8,128)(2,1)S(1)} %get-tuple-element.45), channel_id=1, source_target_pairs={{1,0},{2,1},{3,2},{4,3},{5,4},{6,5},{7,6},{8,7},{9,8},{10,9},{11,1... | collective-permute-start | bytes 110600 | tf_op jit(solution)/shard_map/ppermute | solution.py:684
  47.2 7.5 %collective-permute-start.6 = (bf16[304,128]{1,0:T(8,128)(2,1)S(1)}, bf16[304,128]{1,0:T(8,128)(2,1)S(1)}, u32[]{:S(2)}, u32[]{:S(2)}) collective-permute-start(bf16[304,128]{1,0:T(8,128)(2,1)S(1)} %get-tuple-element.47), channel_id=1, source_target_pairs={{0,16},{16,32},{32,48},{48,64},{64,80},{80,96},{96,112},{1,17},{17... | collective-permute-start | bytes 233480 | tf_op jit(solution)/shard_map/ppermute | solution.py:684
  51.3 5.3 %collective-permute-start.7 = (bf16[304,128]{1,0:T(8,128)(2,1)S(1)}, bf16[304,128]{1,0:T(8,128)(2,1)S(1)}, u32[]{:S(2)}, u32[]{:S(2)}) collective-permute-start(bf16[304,128]{1,0:T(8,128)(2,1)S(1)} %get-tuple-element.48), channel_id=1, source_target_pairs={{16,0},{32,16},{48,32},{64,48},{80,64},{96,80},{112,96},{17,1},{33... | collective-permute-start | bytes 233480 | tf_op jit(solution)/shard_map/ppermute | solution.py:684
  99.1 13.1 %all-to-all-start.3 = ((bf16[16,32,128]{2,1,0:T(8,128)(2,1)}), bf16[16,32,128]{2,1,0:T(8,128)(2,1)S(1)}, u32[]{:S(2)}, u32[]{:S(2)}) async-start(bf16[16,32,128]{2,1,0:T(8,128)(2,1)} %share.1), calls=%async_computation.3 | async-start | bytes 262144 | tf_op jit(solution)/shard_map/all_to_all | solution.py:718

commit v11 on v10

--- a/solution.py
+++ b/solution.py
@@ -45,6 +45,16 @@
     return total * 0.125
 
 
+def odd(axis):
+    return lax.rem(lax.axis_index(axis), 2)
+
+
+def sided(axis, far, near):
+    flag = odd(axis).astype(F32)
+    far, near = far.astype(F32), near.astype(F32)
+    return (near * flag + far * (1.0 - flag)).astype(BF16), (far * flag + near * (1.0 - flag)).astype(BF16)
+
+
 def rounded(value):
     return value.astype(BF16).astype(F32)
 
@@ -74,8 +84,8 @@
 
 
 def forward_kernel(
-    top, mid, bot, cot, k1, k2, biases,
-    to_next, to_previous, hidden2, own_cot, ratio2, patches1, turned_own, fields, w2, w1,
+    near, mid, far, cot, k1, k2, biases,
+    to_far, to_near, hidden2, own_cot, ratio2, patches1, turned_own, fields, w2, w1,
     pick, left, field, turned, pre1, first, spread, pre2, second,
 ):
     lay_weights1(k1, w1)
@@ -93,8 +103,8 @@
         ok_z = (col >= 0) & (col < size_z * (4 // scale))
         return jnp.where(ok_y & ok_z, 1.0, 0.0)
 
-    def lay(source, index, target):
-        rows = source[index].astype(F32)
+    def lay(rows, target):
+        rows = rows.astype(F32)
         pieces = []
         for one, two in PAIRS:
             a, b = 8 * (one + 3), 8 * (two + 3)
@@ -102,13 +112,13 @@
         left[target] = jnp.concatenate(pieces, axis=0).astype(BF16)
 
     def lay_both(step, carry):
-        lay(mid, step, step + 7)
-        lay(mid, step + 4, step + 11)
+        lay(mid[step], step + 7)
+        lay(mid[step + 4], step + 11)
         return carry
 
     def lay_ends(step, carry):
-        lay(top, step + 1, step)
-        lay(bot, step, step + 15)
+        lay(sided("gy", far[step + 1], near[step + 1])[0], step)
+        lay(sided("gy", far[step], near[step])[1], step + 15)
         return carry
 
     lax.fori_loop(0, 4, lay_both, 0)
@@ -196,10 +206,11 @@
     lax.fori_loop(0, 2, block2, 0)
     own = cot[...].astype(F32).T.astype(BF16)
     own_cot[...] = own
-    to_next[:128] = hidden2[:, 0:2].reshape(128, 128)
-    to_previous[:128] = hidden2[:, 2:4].reshape(128, 128)
-    to_next[128:144] = own
-    to_previous[128:144] = own
+    side = odd("gz")
+    to_far[:128] = hidden2[:, pl.ds(2 - 2 * side, 2)].reshape(128, 128)
+    to_near[:128] = hidden2[:, pl.ds(2 * side, 2)].reshape(128, 128)
+    to_far[128:144] = own
+    to_near[128:144] = own
 
 
 def lay_weights1(taps, out):
@@ -282,13 +293,16 @@
     )(*operands)
 
 
-def weave_kernel(lower, hidden2, upper, own_cot, to_next, to_previous):
-    for target, first_row in ((to_next, 0), (to_previous, 2)):
+def weave_kernel(far, near, hidden2, own_cot, to_far, to_near, lower, upper):
+    lower[...], upper[...] = sided("gz", far[...], near[...])
+    side = odd("gy")
+    for target, first_row in ((to_far, 2 - 2 * side), (to_near, 2 * side)):
         for y in range(2):
             row, at = first_row + y, y * 128
-            target[at : at + 32] = lower[row * 32 : row * 32 + 32]
+            rows = pl.ds(pl.multiple_of(row * 32, 32), 32)
+            target[at : at + 32] = lower[rows]
             target[at + 32 : at + 96] = hidden2[row].reshape(64, 128)
-            target[at + 96 : at + 128] = upper[row * 32 : row * 32 + 32]
+            target[at + 96 : at + 128] = upper[rows]
         target[256:272] = lower[128:144]
         target[272:288] = own_cot[...]
         target[288:304] = upper[128:144]
@@ -298,9 +312,9 @@
     return pl.pallas_call(
         weave_kernel,
         name="weave",
-        out_shape=(jax.ShapeDtypeStruct((304, 128), BF16),) * 2,
+        out_shape=(jax.ShapeDtypeStruct((304, 128), BF16),) * 2 + (jax.ShapeDtypeStruct((144, 128), BF16),) * 2,
         in_specs=[VMEM] * 4,
-        out_specs=(VMEM,) * 2,
+        out_specs=(VMEM,) * 4,
         compiler_params=pltpu.CompilerParams(vmem_limit_bytes=LIMIT),
     )(*operands)
 
@@ -406,9 +420,10 @@
 
 
 def backward_kernel(
-    before, lower, middle, upper, after, own_cot, w3, bias3, w2, ratio2, patches1, ratio1, fields, packed3, shift3,
-    packed, patches2, pre3, delta3, patch2, grad2, delta2, patch1, beside, grad1, delta1,
+    far, lower, middle, upper, near, own_cot, w3, bias3, w2, ratio2, patches1, ratio1, fields, packed3, shift3,
+    packed, before, after, patches2, pre3, delta3, patch2, grad2, delta2, patch1, beside, grad1, delta1,
 ):
+    before[...], after[...] = sided("gy", far[...], near[...])
     groups = packed.shape[0]
     half = lane((16, 128)) < 64
 
@@ -561,6 +576,8 @@
         in_specs=[VMEM] * len(operands),
         out_specs=VMEM,
         scratch_shapes=[
+            pltpu.VMEM((304, 128), BF16),
+            pltpu.VMEM((304, 128), BF16),
             pltpu.VMEM((8, 8, 16, 256), BF16),
             pltpu.VMEM((6, 6, 16, 256), F32),
             pltpu.VMEM((6, 6, 16, 256), BF16),
@@ -677,11 +694,14 @@
     )(shared)
 
 
-def both_ways(to_next, to_previous, axis):
+def swap(to_far, to_near, axis):
     devices = lax.axis_size(axis)
-    forth = [(i, i + 1) for i in range(devices - 1)]
-    back = [(i + 1, i) for i in range(devices - 1)]
-    return lax.ppermute(to_next, axis, forth), lax.ppermute(to_previous, axis, back)
+
+    def pairs(first):
+        forth = [(i, i + 1) for i in range(first, devices - 1, 2)]
+        return forth + [(j, i) for i, j in forth]
+
+    return lax.ppermute(to_far, axis, pairs(1)), lax.ppermute(to_near, axis, pairs(0))
 
 
 def shards(universe, kernel1, bias1, kernel2, bias2, kernel3, bias3, cotangent):
@@ -690,26 +710,28 @@
 
     tile = universe.transpose(1, 2, 0, 3).reshape(8, 32, 128)
     cot = lax.all_to_all(cotangent[:, 0].transpose(1, 0, 2), "gz", 0, 0, tiled=True).reshape(128, 16)
-    lower, upper = both_ways(tile, tile, "gz")
-    strip = jnp.concatenate([lower[:, 4:], tile, upper[:, :28], jnp.zeros((8, 8, 128), BF16)], axis=1)
+    far, near = swap(tile, tile, "gz")
+    second = odd("gz") == 1
+    lower, upper = jnp.where(second, near, far), jnp.where(second, far, near)
+    strip = jnp.concatenate([lower[:, 4:], tile, upper[:, :28]], axis=1)
     strip, kernel1, kernel2, bias1, bias2, bias3 = lax.optimization_barrier(
         (strip, kernel1, kernel2, bias1, bias2, bias3)
     )
-    top, bottom = both_ways(strip, strip, "gy")
+    far, near = swap(strip, strip, "gy")
     biases = jnp.stack([jnp.pad(bias1, (0, 96)), jnp.pad(bias2, (0, 64)), bias3])
 
     k1, k2 = kernel1.transpose(0, 2, 1).astype(F32), kernel2.transpose(0, 2, 1).astype(F32)
     k3 = kernel3.transpose(0, 2, 1)
-    to_next, to_previous, hidden2, own_cot, ratio2, patches1, turned_own, fields, w2, w1 = run_forward(
-        top, strip, bottom, cot, k1, k2, biases
+    to_far, to_near, hidden2, own_cot, ratio2, patches1, turned_own, fields, w2, w1 = run_forward(
+        near, strip, far, cot, k1, k2, biases
     )
-    lower, upper = both_ways(to_next, to_previous, "gz")
-    row_next, row_previous = run_weave(lower, hidden2, upper, own_cot)
+    far, near = swap(to_far, to_near, "gz")
+    to_far, to_near, lower, upper = run_weave(far, near, hidden2, own_cot)
     packed3, shift3, w3, wide3, ratio1 = run_own(size_z, hidden2, own_cot, k3, biases, turned_own, w1)
-    before, after = both_ways(row_next, row_previous, "gy")
+    far, near = swap(to_far, to_near, "gy")
     packed = run_backward(
         size_z,
-        before, lower, hidden2, upper, after, own_cot, w3, wide3, w2, ratio2, patches1, ratio1, fields,
+        far, lower, hidden2, upper, near, own_cot, w3, wide3, w2, ratio2, patches1, ratio1, fields,
         packed3, shift3,
     )
     packed = lax.all_to_all(packed, "gz", 0, 0, tiled=True)

time: 114 us -> 99.3 us (0.87)
  starting transfers between devices: 39.4 us -> 31.8 us
  waiting for transfers between devices: 16 us -> 12.8 us
  blocking collectives: 36.7 us -> 34 us
    ppermute x8, starting transfers between devices: 26.5 us -> 20.8 us  [the longest x4 12.9 us: swap(): lax.ppermute(to_far, axis, pairs(1))]
    all_to_all x1, blocking collectives: 18.1 us -> 13.4 us  [shards(): column = lax.all_to_all(column, 'gy', 0, 0, tiled=True)]
    ppermute x8, waiting for transfers between devices: 9.01 us -> 4.77 us  [the longest x4 3.23 us: swap(): lax.ppermute(to_near, axis, pairs(0))]
    all_to_all x1, blocking collectives: 18.6 us -> 20.7 us  [shards(): packed = lax.all_to_all(packed, 'gz', 0, 0, tiled=True)]
    all_to_all x1, starting transfers between devices: 7.55 us -> 5.64 us  [shards(): lax.all_to_all(cotangent[:, 0].transpose(1, 0, 2), 'gz', 0, 0, tiled=True)]
  transfers between devices with their start and end apart: 10 -> 10, of which waited for: 5 -> 5; matrix products, arithmetic and copies ran while one was open for 3% -> 2% of each run, Pallas kernels for 3% -> 3%
where the time goes in v11:
time: 99.3 us; the launch traced here: 98.7 us
  blocking collectives  34 us (34%)
  starting transfers between devices  31.8 us (32%)
  Pallas kernels  16 us (16%)
  waiting for transfers between devices  12.8 us (13%)
  local copies, waits for them, and re-layouts  2.34 us (2%)
    all_to_all x1, blocking collectives, shards(): packed = lax.all_to_all(packed, 'gz', 0, 0, tiled=True)  20.7 us
    all_to_all x1, blocking collectives, shards(): column = lax.all_to_all(column, 'gy', 0, 0, tiled=True)  13.4 us
    ppermute x4, starting transfers between devices, swap(): lax.ppermute(to_far, axis, pairs(1))  12.9 us
    ppermute x4, starting transfers between devices, swap(): lax.ppermute(to_near, axis, pairs(0))  7.93 us
    all_to_all x1, waiting for transfers between devices, shards(): shared = lax.all_to_all(run_share(column, size_z), 'gz', 0, 0, tiled=True)  6.99 us
    pallas_call x1, Pallas kernels, run_forward(): pl.pallas_call(forward_kernel, name='forward', out_shape=(jax.ShapeDtypeS...  6.44 us
    all_to_all x1, starting transfers between devices, shards(): lax.all_to_all(cotangent[:, 0].transpose(1, 0, 2), 'gz', 0, 0, tiled=True)  5.64 us
    all_to_all x1, starting transfers between devices, shards(): shared = lax.all_to_all(run_share(column, size_z), 'gz', 0, 0, tiled=True)  5.36 us
  transfers between devices with their start and end apart: 10, of which 5 were waited for; matrix products, arithmetic and copies ran while one was open for 2% of the time, Pallas kernels for 3%

profile of v11, /device:TPU:1, one launch (start us, length us, event | category | flops | bytes accessed | tf_op | source)
XLA Modules:
  0.0 98.7 jit_solution(17650229224190530939)
XLA Ops:
  0.7 0.9 copy.18
  1.6 6.0 %collective-permute-start.1 = (bf16[8,32,128]{2,1,0:T(8,128)(2,1)S(1)}, bf16[8,32,128]{2,1,0:T(8,128)(2,1)S(1)}, u32[]{:S(2)}, u32[]{:S(2)}) collective-permute-start(bf16[8,32,128]{2,1,0:T(8,128)(2,1)S(1)} %bitcast.28), channel_id=1, source_target_pairs={{1,2},{3,4},{5,6},{7,8},{9,10},{11,12},{13,14},{2,1},{4,3},{6,5},{... | collective-permute-start | bytes 196616 | tf_op jit(solution)/shard_map/ppermute | solution.py:704
  7.7 0.1 collective-permute-start
  7.8 1.4 %copy.22 = bf16[8,1,16,16]{3,0,2,1:T(8,128)(2,1)} copy(bf16[8,1,16,16]{3,2,1,0:T(8,128)(2,1)} %param.15) | data formatting | bytes 8192 | tf_op args[7]
  9.1 5.6 %all-to-all-start = ((bf16[16,8,16]{2,1,0:T(8,128)(2,1)}), bf16[16,8,16]{2,1,0:T(8,128)(2,1)S(1)}, u32[]{:S(2)}, u32[]{:S(2)}) async-start(bf16[16,8,16]{2,1,0:T(8,128)(2,1)} %bitcast.25), calls=%async_computation | async-start | bytes 65536 | tf_op jit(solution)/shard_map/all_to_all | solution.py:712
  14.8 0.0 collective-permute-done.1
  14.8 0.0 collective-permute-done
  14.8 0.1 pad_maximum_fusion.mid
  14.9 0.7 collective-permute-start.3
  15.6 4.6 %collective-permute-start.2 = (bf16[8,88,128]{2,1,0:T(8,128)(2,1)S(1)}, bf16[8,88,128]{2,1,0:T(8,128)(2,1)S(1)}, u32[]{:S(2)}, u32[]{:S(2)}) collective-permute-start(bf16[8,88,128]{2,1,0:T(8,128)(2,1)S(1)} %pad_maximum_fusion.mid), channel_id=1, source_target_pairs={{0,16},{32,48},{64,80},{96,112},{16,0},{48,32},{80,64},{112,96},{1... | collective-permute-start | bytes 540680 | tf_op jit(solution)/shard_map/ppermute | solution.py:704
  20.2 0.8 convert_bitcast_fusion.1.k1
  21.1 1.0 %all-to-all-done = bf16[16,8,16]{2,1,0:T(8,128)(2,1)S(1)} async-done(((bf16[16,8,16]{2,1,0:T(8,128)(2,1)}), bf16[16,8,16]{2,1,0:T(8,128)(2,1)S(1)}, u32[]{:S(2)}, u32[]{:S(2)}) %all-to-all-start) | async-done | bytes 4128 | tf_op jit(solution)/shard_map/all_to_all | solution.py:712
  22.1 0.0 collective-permute-done.3.far
  22.1 2.7 %collective-permute-done.2.near = bf16[8,88,128]{2,1,0:T(8,128)(2,1)S(1)} collective-permute-done((bf16[8,88,128]{2,1,0:T(8,128)(2,1)S(1)}, bf16[8,88,128]{2,1,0:T(8,128)(2,1)S(1)}, u32[]{:S(2)}, u32[]{:S(2)}) %collective-permute-start.2) | collective-permute-done | bytes 180256 | tf_op jit(solution)/shard_map/ppermute | solution.py:704
  24.8 6.4 %forward.1 = (bf16[144,128]{1,0:T(8,128)(2,1)S(1)}, bf16[144,128]{1,0:T(8,128)(2,1)S(1)}, bf16[4,4,16,128]{3,2,1,0:T(8,128)(2,1)S(1)}, bf16[16,128]{1,0:T(8,128)...) custom-call(bf16[8,88,128]{2,1,0:T(8,128)(2,1)S(1)} %collective-perm, ...), custom_call_target="tpu_custom_call" | custom-call | flops 5000000000 | bytes 8000000 | tf_op jit(solution)/shard_map/forward/pallas_call | solution.py:263
  31.3 5.5 %collective-permute-start.4 = (bf16[144,128]{1,0:T(8,128)(2,1)S(1)}, bf16[144,128]{1,0:T(8,128)(2,1)S(1)}, u32[]{:S(2)}, u32[]{:S(2)}) collective-permute-start(bf16[144,128]{1,0:T(8,128)(2,1)S(1)} %get-tuple-element.45), channel_id=1, source_target_pairs={{1,2},{3,4},{5,6},{7,8},{9,10},{11,12},{13,14},{2,1},{4,3},{6,5},{... | collective-permute-start | bytes 110600 | tf_op jit(solution)/shard_map/ppermute | solution.py:704
  36.8 0.1 collective-permute-start.5
  36.9 1.5 %collective-permute-done.4.far = bf16[144,128]{1,0:T(8,128)(2,1)S(1)} collective-permute-done((bf16[144,128]{1,0:T(8,128)(2,1)S(1)}, bf16[144,128]{1,0:T(8,128)(2,1)S(1)}, u32[]{:S(2)}, u32[]{:S(2)}) %collective-permute-start.4) | collective-permute-done | bytes 36896 | tf_op jit(solution)/shard_map/ppermute | solution.py:704
  38.4 0.0 collective-permute-done.5.near
  38.5 0.7 collective-permute-start.6
  39.2 3.1 %collective-permute-start.7 = (bf16[304,128]{1,0:T(8,128)(2,1)S(1)}, bf16[304,128]{1,0:T(8,128)(2,1)S(1)}, u32[]{:S(2)}, u32[]{:S(2)}) collective-permute-start(bf16[304,128]{1,0:T(8,128)(2,1)S(1)} %get-tuple-element.52), channel_id=1, source_target_pairs={{0,16},{32,48},{64,80},{96,112},{16,0},{48,32},{80,64},{112,96},{1... | collective-permute-start | bytes 233480 | tf_op jit(solution)/shard_map/ppermute | solution.py:704
  42.3 2.1 %own.1 = (bf16[16,120,128]{2,1,0:T(8,128)(2,1)S(1)}, f32[1,128]{1,0:T(1,128)S(1)}, bf16[9,256,256]{2,1,0:T(8,128)(2,1)S(1)}, f32[1,256]{1,0:T(1,128)S(1)}, f32[4,256,256]{2,1,0:T(8,128)S(1)}) custom-call(bf16[4,4,16,128]{3,2,1,0:T(8,128)(2,1)S(1)} %get-tuple-element.47.hidden2.middle, bf16[16,128]{1,0:T(8,128)(2,1)S(1)} %get-tuple-element.48.own_cot, ...), custom_call_target="tpu_custom_call" | custom-call | flops 150000000 | bytes 4000000 | tf_op jit(solution)/shard_map/own/pallas_call | solution.py:400
  44.4 0.5 collective-permute-done.7.near
  44.9 4.4 %backward.1 = bf16[16,152,128]{2,1,0:T(8,128)(2,1)S(1)} custom-call(bf16[304,128]{1,0:T(8,128)(2,1)S(1)} %collective-permute-done.6.far, bf16[144,128]{1,0:T(8,128)(2,1)S(1)} %get-tuple-element.50.lower, bf16[4,4,16,128]{3,2,1,0:T(8,128)(2,1)S(1)} %get-tuple-element.47.hidden2.middle, bf16[144,128]{1,0:T(8,128)(2,1)S(1)} %get-tuple-element.51.upper, ...), custom_call_target="tpu_custom_call" | custom-call | tf_op jit(solution)/shard_map/backward/pallas_call | solution.py:572
  49.3 20.7 %all_to_all.20.received = bf16[16,152,128]{2,1,0:T(8,128)(2,1)S(1)} all-to-all(bf16[16,152,128]{2,1,0:T(8,128)(2,1)S(1)} %backward.1), channel_id=1, replica_groups=mesh['gy'=8,'gz'=16] {'gz'}, dimensions={0} | all-to-all | bytes 1245184 | tf_op jit(solution)/shard_map/all_to_all | solution.py:737
  70.0 0.7 sum.1
  70.7 13.4 %all_to_all.21.column = bf16[8,144,128]{2,1,0:T(8,128)(2,1)S(1)} all-to-all(bf16[8,144,128]{2,1,0:T(8,128)(2,1)S(1)} %get-tuple-element.65), channel_id=1, replica_groups=mesh['gy'=8,'gz'=16] {'gy'}, dimensions={0} | all-to-all | bytes 589824 | tf_op jit(solution)/shard_map/all_to_all | solution.py:739
  84.1 0.7 share.1
  84.8 5.4 %all-to-all-start.3 = ((bf16[16,32,128]{2,1,0:T(8,128)(2,1)}), bf16[16,32,128]{2,1,0:T(8,128)(2,1)S(1)}, u32[]{:S(2)}, u32[]{:S(2)}) async-start(bf16[16,32,128]{2,1,0:T(8,128)(2,1)} %share.1), calls=%async_computation.3 | async-start | bytes 262144 | tf_op jit(solution)/shard_map/all_to_all | solution.py:740
  90.1 0.7 third.1
  90.9 7.0 %all-to-all-done.3.shared = bf16[16,32,128]{2,1,0:T(8,128)(2,1)S(1)} async-done(((bf16[16,32,128]{2,1,0:T(8,128)(2,1)}), bf16[16,32,128]{2,1,0:T(8,128)(2,1)S(1)}, u32[]{:S(2)}, u32[]{:S(2)}) %all-to-all-start.3) | async-done | bytes 131104 | tf_op jit(solution)/shard_map/all_to_all | solution.py:740
  97.8 0.9 unpack.1
  (16 shorter events, 0.2 us)
Async XLA Ops:
  0.6 20.4 %copy-start.2 = (f32[128]{0:T(128)S(1)}, f32[128]{0:T(128)}, u32[]{:S(2)}) copy-start(f32[128]{0:T(128)} %param.14) | copy-start | bytes 1540
  0.6 20.4 %copy-start.3 = (f32[64]{0:T(128)S(1)}, f32[64]{0:T(128)}, u32[]{:S(2)}) copy-start(f32[64]{0:T(128)} %param.12) | copy-start | bytes 772
  0.7 20.3 %copy-start.1 = (bf16[27,64,32]{1,2,0:T(8,128)(2,1)S(1)}, bf16[27,64,32]{1,2,0:T(8,128)(2,1)}, u32[]{:S(2)}) copy-start(bf16[27,64,32]{1,2,0:T(8,128)(2,1)} %param.11) | copy-start | bytes 331780
  0.7 20.4 %copy-start.4 = (f32[32]{0:T(128)S(1)}, f32[32]{0:T(128)}, u32[]{:S(2)}) copy-start(f32[32]{0:T(128)} %param.10) | copy-start | bytes 388
  1.6 13.2 %collective-permute-start.1 = (bf16[8,32,128]{2,1,0:T(8,128)(2,1)S(1)}, bf16[8,32,128]{2,1,0:T(8,128)(2,1)S(1)}, u32[]{:S(2)}, u32[]{:S(2)}) collective-permute-start(bf16[8,32,128]{2,1,0:T(8,128)(2,1)S(1)} %bitcast.28), channel_id=1, source_target_pairs={{1,2},{3,4},{5,6},{7,8},{9,10},{11,12},{13,14},{2,1},{4,3},{6,5},{... | collective-permute-start | bytes 196616 | tf_op jit(solution)/shard_map/ppermute | solution.py:704
  7.7 7.1 %collective-permute-start = (bf16[8,32,128]{2,1,0:T(8,128)(2,1)S(1)}, bf16[8,32,128]{2,1,0:T(8,128)(2,1)S(1)}, u32[]{:S(2)}, u32[]{:S(2)}) collective-permute-start(bf16[8,32,128]{2,1,0:T(8,128)(2,1)S(1)} %bitcast.29), channel_id=1, source_target_pairs={{0,1},{2,3},{4,5},{6,7},{8,9},{10,11},{12,13},{14,15},{1,0},{3,2},... | collective-permute-start | bytes 196616 | tf_op jit(solution)/shard_map/ppermute | solution.py:704
  9.1 12.9 %all-to-all-start = ((bf16[16,8,16]{2,1,0:T(8,128)(2,1)}), bf16[16,8,16]{2,1,0:T(8,128)(2,1)S(1)}, u32[]{:S(2)}, u32[]{:S(2)}) async-start(bf16[16,8,16]{2,1,0:T(8,128)(2,1)} %bitcast.25), calls=%async_computation | async-start | bytes 65536 | tf_op jit(solution)/shard_map/all_to_all | solution.py:712
  14.9 7.2 %collective-permute-start.3 = (bf16[8,88,128]{2,1,0:T(8,128)(2,1)S(1)}, bf16[8,88,128]{2,1,0:T(8,128)(2,1)S(1)}, u32[]{:S(2)}, u32[]{:S(2)}) collective-permute-start(bf16[8,88,128]{2,1,0:T(8,128)(2,1)S(1)} %pad_maximum_fusion.mid), channel_id=1, source_target_pairs={{16,32},{48,64},{80,96},{32,16},{64,48},{96,80},{17,33},{49,65},{8... | collective-permute-start | bytes 540680 | tf_op jit(solution)/shard_map/ppermute | solution.py:704
  15.6 9.3 %collective-permute-start.2 = (bf16[8,88,128]{2,1,0:T(8,128)(2,1)S(1)}, bf16[8,88,128]{2,1,0:T(8,128)(2,1)S(1)}, u32[]{:S(2)}, u32[]{:S(2)}) collective-permute-start(bf16[8,88,128]{2,1,0:T(8,128)(2,1)S(1)} %pad_maximum_fusion.mid), channel_id=1, source_target_pairs={{0,16},{32,48},{64,80},{96,112},{16,0},{48,32},{80,64},{112,96},{1... | collective-permute-start | bytes 540680 | tf_op jit(solution)/shard_map/ppermute | solution.py:704
  24.8 17.5 %copy-start = (bf16[27,128,64]{1,2,0:T(8,128)(2,1)S(1)}, bf16[27,128,64]{1,2,0:T(8,128)(2,1)}, u32[]{:S(2)}) copy-start(bf16[27,128,64]{1,2,0:T(8,128)(2,1)} %param.13) | copy-start | bytes 1327108
  31.3 7.2 %collective-permute-start.4 = (bf16[144,128]{1,0:T(8,128)(2,1)S(1)}, bf16[144,128]{1,0:T(8,128)(2,1)S(1)}, u32[]{:S(2)}, u32[]{:S(2)}) collective-permute-start(bf16[144,128]{1,0:T(8,128)(2,1)S(1)} %get-tuple-element.45), channel_id=1, source_target_pairs={{1,2},{3,4},{5,6},{7,8},{9,10},{11,12},{13,14},{2,1},{4,3},{6,5},{... | collective-permute-start | bytes 110600 | tf_op jit(solution)/shard_map/ppermute | solution.py:704
  36.8 1.6 %collective-permute-start.5 = (bf16[144,128]{1,0:T(8,128)(2,1)S(1)}, bf16[144,128]{1,0:T(8,128)(2,1)S(1)}, u32[]{:S(2)}, u32[]{:S(2)}) collective-permute-start(bf16[144,128]{1,0:T(8,128)(2,1)S(1)} %get-tuple-element.46), channel_id=1, source_target_pairs={{0,1},{2,3},{4,5},{6,7},{8,9},{10,11},{12,13},{14,15},{1,0},{3,2},... | collective-permute-start | bytes 110600 | tf_op jit(solution)/shard_map/ppermute | solution.py:704
  38.5 5.9 %collective-permute-start.6 = (bf16[304,128]{1,0:T(8,128)(2,1)S(1)}, bf16[304,128]{1,0:T(8,128)(2,1)S(1)}, u32[]{:S(2)}, u32[]{:S(2)}) collective-permute-start(bf16[304,128]{1,0:T(8,128)(2,1)S(1)} %get-tuple-element.49), channel_id=1, source_target_pairs={{16,32},{48,64},{80,96},{32,16},{64,48},{96,80},{17,33},{49,65},{8... | collective-permute-start | bytes 233480 | tf_op jit(solution)/shard_map/ppermute | solution.py:704
  39.2 5.7 %collective-permute-start.7 = (bf16[304,128]{1,0:T(8,128)(2,1)S(1)}, bf16[304,128]{1,0:T(8,128)(2,1)S(1)}, u32[]{:S(2)}, u32[]{:S(2)}) collective-permute-start(bf16[304,128]{1,0:T(8,128)(2,1)S(1)} %get-tuple-element.52), channel_id=1, source_target_pairs={{0,16},{32,48},{64,80},{96,112},{16,0},{48,32},{80,64},{112,96},{1... | collective-permute-start | bytes 233480 | tf_op jit(solution)/shard_map/ppermute | solution.py:704
  84.8 13.1 %all-to-all-start.3 = ((bf16[16,32,128]{2,1,0:T(8,128)(2,1)}), bf16[16,32,128]{2,1,0:T(8,128)(2,1)S(1)}, u32[]{:S(2)}, u32[]{:S(2)}) async-start(bf16[16,32,128]{2,1,0:T(8,128)(2,1)} %share.1), calls=%async_computation.3 | async-start | bytes 262144 | tf_op jit(solution)/shard_map/all_to_all | solution.py:740

commit v12 on v11

--- a/solution.py
+++ b/solution.py
@@ -338,9 +338,9 @@
 
 
 def own_kernel(
-    hidden2, own_cot, k3, biases, turned_own, w1, packed, shift3, w3, wide3, ratio1, patches2, pre3, turned
+    hidden2, own_cot, k3, biases, turned_own, w1, keep, send, shift3, w3, wide3, ratio1, patches2, pre3, turned
 ):
-    groups = packed.shape[0]
+    groups = 2 * keep.shape[0]
     wide = 128 // groups
     bias1 = jnp.concatenate([biases[0:1, :32]] * 8, axis=1)
     for yw in range(4):
@@ -391,8 +391,17 @@
     for c in range(1, 8):
         feature_rows = feature_rows + roll(turned[pl.ds(c, 16, stride=8), :], 16 * c, 1)
     feature_rows = feature_rows.reshape(groups, wide // 8, 128)
-    fill = jnp.zeros((groups, packed.shape[1] - 14 * wide - wide // 8, 128), F32)
-    packed[...] = jnp.concatenate(kernel3 + [feature_rows, fill], axis=1).astype(BF16)
+    flag = odd("gz").astype(F32)
+    fill = jnp.zeros((groups, keep.shape[1] - 14 * wide - wide // 4, 128), F32)
+    pieces = kernel3 + [feature_rows * (1.0 - flag), feature_rows * flag, fill]
+    keep[...], send[...] = halves(jnp.concatenate(pieces, axis=1))
+
+
+def halves(value):
+    flag = odd("gz").astype(F32)
+    pairs = value.reshape((value.shape[0] // 2, 2) + value.shape[1:])
+    even, other = pairs[:, 0], pairs[:, 1]
+    return (even * (1.0 - flag) + other * flag).astype(BF16), (even * flag + other * (1.0 - flag)).astype(BF16)
 
 
 def run_own(groups, *operands):
@@ -401,14 +410,15 @@
         own_kernel,
         name="own",
         out_shape=(
-            jax.ShapeDtypeStruct((groups, -(-(14 * wide + wide // 8) // 8) * 8, 128), BF16),
+            jax.ShapeDtypeStruct((groups // 2, -(-(14 * wide + wide // 4) // 8) * 8, 128), BF16),
+            jax.ShapeDtypeStruct((groups // 2, -(-(14 * wide + wide // 4) // 8) * 8, 128), BF16),
             jax.ShapeDtypeStruct((1, 128), F32),
             jax.ShapeDtypeStruct((9, 256, 256), BF16),
             jax.ShapeDtypeStruct((1, 256), F32),
             jax.ShapeDtypeStruct((4, 256, 256), F32),
         ),
         in_specs=[VMEM] * len(operands),
-        out_specs=(VMEM,) * 5,
+        out_specs=(VMEM,) * 6,
         scratch_shapes=[
             pltpu.VMEM((4, 4, 16, 256), BF16),
             pltpu.VMEM((64, 256), F32),
@@ -420,11 +430,11 @@
 
 
 def backward_kernel(
-    far, lower, middle, upper, near, own_cot, w3, bias3, w2, ratio2, patches1, ratio1, fields, packed3, shift3,
-    packed, before, after, patches2, pre3, delta3, patch2, grad2, delta2, patch1, beside, grad1, delta1,
+    far, lower, middle, upper, near, own_cot, w3, bias3, w2, ratio2, patches1, ratio1, fields, keep3, send3, shift3,
+    keep, send, before, after, patches2, pre3, delta3, patch2, grad2, delta2, patch1, beside, grad1, delta1,
 ):
     before[...], after[...] = sided("gy", far[...], near[...])
-    groups = packed.shape[0]
+    groups = 2 * keep.shape[0]
     half = lane((16, 128)) < 64
 
     def lay(y, source):
@@ -564,17 +574,18 @@
     )
     shared = jnp.concatenate(kernel2 + kernel1 + [shifts], axis=0)
     rows = 512 // groups
-    packed[:, :rows] = shared.reshape(groups, rows, 128).astype(BF16)
-    packed[:, rows:] = packed3[...]
+    keep[:, :rows], send[:, :rows] = halves(shared.reshape(groups, rows, 128))
+    keep[:, rows:] = keep3[...]
+    send[:, rows:] = send3[...]
 
 
 def run_backward(groups, *operands):
     return pl.pallas_call(
         backward_kernel,
         name="backward",
-        out_shape=jax.ShapeDtypeStruct((groups, 512 // groups + operands[-2].shape[1], 128), BF16),
+        out_shape=(jax.ShapeDtypeStruct((groups // 2, 512 // groups + operands[-2].shape[1], 128), BF16),) * 2,
         in_specs=[VMEM] * len(operands),
-        out_specs=VMEM,
+        out_specs=(VMEM, VMEM),
         scratch_shapes=[
             pltpu.VMEM((304, 128), BF16),
             pltpu.VMEM((304, 128), BF16),
@@ -593,25 +604,44 @@
     )(*operands)
 
 
+def pair_kernel(kept, received, total):
+    total[...] = (kept[...].astype(F32) + received[...].astype(F32)).astype(BF16)
+
+
+def run_pair(kept, received):
+    return pl.pallas_call(
+        pair_kernel,
+        name="pair",
+        out_shape=jax.ShapeDtypeStruct(kept.shape, BF16),
+        in_specs=[VMEM] * 2,
+        out_specs=VMEM,
+        compiler_params=pltpu.CompilerParams(vmem_limit_bytes=LIMIT),
+    )(kept, received)
+
+
 def sum_kernel(received, to_column, features):
-    groups, rows = received.shape[0], to_column.shape[1]
-    wide = 128 // groups
-    own = received[:, rows : rows + wide // 8].astype(F32)
+    half, rows = received.shape[0], to_column.shape[1]
+    wide = 64 // half
+    high = wide // 8
+    own = received[:, rows : rows + 2 * high].astype(F32)
     for c in range(wide):
-        features[c] = own[:, c // 8, (c % 8) * 16 : (c % 8) * 16 + 16].astype(BF16)
+        for parity in range(2):
+            line = own[:, parity * high + c // 8, (c % 8) * 16 : (c % 8) * 16 + 16]
+            for j in range(half):
+                features[c, 2 * j + parity : 2 * j + parity + 1] = line[j : j + 1]
     total = received[:, :rows].astype(F32).sum(axis=0)
     to_column[...] = jnp.broadcast_to(total[None], to_column.shape).astype(BF16)
 
 
 def run_sum(received, rows_y):
-    groups = received.shape[0]
+    groups = 2 * received.shape[0]
     wide = 128 // groups
     return pl.pallas_call(
         sum_kernel,
         name="sum",
         out_shape=(
             jax.ShapeDtypeStruct((rows_y, 512 // groups + 14 * wide, 128), BF16),
-            jax.ShapeDtypeStruct((wide, groups, 16), BF16),
+            jax.ShapeDtypeStruct((wide, groups, 16), F32),
         ),
         in_specs=[VMEM],
         out_specs=(VMEM, VMEM),
@@ -727,21 +757,24 @@
     )
     far, near = swap(to_far, to_near, "gz")
     to_far, to_near, lower, upper = run_weave(far, near, hidden2, own_cot)
-    packed3, shift3, w3, wide3, ratio1 = run_own(size_z, hidden2, own_cot, k3, biases, turned_own, w1)
+    keep3, send3, shift3, w3, wide3, ratio1 = run_own(size_z, hidden2, own_cot, k3, biases, turned_own, w1)
     far, near = swap(to_far, to_near, "gy")
-    packed = run_backward(
+    keep, send = run_backward(
         size_z,
         far, lower, hidden2, upper, near, own_cot, w3, wide3, w2, ratio2, patches1, ratio1, fields,
-        packed3, shift3,
+        keep3, send3, shift3,
     )
-    packed = lax.all_to_all(packed, "gz", 0, 0, tiled=True)
+    mates = [(i, i + 1 - 2 * (i % 2)) for i in range(size_z)]
+    packed = run_pair(keep, lax.ppermute(send, "gz", mates))
+    same = [list(range(parity, size_z, 2)) for parity in range(2)]
+    packed = lax.all_to_all(packed, "gz", 0, 0, tiled=True, axis_index_groups=same)
     column, features = run_sum(packed, size_y)
     column = lax.all_to_all(column, "gy", 0, 0, tiled=True)
     shared = lax.all_to_all(run_share(column, size_z), "gz", 0, 0, tiled=True)
     grad3 = run_third(column, wide)
     grad1, grad2, shift1, shift2, shift3 = run_unpack(shared)
     return (
-        features[:, None], grad1.transpose(0, 2, 1), shift1[0], grad2.transpose(0, 2, 1), shift2[0], grad3, shift3[0]
+        features[:, None].astype(BF16), grad1.transpose(0, 2, 1), shift1[0], grad2.transpose(0, 2, 1), shift2[0], grad3, shift3[0]
     )
 
 

time: 99.3 us -> 96.4 us (0.971)
  blocking collectives: 34 us -> 28.7 us
  starting transfers between devices: 31.8 us -> 33.6 us
    all_to_all x1, blocking collectives: 20.7 us -> 15.5 us  [shards(): lax.all_to_all(packed, 'gz', 0, 0, tiled=True, axis_index_groups=same)]
    ppermute x0 -> x1, waiting for transfers between devices: none -> 1.23 us  [shards(): packed = run_pair(keep, lax.ppermute(send, 'gz', mates))]
    all_to_all x1, starting transfers between devices: 5.36 us -> 6.38 us  [shards(): shared = lax.all_to_all(run_share(column, size_z), 'gz', 0, 0, tiled=True)]
    pallas_call x1 -> x2, Pallas kernels: 4.37 us -> 4.43 us  [the longest x1 4.35 us: run_backward(): pl.pallas_call(backward_kernel, name='backward', out_shape=(jax.ShapeDtyp...]
  transfers between devices with their start and end apart: 10 -> 11, of which waited for: 5 -> 6; matrix products, arithmetic and copies ran while one was open for 2% -> 3% of each run, Pallas kernels for 3% -> 3%
where the time goes in v12:
time: 96.4 us; the launch traced here: 95.9 us
  starting transfers between devices  33.6 us (35%)
  blocking collectives  28.7 us (30%)
  Pallas kernels  15.5 us (16%)
  waiting for transfers between devices  13.3 us (14%)
  local copies, waits for them, and re-layouts  2.34 us (2%)
  other arithmetic  1.51 us (2%)
    all_to_all x1, blocking collectives, shards(): lax.all_to_all(packed, 'gz', 0, 0, tiled=True, axis_index_groups=same)  15.5 us
    all_to_all x1, blocking collectives, shards(): column = lax.all_to_all(column, 'gy', 0, 0, tiled=True)  13.2 us
    ppermute x4, starting transfers between devices, swap(): lax.ppermute(to_far, axis, pairs(1))  12.9 us
    ppermute x4, starting transfers between devices, swap(): lax.ppermute(to_near, axis, pairs(0))  7.93 us
    pallas_call x1, Pallas kernels, run_forward(): pl.pallas_call(forward_kernel, name='forward', out_shape=(jax.ShapeDtypeS...  6.44 us
    all_to_all x1, starting transfers between devices, shards(): shared = lax.all_to_all(run_share(column, size_z), 'gz', 0, 0, tiled=True)  6.38 us
    all_to_all x1, waiting for transfers between devices, shards(): shared = lax.all_to_all(run_share(column, size_z), 'gz', 0, 0, tiled=True)  6.37 us
    all_to_all x1, starting transfers between devices, shards(): lax.all_to_all(cotangent[:, 0].transpose(1, 0, 2), 'gz', 0, 0, tiled=True)  5.64 us
  transfers between devices with their start and end apart: 11, of which 6 were waited for; matrix products, arithmetic and copies ran while one was open for 3% of the time, Pallas kernels for 3%

profile of v12, /device:TPU:1, one launch (start us, length us, event | category | flops | bytes accessed | tf_op | source)
XLA Modules:
  0.0 95.9 jit_solution(18265482227926770518)
XLA Ops:
  0.7 0.9 copy.18
  1.6 6.0 %collective-permute-start.1 = (bf16[8,32,128]{2,1,0:T(8,128)(2,1)S(1)}, bf16[8,32,128]{2,1,0:T(8,128)(2,1)S(1)}, u32[]{:S(2)}, u32[]{:S(2)}) collective-permute-start(bf16[8,32,128]{2,1,0:T(8,128)(2,1)S(1)} %bitcast.29), channel_id=1, source_target_pairs={{1,2},{3,4},{5,6},{7,8},{9,10},{11,12},{13,14},{2,1},{4,3},{6,5},{... | collective-permute-start | bytes 196616 | tf_op jit(solution)/shard_map/ppermute | solution.py:734
  7.7 0.1 collective-permute-start
  7.8 1.4 %copy.22 = bf16[8,1,16,16]{3,0,2,1:T(8,128)(2,1)} copy(bf16[8,1,16,16]{3,2,1,0:T(8,128)(2,1)} %param.15) | data formatting | bytes 8192 | tf_op args[7]
  9.1 5.6 %all-to-all-start = ((bf16[16,8,16]{2,1,0:T(8,128)(2,1)}), bf16[16,8,16]{2,1,0:T(8,128)(2,1)S(1)}, u32[]{:S(2)}, u32[]{:S(2)}) async-start(bf16[16,8,16]{2,1,0:T(8,128)(2,1)} %bitcast.26), calls=%async_computation | async-start | bytes 65536 | tf_op jit(solution)/shard_map/all_to_all | solution.py:742
  14.8 0.1 pad_maximum_fusion.mid
  14.9 0.7 collective-permute-start.3
  15.6 4.6 %collective-permute-start.2 = (bf16[8,88,128]{2,1,0:T(8,128)(2,1)S(1)}, bf16[8,88,128]{2,1,0:T(8,128)(2,1)S(1)}, u32[]{:S(2)}, u32[]{:S(2)}) collective-permute-start(bf16[8,88,128]{2,1,0:T(8,128)(2,1)S(1)} %pad_maximum_fusion.mid), channel_id=1, source_target_pairs={{0,16},{32,48},{64,80},{96,112},{16,0},{48,32},{80,64},{112,96},{1... | collective-permute-start | bytes 540680 | tf_op jit(solution)/shard_map/ppermute | solution.py:734
  20.2 0.8 convert_bitcast_fusion.1.k1
  21.1 1.0 %all-to-all-done = bf16[16,8,16]{2,1,0:T(8,128)(2,1)S(1)} async-done(((bf16[16,8,16]{2,1,0:T(8,128)(2,1)}), bf16[16,8,16]{2,1,0:T(8,128)(2,1)S(1)}, u32[]{:S(2)}, u32[]{:S(2)}) %all-to-all-start) | async-done | bytes 4128 | tf_op jit(solution)/shard_map/all_to_all | solution.py:742
  22.1 2.7 %collective-permute-done.2.near = bf16[8,88,128]{2,1,0:T(8,128)(2,1)S(1)} collective-permute-done((bf16[8,88,128]{2,1,0:T(8,128)(2,1)S(1)}, bf16[8,88,128]{2,1,0:T(8,128)(2,1)S(1)}, u32[]{:S(2)}, u32[]{:S(2)}) %collective-permute-start.2) | collective-permute-done | bytes 180256 | tf_op jit(solution)/shard_map/ppermute | solution.py:734
  24.8 6.4 %forward.1 = (bf16[144,128]{1,0:T(8,128)(2,1)S(1)}, bf16[144,128]{1,0:T(8,128)(2,1)S(1)}, bf16[4,4,16,128]{3,2,1,0:T(8,128)(2,1)S(1)}, bf16[16,128]{1,0:T(8,128)...) custom-call(bf16[8,88,128]{2,1,0:T(8,128)(2,1)S(1)} %collective-perm, ...), custom_call_target="tpu_custom_call" | custom-call | flops 5000000000 | bytes 8000000 | tf_op jit(solution)/shard_map/forward/pallas_call | solution.py:263
  31.3 5.5 %collective-permute-start.4 = (bf16[144,128]{1,0:T(8,128)(2,1)S(1)}, bf16[144,128]{1,0:T(8,128)(2,1)S(1)}, u32[]{:S(2)}, u32[]{:S(2)}) collective-permute-start(bf16[144,128]{1,0:T(8,128)(2,1)S(1)} %get-tuple-element.48), channel_id=1, source_target_pairs={{1,2},{3,4},{5,6},{7,8},{9,10},{11,12},{13,14},{2,1},{4,3},{6,5},{... | collective-permute-start | bytes 110600 | tf_op jit(solution)/shard_map/ppermute | solution.py:734
  36.8 0.1 collective-permute-start.5
  36.9 1.5 %collective-permute-done.4.far = bf16[144,128]{1,0:T(8,128)(2,1)S(1)} collective-permute-done((bf16[144,128]{1,0:T(8,128)(2,1)S(1)}, bf16[144,128]{1,0:T(8,128)(2,1)S(1)}, u32[]{:S(2)}, u32[]{:S(2)}) %collective-permute-start.4) | collective-permute-done | bytes 36896 | tf_op jit(solution)/shard_map/ppermute | solution.py:734
  38.5 0.7 collective-permute-start.6
  39.2 3.1 %collective-permute-start.7 = (bf16[304,128]{1,0:T(8,128)(2,1)S(1)}, bf16[304,128]{1,0:T(8,128)(2,1)S(1)}, u32[]{:S(2)}, u32[]{:S(2)}) collective-permute-start(bf16[304,128]{1,0:T(8,128)(2,1)S(1)} %get-tuple-element.55), channel_id=1, source_target_pairs={{0,16},{32,48},{64,80},{96,112},{16,0},{48,32},{80,64},{112,96},{1... | collective-permute-start | bytes 233480 | tf_op jit(solution)/shard_map/ppermute | solution.py:734
  42.3 2.2 %own.1 = (bf16[8,120,128]{2,1,0:T(8,128)(2,1)S(1)}, bf16[8,120,128]{2,1,0:T(8,128)(2,1)S(1)}, f32[1,128]{1,0:T(1,128)S(1)}, bf16[9,256,256]{2,1,0:T(8,128)(2,1)S...) custom-call(bf16[4,4,16,128]{3,2,1,0:T(8,128)(2,1)S(1)} %get-tuple-element.50.hidden2.middle, ...), custom_call_target="tpu_custom_call" | custom-call | flops 150000000 | bytes 4000000 | tf_op jit(solution)/shard_map/own/pallas_call | solution.py:409
  44.5 0.4 collective-permute-done.7.near
  44.9 4.3 %backward.1 = (bf16[8,152,128]{2,1,0:T(8,128)(2,1)S(1)}, bf16[8,152,128]{2,1,0:T(8,128)(2,1)S(1)}) custom-call(bf16[304,128]{1,0:T(8,128)(2,1)S(1)} %collective-permute-done.6.far, bf16[144,128]{1,0:T(8,128)(2,1)S(1)} %get-tuple-element.53.lower, bf16[4,4,16,128]{3,2,1,0:T(8,128)(2,1)S(1)} %get-tuple-element.50.hidden2.middle, ...), custom_call_target="tpu_custom_call" | custom-call | tf_op jit(solution)/shard_map/backward/pallas_call | solution.py:583
  49.3 0.8 collective-permute-start.8
  50.0 1.2 %collective-permute-done.8.received = bf16[8,152,128]{2,1,0:T(8,128)(2,1)S(1)} collective-permute-done((bf16[8,152,128]{2,1,0:T(8,128)(2,1)S(1)}, bf16[8,152,128]{2,1,0:T(8,128)(2,1)S(1)}, u32[]{:S(2)}, u32[]{:S(2)}) %collective-permute-start.8) | collective-permute-done | bytes 311328 | tf_op jit(solution)/shard_map/ppermute | solution.py:768
  51.3 0.1 pair.1
  51.4 15.5 %all_to_all.20.received = bf16[8,152,128]{2,1,0:T(8,128)(2,1)S(1)} all-to-all(bf16[8,152,128]{2,1,0:T(8,128)(2,1)S(1)} %pair.1), channel_id=1, replica_groups={{0,2,4,6,8,10,12,14},{1,3,5,7,9,11,13,15},{16,18,20,22,24,26,28,30},{17..., dimensions={0} | all-to-all | bytes 622592 | tf_op jit(solution)/shard_map/all_to_all | solution.py:770
  66.9 0.1 sum.1
  67.0 13.2 %all_to_all.21.column = bf16[8,144,128]{2,1,0:T(8,128)(2,1)S(1)} all-to-all(bf16[8,144,128]{2,1,0:T(8,128)(2,1)S(1)} %get-tuple-element.71), channel_id=1, replica_groups=mesh['gy'=8,'gz'=16] {'gy'}, dimensions={0} | all-to-all | bytes 589824 | tf_op jit(solution)/shard_map/all_to_all | solution.py:772
  80.2 0.7 share.1
  80.9 6.4 %all-to-all-start.3 = ((bf16[16,32,128]{2,1,0:T(8,128)(2,1)}), bf16[16,32,128]{2,1,0:T(8,128)(2,1)S(1)}, u32[]{:S(2)}, u32[]{:S(2)}) async-start(bf16[16,32,128]{2,1,0:T(8,128)(2,1)} %share.1), calls=%async_computation.3 | async-start | bytes 262144 | tf_op jit(solution)/shard_map/all_to_all | solution.py:773
  87.3 0.6 convert_bitcast_fusion.2
  87.9 0.7 third.1
  88.6 6.4 %all-to-all-done.3.shared = bf16[16,32,128]{2,1,0:T(8,128)(2,1)S(1)} async-done(((bf16[16,32,128]{2,1,0:T(8,128)(2,1)}), bf16[16,32,128]{2,1,0:T(8,128)(2,1)S(1)}, u32[]{:S(2)}, u32[]{:S(2)}) %all-to-all-start.3) | async-done | bytes 131104 | tf_op jit(solution)/shard_map/all_to_all | solution.py:773
  95.0 0.9 unpack.1
  (20 shorter events, 0.2 us)
Async XLA Ops:
  0.6 20.4 %copy-start.2 = (f32[128]{0:T(128)S(1)}, f32[128]{0:T(128)}, u32[]{:S(2)}) copy-start(f32[128]{0:T(128)} %param.14) | copy-start | bytes 1540
  0.6 20.4 %copy-start.3 = (f32[64]{0:T(128)S(1)}, f32[64]{0:T(128)}, u32[]{:S(2)}) copy-start(f32[64]{0:T(128)} %param.12) | copy-start | bytes 772
  0.7 20.3 %copy-start.1 = (bf16[27,64,32]{1,2,0:T(8,128)(2,1)S(1)}, bf16[27,64,32]{1,2,0:T(8,128)(2,1)}, u32[]{:S(2)}) copy-start(bf16[27,64,32]{1,2,0:T(8,128)(2,1)} %param.11) | copy-start | bytes 331780
  0.7 20.4 %copy-start.4 = (f32[32]{0:T(128)S(1)}, f32[32]{0:T(128)}, u32[]{:S(2)}) copy-start(f32[32]{0:T(128)} %param.10) | copy-start | bytes 388
  1.6 13.2 %collective-permute-start.1 = (bf16[8,32,128]{2,1,0:T(8,128)(2,1)S(1)}, bf16[8,32,128]{2,1,0:T(8,128)(2,1)S(1)}, u32[]{:S(2)}, u32[]{:S(2)}) collective-permute-start(bf16[8,32,128]{2,1,0:T(8,128)(2,1)S(1)} %bitcast.29), channel_id=1, source_target_pairs={{1,2},{3,4},{5,6},{7,8},{9,10},{11,12},{13,14},{2,1},{4,3},{6,5},{... | collective-permute-start | bytes 196616 | tf_op jit(solution)/shard_map/ppermute | solution.py:734
  7.7 7.1 %collective-permute-start = (bf16[8,32,128]{2,1,0:T(8,128)(2,1)S(1)}, bf16[8,32,128]{2,1,0:T(8,128)(2,1)S(1)}, u32[]{:S(2)}, u32[]{:S(2)}) collective-permute-start(bf16[8,32,128]{2,1,0:T(8,128)(2,1)S(1)} %bitcast.30), channel_id=1, source_target_pairs={{0,1},{2,3},{4,5},{6,7},{8,9},{10,11},{12,13},{14,15},{1,0},{3,2},... | collective-permute-start | bytes 196616 | tf_op jit(solution)/shard_map/ppermute | solution.py:734
  9.1 12.9 %all-to-all-start = ((bf16[16,8,16]{2,1,0:T(8,128)(2,1)}), bf16[16,8,16]{2,1,0:T(8,128)(2,1)S(1)}, u32[]{:S(2)}, u32[]{:S(2)}) async-start(bf16[16,8,16]{2,1,0:T(8,128)(2,1)} %bitcast.26), calls=%async_computation | async-start | bytes 65536 | tf_op jit(solution)/shard_map/all_to_all | solution.py:742
  14.9 7.2 %collective-permute-start.3 = (bf16[8,88,128]{2,1,0:T(8,128)(2,1)S(1)}, bf16[8,88,128]{2,1,0:T(8,128)(2,1)S(1)}, u32[]{:S(2)}, u32[]{:S(2)}) collective-permute-start(bf16[8,88,128]{2,1,0:T(8,128)(2,1)S(1)} %pad_maximum_fusion.mid), channel_id=1, source_target_pairs={{16,32},{48,64},{80,96},{32,16},{64,48},{96,80},{17,33},{49,65},{8... | collective-permute-start | bytes 540680 | tf_op jit(solution)/shard_map/ppermute | solution.py:734
  15.6 9.3 %collective-permute-start.2 = (bf16[8,88,128]{2,1,0:T(8,128)(2,1)S(1)}, bf16[8,88,128]{2,1,0:T(8,128)(2,1)S(1)}, u32[]{:S(2)}, u32[]{:S(2)}) collective-permute-start(bf16[8,88,128]{2,1,0:T(8,128)(2,1)S(1)} %pad_maximum_fusion.mid), channel_id=1, source_target_pairs={{0,16},{32,48},{64,80},{96,112},{16,0},{48,32},{80,64},{112,96},{1... | collective-permute-start | bytes 540680 | tf_op jit(solution)/shard_map/ppermute | solution.py:734
  24.8 17.5 %copy-start = (bf16[27,128,64]{1,2,0:T(8,128)(2,1)S(1)}, bf16[27,128,64]{1,2,0:T(8,128)(2,1)}, u32[]{:S(2)}) copy-start(bf16[27,128,64]{1,2,0:T(8,128)(2,1)} %param.13) | copy-start | bytes 1327108
  31.3 7.2 %collective-permute-start.4 = (bf16[144,128]{1,0:T(8,128)(2,1)S(1)}, bf16[144,128]{1,0:T(8,128)(2,1)S(1)}, u32[]{:S(2)}, u32[]{:S(2)}) collective-permute-start(bf16[144,128]{1,0:T(8,128)(2,1)S(1)} %get-tuple-element.48), channel_id=1, source_target_pairs={{1,2},{3,4},{5,6},{7,8},{9,10},{11,12},{13,14},{2,1},{4,3},{6,5},{... | collective-permute-start | bytes 110600 | tf_op jit(solution)/shard_map/ppermute | solution.py:734
  36.8 1.6 %collective-permute-start.5 = (bf16[144,128]{1,0:T(8,128)(2,1)S(1)}, bf16[144,128]{1,0:T(8,128)(2,1)S(1)}, u32[]{:S(2)}, u32[]{:S(2)}) collective-permute-start(bf16[144,128]{1,0:T(8,128)(2,1)S(1)} %get-tuple-element.49), channel_id=1, source_target_pairs={{0,1},{2,3},{4,5},{6,7},{8,9},{10,11},{12,13},{14,15},{1,0},{3,2},... | collective-permute-start | bytes 110600 | tf_op jit(solution)/shard_map/ppermute | solution.py:734
  38.5 6.0 %collective-permute-start.6 = (bf16[304,128]{1,0:T(8,128)(2,1)S(1)}, bf16[304,128]{1,0:T(8,128)(2,1)S(1)}, u32[]{:S(2)}, u32[]{:S(2)}) collective-permute-start(bf16[304,128]{1,0:T(8,128)(2,1)S(1)} %get-tuple-element.52), channel_id=1, source_target_pairs={{16,32},{48,64},{80,96},{32,16},{64,48},{96,80},{17,33},{49,65},{8... | collective-permute-start | bytes 233480 | tf_op jit(solution)/shard_map/ppermute | solution.py:734
  39.2 5.7 %collective-permute-start.7 = (bf16[304,128]{1,0:T(8,128)(2,1)S(1)}, bf16[304,128]{1,0:T(8,128)(2,1)S(1)}, u32[]{:S(2)}, u32[]{:S(2)}) collective-permute-start(bf16[304,128]{1,0:T(8,128)(2,1)S(1)} %get-tuple-element.55), channel_id=1, source_target_pairs={{0,16},{32,48},{64,80},{96,112},{16,0},{48,32},{80,64},{112,96},{1... | collective-permute-start | bytes 233480 | tf_op jit(solution)/shard_map/ppermute | solution.py:734
  49.3 2.0 %collective-permute-start.8 = (bf16[8,152,128]{2,1,0:T(8,128)(2,1)S(1)}, bf16[8,152,128]{2,1,0:T(8,128)(2,1)S(1)}, u32[]{:S(2)}, u32[]{:S(2)}) collective-permute-start(bf16[8,152,128]{2,1,0:T(8,128)(2,1)S(1)} %get-tuple-element.69), channel_id=1, source_target_pairs={{0,1},{1,0},{2,3},{3,2},{4,5},{5,4},{6,7},{7,6},{8,9},{9,8},{10,11... | collective-permute-start | bytes 933896 | tf_op jit(solution)/shard_map/ppermute | solution.py:768
  80.9 14.1 %all-to-all-start.3 = ((bf16[16,32,128]{2,1,0:T(8,128)(2,1)}), bf16[16,32,128]{2,1,0:T(8,128)(2,1)S(1)}, u32[]{:S(2)}, u32[]{:S(2)}) async-start(bf16[16,32,128]{2,1,0:T(8,128)(2,1)} %share.1), calls=%async_computation.3 | async-start | bytes 262144 | tf_op jit(solution)/shard_map/all_to_all | solution.py:773

commit v13 on v12

--- a/solution.py
+++ b/solution.py
@@ -83,14 +83,62 @@
         pick[:, px * 128 : px * 128 + 128] = jnp.where(same & hit, 1.0, 0.0).astype(BF16)
 
 
-def forward_kernel(
-    near, mid, far, cot, k1, k2, biases,
-    to_far, to_near, hidden2, own_cot, ratio2, patches1, turned_own, fields, w2, w1,
-    pick, left, field, turned, pre1, first, spread, pre2, second,
-):
+def lay_rows(rows, target):
+    rows = rows.astype(F32)
+    pieces = []
+    for one, two in PAIRS:
+        a, b = 8 * (one + 3), 8 * (two + 3)
+        pieces.append(jnp.concatenate([rows[a : a + 16], rows[b : b + 16]], axis=1))
+    target[...] = jnp.concatenate(pieces, axis=0).astype(BF16)
+
+
+def select(block, pick):
+    count = block.shape[0]
+    out = dot(block.reshape(count * 80, 256), pick).astype(BF16).reshape(count, 5, 16, 512)
+    return [
+        jnp.concatenate(
+            [
+                jnp.concatenate([out[step, k, :, px * 128 : px * 128 + 128] for k in range(5)], axis=1)
+                for px in range(4)
+            ],
+            axis=0,
+        )
+        for step in range(count)
+    ]
+
+
+def prepare_kernel(mid, k1, k2, w1, w2, pick, chosen, left):
     lay_weights1(k1, w1)
     lay_weights2(k2, w2)
     lay_pick(pick)
+    for step in range(8):
+        lay_rows(mid[step], left.at[step])
+    for step, rows in enumerate(select(left[...], pick[...])):
+        chosen[step] = rows
+
+
+def run_prepare(*operands):
+    return pl.pallas_call(
+        prepare_kernel,
+        name="prepare",
+        out_shape=(
+            jax.ShapeDtypeStruct((256, 256), BF16),
+            jax.ShapeDtypeStruct((3, 512, 256), BF16),
+            jax.ShapeDtypeStruct((256, 512), BF16),
+            jax.ShapeDtypeStruct((8, 64, 640), BF16),
+        ),
+        in_specs=[VMEM] * 3,
+        out_specs=(VMEM,) * 4,
+        scratch_shapes=[pltpu.VMEM((8, 80, 256), BF16)],
+        compiler_params=pltpu.CompilerParams(vmem_limit_bytes=LIMIT),
+    )(*operands)
+
+
+def forward_kernel(
+    near, far, cot, w1, w2, pick, chosen, biases,
+    to_far, to_near, hidden2, own_cot, ratio2, patches1, turned_own, fields,
+    left, field, turned, pre1, first, spread, pre2, second,
+):
     bias1 = jnp.concatenate([biases[0:1, :32]] * 8, axis=1)
     bias2 = jnp.concatenate([biases[1:2, :64]] * 4, axis=1)
     base_y, base_z = lax.axis_index("gy"), lax.axis_index("gz")
@@ -103,38 +151,19 @@
         ok_z = (col >= 0) & (col < size_z * (4 // scale))
         return jnp.where(ok_y & ok_z, 1.0, 0.0)
 
-    def lay(rows, target):
-        rows = rows.astype(F32)
-        pieces = []
-        for one, two in PAIRS:
-            a, b = 8 * (one + 3), 8 * (two + 3)
-            pieces.append(jnp.concatenate([rows[a : a + 16], rows[b : b + 16]], axis=1))
-        left[target] = jnp.concatenate(pieces, axis=0).astype(BF16)
-
-    def lay_both(step, carry):
-        lay(mid[step], step + 7)
-        lay(mid[step + 4], step + 11)
+    def lay_ends(step, carry):
+        lay_rows(sided("gy", far[step + 1], near[step + 1])[0], left.at[step])
+        lay_rows(sided("gy", far[step], near[step])[1], left.at[step + 7])
         return carry
 
-    def lay_ends(step, carry):
-        lay(sided("gy", far[step + 1], near[step + 1])[0], step)
-        lay(sided("gy", far[step], near[step])[1], step + 15)
-        return carry
-
-    lax.fori_loop(0, 4, lay_both, 0)
     lax.fori_loop(0, 7, lay_ends, 0)
-
+    for step in range(8):
+        row = step + 7
+        field[row // 2, row % 2 * 64 : row % 2 * 64 + 64] = chosen[step]
     for part in range(2):
-        block = left[part * 11 : part * 11 + 11].reshape(880, 256)
-        out = dot(block, pick[...]).astype(BF16).reshape(11, 5, 16, 512)
-        for step in range(11):
-            row = part * 11 + step
-            for px in range(4):
-                at = (row % 2 * 4 + px) * 16
-                for k in range(5):
-                    field[row // 2, at : at + 16, k * 128 : k * 128 + 128] = out[
-                        step, k, :, px * 128 : px * 128 + 128
-                    ]
+        for step, rows in enumerate(select(left[7 * part : 7 * part + 7], pick[...])):
+            row = step + 15 * part
+            field[row // 2, row % 2 * 64 : row % 2 * 64 + 64] = rows
     for pair in range(11):
         turned[pair] = field[pair].T
     fields[...] = field[3:8, :, :256]
@@ -272,15 +301,12 @@
             jax.ShapeDtypeStruct((6, 6, 32, 128), BF16),
             jax.ShapeDtypeStruct((5, 256, 128), BF16),
             jax.ShapeDtypeStruct((5, 128, 256), BF16),
-            jax.ShapeDtypeStruct((3, 512, 256), BF16),
-            jax.ShapeDtypeStruct((256, 256), BF16),
         ),
         in_specs=[VMEM] * len(operands),
-        out_specs=(VMEM,) * 10,
+        out_specs=(VMEM,) * 8,
         cost_estimate=pl.CostEstimate(flops=5000000000, bytes_accessed=8000000, transcendentals=8000000),
         scratch_shapes=[
-            pltpu.VMEM((256, 512), BF16),
-            pltpu.VMEM((22, 80, 256), BF16),
+            pltpu.VMEM((14, 80, 256), BF16),
             pltpu.VMEM((11, 128, 640), BF16),
             pltpu.VMEM((11, 640, 128), BF16),
             pltpu.VMEM((2, 640, 256), F32),
@@ -752,8 +778,9 @@
 
     k1, k2 = kernel1.transpose(0, 2, 1).astype(F32), kernel2.transpose(0, 2, 1).astype(F32)
     k3 = kernel3.transpose(0, 2, 1)
-    to_far, to_near, hidden2, own_cot, ratio2, patches1, turned_own, fields, w2, w1 = run_forward(
-        near, strip, far, cot, k1, k2, biases
+    w1, w2, pick, chosen = run_prepare(strip, k1, k2)
+    to_far, to_near, hidden2, own_cot, ratio2, patches1, turned_own, fields = run_forward(
+        near, far, cot, w1, w2, pick, chosen, biases
     )
     far, near = swap(to_far, to_near, "gz")
     to_far, to_near, lower, upper = run_weave(far, near, hidden2, own_cot)

time: 96.4 us -> 95.9 us (level)
  transfers between devices with their start and end apart: 11 -> 11, of which waited for: 6 -> 6; matrix products, arithmetic and copies ran while one was open for 3% -> 3% of each run, Pallas kernels for 3% -> 4%
where the time goes in v13:
time: 95.9 us; the launch traced here: 95.4 us
  starting transfers between devices  33.6 us (35%)
  blocking collectives  28.7 us (30%)
  Pallas kernels  15.5 us (16%)
  waiting for transfers between devices  12.9 us (13%)
  local copies, waits for them, and re-layouts  2.34 us (2%)
  other arithmetic  1.51 us (2%)
    all_to_all x1, blocking collectives, shards(): lax.all_to_all(packed, 'gz', 0, 0, tiled=True, axis_index_groups=same)  15.5 us
    all_to_all x1, blocking collectives, shards(): column = lax.all_to_all(column, 'gy', 0, 0, tiled=True)  13.2 us
    ppermute x4, starting transfers between devices, swap(): lax.ppermute(to_far, axis, pairs(1))  12.9 us
    ppermute x4, starting transfers between devices, swap(): lax.ppermute(to_near, axis, pairs(0))  7.93 us
    all_to_all x1, starting transfers between devices, shards(): shared = lax.all_to_all(run_share(column, size_z), 'gz', 0, 0, tiled=True)  6.38 us
    all_to_all x1, waiting for transfers between devices, shards(): shared = lax.all_to_all(run_share(column, size_z), 'gz', 0, 0, tiled=True)  6.37 us
    pallas_call x1, Pallas kernels, run_forward(): pl.pallas_call(forward_kernel, name='forward', out_shape=(jax.ShapeDtypeS...  6 us
    all_to_all x1, starting transfers between devices, shards(): lax.all_to_all(cotangent[:, 0].transpose(1, 0, 2), 'gz', 0, 0, tiled=True)  5.64 us
  transfers between devices with their start and end apart: 11, of which 6 were waited for; matrix products, arithmetic and copies ran while one was open for 3% of the time, Pallas kernels for 4%

profile of v13, /device:TPU:1, one launch (start us, length us, event | category | flops | bytes accessed | tf_op | source)
XLA Modules:
  0.0 95.4 jit_solution(4449192251975821478)
XLA Ops:
  0.7 0.9 copy.18
  1.6 6.0 %collective-permute-start.1 = (bf16[8,32,128]{2,1,0:T(8,128)(2,1)S(1)}, bf16[8,32,128]{2,1,0:T(8,128)(2,1)S(1)}, u32[]{:S(2)}, u32[]{:S(2)}) collective-permute-start(bf16[8,32,128]{2,1,0:T(8,128)(2,1)S(1)} %bitcast.29), channel_id=1, source_target_pairs={{1,2},{3,4},{5,6},{7,8},{9,10},{11,12},{13,14},{2,1},{4,3},{6,5},{... | collective-permute-start | bytes 196616 | tf_op jit(solution)/shard_map/ppermute | solution.py:760
  7.7 0.1 collective-permute-start
  7.8 1.4 %copy.22 = bf16[8,1,16,16]{3,0,2,1:T(8,128)(2,1)} copy(bf16[8,1,16,16]{3,2,1,0:T(8,128)(2,1)} %param.15) | data formatting | bytes 8192 | tf_op args[7]
  9.1 5.6 %all-to-all-start = ((bf16[16,8,16]{2,1,0:T(8,128)(2,1)}), bf16[16,8,16]{2,1,0:T(8,128)(2,1)S(1)}, u32[]{:S(2)}, u32[]{:S(2)}) async-start(bf16[16,8,16]{2,1,0:T(8,128)(2,1)} %bitcast.26), calls=%async_computation | async-start | bytes 65536 | tf_op jit(solution)/shard_map/all_to_all | solution.py:768
  14.9 0.7 collective-permute-start.3
  15.6 4.6 %collective-permute-start.2 = (bf16[8,88,128]{2,1,0:T(8,128)(2,1)S(1)}, bf16[8,88,128]{2,1,0:T(8,128)(2,1)S(1)}, u32[]{:S(2)}, u32[]{:S(2)}) collective-permute-start(bf16[8,88,128]{2,1,0:T(8,128)(2,1)S(1)} %pad_maximum_fusion.mid), channel_id=1, source_target_pairs={{0,16},{32,48},{64,80},{96,112},{16,0},{48,32},{80,64},{112,96},{1... | collective-permute-start | bytes 540680 | tf_op jit(solution)/shard_map/ppermute | solution.py:760
  20.2 0.8 convert_bitcast_fusion.1.k1
  21.1 0.5 prepare.1
  21.5 0.5 all-to-all-done
  22.1 2.7 %collective-permute-done.2.near = bf16[8,88,128]{2,1,0:T(8,128)(2,1)S(1)} collective-permute-done((bf16[8,88,128]{2,1,0:T(8,128)(2,1)S(1)}, bf16[8,88,128]{2,1,0:T(8,128)(2,1)S(1)}, u32[]{:S(2)}, u32[]{:S(2)}) %collective-permute-start.2) | collective-permute-done | bytes 180256 | tf_op jit(solution)/shard_map/ppermute | solution.py:760
  24.8 6.0 %forward.1 = (bf16[144,128]{1,0:T(8,128)(2,1)S(1)}, bf16[144,128]{1,0:T(8,128)(2,1)S(1)}, bf16[4,4,16,128]{3,2,1,0:T(8,128)(2,1)S(1)}, bf16[16,128]{1,0:T(8,128)...) custom-call(bf16[8,88,128]{2,1,0:T(8,128)(2,1)S(1)} %collective-perm, ...), custom_call_target="tpu_custom_call" | custom-call | flops 5000000000 | bytes 8000000 | tf_op jit(solution)/shard_map/forward/pallas_call | solution.py:292
  30.8 5.5 %collective-permute-start.4 = (bf16[144,128]{1,0:T(8,128)(2,1)S(1)}, bf16[144,128]{1,0:T(8,128)(2,1)S(1)}, u32[]{:S(2)}, u32[]{:S(2)}) collective-permute-start(bf16[144,128]{1,0:T(8,128)(2,1)S(1)} %get-tuple-element.54), channel_id=1, source_target_pairs={{1,2},{3,4},{5,6},{7,8},{9,10},{11,12},{13,14},{2,1},{4,3},{6,5},{... | collective-permute-start | bytes 110600 | tf_op jit(solution)/shard_map/ppermute | solution.py:760
  36.4 0.1 collective-permute-start.5
  36.5 1.5 %collective-permute-done.4.far = bf16[144,128]{1,0:T(8,128)(2,1)S(1)} collective-permute-done((bf16[144,128]{1,0:T(8,128)(2,1)S(1)}, bf16[144,128]{1,0:T(8,128)(2,1)S(1)}, u32[]{:S(2)}, u32[]{:S(2)}) %collective-permute-start.4) | collective-permute-done | bytes 36896 | tf_op jit(solution)/shard_map/ppermute | solution.py:760
  38.1 0.7 collective-permute-start.6
  38.7 3.1 %collective-permute-start.7 = (bf16[304,128]{1,0:T(8,128)(2,1)S(1)}, bf16[304,128]{1,0:T(8,128)(2,1)S(1)}, u32[]{:S(2)}, u32[]{:S(2)}) collective-permute-start(bf16[304,128]{1,0:T(8,128)(2,1)S(1)} %get-tuple-element.61), channel_id=1, source_target_pairs={{0,16},{32,48},{64,80},{96,112},{16,0},{48,32},{80,64},{112,96},{1... | collective-permute-start | bytes 233480 | tf_op jit(solution)/shard_map/ppermute | solution.py:760
  41.9 2.2 %own.1 = (bf16[8,120,128]{2,1,0:T(8,128)(2,1)S(1)}, bf16[8,120,128]{2,1,0:T(8,128)(2,1)S(1)}, f32[1,128]{1,0:T(1,128)S(1)}, bf16[9,256,256]{2,1,0:T(8,128)(2,1)S...) custom-call(bf16[4,4,16,128]{3,2,1,0:T(8,128)(2,1)S(1)} %get-tuple-element.56.hidden2.middle, ...), custom_call_target="tpu_custom_call" | custom-call | flops 150000000 | bytes 4000000 | tf_op jit(solution)/shard_map/own/pallas_call | solution.py:435
  44.0 0.4 collective-permute-done.7.near
  44.5 4.3 %backward.1 = (bf16[8,152,128]{2,1,0:T(8,128)(2,1)S(1)}, bf16[8,152,128]{2,1,0:T(8,128)(2,1)S(1)}) custom-call(bf16[304,128]{1,0:T(8,128)(2,1)S(1)} %collective-permute-done.6.far, bf16[144,128]{1,0:T(8,128)(2,1)S(1)} %get-tuple-element.59.lower, bf16[4,4,16,128]{3,2,1,0:T(8,128)(2,1)S(1)} %get-tuple-element.56.hidden2.middle, ...), custom_call_target="tpu_custom_call" | custom-call | tf_op jit(solution)/shard_map/backward/pallas_call | solution.py:609
  48.8 0.8 collective-permute-start.8
  49.6 1.2 %collective-permute-done.8.received = bf16[8,152,128]{2,1,0:T(8,128)(2,1)S(1)} collective-permute-done((bf16[8,152,128]{2,1,0:T(8,128)(2,1)S(1)}, bf16[8,152,128]{2,1,0:T(8,128)(2,1)S(1)}, u32[]{:S(2)}, u32[]{:S(2)}) %collective-permute-start.8) | collective-permute-done | bytes 311328 | tf_op jit(solution)/shard_map/ppermute | solution.py:795
  50.8 0.1 pair.1
  50.9 15.5 %all_to_all.20.received = bf16[8,152,128]{2,1,0:T(8,128)(2,1)S(1)} all-to-all(bf16[8,152,128]{2,1,0:T(8,128)(2,1)S(1)} %pair.1), channel_id=1, replica_groups={{0,2,4,6,8,10,12,14},{1,3,5,7,9,11,13,15},{16,18,20,22,24,26,28,30},{17..., dimensions={0} | all-to-all | bytes 622592 | tf_op jit(solution)/shard_map/all_to_all | solution.py:797
  66.4 0.1 sum.1
  66.5 13.2 %all_to_all.21.column = bf16[8,144,128]{2,1,0:T(8,128)(2,1)S(1)} all-to-all(bf16[8,144,128]{2,1,0:T(8,128)(2,1)S(1)} %get-tuple-element.75), channel_id=1, replica_groups=mesh['gy'=8,'gz'=16] {'gy'}, dimensions={0} | all-to-all | bytes 589824 | tf_op jit(solution)/shard_map/all_to_all | solution.py:799
  79.7 0.7 share.1
  80.4 6.4 %all-to-all-start.3 = ((bf16[16,32,128]{2,1,0:T(8,128)(2,1)}), bf16[16,32,128]{2,1,0:T(8,128)(2,1)S(1)}, u32[]{:S(2)}, u32[]{:S(2)}) async-start(bf16[16,32,128]{2,1,0:T(8,128)(2,1)} %share.1), calls=%async_computation.3 | async-start | bytes 262144 | tf_op jit(solution)/shard_map/all_to_all | solution.py:800
  86.8 0.6 convert_bitcast_fusion.2
  87.4 0.7 third.1
  88.1 6.4 %all-to-all-done.3.shared = bf16[16,32,128]{2,1,0:T(8,128)(2,1)S(1)} async-done(((bf16[16,32,128]{2,1,0:T(8,128)(2,1)}), bf16[16,32,128]{2,1,0:T(8,128)(2,1)S(1)}, u32[]{:S(2)}, u32[]{:S(2)}) %all-to-all-start.3) | async-done | bytes 131104 | tf_op jit(solution)/shard_map/all_to_all | solution.py:800
  94.5 0.9 unpack.1
  (21 shorter events, 0.2 us)
Async XLA Ops:
  0.6 20.4 %copy-start.2 = (f32[128]{0:T(128)S(1)}, f32[128]{0:T(128)}, u32[]{:S(2)}) copy-start(f32[128]{0:T(128)} %param.14) | copy-start | bytes 1540
  0.6 20.4 %copy-start.3 = (f32[64]{0:T(128)S(1)}, f32[64]{0:T(128)}, u32[]{:S(2)}) copy-start(f32[64]{0:T(128)} %param.12) | copy-start | bytes 772
  0.7 20.3 %copy-start.1 = (bf16[27,64,32]{1,2,0:T(8,128)(2,1)S(1)}, bf16[27,64,32]{1,2,0:T(8,128)(2,1)}, u32[]{:S(2)}) copy-start(bf16[27,64,32]{1,2,0:T(8,128)(2,1)} %param.11) | copy-start | bytes 331780
  0.7 20.4 %copy-start.4 = (f32[32]{0:T(128)S(1)}, f32[32]{0:T(128)}, u32[]{:S(2)}) copy-start(f32[32]{0:T(128)} %param.10) | copy-start | bytes 388
  1.6 13.2 %collective-permute-start.1 = (bf16[8,32,128]{2,1,0:T(8,128)(2,1)S(1)}, bf16[8,32,128]{2,1,0:T(8,128)(2,1)S(1)}, u32[]{:S(2)}, u32[]{:S(2)}) collective-permute-start(bf16[8,32,128]{2,1,0:T(8,128)(2,1)S(1)} %bitcast.29), channel_id=1, source_target_pairs={{1,2},{3,4},{5,6},{7,8},{9,10},{11,12},{13,14},{2,1},{4,3},{6,5},{... | collective-permute-start | bytes 196616 | tf_op jit(solution)/shard_map/ppermute | solution.py:760
  7.7 7.1 %collective-permute-start = (bf16[8,32,128]{2,1,0:T(8,128)(2,1)S(1)}, bf16[8,32,128]{2,1,0:T(8,128)(2,1)S(1)}, u32[]{:S(2)}, u32[]{:S(2)}) collective-permute-start(bf16[8,32,128]{2,1,0:T(8,128)(2,1)S(1)} %bitcast.30), channel_id=1, source_target_pairs={{0,1},{2,3},{4,5},{6,7},{8,9},{10,11},{12,13},{14,15},{1,0},{3,2},... | collective-permute-start | bytes 196616 | tf_op jit(solution)/shard_map/ppermute | solution.py:760
  9.1 12.9 %all-to-all-start = ((bf16[16,8,16]{2,1,0:T(8,128)(2,1)}), bf16[16,8,16]{2,1,0:T(8,128)(2,1)S(1)}, u32[]{:S(2)}, u32[]{:S(2)}) async-start(bf16[16,8,16]{2,1,0:T(8,128)(2,1)} %bitcast.26), calls=%async_computation | async-start | bytes 65536 | tf_op jit(solution)/shard_map/all_to_all | solution.py:768
  14.9 7.2 %collective-permute-start.3 = (bf16[8,88,128]{2,1,0:T(8,128)(2,1)S(1)}, bf16[8,88,128]{2,1,0:T(8,128)(2,1)S(1)}, u32[]{:S(2)}, u32[]{:S(2)}) collective-permute-start(bf16[8,88,128]{2,1,0:T(8,128)(2,1)S(1)} %pad_maximum_fusion.mid), channel_id=1, source_target_pairs={{16,32},{48,64},{80,96},{32,16},{64,48},{96,80},{17,33},{49,65},{8... | collective-permute-start | bytes 540680 | tf_op jit(solution)/shard_map/ppermute | solution.py:760
  15.6 9.3 %collective-permute-start.2 = (bf16[8,88,128]{2,1,0:T(8,128)(2,1)S(1)}, bf16[8,88,128]{2,1,0:T(8,128)(2,1)S(1)}, u32[]{:S(2)}, u32[]{:S(2)}) collective-permute-start(bf16[8,88,128]{2,1,0:T(8,128)(2,1)S(1)} %pad_maximum_fusion.mid), channel_id=1, source_target_pairs={{0,16},{32,48},{64,80},{96,112},{16,0},{48,32},{80,64},{112,96},{1... | collective-permute-start | bytes 540680 | tf_op jit(solution)/shard_map/ppermute | solution.py:760
  24.8 17.0 %copy-start = (bf16[27,128,64]{1,2,0:T(8,128)(2,1)S(1)}, bf16[27,128,64]{1,2,0:T(8,128)(2,1)}, u32[]{:S(2)}) copy-start(bf16[27,128,64]{1,2,0:T(8,128)(2,1)} %param.13) | copy-start | bytes 1327108
  30.8 7.2 %collective-permute-start.4 = (bf16[144,128]{1,0:T(8,128)(2,1)S(1)}, bf16[144,128]{1,0:T(8,128)(2,1)S(1)}, u32[]{:S(2)}, u32[]{:S(2)}) collective-permute-start(bf16[144,128]{1,0:T(8,128)(2,1)S(1)} %get-tuple-element.54), channel_id=1, source_target_pairs={{1,2},{3,4},{5,6},{7,8},{9,10},{11,12},{13,14},{2,1},{4,3},{6,5},{... | collective-permute-start | bytes 110600 | tf_op jit(solution)/shard_map/ppermute | solution.py:760
  36.4 1.6 %collective-permute-start.5 = (bf16[144,128]{1,0:T(8,128)(2,1)S(1)}, bf16[144,128]{1,0:T(8,128)(2,1)S(1)}, u32[]{:S(2)}, u32[]{:S(2)}) collective-permute-start(bf16[144,128]{1,0:T(8,128)(2,1)S(1)} %get-tuple-element.55), channel_id=1, source_target_pairs={{0,1},{2,3},{4,5},{6,7},{8,9},{10,11},{12,13},{14,15},{1,0},{3,2},... | collective-permute-start | bytes 110600 | tf_op jit(solution)/shard_map/ppermute | solution.py:760
  38.1 6.0 %collective-permute-start.6 = (bf16[304,128]{1,0:T(8,128)(2,1)S(1)}, bf16[304,128]{1,0:T(8,128)(2,1)S(1)}, u32[]{:S(2)}, u32[]{:S(2)}) collective-permute-start(bf16[304,128]{1,0:T(8,128)(2,1)S(1)} %get-tuple-element.58), channel_id=1, source_target_pairs={{16,32},{48,64},{80,96},{32,16},{64,48},{96,80},{17,33},{49,65},{8... | collective-permute-start | bytes 233480 | tf_op jit(solution)/shard_map/ppermute | solution.py:760
  38.7 5.7 %collective-permute-start.7 = (bf16[304,128]{1,0:T(8,128)(2,1)S(1)}, bf16[304,128]{1,0:T(8,128)(2,1)S(1)}, u32[]{:S(2)}, u32[]{:S(2)}) collective-permute-start(bf16[304,128]{1,0:T(8,128)(2,1)S(1)} %get-tuple-element.61), channel_id=1, source_target_pairs={{0,16},{32,48},{64,80},{96,112},{16,0},{48,32},{80,64},{112,96},{1... | collective-permute-start | bytes 233480 | tf_op jit(solution)/shard_map/ppermute | solution.py:760
  48.8 2.0 %collective-permute-start.8 = (bf16[8,152,128]{2,1,0:T(8,128)(2,1)S(1)}, bf16[8,152,128]{2,1,0:T(8,128)(2,1)S(1)}, u32[]{:S(2)}, u32[]{:S(2)}) collective-permute-start(bf16[8,152,128]{2,1,0:T(8,128)(2,1)S(1)} %get-tuple-element.73), channel_id=1, source_target_pairs={{0,1},{1,0},{2,3},{3,2},{4,5},{5,4},{6,7},{7,6},{8,9},{9,8},{10,11... | collective-permute-start | bytes 933896 | tf_op jit(solution)/shard_map/ppermute | solution.py:795
  80.4 14.1 %all-to-all-start.3 = ((bf16[16,32,128]{2,1,0:T(8,128)(2,1)}), bf16[16,32,128]{2,1,0:T(8,128)(2,1)S(1)}, u32[]{:S(2)}, u32[]{:S(2)}) async-start(bf16[16,32,128]{2,1,0:T(8,128)(2,1)} %share.1), calls=%async_computation.3 | async-start | bytes 262144 | tf_op jit(solution)/shard_map/all_to_all | solution.py:800

commit v14 on v13

--- a/solution.py
+++ b/solution.py
@@ -684,7 +684,7 @@
     return pl.pallas_call(
         share_kernel,
         name="share",
-        out_shape=jax.ShapeDtypeStruct((groups, 512 // groups, 128), BF16),
+        out_shape=jax.ShapeDtypeStruct((groups, 256 // groups, 128), BF16),
         in_specs=[VMEM],
         out_specs=VMEM,
         compiler_params=pltpu.CompilerParams(vmem_limit_bytes=LIMIT),
@@ -714,9 +714,10 @@
     )(column)
 
 
-def unpack_kernel(shared, grad1, grad2, shift1, shift2, shift3):
+def unpack_kernel(mine, other, grad1, grad2, shift1, shift2, shift3):
     wide = shift3.shape[1]
-    rows = shared[...].astype(F32).reshape(512, 128)
+    even, uneven = sided("gz", mine[...], other[...])
+    rows = jnp.concatenate([even.astype(F32)[:, None], uneven.astype(F32)[:, None]], axis=1).reshape(512, 128)
     for tap in range(27):
         at = (tap // 2) * 32
         grad2[tap] = rows[at : at + 32, (tap % 2) * 64 : (tap % 2) * 64 + 64]
@@ -732,8 +733,8 @@
     shift3[...] = roll(biases, lax.rem(128 - place * wide, 128), 1)[0:1, :wide]
 
 
-def run_unpack(shared):
-    wide = 128 // shared.shape[0]
+def run_unpack(mine, other):
+    wide = 64 // mine.shape[0]
     return pl.pallas_call(
         unpack_kernel,
         name="unpack",
@@ -744,10 +745,10 @@
             jax.ShapeDtypeStruct((1, 64), F32),
             jax.ShapeDtypeStruct((1, wide), F32),
         ),
-        in_specs=[VMEM],
+        in_specs=[VMEM] * 2,
         out_specs=(VMEM,) * 5,
         compiler_params=pltpu.CompilerParams(vmem_limit_bytes=LIMIT),
-    )(shared)
+    )(mine, other)
 
 
 def swap(to_far, to_near, axis):
@@ -797,9 +798,11 @@
     packed = lax.all_to_all(packed, "gz", 0, 0, tiled=True, axis_index_groups=same)
     column, features = run_sum(packed, size_y)
     column = lax.all_to_all(column, "gy", 0, 0, tiled=True)
-    shared = lax.all_to_all(run_share(column, size_z), "gz", 0, 0, tiled=True)
+    shared = run_share(column, size_z // 2)
+    shared = lax.all_to_all(shared, "gz", 0, 0, tiled=True, axis_index_groups=same)
+    other = lax.ppermute(shared, "gz", mates)
     grad3 = run_third(column, wide)
-    grad1, grad2, shift1, shift2, shift3 = run_unpack(shared)
+    grad1, grad2, shift1, shift2, shift3 = run_unpack(shared, other)
     return (
         features[:, None].astype(BF16), grad1.transpose(0, 2, 1), shift1[0], grad2.transpose(0, 2, 1), shift2[0], grad3, shift3[0]
     )

time: 95.9 us -> 95.8 us (level)
  blocking collectives: 28.7 us -> 38.2 us
  waiting for transfers between devices: 12.9 us -> 6.51 us
  starting transfers between devices: 33.6 us -> 31 us
    all_to_all x0 -> x1, blocking collectives: none -> 9.54 us  [shards(): lax.all_to_all(shared, 'gz', 0, 0, tiled=True, axis_index_groups=same)]
    all_to_all x1 -> x0, starting transfers between devices: 6.38 us -> none  [shards(): shared = lax.all_to_all(run_share(column, size_z), 'gz', 0, 0, tiled=True)]
    all_to_all x1 -> x0, waiting for transfers between devices: 6.37 us -> none  [shards(): shared = lax.all_to_all(run_share(column, size_z), 'gz', 0, 0, tiled=True)]
    ppermute x0 -> x1, starting transfers between devices: none -> 3.77 us  [shards(): other = lax.ppermute(shared, 'gz', mates)]
  transfers between devices with their start and end apart: 11 -> 11, of which waited for: 6 -> 5; matrix products, arithmetic and copies ran while one was open for 3% -> 3% of each run, Pallas kernels for 4% -> 4%
where the time goes in v14:
time: 95.8 us; the launch traced here: 95.3 us
  blocking collectives  38.2 us (40%)
  starting transfers between devices  31 us (32%)
  Pallas kernels  14.9 us (16%)
  waiting for transfers between devices  6.51 us (7%)
  local copies, waits for them, and re-layouts  2.34 us (2%)
  other arithmetic  1.51 us (2%)
    all_to_all x1, blocking collectives, shards(): lax.all_to_all(packed, 'gz', 0, 0, tiled=True, axis_index_groups=same)  15.5 us
    all_to_all x1, blocking collectives, shards(): column = lax.all_to_all(column, 'gy', 0, 0, tiled=True)  13.2 us
    ppermute x4, starting transfers between devices, swap(): lax.ppermute(to_far, axis, pairs(1))  12.9 us
    all_to_all x1, blocking collectives, shards(): lax.all_to_all(shared, 'gz', 0, 0, tiled=True, axis_index_groups=same)  9.54 us
    ppermute x4, starting transfers between devices, swap(): lax.ppermute(to_near, axis, pairs(0))  7.93 us
    pallas_call x1, Pallas kernels, run_forward(): pl.pallas_call(forward_kernel, name='forward', out_shape=(jax.ShapeDtypeS...  6 us
    all_to_all x1, starting transfers between devices, shards(): lax.all_to_all(cotangent[:, 0].transpose(1, 0, 2), 'gz', 0, 0, tiled=True)  5.64 us
    pallas_call x1, Pallas kernels, run_backward(): pl.pallas_call(backward_kernel, name='backward', out_shape=(jax.ShapeDtyp...  4.34 us
  transfers between devices with their start and end apart: 11, of which 5 were waited for; matrix products, arithmetic and copies ran while one was open for 3% of the time, Pallas kernels for 4%

profile of v14, /device:TPU:1, one launch (start us, length us, event | category | flops | bytes accessed | tf_op | source)
XLA Modules:
  0.0 95.3 jit_solution(14912926221005895928)
XLA Ops:
  0.7 0.9 copy.18
  1.6 6.0 %collective-permute-start.1 = (bf16[8,32,128]{2,1,0:T(8,128)(2,1)S(1)}, bf16[8,32,128]{2,1,0:T(8,128)(2,1)S(1)}, u32[]{:S(2)}, u32[]{:S(2)}) collective-permute-start(bf16[8,32,128]{2,1,0:T(8,128)(2,1)S(1)} %bitcast.29), channel_id=1, source_target_pairs={{1,2},{3,4},{5,6},{7,8},{9,10},{11,12},{13,14},{2,1},{4,3},{6,5},{... | collective-permute-start | bytes 196616 | tf_op jit(solution)/shard_map/ppermute | solution.py:761
  7.7 0.1 collective-permute-start
  7.8 1.4 %copy.22 = bf16[8,1,16,16]{3,0,2,1:T(8,128)(2,1)} copy(bf16[8,1,16,16]{3,2,1,0:T(8,128)(2,1)} %param.15) | data formatting | bytes 8192 | tf_op args[7]
  9.1 5.6 %all-to-all-start = ((bf16[16,8,16]{2,1,0:T(8,128)(2,1)}), bf16[16,8,16]{2,1,0:T(8,128)(2,1)S(1)}, u32[]{:S(2)}, u32[]{:S(2)}) async-start(bf16[16,8,16]{2,1,0:T(8,128)(2,1)} %bitcast.26), calls=%async_computation | async-start | bytes 65536 | tf_op jit(solution)/shard_map/all_to_all | solution.py:769
  14.8 0.1 pad_maximum_fusion.mid
  14.9 0.7 collective-permute-start.3
  15.6 4.6 %collective-permute-start.2 = (bf16[8,88,128]{2,1,0:T(8,128)(2,1)S(1)}, bf16[8,88,128]{2,1,0:T(8,128)(2,1)S(1)}, u32[]{:S(2)}, u32[]{:S(2)}) collective-permute-start(bf16[8,88,128]{2,1,0:T(8,128)(2,1)S(1)} %pad_maximum_fusion.mid), channel_id=1, source_target_pairs={{0,16},{32,48},{64,80},{96,112},{16,0},{48,32},{80,64},{112,96},{1... | collective-permute-start | bytes 540680 | tf_op jit(solution)/shard_map/ppermute | solution.py:761
  20.2 0.8 convert_bitcast_fusion.1.k1
  21.1 0.5 prepare.1
  21.5 0.5 all-to-all-done
  22.1 2.7 %collective-permute-done.2.near = bf16[8,88,128]{2,1,0:T(8,128)(2,1)S(1)} collective-permute-done((bf16[8,88,128]{2,1,0:T(8,128)(2,1)S(1)}, bf16[8,88,128]{2,1,0:T(8,128)(2,1)S(1)}, u32[]{:S(2)}, u32[]{:S(2)}) %collective-permute-start.2) | collective-permute-done | bytes 180256 | tf_op jit(solution)/shard_map/ppermute | solution.py:761
  24.8 6.0 %forward.1 = (bf16[144,128]{1,0:T(8,128)(2,1)S(1)}, bf16[144,128]{1,0:T(8,128)(2,1)S(1)}, bf16[4,4,16,128]{3,2,1,0:T(8,128)(2,1)S(1)}, bf16[16,128]{1,0:T(8,128)...) custom-call(bf16[8,88,128]{2,1,0:T(8,128)(2,1)S(1)} %collective-perm, ...), custom_call_target="tpu_custom_call" | custom-call | flops 5000000000 | bytes 8000000 | tf_op jit(solution)/shard_map/forward/pallas_call | solution.py:292
  30.8 5.5 %collective-permute-start.4 = (bf16[144,128]{1,0:T(8,128)(2,1)S(1)}, bf16[144,128]{1,0:T(8,128)(2,1)S(1)}, u32[]{:S(2)}, u32[]{:S(2)}) collective-permute-start(bf16[144,128]{1,0:T(8,128)(2,1)S(1)} %get-tuple-element.54), channel_id=1, source_target_pairs={{1,2},{3,4},{5,6},{7,8},{9,10},{11,12},{13,14},{2,1},{4,3},{6,5},{... | collective-permute-start | bytes 110600 | tf_op jit(solution)/shard_map/ppermute | solution.py:761
  36.4 0.1 collective-permute-start.5
  36.5 1.5 %collective-permute-done.4.far = bf16[144,128]{1,0:T(8,128)(2,1)S(1)} collective-permute-done((bf16[144,128]{1,0:T(8,128)(2,1)S(1)}, bf16[144,128]{1,0:T(8,128)(2,1)S(1)}, u32[]{:S(2)}, u32[]{:S(2)}) %collective-permute-start.4) | collective-permute-done | bytes 36896 | tf_op jit(solution)/shard_map/ppermute | solution.py:761
  38.1 0.7 collective-permute-start.6
  38.7 3.1 %collective-permute-start.7 = (bf16[304,128]{1,0:T(8,128)(2,1)S(1)}, bf16[304,128]{1,0:T(8,128)(2,1)S(1)}, u32[]{:S(2)}, u32[]{:S(2)}) collective-permute-start(bf16[304,128]{1,0:T(8,128)(2,1)S(1)} %get-tuple-element.61), channel_id=1, source_target_pairs={{0,16},{32,48},{64,80},{96,112},{16,0},{48,32},{80,64},{112,96},{1... | collective-permute-start | bytes 233480 | tf_op jit(solution)/shard_map/ppermute | solution.py:761
  41.9 2.2 %own.1 = (bf16[8,120,128]{2,1,0:T(8,128)(2,1)S(1)}, bf16[8,120,128]{2,1,0:T(8,128)(2,1)S(1)}, f32[1,128]{1,0:T(1,128)S(1)}, bf16[9,256,256]{2,1,0:T(8,128)(2,1)S...) custom-call(bf16[4,4,16,128]{3,2,1,0:T(8,128)(2,1)S(1)} %get-tuple-element.56.hidden2.middle, ...), custom_call_target="tpu_custom_call" | custom-call | flops 150000000 | bytes 4000000 | tf_op jit(solution)/shard_map/own/pallas_call | solution.py:435
  44.0 0.4 collective-permute-done.7.near
  44.5 4.3 %backward.1 = (bf16[8,152,128]{2,1,0:T(8,128)(2,1)S(1)}, bf16[8,152,128]{2,1,0:T(8,128)(2,1)S(1)}) custom-call(bf16[304,128]{1,0:T(8,128)(2,1)S(1)} %collective-permute-done.6.far, bf16[144,128]{1,0:T(8,128)(2,1)S(1)} %get-tuple-element.59.lower, bf16[4,4,16,128]{3,2,1,0:T(8,128)(2,1)S(1)} %get-tuple-element.56.hidden2.middle, ...), custom_call_target="tpu_custom_call" | custom-call | tf_op jit(solution)/shard_map/backward/pallas_call | solution.py:609
  48.8 0.8 collective-permute-start.8
  49.6 1.2 %collective-permute-done.8.received = bf16[8,152,128]{2,1,0:T(8,128)(2,1)S(1)} collective-permute-done((bf16[8,152,128]{2,1,0:T(8,128)(2,1)S(1)}, bf16[8,152,128]{2,1,0:T(8,128)(2,1)S(1)}, u32[]{:S(2)}, u32[]{:S(2)}) %collective-permute-start.8) | collective-permute-done | bytes 311328 | tf_op jit(solution)/shard_map/ppermute | solution.py:796
  50.8 0.1 pair.1
  50.9 15.5 %all_to_all.20.received = bf16[8,152,128]{2,1,0:T(8,128)(2,1)S(1)} all-to-all(bf16[8,152,128]{2,1,0:T(8,128)(2,1)S(1)} %pair.1), channel_id=1, replica_groups={{0,2,4,6,8,10,12,14},{1,3,5,7,9,11,13,15},{16,18,20,22,24,26,28,30},{17..., dimensions={0} | all-to-all | bytes 622592 | tf_op jit(solution)/shard_map/all_to_all | solution.py:798
  66.4 0.1 sum.1
  66.5 13.2 %all_to_all.21.column = bf16[8,144,128]{2,1,0:T(8,128)(2,1)S(1)} all-to-all(bf16[8,144,128]{2,1,0:T(8,128)(2,1)S(1)} %get-tuple-element.75), channel_id=1, replica_groups=mesh['gy'=8,'gz'=16] {'gy'}, dimensions={0} | all-to-all | bytes 589824 | tf_op jit(solution)/shard_map/all_to_all | solution.py:800
  79.7 9.5 %all_to_all.22.mine = bf16[8,32,128]{2,1,0:T(8,128)(2,1)S(1)} all-to-all(bf16[8,32,128]{2,1,0:T(8,128)(2,1)S(1)} %share.1), channel_id=1, replica_groups={{0,2,4,6,8,10,12,14},{1,3,5,7,9,11,13,15},{16,18,20,22,24,26,28,30},{17..., dimensions={0} | all-to-all | bytes 131072 | tf_op jit(solution)/shard_map/all_to_all | solution.py:802
  89.3 3.8 %collective-permute-start.9 = (bf16[8,32,128]{2,1,0:T(8,128)(2,1)S(1)}, bf16[8,32,128]{2,1,0:T(8,128)(2,1)S(1)}, u32[]{:S(2)}, u32[]{:S(2)}) collective-permute-start(bf16[8,32,128]{2,1,0:T(8,128)(2,1)S(1)} %all_to_all.22.mine), channel_id=1, source_target_pairs={{0,1},{1,0},{2,3},{3,2},{4,5},{5,4},{6,7},{7,6},{8,9},{9,8},{10,11... | collective-permute-start | bytes 196616 | tf_op jit(solution)/shard_map/ppermute | solution.py:803
  93.0 0.6 convert_bitcast_fusion.2
  93.7 0.7 third.1
  94.4 0.9 unpack.1
  (22 shorter events, 0.2 us)
Async XLA Ops:
  0.6 20.4 %copy-start.2 = (f32[128]{0:T(128)S(1)}, f32[128]{0:T(128)}, u32[]{:S(2)}) copy-start(f32[128]{0:T(128)} %param.14) | copy-start | bytes 1540
  0.6 20.4 %copy-start.3 = (f32[64]{0:T(128)S(1)}, f32[64]{0:T(128)}, u32[]{:S(2)}) copy-start(f32[64]{0:T(128)} %param.12) | copy-start | bytes 772
  0.7 20.3 %copy-start.1 = (bf16[27,64,32]{1,2,0:T(8,128)(2,1)S(1)}, bf16[27,64,32]{1,2,0:T(8,128)(2,1)}, u32[]{:S(2)}) copy-start(bf16[27,64,32]{1,2,0:T(8,128)(2,1)} %param.11) | copy-start | bytes 331780
  0.7 20.4 %copy-start.4 = (f32[32]{0:T(128)S(1)}, f32[32]{0:T(128)}, u32[]{:S(2)}) copy-start(f32[32]{0:T(128)} %param.10) | copy-start | bytes 388
  1.6 13.2 %collective-permute-start.1 = (bf16[8,32,128]{2,1,0:T(8,128)(2,1)S(1)}, bf16[8,32,128]{2,1,0:T(8,128)(2,1)S(1)}, u32[]{:S(2)}, u32[]{:S(2)}) collective-permute-start(bf16[8,32,128]{2,1,0:T(8,128)(2,1)S(1)} %bitcast.29), channel_id=1, source_target_pairs={{1,2},{3,4},{5,6},{7,8},{9,10},{11,12},{13,14},{2,1},{4,3},{6,5},{... | collective-permute-start | bytes 196616 | tf_op jit(solution)/shard_map/ppermute | solution.py:761
  7.7 7.1 %collective-permute-start = (bf16[8,32,128]{2,1,0:T(8,128)(2,1)S(1)}, bf16[8,32,128]{2,1,0:T(8,128)(2,1)S(1)}, u32[]{:S(2)}, u32[]{:S(2)}) collective-permute-start(bf16[8,32,128]{2,1,0:T(8,128)(2,1)S(1)} %bitcast.30), channel_id=1, source_target_pairs={{0,1},{2,3},{4,5},{6,7},{8,9},{10,11},{12,13},{14,15},{1,0},{3,2},... | collective-permute-start | bytes 196616 | tf_op jit(solution)/shard_map/ppermute | solution.py:761
  9.1 12.9 %all-to-all-start = ((bf16[16,8,16]{2,1,0:T(8,128)(2,1)}), bf16[16,8,16]{2,1,0:T(8,128)(2,1)S(1)}, u32[]{:S(2)}, u32[]{:S(2)}) async-start(bf16[16,8,16]{2,1,0:T(8,128)(2,1)} %bitcast.26), calls=%async_computation | async-start | bytes 65536 | tf_op jit(solution)/shard_map/all_to_all | solution.py:769
  14.9 7.2 %collective-permute-start.3 = (bf16[8,88,128]{2,1,0:T(8,128)(2,1)S(1)}, bf16[8,88,128]{2,1,0:T(8,128)(2,1)S(1)}, u32[]{:S(2)}, u32[]{:S(2)}) collective-permute-start(bf16[8,88,128]{2,1,0:T(8,128)(2,1)S(1)} %pad_maximum_fusion.mid), channel_id=1, source_target_pairs={{16,32},{48,64},{80,96},{32,16},{64,48},{96,80},{17,33},{49,65},{8... | collective-permute-start | bytes 540680 | tf_op jit(solution)/shard_map/ppermute | solution.py:761
  15.6 9.3 %collective-permute-start.2 = (bf16[8,88,128]{2,1,0:T(8,128)(2,1)S(1)}, bf16[8,88,128]{2,1,0:T(8,128)(2,1)S(1)}, u32[]{:S(2)}, u32[]{:S(2)}) collective-permute-start(bf16[8,88,128]{2,1,0:T(8,128)(2,1)S(1)} %pad_maximum_fusion.mid), channel_id=1, source_target_pairs={{0,16},{32,48},{64,80},{96,112},{16,0},{48,32},{80,64},{112,96},{1... | collective-permute-start | bytes 540680 | tf_op jit(solution)/shard_map/ppermute | solution.py:761
  24.8 17.0 %copy-start = (bf16[27,128,64]{1,2,0:T(8,128)(2,1)S(1)}, bf16[27,128,64]{1,2,0:T(8,128)(2,1)}, u32[]{:S(2)}) copy-start(bf16[27,128,64]{1,2,0:T(8,128)(2,1)} %param.13) | copy-start | bytes 1327108
  30.8 7.2 %collective-permute-start.4 = (bf16[144,128]{1,0:T(8,128)(2,1)S(1)}, bf16[144,128]{1,0:T(8,128)(2,1)S(1)}, u32[]{:S(2)}, u32[]{:S(2)}) collective-permute-start(bf16[144,128]{1,0:T(8,128)(2,1)S(1)} %get-tuple-element.54), channel_id=1, source_target_pairs={{1,2},{3,4},{5,6},{7,8},{9,10},{11,12},{13,14},{2,1},{4,3},{6,5},{... | collective-permute-start | bytes 110600 | tf_op jit(solution)/shard_map/ppermute | solution.py:761
  36.4 1.6 %collective-permute-start.5 = (bf16[144,128]{1,0:T(8,128)(2,1)S(1)}, bf16[144,128]{1,0:T(8,128)(2,1)S(1)}, u32[]{:S(2)}, u32[]{:S(2)}) collective-permute-start(bf16[144,128]{1,0:T(8,128)(2,1)S(1)} %get-tuple-element.55), channel_id=1, source_target_pairs={{0,1},{2,3},{4,5},{6,7},{8,9},{10,11},{12,13},{14,15},{1,0},{3,2},... | collective-permute-start | bytes 110600 | tf_op jit(solution)/shard_map/ppermute | solution.py:761
  38.1 6.0 %collective-permute-start.6 = (bf16[304,128]{1,0:T(8,128)(2,1)S(1)}, bf16[304,128]{1,0:T(8,128)(2,1)S(1)}, u32[]{:S(2)}, u32[]{:S(2)}) collective-permute-start(bf16[304,128]{1,0:T(8,128)(2,1)S(1)} %get-tuple-element.58), channel_id=1, source_target_pairs={{16,32},{48,64},{80,96},{32,16},{64,48},{96,80},{17,33},{49,65},{8... | collective-permute-start | bytes 233480 | tf_op jit(solution)/shard_map/ppermute | solution.py:761
  38.7 5.7 %collective-permute-start.7 = (bf16[304,128]{1,0:T(8,128)(2,1)S(1)}, bf16[304,128]{1,0:T(8,128)(2,1)S(1)}, u32[]{:S(2)}, u32[]{:S(2)}) collective-permute-start(bf16[304,128]{1,0:T(8,128)(2,1)S(1)} %get-tuple-element.61), channel_id=1, source_target_pairs={{0,16},{32,48},{64,80},{96,112},{16,0},{48,32},{80,64},{112,96},{1... | collective-permute-start | bytes 233480 | tf_op jit(solution)/shard_map/ppermute | solution.py:761
  48.8 2.0 %collective-permute-start.8 = (bf16[8,152,128]{2,1,0:T(8,128)(2,1)S(1)}, bf16[8,152,128]{2,1,0:T(8,128)(2,1)S(1)}, u32[]{:S(2)}, u32[]{:S(2)}) collective-permute-start(bf16[8,152,128]{2,1,0:T(8,128)(2,1)S(1)} %get-tuple-element.73), channel_id=1, source_target_pairs={{0,1},{1,0},{2,3},{3,2},{4,5},{5,4},{6,7},{7,6},{8,9},{9,8},{10,11... | collective-permute-start | bytes 933896 | tf_op jit(solution)/shard_map/ppermute | solution.py:796
  89.3 5.1 %collective-permute-start.9 = (bf16[8,32,128]{2,1,0:T(8,128)(2,1)S(1)}, bf16[8,32,128]{2,1,0:T(8,128)(2,1)S(1)}, u32[]{:S(2)}, u32[]{:S(2)}) collective-permute-start(bf16[8,32,128]{2,1,0:T(8,128)(2,1)S(1)} %all_to_all.22.mine), channel_id=1, source_target_pairs={{0,1},{1,0},{2,3},{3,2},{4,5},{5,4},{6,7},{7,6},{8,9},{9,8},{10,11... | collective-permute-start | bytes 196616 | tf_op jit(solution)/shard_map/ppermute | solution.py:803
